TPU v7x, 32 devices: a whole 2x2x4 slice. The times are simulated.
32 devices in a mesh: wide: 8 (over y, x, core), tp: 4 (over z).
Axes of the slice: x: 2, y: 2, z: 4, core: 2. Of those that a mesh axis runs over, the one named last changes fastest.
Arguments:
- tokens: bfloat16 [17408, 2048], P(('wide', 'tp')), may hold values from -6 to 6
- out_grad: bfloat16 [17408, 2048], P(('wide', 'tp')), may hold values from -6 to 6
- seg_ids: int32 [17408], P('wide'), may hold values from 0 to 71, as said below
- parent_table: int32 [72], P('wide'), may hold values from 0 to 71, as said below
- path_pos: int32 [17408], P('wide'), may hold values from 0 to 1407, as said below
- attn_gain: bfloat16 [2048], P('wide'), may hold values from 0.099609375 to 1.8984375
- w_query: bfloat16 [2048, 2048], P('wide', 'tp'), may hold values from -0.125 to 0.125
- w_key: bfloat16 [2048, 1024], P('wide', 'tp'), may hold values from -0.125 to 0.125
- w_value: bfloat16 [2048, 1024], P('wide', 'tp'), may hold values from -0.125 to 0.125
- w_out: bfloat16 [2048, 2048], P('tp', 'wide'), may hold values from -2 to 2
- q_gain: bfloat16 [128], P('wide'), may hold values from 0.099609375 to 1.8984375
- k_gain: bfloat16 [128], P('wide'), may hold values from 0.099609375 to 1.8984375
- ffn_gain: bfloat16 [2048], P('wide'), may hold values from 0.099609375 to 1.8984375
- w_gate: bfloat16 [2048, 6144], P('wide', 'tp'), may hold values from -0.125 to 0.125
- w_up: bfloat16 [2048, 6144], P('wide', 'tp'), may hold values from -0.125 to 0.125
- w_down: bfloat16 [6144, 2048], P('tp', 'wide'), may hold values from -0.078125 to 0.078125
Outputs:
- mixed: bfloat16 [17408, 2048], P(('wide', 'tp'))
- tokens_grad: bfloat16 [17408, 2048], P(('wide', 'tp'))
- attn_gain_grad: float32 [2048], P('wide')
- w_query_grad: float32 [2048, 2048], P('wide', 'tp')
- w_key_grad: float32 [2048, 1024], P('wide', 'tp')
- w_value_grad: float32 [2048, 1024], P('wide', 'tp')
- w_out_grad: float32 [2048, 2048], P('tp', 'wide')
- q_gain_grad: float32 [128], P('wide')
- k_gain_grad: float32 [128], P('wide')
- ffn_gain_grad: float32 [2048], P('wide')
- w_gate_grad: float32 [2048, 6144], P('wide', 'tp')
- w_up_grad: float32 [2048, 6144], P('wide', 'tp')
- w_down_grad: float32 [6144, 2048], P('tp', 'wide')
Inputs may be any that keep to these rules, and one draw needn't show every extreme that they name: `seg_ids`: tokens come as whole trees of 2176: first a trunk of 1152 tokens (segment tree * 9), then 2 * 4 blocks of 128 tokens, each a segment of its own with an id of tree * 9 + 1 to tree * 9 + 2 * 4, in drawn order. `parent_table`: A trunk is its own parent; 4 blocks of each tree are branches whose parent is the trunk, the others are leaves, one under each branch. The segment tree * 9 + 2 * 4 is a branch. `path_pos`: the trunk's t-th token is at t, a branch's t-th at 1152 + t, a leaf's t-th at 1280 + t.
All inputs are finite; a program needn't handle non-finite values.
Results may differ from a plain program's by a relative error of at most 0.025.
Values may be sent and summed in bfloat16 or wider, within the bound.
A program may use at most 320 MiB of HBM per device.

v0:
```python
import jax
import jax.numpy as jnp
from jax import lax
from jax.sharding import PartitionSpec as P

HEAD_DIM = 128
TREE_TOK = 2176


norm_eps = 1e-06
rope_base = 1000000.0
masked_score = -1e30


def matmul(left, right):
    return jnp.dot(left, right, preferred_element_type=jnp.float32)


def contract_rows(left, right):
    return lax.dot_general(
        left, right, (((0,), (0,)), ((), ())), preferred_element_type=jnp.float32
    )


def against_columns(left, right):
    return lax.dot_general(
        left, right, (((1,), (1,)), ((), ())), preferred_element_type=jnp.float32
    )


def inverse_rms(values):
    return lax.rsqrt(jnp.mean(values * values, axis=-1, keepdims=True) + norm_eps)


def norm_back(grads, unit_values, inverse, gain):
    scaled = grads * gain
    return inverse * (scaled - unit_values * jnp.mean(scaled * unit_values, axis=-1, keepdims=True))


def rotary_tables(positions, head_width):
    half_width = head_width // 2
    frequency = rope_base ** (-(jnp.arange(half_width, dtype=jnp.float32) * 2.0) / head_width)
    angles = positions.astype(jnp.float32)[:, None] * frequency[None, :]
    cosine = jnp.cos(angles)
    sine_table = jnp.sin(angles)
    return (
        jnp.concatenate([cosine, cosine], axis=-1),
        jnp.concatenate([sine_table, sine_table], axis=-1),
    )


def rotate(values, cosine, sine_table):
    half_width = values.shape[-1] // 2
    turned = jnp.concatenate([-values[..., half_width:], values[..., :half_width]], axis=-1)
    return values * cosine[:, None, :] + turned * sine_table[:, None, :]


def rotate_back(grads, cosine, sine_table):
    half_width = grads.shape[-1] // 2
    scaled = grads * sine_table[:, None, :]
    turned = jnp.concatenate([scaled[..., half_width:], -scaled[..., :half_width]], axis=-1)
    return grads * cosine[:, None, :] + turned


def ancestry(seg_ids, parent_table, base):
    slot_range = jnp.arange(parent_table.shape[0], dtype=jnp.int32)
    first_hit = (seg_ids - base)[:, None] == slot_range[None, :]
    parent_ids = jnp.sum(jnp.where(first_hit, parent_table[None, :], 0), axis=1)
    second_hit = (parent_ids - base)[:, None] == slot_range[None, :]
    grand_ids = jnp.sum(jnp.where(second_hit, parent_table[None, :], 0), axis=1)
    return (parent_ids, grand_ids)


def allowed(row_seg, row_parent, row_grand, row_pos, col_seg, col_pos):
    related = (
        (col_seg[None, :] == row_seg[:, None])
        | (col_seg[None, :] == row_parent[:, None])
        | (col_seg[None, :] == row_grand[:, None])
    )
    return related & (col_pos[None, :] <= row_pos[:, None])


def local(
    tokens,
    out_grad,
    seg_ids,
    parent_table,
    path_pos,
    attn_gain,
    w_query,
    w_key,
    w_value,
    w_out,
    q_gain,
    k_gain,
    ffn_gain,
    w_gate,
    w_up,
    w_down,
):
    gathered = (
        lax.all_gather(attn_gain, "wide", axis=0, tiled=True),
        lax.all_gather(w_query, "wide", axis=0, tiled=True),
        lax.all_gather(w_key, "wide", axis=0, tiled=True),
        lax.all_gather(w_value, "wide", axis=0, tiled=True),
        lax.all_gather(w_out, "wide", axis=1, tiled=True),
        lax.all_gather(q_gain, "wide", axis=0, tiled=True),
        lax.all_gather(k_gain, "wide", axis=0, tiled=True),
        lax.all_gather(ffn_gain, "wide", axis=0, tiled=True),
        lax.all_gather(w_gate, "wide", axis=0, tiled=True),
        lax.all_gather(w_up, "wide", axis=0, tiled=True),
        lax.all_gather(w_down, "wide", axis=1, tiled=True),
    )
    all_rows = seg_ids.shape[0]
    query_heads = gathered[1].shape[1] // HEAD_DIM
    kv_heads = gathered[2].shape[1] // HEAD_DIM
    group_size = query_heads // kv_heads
    score_scale = HEAD_DIM ** (-0.5)
    block_rows = TREE_TOK // 4
    block_count = all_rows // block_rows
    base = lax.axis_index("wide") * parent_table.shape[0]
    parent_ids, grand_ids = ancestry(seg_ids, parent_table, base)
    cosine, sine_table = rotary_tables(path_pos, HEAD_DIM)
    stream = tokens.astype(jnp.float32)
    inverse_one = inverse_rms(stream)
    unit_one = stream * inverse_one
    normed_one = (unit_one * gathered[0].astype(jnp.float32)).astype(jnp.bfloat16)
    normed_all = lax.all_gather(normed_one, "tp", axis=0, tiled=True)
    query_raw = matmul(normed_all, gathered[1]).reshape(all_rows, query_heads, HEAD_DIM)
    key_raw = matmul(normed_all, gathered[2]).reshape(all_rows, kv_heads, HEAD_DIM)
    value_rows = (
        matmul(normed_all, gathered[3]).astype(jnp.bfloat16).reshape(all_rows, kv_heads, HEAD_DIM)
    )
    query_inverse = inverse_rms(query_raw)
    query_unit = query_raw * query_inverse
    key_inverse = inverse_rms(key_raw)
    key_unit = key_raw * key_inverse
    queries = rotate(query_unit * gathered[5].astype(jnp.float32), cosine, sine_table).astype(
        jnp.bfloat16
    )
    queries = queries.reshape(all_rows, kv_heads, group_size, HEAD_DIM)
    key_rows = rotate(key_unit * gathered[6].astype(jnp.float32), cosine, sine_table).astype(
        jnp.bfloat16
    )

    def block_scores(number):
        row_start = number * block_rows
        tree_start = number // 4 * TREE_TOK
        query_block = lax.dynamic_slice_in_dim(queries, row_start, block_rows, 0)
        pair_mask = allowed(
            lax.dynamic_slice_in_dim(seg_ids, row_start, block_rows, 0),
            lax.dynamic_slice_in_dim(parent_ids, row_start, block_rows, 0),
            lax.dynamic_slice_in_dim(grand_ids, row_start, block_rows, 0),
            lax.dynamic_slice_in_dim(path_pos, row_start, block_rows, 0),
            seg_ids,
            path_pos,
        )
        scores = (
            jnp.einsum("qngd,knd->ngqk", query_block, key_rows, preferred_element_type=jnp.float32)
            * score_scale
        )
        scores = jnp.where(pair_mask[None, None], scores, masked_score)
        return (scores, query_block, key_rows, value_rows, row_start, tree_start)

    def attend(number):
        scores, query_block, key_block, value_block, row_start, tree_start = block_scores(number)
        row_peak = jnp.max(scores, axis=-1, keepdims=True)
        exponent = jnp.exp(scores - row_peak)
        row_total = jnp.sum(exponent, axis=-1, keepdims=True)
        probabilities = (exponent / row_total).astype(jnp.bfloat16)
        block_out = jnp.einsum(
            "ngqk,knd->qngd", probabilities, value_block, preferred_element_type=jnp.float32
        )
        return (
            block_out.reshape(block_rows, -1).astype(jnp.bfloat16),
            (row_peak + jnp.log(row_total))[..., 0],
        )

    attended_blocks, log_sums = lax.map(attend, jnp.arange(block_count, dtype=jnp.int32))
    attended = attended_blocks.reshape(all_rows, query_heads * HEAD_DIM)
    after_attn = stream + lax.psum_scatter(
        matmul(attended, gathered[4]).astype(jnp.bfloat16), "tp", scatter_dimension=0, tiled=True
    ).astype(jnp.float32)
    inverse_two = inverse_rms(after_attn)
    unit_two = after_attn * inverse_two
    normed_two = (unit_two * gathered[7].astype(jnp.float32)).astype(jnp.bfloat16)
    normed_two_all = lax.all_gather(normed_two, "tp", axis=0, tiled=True)
    gate_act = matmul(normed_two_all, gathered[8])
    up_act = matmul(normed_two_all, gathered[9])
    sigmoid_gate = jax.nn.sigmoid(gate_act)
    silu_gate = gate_act * sigmoid_gate
    hidden = (silu_gate * up_act).astype(jnp.bfloat16)
    mixed = (
        after_attn
        + lax.psum_scatter(
            matmul(hidden, gathered[10]).astype(jnp.bfloat16), "tp", scatter_dimension=0, tiled=True
        ).astype(jnp.float32)
    ).astype(jnp.bfloat16)
    regathered = (
        lax.all_gather(attn_gain, "wide", axis=0, tiled=True),
        lax.all_gather(w_query, "wide", axis=0, tiled=True),
        lax.all_gather(w_key, "wide", axis=0, tiled=True),
        lax.all_gather(w_value, "wide", axis=0, tiled=True),
        lax.all_gather(w_out, "wide", axis=1, tiled=True),
        lax.all_gather(q_gain, "wide", axis=0, tiled=True),
        lax.all_gather(k_gain, "wide", axis=0, tiled=True),
        lax.all_gather(ffn_gain, "wide", axis=0, tiled=True),
        lax.all_gather(w_gate, "wide", axis=0, tiled=True),
        lax.all_gather(w_up, "wide", axis=0, tiled=True),
        lax.all_gather(w_down, "wide", axis=1, tiled=True),
    )
    cotangent_all = lax.all_gather(out_grad, "tp", axis=0, tiled=True)
    down_w_grad = contract_rows(hidden, cotangent_all)
    hidden_grad = against_columns(cotangent_all, regathered[10])
    gate_grad = (
        hidden_grad * up_act * sigmoid_gate * (1.0 + gate_act * (1.0 - sigmoid_gate))
    ).astype(jnp.bfloat16)
    up_grad = (hidden_grad * silu_gate).astype(jnp.bfloat16)
    gate_w_grad = contract_rows(normed_two_all, gate_grad)
    up_w_grad = contract_rows(normed_two_all, up_grad)
    normed_two_grad = lax.psum_scatter(
        (
            against_columns(gate_grad, regathered[8]) + against_columns(up_grad, regathered[9])
        ).astype(jnp.bfloat16),
        "tp",
        scatter_dimension=0,
        tiled=True,
    ).astype(jnp.float32)
    ffn_gain_part = jnp.sum(normed_two_grad * unit_two, axis=0)
    stream_grad = out_grad.astype(jnp.float32) + norm_back(
        normed_two_grad, unit_two, inverse_two, regathered[7].astype(jnp.float32)
    )
    stream_all = lax.all_gather(stream_grad.astype(jnp.bfloat16), "tp", axis=0, tiled=True)
    out_w_grad = contract_rows(attended, stream_all)
    attended_grad = against_columns(stream_all, regathered[4]).astype(jnp.bfloat16)
    attended_grad = attended_grad.reshape(all_rows, kv_heads, group_size, HEAD_DIM)

    def attend_back(carry, block_item):
        key_grads, value_grads = carry
        number, log_block = block_item
        scores, query_block, key_block, value_block, row_start, tree_start = block_scores(number)
        probabilities = jnp.exp(scores - log_block[..., None])
        grad_block = lax.dynamic_slice_in_dim(attended_grad, row_start, block_rows, 0)
        prob_grad = jnp.einsum(
            "qngd,knd->ngqk", grad_block, value_block, preferred_element_type=jnp.float32
        )
        row_delta = jnp.sum(probabilities * prob_grad, axis=-1, keepdims=True)
        score_grad = (probabilities * (prob_grad - row_delta)).astype(jnp.bfloat16)
        query_part = (
            jnp.einsum("ngqk,knd->qngd", score_grad, key_block, preferred_element_type=jnp.float32)
            * score_scale
        )
        key_part = (
            jnp.einsum(
                "ngqk,qngd->knd", score_grad, query_block, preferred_element_type=jnp.float32
            )
            * score_scale
        )
        value_part = jnp.einsum(
            "ngqk,qngd->knd",
            probabilities.astype(jnp.bfloat16),
            grad_block,
            preferred_element_type=jnp.float32,
        )
        key_grads = key_grads + key_part
        value_grads = value_grads + value_part
        return ((key_grads, value_grads), query_part)

    empty_grads = jnp.zeros((all_rows, kv_heads, HEAD_DIM), jnp.float32)
    (key_grads, value_grads), query_parts = lax.scan(
        attend_back,
        (empty_grads, empty_grads),
        (jnp.arange(block_count, dtype=jnp.int32), log_sums),
    )
    query_unit_grad = rotate_back(
        query_parts.reshape(all_rows, query_heads, HEAD_DIM), cosine, sine_table
    )
    key_unit_grad = rotate_back(key_grads, cosine, sine_table)
    q_gain_part = jnp.sum(query_unit_grad * query_unit, axis=(0, 1))
    k_gain_part = jnp.sum(key_unit_grad * key_unit, axis=(0, 1))
    query_raw_grad = (
        norm_back(query_unit_grad, query_unit, query_inverse, regathered[5].astype(jnp.float32))
        .astype(jnp.bfloat16)
        .reshape(all_rows, -1)
    )
    key_raw_grad = (
        norm_back(key_unit_grad, key_unit, key_inverse, regathered[6].astype(jnp.float32))
        .astype(jnp.bfloat16)
        .reshape(all_rows, -1)
    )
    value_low = value_grads.astype(jnp.bfloat16).reshape(all_rows, -1)
    query_w_grad = contract_rows(normed_all, query_raw_grad)
    key_w_grad = contract_rows(normed_all, key_raw_grad)
    value_w_grad = contract_rows(normed_all, value_low)
    normed_one_grad = lax.psum_scatter(
        (
            against_columns(query_raw_grad, regathered[1])
            + against_columns(key_raw_grad, regathered[2])
            + against_columns(value_low, regathered[3])
        ).astype(jnp.bfloat16),
        "tp",
        scatter_dimension=0,
        tiled=True,
    ).astype(jnp.float32)
    attn_gain_part = jnp.sum(normed_one_grad * unit_one, axis=0)
    tokens_grad = (
        stream_grad
        + norm_back(normed_one_grad, unit_one, inverse_one, regathered[0].astype(jnp.float32))
    ).astype(jnp.bfloat16)
    gain_sums = lax.psum((attn_gain_part, q_gain_part, k_gain_part, ffn_gain_part), "tp")
    shares = (
        lax.psum_scatter(
            gain_sums[0].astype(jnp.bfloat16), "wide", scatter_dimension=0, tiled=True
        ).astype(jnp.float32),
        lax.psum_scatter(
            query_w_grad.astype(jnp.bfloat16), "wide", scatter_dimension=0, tiled=True
        ).astype(jnp.float32),
        lax.psum_scatter(
            key_w_grad.astype(jnp.bfloat16), "wide", scatter_dimension=0, tiled=True
        ).astype(jnp.float32),
        lax.psum_scatter(
            value_w_grad.astype(jnp.bfloat16), "wide", scatter_dimension=0, tiled=True
        ).astype(jnp.float32),
        lax.psum_scatter(
            out_w_grad.astype(jnp.bfloat16), "wide", scatter_dimension=1, tiled=True
        ).astype(jnp.float32),
        lax.psum_scatter(
            gain_sums[1].astype(jnp.bfloat16), "wide", scatter_dimension=0, tiled=True
        ).astype(jnp.float32),
        lax.psum_scatter(
            gain_sums[2].astype(jnp.bfloat16), "wide", scatter_dimension=0, tiled=True
        ).astype(jnp.float32),
        lax.psum_scatter(
            gain_sums[3].astype(jnp.bfloat16), "wide", scatter_dimension=0, tiled=True
        ).astype(jnp.float32),
        lax.psum_scatter(
            gate_w_grad.astype(jnp.bfloat16), "wide", scatter_dimension=0, tiled=True
        ).astype(jnp.float32),
        lax.psum_scatter(
            up_w_grad.astype(jnp.bfloat16), "wide", scatter_dimension=0, tiled=True
        ).astype(jnp.float32),
        lax.psum_scatter(
            down_w_grad.astype(jnp.bfloat16), "wide", scatter_dimension=1, tiled=True
        ).astype(jnp.float32),
    )
    return (
        mixed,
        tokens_grad,
        shares[0],
        shares[1],
        shares[2],
        shares[3],
        shares[4],
        shares[5],
        shares[6],
        shares[7],
        shares[8],
        shares[9],
        shares[10],
    )


def solution(mesh):
    placed = (
        P(("wide", "tp"), None),
        P(("wide", "tp"), None),
        P("wide"),
        P("wide"),
        P("wide"),
        P("wide"),
        P("wide", "tp"),
        P("wide", "tp"),
        P("wide", "tp"),
        P("tp", "wide"),
        P("wide"),
        P("wide"),
        P("wide"),
        P("wide", "tp"),
        P("wide", "tp"),
        P("tp", "wide"),
    )
    return jax.shard_map(
        local,
        mesh=mesh,
        in_specs=placed,
        out_specs=(
            P(("wide", "tp"), None),
            P(("wide", "tp"), None),
            P("wide"),
            P("wide", "tp"),
            P("wide", "tp"),
            P("wide", "tp"),
            P("tp", "wide"),
            P("wide"),
            P("wide"),
            P("wide"),
            P("wide", "tp"),
            P("wide", "tp"),
            P("tp", "wide"),
        ),
        check_vma=False,
    )
```

profile of v0, /device:TPU:0, one launch (start us, length us, event | category | flops | bytes accessed | tf_op | source)
XLA Modules:
  0.0 2205.8 jit_solution(3504003605035257773)
XLA Ops:
  8.6 10.3 all-gather
  29.3 13.2 all-reduce.8
  49.4 147.2 %all-gather.14.cloned.1.call-done = bf16[2176,2048]{1,0:T(8,128)(2,1)} async-done(((bf16[544,2048]{1,0:T(8,128)(2,1)}), bf16[2176,2048]{1,0:T(8,128)(2,1)}) %all-gather.14.cloned.1.call-update) | async-done | bytes 8912912 | tf_op jit(solution)/shard_map/all_gather | solution.py:128
  206.2 14.0 all-gather.18.cloned.1.call-done
  232.1 17.8 all-gather.16.cloned.1.call-done
  249.9 10.6 multiply_reduce_fusion.3
  288.2 88.8 %while.27 = (s32[]{:T(128)}, bf16[4,544,512]{2,1,0:T(8,128)(2,1)}, f32[4,2,2,544]{3,2,1,0:T(2,128)}, s32[2176]{0:T(1024)S(1)}, s32[4]{0:T(128)S(1)}, /*index=5*/...) while((s32[]{:T(128)}, bf16[4,544,512]{2,1,0:T(8,128)(2,1)}, ...), condition=%wide.region_8.9_spmd, body=%wide.region_5.8_spmd.sunk | while | flops 2489690112 | bytes 68354272 | solution.py:179
  377.1 11.3 convolution_convert_fusion.1
  398.1 143.3 %reduce-scatter.12.cloned.1.call-done = bf16[544,2048]{1,0:T(8,128)(2,1)} async-done(((bf16[2176,2048]{1,0:T(8,128)(2,1)}), bf16[544,2048]{1,0:T(8,128)(2,1)}) %reduce-scatter.12.cloned.1.call-update) | async-done | bytes 2228240 | tf_op jit(solution)/shard_map/reduce_scatter | solution.py:181
  549.2 40.6 %all-gather.28.cloned.1.call-done = bf16[2048,1536]{1,0:T(8,128)(2,1)} async-done(((bf16[256,1536]{1,0:T(8,128)(2,1)}), bf16[2048,1536]{1,0:T(8,128)(2,1)}) %all-gather.28.cloned.1.call-update) | async-done | bytes 6291472 | tf_op jit(solution)/shard_map/all_gather | solution.py:111
  589.7 160.4 %all-gather.24.cloned.1.call-done = bf16[2176,2048]{1,0:T(8,128)(2,1)} async-done(((bf16[544,2048]{1,0:T(8,128)(2,1)}), bf16[2176,2048]{1,0:T(8,128)(2,1)}) %all-gather.24.cloned.1.call-update) | async-done | bytes 8912912 | tf_op jit(solution)/shard_map/all_gather | solution.py:187
  750.1 20.1 fusion.74
  770.3 25.5 %all-gather.26.cloned.1.call-done = bf16[2048,1536]{1,0:T(8,128)(2,1)} async-done(((bf16[256,1536]{1,0:T(8,128)(2,1)}), bf16[2048,1536]{1,0:T(8,128)(2,1)}) %all-gather.26.cloned.1.call-update) | async-done | bytes 6291472 | tf_op jit(solution)/shard_map/all_gather | solution.py:110
  795.8 19.8 fusion.73
  815.6 28.6 %all-gather.30.cloned.1.call-done = bf16[1536,2048]{1,0:T(8,128)(2,1)} async-done(((bf16[1536,256]{1,0:T(8,128)(2,1)}), bf16[1536,2048]{1,0:T(8,128)(2,1)}) %all-gather.30.cloned.1.call-update) | async-done | bytes 6291472 | tf_op jit(solution)/shard_map/all_gather | solution.py:112
  844.2 159.8 %all-gather.32.cloned.1.call-done = bf16[2176,2048]{1,0:T(8,128)(2,1)} async-done(((bf16[544,2048]{1,0:T(8,128)(2,1)}), bf16[2176,2048]{1,0:T(8,128)(2,1)}) %all-gather.32.cloned.1.call-update) | async-done | bytes 8912912 | tf_op jit(solution)/shard_map/all_gather | solution.py:212
  1004.0 31.4 %multiply_convert_fusion = (bf16[2176,1536]{1,0:T(8,128)(2,1)}, bf16[2176,1536]{1,0:T(8,128)(2,1)}, bf16[2176,1536]{1,0:T(8,128)(2,1)}) fusion(f32[2176,1536]{1,0:T(8,128)} %fusion.73, f32[2176,1536]{1,0:T(8,128)} %fusion.74, bf16[2176,2048]{1,0:T(8,128)(2,1)} %all-gather.32.cloned.1.call-done, bf16[1536,2048]{1,0:T(8,128)(2,1)} %all-gather.30.cloned.1.call-done), kind=kOutput, calls=%fused_computation.53 | convolution fusion | flops 13740343296 | bytes 61997056 | tf_op jit(solution)/shard_map/dot_general | solution.py:26
  1035.4 20.6 fusion.75
  1055.9 22.9 %add_convert_fusion.1 = bf16[2176,2048]{1,0:T(8,128)(2,1)} fusion(f32[2176,2048]{1,0:T(8,128)} %fusion.75, bf16[2176,1536]{1,0:T(8,128)(2,1)} %get-tuple-element.368, bf16[2048,1536]{1,0:T(8,128)(2,1)} %all-gather.28.cloned.1.call-done), kind=kOutput, calls=%fused_computation.52 | convolution fusion | flops 13699121152 | bytes 39714816 | tf_op jit(solution)/shard_map/dot_general | solution.py:26
  1078.9 151.0 %reduce-scatter.16.cloned.1.call-done = bf16[544,2048]{1,0:T(8,128)(2,1)} async-done(((bf16[2176,2048]{1,0:T(8,128)(2,1)}), bf16[544,2048]{1,0:T(8,128)(2,1)}) %reduce-scatter.16.cloned.1.call-update) | async-done | bytes 2228240 | tf_op jit(solution)/shard_map/reduce_scatter | solution.py:221
  1239.2 20.4 convolution_convert_fusion.2
  1259.7 20.3 convolution_convert_fusion.3
  1295.6 20.3 convolution_convert_fusion.4
  1315.9 82.4 %all-gather.34.cloned.1.call-done = bf16[2176,2048]{1,0:T(8,128)(2,1)} async-done(((bf16[544,2048]{1,0:T(8,128)(2,1)}), bf16[2176,2048]{1,0:T(8,128)(2,1)}) %all-gather.34.cloned.1.call-update) | async-done | bytes 8912912 | tf_op jit(solution)/shard_map/all_gather | solution.py:233
  1398.4 9.9 convolution_convert_fusion.5
  1413.0 285.1 %while.28 = (s32[]{:T(128)}, f32[2176,2,128]{0,2,1:T(8,128)}, f32[2176,2,128]{0,2,1:T(8,128)}, f32[4,544,2,2,128]{4,1,3,2,0:T(8,128)}, s32[4]{0:T(128)S(1)}, /*i...) while((s32[]{:T(128)}, f32[2176,2,128]{0,2,1:T(8,128)}, ...), condition=%wide.region_16.17_spmd.clone, body=%wide.region_14.16_spmd.clone.sunk | while | flops 6114732032 | bytes 278197632 | solution.py:270
  1418.7 11.0 fusion.150
  1429.7 17.2 fusion.151
  1446.9 17.3 fusion.152
  1491.6 10.2 fusion.150
  1501.8 17.1 fusion.151
  1518.9 16.7 fusion.152
  1563.5 10.2 fusion.150
  1573.6 17.3 fusion.151
  1590.9 16.6 fusion.152
  1633.6 10.2 fusion.150
  1643.7 17.1 fusion.151
  1660.8 16.6 fusion.152
  1762.3 9.4 convolution_convert_fusion.7
  1771.9 9.8 multiply_reduce_fusion
  1802.5 10.4 convolution_convert_fusion.8
  1813.1 10.1 fusion.77
  1831.8 16.9 add_convert_fusion
  1849.0 19.5 convolution_convert_fusion
  1884.2 149.1 %reduce-scatter.18.cloned.1.call-done = bf16[544,2048]{1,0:T(8,128)(2,1)} async-done(((bf16[2176,2048]{1,0:T(8,128)(2,1)}), bf16[544,2048]{1,0:T(8,128)(2,1)}) %reduce-scatter.18.cloned.1.call-update) | async-done | bytes 2228240 | tf_op jit(solution)/shard_map/reduce_scatter | solution.py:295
  2036.5 19.2 all-reduce.6
  2055.7 12.4 all-reduce.7
  2070.5 119.8 %reduce-scatter.14.cloned.1.call-done = bf16[544,2048]{1,0:T(8,128)(2,1)} async-done(((bf16[2176,2048]{1,0:T(8,128)(2,1)}), bf16[544,2048]{1,0:T(8,128)(2,1)}) %reduce-scatter.14.cloned.1.call-update) | async-done | bytes 2228240 | tf_op jit(solution)/shard_map/reduce_scatter | solution.py:195
  (412 shorter events, 426.5 us)
Async XLA Ops:
  7.2 42.3 %all-gather.20.cloned.1.call-start = ((), (), s32[]{:S(2)}) async-start(), calls=%async_computation.14 | async-start | bytes 1179648 | tf_op jit(solution)/shard_map/all_gather | solution.py:105
  7.9 188.7 %all-gather.14.cloned.1.call-start = ((), (), s32[]{:S(2)}) async-start(), calls=%async_computation.11 | async-start | bytes 11141120 | tf_op jit(solution)/shard_map/all_gather | solution.py:128
  19.0 23.5 %copy-start.31 = (s32[2176]{0:T(1024)S(1)}, s32[2176]{0:T(1024)}, u32[]{:S(2)}) copy-start(s32[2176]{0:T(1024)} %param.24) | copy-start | bytes 26116
  19.0 23.5 %copy-start.29 = (s32[2176]{0:T(1024)S(1)}, s32[2176]{0:T(1024)}, u32[]{:S(2)}) copy-start(s32[2176]{0:T(1024)} %param.22) | copy-start | bytes 26116
  19.0 23.5 %copy-start.66 = (s32[9]{0:T(128)S(1)}, s32[9]{0:T(128)}, u32[]{:S(2)}) copy-start(s32[9]{0:T(128)} %param.23) | copy-start | bytes 112
  25.5 194.7 %all-gather.18.cloned.1.call-start = ((), (), s32[]{:S(2)}) async-start(), calls=%async_computation.13 | async-start | bytes 1179648 | tf_op jit(solution)/shard_map/all_gather | solution.py:104
  26.2 223.7 %all-gather.16.cloned.1.call-start = ((), (), s32[]{:S(2)}) async-start(), calls=%async_computation.12 | async-start | bytes 2359296 | tf_op jit(solution)/shard_map/all_gather | solution.py:103
  26.8 350.3 %all-gather.22.cloned.1.call-start = ((), (), s32[]{:S(2)}) async-start(), calls=%async_computation.15 | async-start | bytes 2359296 | tf_op jit(solution)/shard_map/all_gather | solution.py:106
  27.4 514.0 %reduce-scatter.12.cloned.1.call-start = ((), (), s32[]{:S(2)}) async-start(), calls=%async_computation.16 | async-start | bytes 11141120 | tf_op jit(solution)/shard_map/reduce_scatter | solution.py:181
  27.4 20.3 copy-start.64
  42.5 238.4 %copy-start.58 = (f32[128]{0:T(128)}, f32[128]{0:T(128)S(1)}, u32[]{:S(2)}) copy-start(f32[128]{0:T(128)S(1)} %convert_element_type.190) | copy-start | bytes 1540
  42.5 184.8 %copy-start.62 = (f32[128]{0:T(128)}, f32[128]{0:T(128)S(1)}, u32[]{:S(2)}) copy-start(f32[128]{0:T(128)S(1)} %convert_element_type.193) | copy-start | bytes 1540
  47.3 156.7 %copy-start.21 = (f32[2176,128]{1,0:T(8,128)}, f32[2176,128]{1,0:T(8,128)S(1)}, u32[]{:S(2)}) copy-start(f32[2176,128]{1,0:T(8,128)S(1)} %get-tuple-element.389) | copy-start | bytes 3342340
  47.3 233.5 %copy-start.17 = (f32[2176,128]{1,0:T(8,128)}, f32[2176,128]{1,0:T(8,128)S(1)}, u32[]{:S(2)}) copy-start(f32[2176,128]{1,0:T(8,128)S(1)} %get-tuple-element.390) | copy-start | bytes 3342340
  47.7 179.6 %copy-start.19 = (f32[2176,128]{0,1:T(8,128)}, f32[2176,128]{0,1:T(8,128)S(1)}, u32[]{:S(2)}) copy-start(f32[2176,128]{0,1:T(8,128)S(1)} %copy.87) | copy-start | bytes 3342340
  388.4 153.0 %copy-start.3 = (bf16[544,2048]{1,0:T(8,128)(2,1)S(1)}, bf16[544,2048]{1,0:T(8,128)(2,1)}, u32[]{:S(2)}) copy-start(bf16[544,2048]{1,0:T(8,128)(2,1)} %param.20) | copy-start | bytes 6684676
  388.4 201.3 %all-gather.28.cloned.1.call-start = ((), (), s32[]{:S(2)}) async-start(), calls=%async_computation.19 | async-start | bytes 7077888 | tf_op jit(solution)/shard_map/all_gather | solution.py:111
  389.2 361.0 %all-gather.24.cloned.1.call-start = ((), (), s32[]{:S(2)}) async-start(), calls=%async_computation.17 | async-start | bytes 11141120 | tf_op jit(solution)/shard_map/all_gather | solution.py:187
  398.1 149.0 %copy-start.42 = (f32[8,1,256]{2,1,0:T(1,128)}, f32[8,1,256]{2,1,0:T(1,128)S(1)}, u32[]{:S(2)}) copy-start(f32[8,1,256]{2,1,0:T(1,128)S(1)} %convert_element_type.240) | copy-start | bytes 24580
  547.1 248.7 %all-gather.26.cloned.1.call-start = ((), (), s32[]{:S(2)}) async-start(), calls=%async_computation.18 | async-start | bytes 7077888 | tf_op jit(solution)/shard_map/all_gather | solution.py:110
  547.8 296.4 %all-gather.30.cloned.1.call-start = ((), (), s32[]{:S(2)}) async-start(), calls=%async_computation.20 | async-start | bytes 7077888 | tf_op jit(solution)/shard_map/all_gather | solution.py:112
  548.4 455.6 %all-gather.32.cloned.1.call-start = ((), (), s32[]{:S(2)}) async-start(), calls=%async_computation.22 | async-start | bytes 11141120 | tf_op jit(solution)/shard_map/all_gather | solution.py:212
  549.1 680.8 %reduce-scatter.16.cloned.1.call-start = ((), (), s32[]{:S(2)}) async-start(), calls=%async_computation.23 | async-start | bytes 11141120 | tf_op jit(solution)/shard_map/reduce_scatter | solution.py:221
  1078.9 151.1 %copy-start.4 = (bf16[544,2048]{1,0:T(8,128)(2,1)S(1)}, bf16[544,2048]{1,0:T(8,128)(2,1)}, u32[]{:S(2)}) copy-start(bf16[544,2048]{1,0:T(8,128)(2,1)} %param.20) | copy-start | bytes 6684676
  1078.9 151.1 %copy-start.43 = (f32[8,1,256]{2,1,0:T(1,128)S(1)}, f32[8,1,256]{2,1,0:T(1,128)}, u32[]{:S(2)}) copy-start(f32[8,1,256]{2,1,0:T(1,128)} %copy-done.42) | copy-start | bytes 24580
  1078.9 151.1 %copy-start.51 = (f32[544]{0:T(1024)S(1)}, f32[544]{0:T(1024)}, u32[]{:S(2)}) copy-start(f32[544]{0:T(1024)} %copy-done.50) | copy-start | bytes 6532
  1078.9 319.5 %all-gather.34.cloned.1.call-start = ((), (), s32[]{:S(2)}) async-start(), calls=%async_computation.24 | async-start | bytes 11141120 | tf_op jit(solution)/shard_map/all_gather | solution.py:233
  1239.1 630.7 %reduce-scatter.32.cloned.1.call-start = ((), (), s32[]{:S(2)}) async-start(), calls=%async_computation.32 | async-start | bytes 7077888 | tf_op jit(solution)/shard_map/reduce_scatter | solution.py:342
  1259.6 612.8 %reduce-scatter.30.cloned.1.call-start = ((), (), s32[]{:S(2)}) async-start(), calls=%async_computation.31 | async-start | bytes 7077888 | tf_op jit(solution)/shard_map/reduce_scatter | solution.py:339
  1280.0 594.9 %reduce-scatter.28.cloned.1.call-start = ((), (), s32[]{:S(2)}) async-start(), calls=%async_computation.30 | async-start | bytes 7077888 | tf_op jit(solution)/shard_map/reduce_scatter | solution.py:336
  1315.9 82.5 %copy-start.69 = (bf16[512,2048]{1,0:T(8,128)(2,1)S(1)}, bf16[512,2048]{1,0:T(8,128)(2,1)}, u32[]{:S(2)}) copy-start(bf16[512,2048]{1,0:T(8,128)(2,1)} %all-gather.22.cloned.1.call-done) | copy-start | bytes 6291460
  1315.9 561.5 %reduce-scatter.24.cloned.1.call-start = ((), (), s32[]{:S(2)}) async-start(), calls=%async_computation.28 | async-start | bytes 1179648 | tf_op jit(solution)/shard_map/reduce_scatter | solution.py:321
  1446.9 21.3 copy-start
  1518.9 22.2 %copy-start = (f32[2,2,544,2176]{3,2,1,0:T(8,128)S(1)}, f32[2,2,544,2176]{3,2,1,0:T(8,128)}, u32[]{:S(2)}) copy-start(f32[2,2,544,2176]{3,2,1,0:T(8,128)} %get-tuple-element.549) | copy-start | bytes 56819716 | tf_op jit(solution)/shard_map/while
  1590.9 20.7 copy-start
  1660.8 20.6 copy-start
  1714.4 164.6 %reduce-scatter.22.cloned.1.call-start = ((), (), s32[]{:S(2)}) async-start(), calls=%async_computation.27 | async-start | bytes 1179648 | tf_op jit(solution)/shard_map/reduce_scatter | solution.py:318
  1729.8 150.9 %reduce-scatter.26.cloned.1.call-start = ((), (), s32[]{:S(2)}) async-start(), calls=%async_computation.29 | async-start | bytes 2359296 | tf_op jit(solution)/shard_map/reduce_scatter | solution.py:324
  1771.8 110.6 %reduce-scatter.20.cloned.1.call-start = ((), (), s32[]{:S(2)}) async-start(), calls=%async_computation.26 | async-start | bytes 2359296 | tf_op jit(solution)/shard_map/reduce_scatter | solution.py:315
  1812.9 220.5 %reduce-scatter.18.cloned.1.call-start = ((), (), s32[]{:S(2)}) async-start(), calls=%async_computation.25 | async-start | bytes 11141120 | tf_op jit(solution)/shard_map/reduce_scatter | solution.py:295
  1848.7 341.5 %reduce-scatter.14.cloned.1.call-start = ((), (), s32[]{:S(2)}) async-start(), calls=%async_computation.21 | async-start | bytes 11141120 | tf_op jit(solution)/shard_map/reduce_scatter | solution.py:195
  1869.8 163.5 %copy-start.5 = (bf16[544,2048]{1,0:T(8,128)(2,1)S(1)}, bf16[544,2048]{1,0:T(8,128)(2,1)}, u32[]{:S(2)}) copy-start(bf16[544,2048]{1,0:T(8,128)(2,1)} %param.20) | copy-start | bytes 6684676
  1869.8 163.5 %copy-start.47 = (f32[8,1,256]{2,1,0:T(1,128)S(1)}, f32[8,1,256]{2,1,0:T(1,128)}, u32[]{:S(2)}) copy-start(f32[8,1,256]{2,1,0:T(1,128)} %copy-done.46) | copy-start | bytes 24580
  1869.8 163.5 %copy-start.54 = (f32[544]{0:T(1024)S(1)}, f32[544]{0:T(1024)}, u32[]{:S(2)}) copy-start(f32[544]{0:T(1024)} %copy-done.53) | copy-start | bytes 6532
  1874.9 161.6 %copy-start.57 = (f32[2048]{0:T(1024)S(1)}, f32[2048]{0:T(1024)}, u32[]{:S(2)}) copy-start(f32[2048]{0:T(1024)} %get-tuple-element.297) | copy-start | bytes 24580
  1874.9 315.4 %copy-start.44 = (f32[8,1,256]{2,1,0:T(1,128)S(1)}, f32[8,1,256]{2,1,0:T(1,128)}, u32[]{:S(2)}) copy-start(f32[8,1,256]{2,1,0:T(1,128)} %copy-done.42) | copy-start | bytes 24580
  1874.9 315.4 %copy-start.52 = (f32[544]{0:T(1024)S(1)}, f32[544]{0:T(1024)}, u32[]{:S(2)}) copy-start(f32[544]{0:T(1024)} %copy-done.50) | copy-start | bytes 6532
  1874.9 315.4 %copy-start.56 = (f32[544]{0:T(1024)S(1)}, f32[544]{0:T(1024)}, u32[]{:S(2)}) copy-start(f32[544]{0:T(1024)} %copy-done.55) | copy-start | bytes 6532
  (59 other events, 343.7 us)
Sparse Core Ops, SparseCore 0:
  9.9 26.3 all-gather.19
  38.4 158.1 all-gather.13
  198.5 21.6 all-gather.17
  221.9 27.8 all-gather.15
  251.6 28.1 all-gather.21
  388.5 152.8 reduce-scatter.11
  543.3 46.4 all-gather.27
  591.9 158.1 all-gather.23
  752.0 43.7 all-gather.25
  797.5 46.6 all-gather.29
  845.8 158.1 all-gather.31
  1079.0 150.9 reduce-scatter.15
  1239.2 159.1 all-gather.33
  1401.6 59.9 reduce-scatter.31
  1465.2 61.7 reduce-scatter.29
  1530.2 61.7 reduce-scatter.27
  1714.5 34.1 reduce-scatter.23
  1752.1 36.0 reduce-scatter.21
  1791.9 41.1 reduce-scatter.25
  1836.8 41.2 reduce-scatter.19
  1880.6 152.7 reduce-scatter.17
  2035.8 154.3 reduce-scatter.13
where the time goes:
time: 2220 us; the launch traced here: 2210 us
  waiting for transfers between devices  1240 us (56%)
  matrix products  530 us (24%)
  other arithmetic  221 us (10%)
  local copies, waits for them, and re-layouts  121 us (5%)
  blocking collectives  63.9 us (3%)
    all_gather x1, waiting for transfers between devices, local(): normed_two_all = lax.all_gather(normed_two, 'tp', axis=0, tiled=True)  160 us
    all_gather x1, waiting for transfers between devices, local(): cotangent_all = lax.all_gather(out_grad, 'tp', axis=0, tiled=True)  160 us
    reduce_scatter x1, waiting for transfers between devices, local(): lax.psum_scatter((against_columns(gate_grad, regathered[8]) + against_col...  151 us
    reduce_scatter x1, waiting for transfers between devices, local(): lax.psum_scatter((against_columns(query_raw_grad, regathered[1]) + agains...  149 us
    all_gather x1, waiting for transfers between devices, local(): normed_all = lax.all_gather(normed_one, 'tp', axis=0, tiled=True)  147 us
    reduce_scatter x1, waiting for transfers between devices, local(): lax.psum_scatter(matmul(attended, gathered[4]).astype(jnp.bfloat16), 'tp'...  143 us
    dot_general x7, matrix products, against_columns(): lax.dot_general(left, right, (((1,), (1,)), ((), ())), preferred_element_...  120 us
    reduce_scatter x1, waiting for transfers between devices, local(): lax.psum_scatter(matmul(hidden, gathered[10]).astype(jnp.bfloat16), 'tp',...  120 us
  transfers between devices with their start and end apart: 22, of which 13 were waited for; matrix products, arithmetic and copies ran while one was open for 34% of the time, Pallas kernels for 0%

commit v1 on v0

v1 whole, which is shorter than its diff:
```python
import functools
import math

import jax
import jax.numpy as jnp
from jax import lax
from jax.experimental import pallas as pl
from jax.experimental.pallas import tpu as pltpu
from jax.sharding import PartitionSpec as P

HEAD_DIM = 128
TRUNK = 1152
BRANCH = 128
FORKS2 = 8
TREE_TOK = 2176
GROUP = 2

norm_eps = 1e-06
rope_base = 1000000.0
score_scale = HEAD_DIM ** (-0.5)
key_scale = score_scale * math.log2(math.e)
LN2 = math.log(2.0)
VMEM = 52 * 1024 * 1024

f32 = jnp.float32
bf16 = jnp.bfloat16


def dot_nn(a, b):
    return lax.dot_general(a, b, (((1,), (0,)), ((), ())), preferred_element_type=f32)


def dot_nt(a, b):
    return lax.dot_general(a, b, (((1,), (1,)), ((), ())), preferred_element_type=f32)


def contract_rows(a, b):
    return lax.dot_general(a, b, (((0,), (0,)), ((), ())), preferred_element_type=f32)


def params():
    return pltpu.CompilerParams(vmem_limit_bytes=VMEM)


def cost(flops, nbytes):
    return pl.CostEstimate(flops=int(flops), bytes_accessed=int(nbytes), transcendentals=0)


def nbytes(arrays):
    return sum(a.size * a.dtype.itemsize for a in arrays)


def offsets(pieces):
    offs, at = [], 0
    for piece in pieces:
        offs.append((at, piece.shape[0]))
        at += piece.shape[0]
    return offs


class Tiles:
    def __init__(self, first, rest, quarters, parts, base, per, width):
        self.first, self.rest = list(first), list(rest) if quarters > 1 else []
        self.quarters, self.parts, self.base, self.per, self.width = quarters, parts, base, per, width
        self.offs = offsets(self.first)
        self.steps = quarters * parts

    def arrays(self):
        return self.first + self.rest

    def scratch(self):
        depth = sum(r for _, r in self.offs)
        return [
            pltpu.VMEM((2, depth, self.width), bf16),
            pltpu.SemaphoreType.DMA((2, len(self.offs))),
        ]

    def fetch(self, refs, buf, sems, step):
        first, rest = refs[: len(self.first)], refs[len(self.first) :]
        slot = lax.rem(step, 2)
        quarter = lax.div(step, self.parts)
        part = step - quarter * self.parts

        def begin(group, tile):
            col = pl.multiple_of(tile * self.width, 128)
            for k, (at, r) in enumerate(self.offs):
                pltpu.make_async_copy(
                    group[k].at[:, pl.ds(col, self.width)],
                    buf.at[slot, pl.ds(at, r), :],
                    sems.at[slot, k],
                ).start()

        if not rest:
            begin(first, self.base + part)
        else:

            @pl.when(quarter == 0)
            def _():
                begin(first, self.base + part)

            @pl.when(quarter > 0)
            def _():
                begin(rest, (quarter - 1) * self.per + self.base + part)

    def wait(self, refs, buf, sems, step):
        slot = lax.rem(step, 2)
        for k, (at, r) in enumerate(self.offs):
            pltpu.make_async_copy(
                refs[k].at[:, pl.ds(0, self.width)], buf.at[slot, pl.ds(at, r), :], sems.at[slot, k]
            ).wait()
        return slot


def tiled_call(body, sets, ins, in_specs, out_shape, out_specs, scratch, flops):
    steps = sets[0].steps
    counts = [len(s.arrays()) for s in sets]
    n_in, n_out = len(ins), len(out_shape)

    def kernel(*refs):
        at = 0
        piece_refs = []
        for c in counts:
            piece_refs.append(refs[at : at + c])
            at += c
        in_refs = refs[at : at + n_in]
        at += n_in
        out_refs = refs[at : at + n_out]
        at += n_out
        bufs = [(refs[at + 2 * i], refs[at + 2 * i + 1]) for i in range(len(sets))]
        own = refs[at + 2 * len(sets) :]
        step = pl.program_id(0)

        @pl.when(step == 0)
        def _():
            for s, p, (buf, sems) in zip(sets, piece_refs, bufs):
                s.fetch(p, buf, sems, step)

        @pl.when(step + 1 < steps)
        def _():
            for s, p, (buf, sems) in zip(sets, piece_refs, bufs):
                s.fetch(p, buf, sems, step + 1)

        tiles = []
        for s, p, (buf, sems) in zip(sets, piece_refs, bufs):
            slot = s.wait(p, buf, sems, step)
            tiles.append(buf.at[slot])
        body(step, tiles, in_refs, out_refs, own)

    weights = [a for s in sets for a in s.arrays()]
    return pl.pallas_call(
        kernel,
        grid=(steps,),
        in_specs=[pl.BlockSpec(memory_space=pl.ANY)] * len(weights) + in_specs,
        out_specs=out_specs,
        out_shape=out_shape,
        scratch_shapes=[x for s in sets for x in s.scratch()] + scratch,
        compiler_params=params(),
        cost_estimate=cost(flops, nbytes(weights) + nbytes(ins) + nbytes(out_shape)),
    )(*weights, *ins)


def whole(array):
    return pl.BlockSpec(array.shape, lambda t: (0,) * len(array.shape))


def head_slices(width):
    return [slice(h * HEAD_DIM, (h + 1) * HEAD_DIM) for h in range(width // HEAD_DIM)]


def project_qkv(normed, tiles, cosine, sine, q_gain, k_gain):
    rows, tw = normed.shape[0], tiles.width

    def body(step, weights, ins, outs, own):
        a, cos_ref, sin_ref, qg, kg = ins
        hat, raw = outs
        acc = dot_nn(a[...], weights[0][...])

        def turned(x, gain):
            inverse = lax.rsqrt(jnp.mean(x * x, axis=-1, keepdims=True) + norm_eps)
            u = x * inverse * gain
            return u * cos_ref[...] + pltpu.roll(u, HEAD_DIM // 2, 1) * sin_ref[...]

        @pl.when(step == 0)
        def _():
            for cut in head_slices(tw):
                hat[:, cut] = turned(acc[:, cut], qg[...]).astype(bf16)
            raw[...] = acc.astype(bf16)

        @pl.when(step == 1)
        def _():
            for cut in head_slices(tw // 2):
                hat[:, cut] = (turned(acc[:, cut], kg[...]) * key_scale).astype(bf16)
            hat[:, tw // 2 :] = acc[:, tw // 2 :].astype(bf16)
            raw[...] = acc.astype(bf16)

    ins = [normed, cosine, sine, q_gain, k_gain]
    shape = jax.ShapeDtypeStruct((rows, 2 * tw), bf16)
    return tiled_call(
        body,
        [tiles],
        ins,
        [whole(x) for x in ins],
        [shape, shape],
        [pl.BlockSpec((rows, tw), lambda t: (0, t))] * 2,
        [],
        4 * rows * normed.shape[1] * tw,
    )


def project_rows(a, tiles, out_dtype=bf16):
    rows, tw = a.shape[0], tiles.width

    def body(step, weights, ins, outs, own):
        outs[0][...] = dot_nn(ins[0][...], weights[0][...]).astype(out_dtype)

    return tiled_call(
        body,
        [tiles],
        [a],
        [whole(a)],
        [jax.ShapeDtypeStruct((rows, tiles.steps * tw), out_dtype)],
        [pl.BlockSpec((rows, tw), lambda t: (0, t))],
        [],
        2 * rows * a.shape[1] * tw * tiles.steps,
    )[0]


def project_columns(lefts, sets, depth, out_dtype):
    rows, tw, steps = lefts[0].shape[0], sets[0].width, sets[0].steps

    def body(step, weights, ins, outs, own):
        acc = own[0]
        total = dot_nt(ins[0][...], weights[0][...])
        for left, weight in zip(ins[1:], weights[1:]):
            total = total + dot_nt(left[...], weight[...])

        @pl.when(step == 0)
        def _():
            acc[...] = total

        @pl.when(step > 0)
        def _():
            acc[...] += total

        @pl.when(step == steps - 1)
        def _():
            outs[0][...] = acc[...].astype(out_dtype)

    return tiled_call(
        body,
        sets,
        list(lefts),
        [pl.BlockSpec((rows, tw), lambda t: (0, t))] * len(lefts),
        [jax.ShapeDtypeStruct((rows, depth), out_dtype)],
        [pl.BlockSpec((rows, depth), lambda t: (0, 0))],
        [pltpu.VMEM((rows, depth), f32)],
        2 * rows * depth * tw * steps * len(sets),
    )[0]


def feed_forward(normed, gate_tiles, up_tiles):
    rows, tw = normed.shape[0], gate_tiles.width

    def body(step, weights, ins, outs, own):
        a = ins[0][...]
        gate = dot_nn(a, weights[0][...])
        up = dot_nn(a, weights[1][...])
        outs[0][...] = (gate * jax.nn.sigmoid(gate) * up).astype(bf16)
        outs[1][...] = gate.astype(bf16)
        outs[2][...] = up.astype(bf16)

    shape = jax.ShapeDtypeStruct((rows, gate_tiles.steps * tw), bf16)
    return tiled_call(
        body,
        [gate_tiles, up_tiles],
        [normed],
        [whole(normed)],
        [shape] * 3,
        [pl.BlockSpec((rows, tw), lambda t: (0, t))] * 3,
        [],
        4 * rows * normed.shape[1] * tw * gate_tiles.steps,
    )


def feed_back(cotangent, gate, up, down_tiles):
    rows, tw = cotangent.shape[0], down_tiles.width

    def body(step, weights, ins, outs, own):
        grad = dot_nn(ins[0][...], weights[0][...])
        g = ins[1][...].astype(f32)
        u = ins[2][...].astype(f32)
        s = jax.nn.sigmoid(g)
        outs[0][...] = (grad * u * s * (1.0 + g * (1.0 - s))).astype(bf16)
        outs[1][...] = (grad * (g * s)).astype(bf16)

    shape = jax.ShapeDtypeStruct(gate.shape, bf16)
    tile = pl.BlockSpec((rows, tw), lambda t: (0, t))
    return tiled_call(
        body,
        [down_tiles],
        [cotangent, gate, up],
        [whole(cotangent), tile, tile],
        [shape] * 2,
        [tile] * 2,
        [],
        2 * rows * cotangent.shape[1] * tw * down_tiles.steps,
    )


def qkv_back(grad_hat, raw, cosine, sine, q_gain, k_gain):
    rows, width = grad_hat.shape
    tw = width // 2

    def kernel(g_ref, r_ref, cos_ref, sin_ref, qg, kg, out, qsum, ksum):
        def back(cut, gain, total):
            w = g_ref[:, cut].astype(f32)
            w = w * cos_ref[...] + pltpu.roll(w * sin_ref[...], HEAD_DIM // 2, 1)
            x = r_ref[:, cut].astype(f32)
            inverse = lax.rsqrt(jnp.mean(x * x, axis=-1, keepdims=True) + norm_eps)
            u = x * inverse
            wu = w * u
            scaled = w * gain
            out[:, cut] = (
                inverse * (scaled - u * jnp.mean(wu * gain, axis=-1, keepdims=True))
            ).astype(bf16)
            return total + jnp.sum(wu, axis=0, keepdims=True)

        total = jnp.zeros((1, HEAD_DIM), f32)
        cuts = head_slices(width)
        n_query, n_key = tw // HEAD_DIM, tw // HEAD_DIM // 2
        for cut in cuts[:n_query]:
            total = back(cut, qg[...], total)
        qsum[...] = total
        total = jnp.zeros((1, HEAD_DIM), f32)
        for cut in cuts[n_query : n_query + n_key]:
            total = back(cut, kg[...], total)
        ksum[...] = total
        out[:, tw + tw // 2 :] = g_ref[:, tw + tw // 2 :]

    ins = [grad_hat, raw, cosine, sine, q_gain, k_gain]
    gain_shape = jax.ShapeDtypeStruct((1, HEAD_DIM), f32)
    out_shape = [jax.ShapeDtypeStruct((rows, width), bf16), gain_shape, gain_shape]
    return pl.pallas_call(
        kernel,
        out_shape=out_shape,
        compiler_params=params(),
        cost_estimate=cost(40 * rows * width, nbytes(ins) + nbytes(out_shape)),
    )(*ins)


def attention_specs(kv):
    q = pl.BlockSpec((TREE_TOK, GROUP * HEAD_DIM), lambda n, s: (0, n))
    k = pl.BlockSpec((TREE_TOK, HEAD_DIM), lambda n, s: (0, GROUP * kv + n))
    v = pl.BlockSpec((TREE_TOK, HEAD_DIM), lambda n, s: (0, (GROUP + 1) * kv + n))
    return q, k, v


def stacked(ref, start):
    rows = pl.ds(start, BRANCH)
    return jnp.concatenate(
        [ref[rows, h * HEAD_DIM : (h + 1) * HEAD_DIM] for h in range(GROUP)], axis=0
    )


def causal():
    key = lax.broadcasted_iota(jnp.int32, (BRANCH, GROUP * BRANCH), 0)
    query = lax.rem(lax.broadcasted_iota(jnp.int32, (BRANCH, GROUP * BRANCH), 1), BRANCH)
    return key <= query


TRUNK_BLOCKS = TRUNK // BRANCH
BLOCKS = TREE_TOK // BRANCH


def attention_forward(qkv, parents, kv):
    def kernel(parent_ref, q_ref, k_ref, v_ref, out_ref, log_ref, vt):
        vt[...] = v_ref[...].T
        mask = causal()

        def part(q, start, size, rule):
            score = dot_nt(k_ref[pl.ds(start, size), :], q)
            weight = jnp.exp2(score)
            if rule is not None:
                weight = rule(weight)
            out = dot_nn(vt[:, pl.ds(start, size)], weight.astype(bf16))
            return out, jnp.sum(weight, axis=0, keepdims=True)

        def finish(block, start, pieces):
            out = sum(p[0] for p in pieces)
            total = sum(p[1] for p in pieces)
            out = (out / total).T.astype(bf16)
            for h in range(GROUP):
                out_ref[pl.ds(start, BRANCH), h * HEAD_DIM : (h + 1) * HEAD_DIM] = out[
                    h * BRANCH : (h + 1) * BRANCH
                ]
            log_ref[0, pl.ds(block, 1), :] = jnp.log2(total)

        diagonal = lambda w: jnp.where(mask, w, 0.0)
        for block in range(TRUNK_BLOCKS):
            q = stacked(q_ref, block * BRANCH)
            pieces = [part(q, block * BRANCH, BRANCH, diagonal)]
            if block > 0:
                pieces.append(part(q, 0, block * BRANCH, None))
            finish(block, block * BRANCH, pieces)

        def branch(i, carry):
            block = TRUNK_BLOCKS + i
            start = pl.multiple_of(block * BRANCH, BRANCH)
            q = stacked(q_ref, start)
            parent = parent_ref[i]
            has = (parent != block).astype(f32)
            pieces = [
                part(q, start, BRANCH, diagonal),
                part(q, pl.multiple_of(parent * BRANCH, BRANCH), BRANCH, lambda w: w * has),
                part(q, 0, TRUNK, None),
            ]
            finish(block, start, pieces)
            return carry

        lax.fori_loop(0, FORKS2, branch, 0)

    q, k, v = attention_specs(kv)
    out_shape = [
        jax.ShapeDtypeStruct((TREE_TOK, GROUP * kv * HEAD_DIM), bf16),
        jax.ShapeDtypeStruct((kv, BLOCKS, GROUP * BRANCH), f32),
    ]
    return pl.pallas_call(
        kernel,
        grid_spec=pltpu.PrefetchScalarGridSpec(
            num_scalar_prefetch=1,
            grid=(kv,),
            in_specs=[q, k, v],
            out_specs=[
                q,
                pl.BlockSpec((1, BLOCKS, GROUP * BRANCH), lambda n, s: (n, 0, 0)),
            ],
            scratch_shapes=[pltpu.VMEM((HEAD_DIM, TREE_TOK), bf16)],
        ),
        out_shape=out_shape,
        compiler_params=params(),
        cost_estimate=cost(kv * 2.2e6 * 2 * GROUP * 256 * 2, nbytes([qkv]) + nbytes(out_shape)),
    )(parents, qkv, qkv, qkv)


def attention_backward(qkv, attended, grads, logs, parents, kv):
    def kernel(
        parent_ref, q_ref, k_ref, v_ref, o_ref, do_ref, log_ref, dq_ref, dk_ref, dv_ref, kt, dk, dv
    ):
        kt[...] = k_ref[...].T
        dk[...] = jnp.zeros_like(dk)
        dv[...] = jnp.zeros_like(dv)
        mask = causal()

        def part(q, do, log, delta, start, size, rule):
            rows = pl.ds(start, size)
            prob = jnp.exp2(dot_nt(k_ref[rows, :], q) - log)
            if rule is not None:
                prob = rule(prob)
            grad = dot_nt(v_ref[rows, :], do)
            score_grad = (prob * (grad - delta)).astype(bf16)
            dk[rows, :] += dot_nn(score_grad, q)
            dv[rows, :] += dot_nn(prob.astype(bf16), do)
            return dot_nn(kt[:, rows], score_grad)

        def one(block, start, ranges):
            q = stacked(q_ref, start)
            do = stacked(do_ref, start)
            o = stacked(o_ref, start)
            delta = jnp.sum((do.astype(f32) * o.astype(f32)).T, axis=0, keepdims=True)
            log = log_ref[0, pl.ds(block, 1), :]
            total = sum(part(q, do, log, delta, *r) for r in ranges)
            out = (total * LN2).T.astype(bf16)
            for h in range(GROUP):
                dq_ref[pl.ds(start, BRANCH), h * HEAD_DIM : (h + 1) * HEAD_DIM] = out[
                    h * BRANCH : (h + 1) * BRANCH
                ]

        diagonal = lambda p: jnp.where(mask, p, 0.0)
        for block in range(TRUNK_BLOCKS):
            ranges = [(block * BRANCH, BRANCH, diagonal)]
            if block > 0:
                ranges.append((0, block * BRANCH, None))
            one(block, block * BRANCH, ranges)

        def branch(i, carry):
            block = TRUNK_BLOCKS + i
            start = pl.multiple_of(block * BRANCH, BRANCH)
            parent = parent_ref[i]
            has = (parent != block).astype(f32)
            one(
                block,
                start,
                [
                    (start, BRANCH, diagonal),
                    (pl.multiple_of(parent * BRANCH, BRANCH), BRANCH, lambda p: p * has),
                    (0, TRUNK, None),
                ],
            )
            return carry

        lax.fori_loop(0, FORKS2, branch, 0)
        dk_ref[...] = (dk[...] * score_scale).astype(bf16)
        dv_ref[...] = dv[...].astype(bf16)

    q, k, v = attention_specs(kv)
    single = pl.BlockSpec((TREE_TOK, HEAD_DIM), lambda n, s: (0, n))
    out_shape = [
        jax.ShapeDtypeStruct((TREE_TOK, GROUP * kv * HEAD_DIM), bf16),
        jax.ShapeDtypeStruct((TREE_TOK, kv * HEAD_DIM), bf16),
        jax.ShapeDtypeStruct((TREE_TOK, kv * HEAD_DIM), bf16),
    ]
    return pl.pallas_call(
        kernel,
        grid_spec=pltpu.PrefetchScalarGridSpec(
            num_scalar_prefetch=1,
            grid=(kv,),
            in_specs=[
                q,
                k,
                v,
                q,
                q,
                pl.BlockSpec((1, BLOCKS, GROUP * BRANCH), lambda n, s: (n, 0, 0)),
            ],
            out_specs=[q, single, single],
            scratch_shapes=[
                pltpu.VMEM((HEAD_DIM, TREE_TOK), bf16),
                pltpu.VMEM((TREE_TOK, HEAD_DIM), f32),
                pltpu.VMEM((TREE_TOK, HEAD_DIM), f32),
            ],
        ),
        out_shape=out_shape,
        compiler_params=params(),
        cost_estimate=cost(
            kv * 2.2e6 * 2 * GROUP * 640 * 2, nbytes([qkv, attended, grads]) + nbytes(out_shape)
        ),
    )(parents, qkv, qkv, qkv, attended, grads, logs)


def shuffle_columns(a, order):
    rows, count = a.shape[0], order.shape[0]
    width = a.shape[1] // count

    def kernel(order_ref, in_ref, out_ref):
        out_ref[...] = in_ref[...]

    return pl.pallas_call(
        kernel,
        grid_spec=pltpu.PrefetchScalarGridSpec(
            num_scalar_prefetch=1,
            grid=(count,),
            in_specs=[pl.BlockSpec((rows, width), lambda k, s: (0, s[k]))],
            out_specs=pl.BlockSpec((rows, width), lambda k, s: (0, k)),
        ),
        out_shape=jax.ShapeDtypeStruct(a.shape, a.dtype),
        cost_estimate=cost(0, 2 * nbytes([a])),
    )(order, a)


def place_rows(pieces, order):
    rows, width = pieces[0].shape
    count = len(pieces)

    def kernel(order_ref, *refs):
        ins, out, sems = refs[:count], refs[count], refs[count + 1]
        copies = [
            pltpu.make_async_copy(
                ins[e], out.at[pl.ds(pl.multiple_of(order_ref[e] * rows, 16), rows), :], sems.at[e]
            )
            for e in range(count)
        ]
        for c in copies:
            c.start()
        for c in copies:
            c.wait()

    return pl.pallas_call(
        kernel,
        grid_spec=pltpu.PrefetchScalarGridSpec(
            num_scalar_prefetch=1,
            grid=(),
            in_specs=[pl.BlockSpec(memory_space=pl.ANY)] * count,
            out_specs=pl.BlockSpec(memory_space=pl.ANY),
            scratch_shapes=[pltpu.SemaphoreType.DMA((count,))],
        ),
        out_shape=jax.ShapeDtypeStruct((rows * count, width), pieces[0].dtype),
        cost_estimate=cost(0, 2 * nbytes(pieces)),
    )(order, *pieces)


def inverse_rms(values):
    return lax.rsqrt(jnp.mean(values * values, axis=-1, keepdims=True) + norm_eps)


def norm_back(grads, unit_values, inverse, gain):
    scaled = grads * gain
    return inverse * (scaled - unit_values * jnp.mean(scaled * unit_values, axis=-1, keepdims=True))


def local(
    m,
    n,
    tokens,
    out_grad,
    seg_ids,
    parent_table,
    path_pos,
    attn_gain,
    w_query,
    w_key,
    w_value,
    w_out,
    q_gain,
    k_gain,
    ffn_gain,
    w_gate,
    w_up,
    w_down,
):
    rows, depth = tokens.shape
    block = depth // m
    order = [0, 2, 4, 6, 1, 3, 5, 7] if m == 8 else list(range(m))
    where = lax.axis_index("wide").astype(jnp.int32)
    seat = lax.axis_index("tp").astype(jnp.int32)
    relative = jnp.asarray(order, jnp.int32) ^ where
    inverse_order = [order.index(k) for k in range(m)]
    absolute = jnp.take(jnp.asarray(inverse_order, jnp.int32), jnp.arange(m, dtype=jnp.int32) ^ where)
    seats = jnp.arange(n, dtype=jnp.int32) ^ seat

    def over(axis, a, mask):
        size = m if axis == "wide" else n
        return lax.ppermute(a, axis, [(i, i ^ mask) for i in range(size)])

    def gather(a):
        if m == 8:
            half = a.shape[0] // 2
            along_x = over("wide", a, 2)
            along_y = over("wide", a, 4)
            top = over("wide", along_y[:half], 2)
            low = over("wide", along_x[half:], 4)
            mine = [a, along_x, along_y, top, low]
            return mine + [over("wide", p, 1) for p in mine]
        return [a] + [over("wide", a, k) for k in range(1, m)]

    def scatter(mine, other):
        if m == 8:
            half = block // 2
            total = mine.astype(f32) + over("wide", other, 1).astype(f32)
            top = over("wide", total[3 * block : 3 * block + half].astype(bf16), 2)
            low = over("wide", total[3 * block + half :].astype(bf16), 4)
            for_x = jnp.concatenate(
                [
                    total[block : block + half],
                    total[block + half : 2 * block] + low.astype(f32),
                ]
            ).astype(bf16)
            for_y = jnp.concatenate(
                [
                    total[2 * block : 2 * block + half] + top.astype(f32),
                    total[2 * block + half : 3 * block],
                ]
            ).astype(bf16)
            return (
                total[:block]
                + over("wide", for_x, 2).astype(f32)
                + over("wide", for_y, 4).astype(f32)
            )
        both = jnp.concatenate([mine, other])
        total = both[:block].astype(f32)
        for k in range(1, m):
            total = total + over("wide", both[k * block : (k + 1) * block], k).astype(f32)
        return total

    def gradient(left, right):
        half = depth // 2
        return (
            contract_rows(left[:, :half], right).astype(bf16),
            contract_rows(left[:, half:], right).astype(bf16),
        )

    attn_block = jnp.concatenate([w_query, w_key, w_value, w_out.T], axis=1)
    ffn_block = jnp.concatenate([w_gate, w_up, w_down.T], axis=1)
    attn_first = gather(attn_block)
    attn_rest = gather(
        jnp.concatenate([over("tp", attn_block, e) for e in range(1, n)], axis=1)
    )
    ffn_first = gather(ffn_block)
    ffn_rest = gather(
        jnp.concatenate([over("tp", ffn_block, 2 * e) for e in range(1, n // 2)], axis=1)
    )
    aw = w_query.shape[1]
    kv = w_key.shape[1] // HEAD_DIM
    fcols = w_gate.shape[1]
    fw = fcols // 3

    def attn_tiles(parts, base):
        return Tiles(attn_first, attn_rest, n, parts, base, 3, aw)

    def ffn_tiles(base):
        return Tiles(ffn_first, ffn_rest, n // 2, 3, base, 9, fw)

    gains = lax.all_gather(
        jnp.concatenate([attn_gain, ffn_gain, q_gain, k_gain]), "wide", axis=0, tiled=False
    ).astype(f32)
    gain_one = jnp.take(gains[:, :block], relative, axis=0).reshape(1, depth)
    gain_two = jnp.take(gains[:, block : 2 * block], relative, axis=0).reshape(1, depth)
    small = q_gain.shape[0]
    gain_q = gains[:, 2 * block : 2 * block + small].reshape(1, HEAD_DIM)
    gain_k = gains[:, 2 * block + small :].reshape(1, HEAD_DIM)

    base = where * parent_table.shape[0]
    block_segs = seg_ids[TRUNK::BRANCH] - base
    hit = block_segs[:, None] == jnp.arange(parent_table.shape[0], dtype=jnp.int32)[None, :]
    block_parents = jnp.sum(jnp.where(hit, parent_table[None, :] - base, 0), axis=1)
    match = block_parents[:, None] == block_segs[None, :]
    number = TRUNK_BLOCKS + jnp.arange(FORKS2, dtype=jnp.int32)
    parents = jnp.where(
        jnp.any(match, axis=1), jnp.sum(jnp.where(match, number[None, :], 0), axis=1), number
    ).astype(jnp.int32)

    own_pos = lax.dynamic_slice_in_dim(path_pos, seat * rows, rows, 0).astype(f32)
    frequency = rope_base ** (-(jnp.arange(HEAD_DIM // 2, dtype=f32) * 2.0) / HEAD_DIM)
    angles = own_pos[:, None] * frequency[None, :]
    cosine, sine = jnp.cos(angles), jnp.sin(angles)
    cosine = jnp.concatenate([cosine, cosine], axis=-1)
    sine = jnp.concatenate([-sine, sine], axis=-1)

    stream = shuffle_columns(tokens, relative).astype(f32)
    cotangent = shuffle_columns(out_grad, relative)
    cotangent_next = over("tp", cotangent, 1)
    inverse_one = inverse_rms(stream)
    unit_one = stream * inverse_one
    normed_one = (unit_one * gain_one).astype(bf16)
    hats, raws = [None] * n, [None] * n
    for e in list(range(1, n)) + [0]:
        tiles = (
            Tiles(attn_first, [], 1, 2, 0, 3, aw)
            if e == 0
            else Tiles(attn_rest, [], 1, 2, 3 * (e - 1), 3, aw)
        )
        hats[e], raws[e] = project_qkv(normed_one, tiles, cosine, sine, gain_q, gain_k)

    def exchange(parts):
        return [parts[0]] + [over("tp", parts[e], e) for e in range(1, n)]

    def rows_for(a, e):
        return lax.dynamic_slice_in_dim(a, seats[e] * rows, rows, 0)

    qkv = place_rows(exchange(hats), seats)
    attended_heads, logs = attention_forward(qkv, parents, kv)
    attended = jnp.concatenate(
        exchange([rows_for(attended_heads, e) for e in range(n)]), axis=1
    )
    after_attn = stream + project_columns([attended], [attn_tiles(1, 2)], depth, f32)

    inverse_two = inverse_rms(after_attn)
    unit_two = after_attn * inverse_two
    normed_two = (unit_two * gain_two).astype(bf16)
    normed_two_next = over("tp", normed_two, 1)
    hidden, gate, up = feed_forward(normed_two, ffn_tiles(0), ffn_tiles(3))
    hidden_next, gate_next, up_next = feed_forward(normed_two_next, ffn_tiles(0), ffn_tiles(3))
    down_next = over("tp", project_columns([hidden_next], [ffn_tiles(6)], depth, bf16), 1)
    down = project_columns([hidden], [ffn_tiles(6)], depth, f32)
    mixed = (after_attn + down + down_next.astype(f32)).astype(bf16)
    mixed = shuffle_columns(mixed, absolute)

    gate_grad_next, up_grad_next = feed_back(cotangent_next, gate_next, up_next, ffn_tiles(6))
    back_next = over(
        "tp",
        project_columns([gate_grad_next, up_grad_next], [ffn_tiles(0), ffn_tiles(3)], depth, bf16),
        1,
    )
    gate_grad, up_grad = feed_back(cotangent, gate, up, ffn_tiles(6))
    back = project_columns([gate_grad, up_grad], [ffn_tiles(0), ffn_tiles(3)], depth, f32)
    normed_two_grad = back + back_next.astype(f32)

    cotangent_pair = jnp.concatenate([cotangent, cotangent_next])
    normed_two_pair = jnp.concatenate([normed_two, normed_two_next])

    def ffn_share(left, right):
        total = scatter(*gradient(left, right))
        shares = total[:, :fcols]
        for e in range(1, n // 2):
            shares = shares + over(
                "tp", total[:, e * fcols : (e + 1) * fcols].astype(bf16), 2 * e
            ).astype(f32)
        return shares

    down_share = ffn_share(cotangent_pair, jnp.concatenate([hidden, hidden_next])).T
    gate_share = ffn_share(normed_two_pair, jnp.concatenate([gate_grad, gate_grad_next]))
    up_share = ffn_share(normed_two_pair, jnp.concatenate([up_grad, up_grad_next]))

    ffn_gain_part = jnp.sum(normed_two_grad * unit_two, axis=0)
    stream_grad = cotangent.astype(f32) + norm_back(
        normed_two_grad, unit_two, inverse_two, gain_two
    )
    grad_low = stream_grad.astype(bf16)
    attended_grad = project_rows(grad_low, attn_tiles(1, 2))
    grad_heads = place_rows(
        exchange([attended_grad[:, e * aw : (e + 1) * aw] for e in range(n)]), seats
    )
    dq, dk, dv = attention_backward(qkv, attended_heads, grad_heads, logs, parents, kv)
    back_hats = exchange(
        [
            jnp.concatenate([rows_for(dq, e), rows_for(dk, e), rows_for(dv, e)], axis=1)
            for e in range(n)
        ]
    )
    raw_grads, q_parts, k_parts = zip(
        *[
            qkv_back(back_hats[e], raws[e], cosine, sine, gain_q, gain_k)
            for e in range(n)
        ]
    )
    raw_grads = jnp.concatenate(raw_grads, axis=1)
    normed_one_grad = project_columns([raw_grads], [attn_tiles(2, 0)], depth, f32)

    def attn_share(left, right, width):
        total = scatter(*gradient(left, right))
        shares = total[:, :width]
        for e in range(1, n):
            shares = shares + over(
                "tp", total[:, e * width : (e + 1) * width].astype(bf16), e
            ).astype(f32)
        return shares

    out_share = attn_share(grad_low, attended, aw).T
    qkv_share = attn_share(normed_one, raw_grads, 2 * aw)

    attn_gain_part = jnp.sum(normed_one_grad * unit_one, axis=0)
    tokens_grad = (
        stream_grad + norm_back(normed_one_grad, unit_one, inverse_one, gain_one)
    ).astype(bf16)
    tokens_grad = shuffle_columns(tokens_grad, absolute)

    parts = jnp.concatenate(
        [
            jnp.take(attn_gain_part.reshape(m, block), absolute, axis=0),
            jnp.take(ffn_gain_part.reshape(m, block), absolute, axis=0),
            sum(q_parts).reshape(m, small),
            sum(k_parts).reshape(m, small),
        ],
        axis=1,
    )
    sums = lax.dynamic_index_in_dim(lax.psum(parts, ("wide", "tp")), where, 0, False)
    return (
        mixed,
        tokens_grad,
        sums[:block],
        qkv_share[:, :aw],
        qkv_share[:, aw : aw + aw // 2],
        qkv_share[:, aw + aw // 2 :],
        out_share,
        sums[2 * block : 2 * block + small],
        sums[2 * block + small :],
        sums[block : 2 * block],
        gate_share,
        up_share,
        down_share,
    )


def solution(mesh):
    both = P(("wide", "tp"), None)
    w, wt, tw = P("wide"), P("wide", "tp"), P("tp", "wide")
    return jax.shard_map(
        functools.partial(local, mesh.shape["wide"], mesh.shape["tp"]),
        mesh=mesh,
        in_specs=(both, both, w, w, w, w, wt, wt, wt, tw, w, w, w, wt, wt, tw),
        out_specs=(both, both, w, wt, wt, wt, tw, w, w, w, wt, wt, tw),
        check_vma=False,
    )
```

time: 2220 us -> 1780 us (0.80)
  Pallas kernels: 0 us -> 531 us
  waiting for transfers between devices: 1240 us -> 733 us
  matrix products: 530 us -> 121 us
  starting transfers between devices: 1.27 us -> 124 us
  other arithmetic: 221 us -> 102 us
  local copies, waits for them, and re-layouts: 121 us -> 75.4 us
    ppermute x0 -> x90, waiting for transfers between devices: none -> 733 us  [over(): return lax.ppermute(a, axis, [(i, i ^ mask) for i in range(size)])]
    all_gather x11 -> x0, waiting for transfers between devices: 676 us -> none  [the longest x1 160 us: local(): normed_two_all = lax.all_gather(normed_two, 'tp', axis=0, tiled=True)]
    reduce_scatter x11 -> x0, waiting for transfers between devices: 563 us -> none  [the longest x1 151 us: local(): lax.psum_scatter((against_columns(gate_grad, regathered[8]) + against_col...]
    pallas_call x0 -> x27, Pallas kernels: none -> 531 us  [the longest x15 230 us: tiled_call(): pl.pallas_call(kernel, grid=(steps,), in_specs=[pl.BlockSpec(memory_space...]
    dot_general x49 -> x10, matrix products: 530 us -> 121 us  [contract_rows(): lax.dot_general(a, b, (((0,), (0,)), ((), ())), preferred_element_type=f32)]
    ppermute x0 -> x90, starting transfers between devices: none -> 124 us  [over(): return lax.ppermute(a, axis, [(i, i ^ mask) for i in range(size)])]
    convert_element_type x28 -> x4, other arithmetic: 113 us -> 11.7 us  [the longest x1 5.36 us: local(): grad_low = stream_grad.astype(bf16)]
    psum x1, blocking collectives: 19.2 us -> 60.3 us  [local(): lax.psum(parts, ('wide', 'tp'))]
  transfers between devices with their start and end apart: 22 -> 90, of which waited for: 13 -> 31; matrix products, arithmetic and copies ran while one was open for 34% -> 16% of each run, Pallas kernels for 0% -> 30%
where the time goes in v1:
time: 1780 us
  waiting for transfers between devices  733 us (41%)
  Pallas kernels  531 us (30%)
  starting transfers between devices  124 us (7%)
  matrix products  121 us (7%)
  other arithmetic  102 us (6%)
  blocking collectives  85.5 us (5%)
  local copies, waits for them, and re-layouts  75.4 us (4%)
    ppermute x90, waiting for transfers between devices, over(): return lax.ppermute(a, axis, [(i, i ^ mask) for i in range(size)])  733 us
    pallas_call x15, Pallas kernels, tiled_call(): pl.pallas_call(kernel, grid=(steps,), in_specs=[pl.BlockSpec(memory_space...  230 us
    pallas_call x2, Pallas kernels, place_rows(): pl.pallas_call(kernel, grid_spec=pltpu.PrefetchScalarGridSpec(num_scalar_...  206 us
    ppermute x90, starting transfers between devices, over(): return lax.ppermute(a, axis, [(i, i ^ mask) for i in range(size)])  124 us
    dot_general x10, matrix products, contract_rows(): lax.dot_general(a, b, (((0,), (0,)), ((), ())), preferred_element_type=f32)  121 us
    psum x1, blocking collectives, local(): lax.psum(parts, ('wide', 'tp'))  60.3 us
    pallas_call x1, Pallas kernels, attention_backward(): pl.pallas_call(kernel, grid_spec=pltpu.PrefetchScalarGridSpec(num_scalar_...  35.6 us
  transfers between devices with their start and end apart: 90, of which 31 were waited for; matrix products, arithmetic and copies ran while one was open for 16% of the time, Pallas kernels for 30%

profile of v1, /device:TPU:0, one launch (start us, length us, event | category | flops | bytes accessed | tf_op | source)
XLA Modules:
  0.0 1776.4 jit_solution(805997530991634629)
XLA Ops:
  8.6 31.0 %collective-permute-done.9 = bf16[256,1536]{1,0:T(8,128)(2,1)S(1)} collective-permute-done((bf16[256,1536]{1,0:T(8,128)(2,1)S(1)}, bf16[256,1536]{1,0:T(8,128)(2,1)S(1)}, u32[]{:S(2)}, u32[]{:S(2)}) %collective-permute-start.9) | collective-permute-done | bytes 786464 | tf_op jit(solution)/shard_map/ppermute | solution.py:632
  40.6 20.4 %collective-permute-done.10 = bf16[256,1536]{1,0:T(8,128)(2,1)S(1)} collective-permute-done((bf16[256,1536]{1,0:T(8,128)(2,1)S(1)}, bf16[256,1536]{1,0:T(8,128)(2,1)S(1)}, u32[]{:S(2)}, u32[]{:S(2)}) %collective-permute-start.10) | collective-permute-done | bytes 786464 | tf_op jit(solution)/shard_map/ppermute | solution.py:632
  72.6 58.6 %collective-permute-done.1.refs_2_ = bf16[256,1536]{1,0:T(8,128)(2,1)S(1)} collective-permute-done((bf16[256,1536]{1,0:T(8,128)(2,1)S(1)}, bf16[256,1536]{1,0:T(8,128)(2,1)S(1)}, u32[]{:S(2)}, u32[]{:S(2)}) %collective-permute-start.1) | collective-permute-done | bytes 786464 | tf_op jit(solution)/shard_map/ppermute | solution.py:632
  144.0 44.6 %collective-permute-done.3.refs_4_ = bf16[128,1536]{1,0:T(8,128)(2,1)S(1)} collective-permute-done((bf16[128,1536]{1,0:T(8,128)(2,1)S(1)}, bf16[128,1536]{1,0:T(8,128)(2,1)S(1)}, u32[]{:S(2)}, u32[]{:S(2)}) %collective-permute-start.3) | collective-permute-done | bytes 393248 | tf_op jit(solution)/shard_map/ppermute | solution.py:632
  200.4 61.7 %collective-permute-done.14.refs_3_.refs_13_ = bf16[128,4608]{1,0:T(8,128)(2,1)S(1)} collective-permute-done((bf16[128,4608]{1,0:T(8,128)(2,1)}, bf16[128,4608]{1,0:T(8,128)(2,1)S(1)}, u32[]{:S(2)}, u32[]{:S(2)}) %collective-permute-start.14) | collective-permute-done | bytes 1179680 | tf_op jit(solution)/shard_map/ppermute | solution.py:632
  264.0 25.2 %all-reduce = bf16[4352]{0:T(1024)(128)(2,1)S(1)} all-reduce(bf16[4352]{0:T(1024)(128)(2,1)S(1)} %dynamic-update-slice), channel_id=2, replica_groups=mesh['wide'=8,'tp'=4] {'wide'}, use_global_device_ids=true, to_apply=%add | all-reduce | flops 4352 | bytes 17408
  297.3 21.2 %collective-permute-start.36 = (bf16[256,4608]{1,0:T(8,128)(2,1)}, bf16[256,4608]{1,0:T(8,128)(2,1)}, u32[]{:S(2)}, u32[]{:S(2)}) collective-permute-start(bf16[256,4608]{1,0:T(8,128)(2,1)} %pad_maximum_fusion.refs_0_.refs_20_), channel_id=1, source_target_pairs={{0,2},{1,3},{2,0},{3,1},{4,6},{5,7},{6,4},{7,5},{8,10},{9,11},{10,... | collective-permute-start | bytes 7077896 | tf_op jit(solution)/shard_map/ppermute | solution.py:632
  342.8 102.6 %collective-permute-done.36.refs_10_.refs_30_ = bf16[256,4608]{1,0:T(8,128)(2,1)} collective-permute-done((bf16[256,4608]{1,0:T(8,128)(2,1)}, bf16[256,4608]{1,0:T(8,128)(2,1)}, u32[]{:S(2)}, u32[]{:S(2)}) %collective-permute-start.36) | collective-permute-done | bytes 2359328 | tf_op jit(solution)/shard_map/ppermute | solution.py:632
  466.7 27.0 %collective-permute-start.21 = (bf16[544,1024]{1,0:T(8,128)(2,1)S(1)}, bf16[544,1024]{1,0:T(8,128)(2,1)S(1)}, u32[]{:S(2)}, u32[]{:S(2)}) collective-permute-start(bf16[544,1024]{1,0:T(8,128)(2,1)S(1)} %get-tuple-element.50), channel_id=1, source_target_pairs={{0,1},{1,0},{2,3},{3,2},{4,5},{5,4},{6,7},{7,6},{8,9},{9,8},{10,11... | collective-permute-start | bytes 3342344 | tf_op jit(solution)/shard_map/ppermute | solution.py:632
  493.7 23.2 %collective-permute-done.22.refs_2_ = bf16[544,1024]{1,0:T(8,128)(2,1)} collective-permute-done((bf16[544,1024]{1,0:T(8,128)(2,1)}, bf16[544,1024]{1,0:T(8,128)(2,1)}, u32[]{:S(2)}, u32[]{:S(2)}) %collective-permute-start.22) | collective-permute-done | bytes 1114144 | tf_op jit(solution)/shard_map/ppermute | solution.py:632
  517.5 23.1 %collective-permute-done.21.refs_1_ = bf16[544,1024]{1,0:T(8,128)(2,1)S(1)} collective-permute-done((bf16[544,1024]{1,0:T(8,128)(2,1)S(1)}, bf16[544,1024]{1,0:T(8,128)(2,1)S(1)}, u32[]{:S(2)}, u32[]{:S(2)}) %collective-permute-start.21) | collective-permute-done | bytes 1114144 | tf_op jit(solution)/shard_map/ppermute | solution.py:632
  549.1 136.8 %shard_map.278.q_ref.k_ref.v_ref = bf16[2176,1024]{1,0:T(8,128)(2,1)} custom-call(s32[4]{0:T(128)} %copy-done.58, bf16[544,1024]{1,0:T(8,128)(2,1)} %get-tuple-element.49.refs_0_, bf16[544,1024]{1,0:T(8,128)(2,1)} %copy-done.41, bf16[544,1024]{1,0:T(8,128)(2,1)} %collective-permute-done.22.refs_2_, bf16[544,1024]{1,0:T(8,128)(2,1)} %collective-permute-done.23.refs_3_), custom_call_target="tpu_custom_call" | custom-call | bytes 8912896 | tf_op jit(solution)/shard_map/pallas_call | solution.py:577
  686.3 20.6 %shard_map.279 = (bf16[2176,512]{1,0:T(8,128)(2,1)}, f32[2,17,256]{2,1,0:T(8,128)S(1)}) custom-call(s32[8]{0:T(128)S(1)} %fusion.46.parent_ref, bf16[2176,1024]{1,0:T(8,128)(2,1)} %shard_map.278.q_ref.k_ref.v_ref, bf16[2176,1024]{1,0:T(8,128)(2,1)} %shard_map.278.q_ref.k_ref.v_ref, bf16[2176,1024]{1,0:T(8,128)(2,1)} %shard_map.278.q_ref.k_ref.v_ref), custom_call_target="tpu_custom_call" | custom-call | flops 9011200000 | bytes 6719488 | tf_op jit(solution)/shard_map/pallas_call | solution.py:427
  727.0 32.1 %collective-permute-done.25 = bf16[544,512]{1,0:T(8,128)(2,1)} collective-permute-done((bf16[544,512]{1,0:T(8,128)(2,1)S(1)}, bf16[544,512]{1,0:T(8,128)(2,1)}, u32[]{:S(2)}, u32[]{:S(2)}) %collective-permute-start.25) | collective-permute-done | bytes 557088 | tf_op jit(solution)/shard_map/ppermute | solution.py:632
  769.4 12.3 shard_map.280
  791.6 20.7 %shard_map.281 = (bf16[544,3072]{1,0:T(8,128)(2,1)}, bf16[544,3072]{1,0:T(8,128)(2,1)}, bf16[544,3072]{1,0:T(8,128)(2,1)}) custom-call(bf16[256,4608]{1,0:T(8,128)(2,1)} %pad_maximum_fusion.refs_0_.refs_20_, bf16[256,4608]{1,0:T(8,128)(2,1)} %collective-permute-done.27.refs_1_.refs_21_, bf16[256,4608]{1,0:T(8,128)(2,1)} %collective-permute-done.28.refs_2_.refs_22_, ...), custom_call_target="tpu_custom_call" | custom-call | flops 13690208256 | bytes 87752704 | tf_op jit(solution)/shard_map/pallas_call | solution.py:150
  812.3 16.3 shard_map.282
  828.6 16.4 shard_map.287
  850.2 24.4 %shard_map.288 = f32[544,2048]{1,0:T(8,128)} custom-call(bf16[256,4608]{1,0:T(8,128)(2,1)} %pad_maximum_fusion.refs_0_.refs_20_, bf16[256,4608]{1,0:T(8,128)(2,1)} %collective-permute-done.27.refs_1_.refs_21_, bf16[256,4608]{1,0:T(8,128)(2,1)} %collective-permute-done.28.refs_2_.refs_22_, bf16[128,4608]{1,0:T(8,128)(2,1)S(1)} %collective-permute-done.29.refs_3_.refs_23_, ...), custom_call_target="tpu_custom_call" | custom-call | flops 13690208256 | bytes 86638592 | tf_op jit(solution)/shard_map/pallas_call | solution.py:150
  886.8 20.7 %shard_map.283 = (bf16[544,3072]{1,0:T(8,128)(2,1)}, bf16[544,3072]{1,0:T(8,128)(2,1)}, bf16[544,3072]{1,0:T(8,128)(2,1)}) custom-call(bf16[256,4608]{1,0:T(8,128)(2,1)} %pad_maximum_fusion.refs_0_.refs_20_, bf16[256,4608]{1,0:T(8,128)(2,1)} %collective-permute-done.27.refs_1_.refs_21_, bf16[256,4608]{1,0:T(8,128)(2,1)} %collective-permute-done.28.refs_2_.refs_22_, ...), custom_call_target="tpu_custom_call" | custom-call | flops 13690208256 | bytes 87752704 | tf_op jit(solution)/shard_map/pallas_call | solution.py:150
  907.6 15.3 shard_map.284
  923.2 16.4 shard_map.289
  939.7 23.8 %shard_map.290 = bf16[544,2048]{1,0:T(8,128)(2,1)} custom-call(bf16[256,4608]{1,0:T(8,128)(2,1)} %pad_maximum_fusion.refs_0_.refs_20_, bf16[256,4608]{1,0:T(8,128)(2,1)} %collective-permute-done.27.refs_1_.refs_21_, bf16[256,4608]{1,0:T(8,128)(2,1)} %collective-permute-done.28.refs_2_.refs_22_, ...), custom_call_target="tpu_custom_call" | custom-call | flops 13690208256 | bytes 84410368 | tf_op jit(solution)/shard_map/pallas_call | solution.py:150
  967.3 12.8 convolution_convert_fusion.1
  982.1 13.7 convolution_convert_fusion.2
  998.2 22.3 %collective-permute-done.49 = bf16[544,2048]{1,0:T(8,128)(2,1)S(1)} collective-permute-done((bf16[544,2048]{1,0:T(8,128)(2,1)}, bf16[544,2048]{1,0:T(8,128)(2,1)S(1)}, u32[]{:S(2)}, u32[]{:S(2)}) %collective-permute-start.49) | collective-permute-done | bytes 2228256 | tf_op jit(solution)/shard_map/ppermute | solution.py:632
  1044.1 13.1 convolution_convert_fusion.3
  1057.2 31.5 %collective-permute-done.51.refs_2_ = bf16[544,512]{1,0:T(8,128)(2,1)S(1)} collective-permute-done((bf16[544,512]{1,0:T(8,128)(2,1)S(1)}, bf16[544,512]{1,0:T(8,128)(2,1)S(1)}, u32[]{:S(2)}, u32[]{:S(2)}) %collective-permute-start.51) | collective-permute-done | bytes 557088 | tf_op jit(solution)/shard_map/ppermute | solution.py:632
  1090.4 69.3 %shard_map.292.do_ref = bf16[2176,512]{1,0:T(8,128)(2,1)} custom-call(s32[4]{0:T(128)} %copy-done.58, bf16[544,512]{1,0:T(8,128)(2,1)} %get-tuple-element.181.refs_0_, bf16[544,512]{1,0:T(8,128)(2,1)} %copy-done.49, bf16[544,512]{1,0:T(8,128)(2,1)} %copy-done.48, bf16[544,512]{1,0:T(8,128)(2,1)} %copy-done.47), custom_call_target="tpu_custom_call" | custom-call | bytes 4456448 | tf_op jit(solution)/shard_map/pallas_call | solution.py:577
  1159.7 35.6 %shard_map.293 = (bf16[2176,512]{1,0:T(8,128)(2,1)}, bf16[2176,256]{1,0:T(8,128)(2,1)S(1)}, bf16[2176,256]{1,0:T(8,128)(2,1)}) custom-call(s32[8]{0:T(128)S(1)} %copy-done.7, bf16[2176,1024]{1,0:T(8,128)(2,1)} %shard_map.278.q_ref.k_ref.v_ref, bf16[2176,1024]{1,0:T(8,128)(2,1)} %shard_map.278.q_ref.k_ref.v_ref, ...), custom_call_target="tpu_custom_call" | custom-call | flops 22528000000 | bytes 13369344 | tf_op jit(solution)/shard_map/pallas_call | solution.py:512
  1233.2 14.3 collective-permute-done.53.g_ref
  1250.8 27.5 %collective-permute-done.54.g_ref = bf16[544,1024]{1,0:T(8,128)(2,1)} collective-permute-done((bf16[544,1024]{1,0:T(8,128)(2,1)}, bf16[544,1024]{1,0:T(8,128)(2,1)}, u32[]{:S(2)}, u32[]{:S(2)}) %collective-permute-start.54) | collective-permute-done | bytes 1114144 | tf_op jit(solution)/shard_map/ppermute | solution.py:632
  1287.2 20.0 %shard_map.298 = f32[544,2048]{1,0:T(8,128)} custom-call(bf16[256,1536]{1,0:T(8,128)(2,1)} %copy-done.20, bf16[256,1536]{1,0:T(8,128)(2,1)} %copy-done.22, bf16[256,1536]{1,0:T(8,128)(2,1)} %copy-done.21, bf16[128,1536]{1,0:T(8,128)(2,1)S(1)} %collective-permute-done.2.refs_3_, bf16[128,1536]{1,0:T(8,128)(2,1)S(1)} %collective-permute-done.3.refs_4_, ...), custom_call_target="tpu_custom_call" | custom-call | flops 9126805504 | bytes 34078720 | tf_op jit(solution)/shard_map/pallas_call | solution.py:150
  1323.1 11.1 convolution_convert_fusion
  1334.9 60.3 %psum.7 = f32[8,544]{1,0:T(8,128)S(1)} all-reduce(f32[8,544]{1,0:T(8,128)S(1)} %pad_maximum_fusion.24), channel_id=1, replica_groups=mesh['wide'=8,'tp'=4] {'wide','tp'}, use_global_device_ids=true, to_apply=%region_9.11 | all-reduce | flops 4352 | bytes 34816 | tf_op jit(solution)/shard_map/psum | solution.py:845
  1396.5 11.4 fusion.34
  1407.9 16.0 fusion.75
  1431.1 14.2 fusion.74
  1448.6 14.5 fusion.73
  1488.4 13.1 collective-permute-done.81
  1526.5 15.2 collective-permute-done.68
  1564.3 11.2 collective-permute-done.88
  1581.1 16.0 collective-permute-done.59
  1598.0 33.7 %collective-permute-done.57 = bf16[128,4096]{1,0:T(8,128)(2,1)} collective-permute-done((bf16[128,4096]{1,0:T(8,128)(2,1)}, bf16[128,4096]{1,0:T(8,128)(2,1)}, u32[]{:S(2)}, u32[]{:S(2)}) %collective-permute-start.57) | collective-permute-done | bytes 1048608 | tf_op jit(solution)/shard_map/ppermute | solution.py:632
  1646.2 19.1 %collective-permute-done.76 = bf16[256,3072]{1,0:T(8,128)(2,1)S(1)} collective-permute-done((bf16[256,3072]{1,0:T(8,128)(2,1)}, bf16[256,3072]{1,0:T(8,128)(2,1)S(1)}, u32[]{:S(2)}, u32[]{:S(2)}) %collective-permute-start.76) | collective-permute-done | bytes 1572896 | tf_op jit(solution)/shard_map/ppermute | solution.py:632
  1674.6 39.2 %collective-permute-done.83 = bf16[256,1536]{1,0:T(8,128)(2,1)} collective-permute-done((bf16[256,1536]{1,0:T(8,128)(2,1)S(1)}, bf16[256,1536]{1,0:T(8,128)(2,1)}, u32[]{:S(2)}, u32[]{:S(2)}) %collective-permute-start.83) | collective-permute-done | bytes 786464 | tf_op jit(solution)/shard_map/ppermute | solution.py:632
  1736.6 15.1 collective-permute-done.61
  1751.7 22.5 %collective-permute-done.62 = bf16[256,1024]{1,0:T(8,128)(2,1)S(1)} collective-permute-done((bf16[256,1024]{1,0:T(8,128)(2,1)S(1)}, bf16[256,1024]{1,0:T(8,128)(2,1)S(1)}, u32[]{:S(2)}, u32[]{:S(2)}) %collective-permute-start.62) | collective-permute-done | bytes 524320 | tf_op jit(solution)/shard_map/ppermute | solution.py:632
  (473 shorter events, 403.8 us)
Async XLA Ops:
  63.1 127.1 %collective-permute-start.13 = (bf16[256,4608]{1,0:T(8,128)(2,1)}, bf16[256,4608]{1,0:T(8,128)(2,1)}, u32[]{:S(2)}, u32[]{:S(2)}) collective-permute-start(bf16[256,4608]{1,0:T(8,128)(2,1)} %constant_dynamic-update-slice_fusion.refs_0_.refs_10_), channel_id=1, source_target_pairs={{0,16},{4,20},{8,24},{12,28},{16,0},{20,4},{24,8},{28,12},{1,17},{... | collective-permute-start | bytes 7077896 | tf_op jit(solution)/shard_map/ppermute | solution.py:632
  64.6 66.6 %collective-permute-start.1 = (bf16[256,1536]{1,0:T(8,128)(2,1)S(1)}, bf16[256,1536]{1,0:T(8,128)(2,1)S(1)}, u32[]{:S(2)}, u32[]{:S(2)}) collective-permute-start(bf16[256,1536]{1,0:T(8,128)(2,1)S(1)} %pad_maximum_fusion.19.refs_0_), channel_id=1, source_target_pairs={{0,16},{4,20},{8,24},{12,28},{16,0},{20,4},{24,8},{28,12},{1,17},{... | collective-permute-start | bytes 2359304 | tf_op jit(solution)/shard_map/ppermute | solution.py:632
  65.1 69.4 %collective-permute-start.4 = (bf16[256,1536]{1,0:T(8,128)(2,1)S(1)}, bf16[256,1536]{1,0:T(8,128)(2,1)}, u32[]{:S(2)}, u32[]{:S(2)}) collective-permute-start(bf16[256,1536]{1,0:T(8,128)(2,1)S(1)} %pad_maximum_fusion.19.refs_0_), channel_id=1, source_target_pairs={{0,4},{4,0},{8,12},{12,8},{16,20},{20,16},{24,28},{28,24},{1,5},{5... | collective-permute-start | bytes 2359304 | tf_op jit(solution)/shard_map/ppermute | solution.py:632
  65.1 67.7 %collective-permute-start = (bf16[256,1536]{1,0:T(8,128)(2,1)S(1)}, bf16[256,1536]{1,0:T(8,128)(2,1)S(1)}, u32[]{:S(2)}, u32[]{:S(2)}) collective-permute-start(bf16[256,1536]{1,0:T(8,128)(2,1)S(1)} %pad_maximum_fusion.19.refs_0_), channel_id=1, source_target_pairs={{0,8},{4,12},{8,0},{12,4},{16,24},{20,28},{24,16},{28,20},{1,9},{5... | collective-permute-start | bytes 2359304 | tf_op jit(solution)/shard_map/ppermute | solution.py:632
  68.9 125.6 %collective-permute-start.12 = (bf16[256,4608]{1,0:T(8,128)(2,1)}, bf16[256,4608]{1,0:T(8,128)(2,1)}, u32[]{:S(2)}, u32[]{:S(2)}) collective-permute-start(bf16[256,4608]{1,0:T(8,128)(2,1)} %constant_dynamic-update-slice_fusion.refs_0_.refs_10_), channel_id=1, source_target_pairs={{0,8},{4,12},{8,0},{12,4},{16,24},{20,28},{24,16},{28,20},{1,9},{5... | collective-permute-start | bytes 7077896 | tf_op jit(solution)/shard_map/ppermute | solution.py:632
  131.2 68.4 %collective-permute-start.28 = (bf16[256,4608]{1,0:T(8,128)(2,1)}, bf16[256,4608]{1,0:T(8,128)(2,1)}, u32[]{:S(2)}, u32[]{:S(2)}) collective-permute-start(bf16[256,4608]{1,0:T(8,128)(2,1)} %pad_maximum_fusion.refs_0_.refs_20_), channel_id=1, source_target_pairs={{0,16},{4,20},{8,24},{12,28},{16,0},{20,4},{24,8},{28,12},{1,17},{... | collective-permute-start | bytes 7077896 | tf_op jit(solution)/shard_map/ppermute | solution.py:632
  188.7 100.5 %collective-permute-start.27 = (bf16[256,4608]{1,0:T(8,128)(2,1)}, bf16[256,4608]{1,0:T(8,128)(2,1)}, u32[]{:S(2)}, u32[]{:S(2)}) collective-permute-start(bf16[256,4608]{1,0:T(8,128)(2,1)} %pad_maximum_fusion.refs_0_.refs_20_), channel_id=1, source_target_pairs={{0,8},{4,12},{8,0},{12,4},{16,24},{20,28},{24,16},{28,20},{1,9},{5... | collective-permute-start | bytes 7077896 | tf_op jit(solution)/shard_map/ppermute | solution.py:632
  190.2 107.2 %collective-permute-start.16 = (bf16[256,4608]{1,0:T(8,128)(2,1)}, bf16[256,4608]{1,0:T(8,128)(2,1)}, u32[]{:S(2)}, u32[]{:S(2)}) collective-permute-start(bf16[256,4608]{1,0:T(8,128)(2,1)} %constant_dynamic-update-slice_fusion.refs_0_.refs_10_), channel_id=1, source_target_pairs={{0,4},{4,0},{8,12},{12,8},{16,20},{20,16},{24,28},{28,24},{1,5},{5... | collective-permute-start | bytes 7077896 | tf_op jit(solution)/shard_map/ppermute | solution.py:632
  194.0 68.2 %collective-permute-start.14 = (bf16[128,4608]{1,0:T(8,128)(2,1)}, bf16[128,4608]{1,0:T(8,128)(2,1)S(1)}, u32[]{:S(2)}, u32[]{:S(2)}) collective-permute-start(bf16[128,4608]{1,0:T(8,128)(2,1)} %slice.411), channel_id=1, source_target_pairs={{0,8},{4,12},{8,0},{12,4},{16,24},{20,28},{24,16},{28,20},{1,9},{5... | collective-permute-start | bytes 3538952 | tf_op jit(solution)/shard_map/ppermute | solution.py:632
  198.1 120.5 %collective-permute-start.15 = (bf16[128,4608]{1,0:T(8,128)(2,1)}, bf16[128,4608]{1,0:T(8,128)(2,1)}, u32[]{:S(2)}, u32[]{:S(2)}) collective-permute-start(bf16[128,4608]{1,0:T(8,128)(2,1)} %slice.412), channel_id=1, source_target_pairs={{0,16},{4,20},{8,24},{12,28},{16,0},{20,4},{24,8},{28,12},{1,17},{... | collective-permute-start | bytes 3538952 | tf_op jit(solution)/shard_map/ppermute | solution.py:632
  199.6 123.8 %collective-permute-start.18 = (bf16[256,4608]{1,0:T(8,128)(2,1)}, bf16[256,4608]{1,0:T(8,128)(2,1)}, u32[]{:S(2)}, u32[]{:S(2)}) collective-permute-start(bf16[256,4608]{1,0:T(8,128)(2,1)} %collective-permute-done.13.refs_2_.refs_12_), channel_id=1, source_target_pairs={{0,4},{4,0},{8,12},{12,8},{16,20},{20,16},{24,28},{28,24},{1,5},{5... | collective-permute-start | bytes 7077896 | tf_op jit(solution)/shard_map/ppermute | solution.py:632
  262.2 58.8 %collective-permute-start.19 = (bf16[128,4608]{1,0:T(8,128)(2,1)S(1)}, bf16[128,4608]{1,0:T(8,128)(2,1)}, u32[]{:S(2)}, u32[]{:S(2)}) collective-permute-start(bf16[128,4608]{1,0:T(8,128)(2,1)S(1)} %collective-permute-done.14.refs_3_.refs_13_), channel_id=1, source_target_pairs={{0,4},{4,0},{8,12},{12,8},{16,20},{20,16},{24,28},{28,24},{1,5},{5... | collective-permute-start | bytes 3538952 | tf_op jit(solution)/shard_map/ppermute | solution.py:632
  297.3 148.0 %collective-permute-start.36 = (bf16[256,4608]{1,0:T(8,128)(2,1)}, bf16[256,4608]{1,0:T(8,128)(2,1)}, u32[]{:S(2)}, u32[]{:S(2)}) collective-permute-start(bf16[256,4608]{1,0:T(8,128)(2,1)} %pad_maximum_fusion.refs_0_.refs_20_), channel_id=1, source_target_pairs={{0,2},{1,3},{2,0},{3,1},{4,6},{5,7},{6,4},{7,5},{8,10},{9,11},{10,... | collective-permute-start | bytes 7077896 | tf_op jit(solution)/shard_map/ppermute | solution.py:632
  318.6 135.1 %collective-permute-start.31 = (bf16[256,4608]{1,0:T(8,128)(2,1)}, bf16[256,4608]{1,0:T(8,128)(2,1)}, u32[]{:S(2)}, u32[]{:S(2)}) collective-permute-start(bf16[256,4608]{1,0:T(8,128)(2,1)} %pad_maximum_fusion.refs_0_.refs_20_), channel_id=1, source_target_pairs={{0,4},{4,0},{8,12},{12,8},{16,20},{20,16},{24,28},{28,24},{1,5},{5... | collective-permute-start | bytes 7077896 | tf_op jit(solution)/shard_map/ppermute | solution.py:632
  332.1 125.7 %collective-permute-start.29 = (bf16[128,4608]{1,0:T(8,128)(2,1)}, bf16[128,4608]{1,0:T(8,128)(2,1)S(1)}, u32[]{:S(2)}, u32[]{:S(2)}) collective-permute-start(bf16[128,4608]{1,0:T(8,128)(2,1)} %slice.416), channel_id=1, source_target_pairs={{0,8},{4,12},{8,0},{12,4},{16,24},{20,28},{24,16},{28,20},{1,9},{5... | collective-permute-start | bytes 3538952 | tf_op jit(solution)/shard_map/ppermute | solution.py:632
  332.1 126.3 %collective-permute-start.30 = (bf16[128,4608]{1,0:T(8,128)(2,1)}, bf16[128,4608]{1,0:T(8,128)(2,1)}, u32[]{:S(2)}, u32[]{:S(2)}) collective-permute-start(bf16[128,4608]{1,0:T(8,128)(2,1)} %slice.417), channel_id=1, source_target_pairs={{0,16},{4,20},{8,24},{12,28},{16,0},{20,4},{24,8},{28,12},{1,17},{... | collective-permute-start | bytes 3538952 | tf_op jit(solution)/shard_map/ppermute | solution.py:632
  341.4 125.3 %collective-permute-start.23 = (bf16[544,1024]{1,0:T(8,128)(2,1)}, bf16[544,1024]{1,0:T(8,128)(2,1)}, u32[]{:S(2)}, u32[]{:S(2)}) collective-permute-start(bf16[544,1024]{1,0:T(8,128)(2,1)} %get-tuple-element.52), channel_id=1, source_target_pairs={{0,3},{1,2},{2,1},{3,0},{4,7},{5,6},{6,5},{7,4},{8,11},{9,10},{10,... | collective-permute-start | bytes 3342344 | tf_op jit(solution)/shard_map/ppermute | solution.py:632
  445.4 240.6 %collective-permute-start.41 = (bf16[256,4608]{1,0:T(8,128)(2,1)}, bf16[256,4608]{1,0:T(8,128)(2,1)}, u32[]{:S(2)}, u32[]{:S(2)}) collective-permute-start(bf16[256,4608]{1,0:T(8,128)(2,1)} %collective-permute-done.36.refs_10_.refs_30_), channel_id=1, source_target_pairs={{0,4},{4,0},{8,12},{12,8},{16,20},{20,16},{24,28},{28,24},{1,5},{5... | collective-permute-start | bytes 7077896 | tf_op jit(solution)/shard_map/ppermute | solution.py:632
  453.7 63.2 %collective-permute-start.22 = (bf16[544,1024]{1,0:T(8,128)(2,1)}, bf16[544,1024]{1,0:T(8,128)(2,1)}, u32[]{:S(2)}, u32[]{:S(2)}) collective-permute-start(bf16[544,1024]{1,0:T(8,128)(2,1)} %get-tuple-element.51), channel_id=1, source_target_pairs={{0,2},{1,3},{2,0},{3,1},{4,6},{5,7},{6,4},{7,5},{8,10},{9,11},{10,... | collective-permute-start | bytes 3342344 | tf_op jit(solution)/shard_map/ppermute | solution.py:632
  457.8 251.7 %collective-permute-start.38 = (bf16[256,4608]{1,0:T(8,128)(2,1)}, bf16[256,4608]{1,0:T(8,128)(2,1)}, u32[]{:S(2)}, u32[]{:S(2)}) collective-permute-start(bf16[256,4608]{1,0:T(8,128)(2,1)} %collective-permute-done.36.refs_10_.refs_30_), channel_id=1, source_target_pairs={{0,16},{4,20},{8,24},{12,28},{16,0},{20,4},{24,8},{28,12},{1,17},{... | collective-permute-start | bytes 7077896 | tf_op jit(solution)/shard_map/ppermute | solution.py:632
  458.4 252.5 %collective-permute-start.37 = (bf16[256,4608]{1,0:T(8,128)(2,1)}, bf16[256,4608]{1,0:T(8,128)(2,1)}, u32[]{:S(2)}, u32[]{:S(2)}) collective-permute-start(bf16[256,4608]{1,0:T(8,128)(2,1)} %collective-permute-done.36.refs_10_.refs_30_), channel_id=1, source_target_pairs={{0,8},{4,12},{8,0},{12,4},{16,24},{20,28},{24,16},{28,20},{1,9},{5... | collective-permute-start | bytes 7077896 | tf_op jit(solution)/shard_map/ppermute | solution.py:632
  466.7 73.9 %collective-permute-start.21 = (bf16[544,1024]{1,0:T(8,128)(2,1)S(1)}, bf16[544,1024]{1,0:T(8,128)(2,1)S(1)}, u32[]{:S(2)}, u32[]{:S(2)}) collective-permute-start(bf16[544,1024]{1,0:T(8,128)(2,1)S(1)} %get-tuple-element.50), channel_id=1, source_target_pairs={{0,1},{1,0},{2,3},{3,2},{4,5},{5,4},{6,7},{7,6},{8,9},{9,8},{10,11... | collective-permute-start | bytes 3342344 | tf_op jit(solution)/shard_map/ppermute | solution.py:632
  516.9 201.7 %collective-permute-start.33 = (bf16[256,4608]{1,0:T(8,128)(2,1)}, bf16[256,4608]{1,0:T(8,128)(2,1)}, u32[]{:S(2)}, u32[]{:S(2)}) collective-permute-start(bf16[256,4608]{1,0:T(8,128)(2,1)} %collective-permute-done.28.refs_2_.refs_22_), channel_id=1, source_target_pairs={{0,4},{4,0},{8,12},{12,8},{16,20},{20,16},{24,28},{28,24},{1,5},{5... | collective-permute-start | bytes 7077896 | tf_op jit(solution)/shard_map/ppermute | solution.py:632
  540.5 170.3 %collective-permute-start.34 = (bf16[128,4608]{1,0:T(8,128)(2,1)S(1)}, bf16[128,4608]{1,0:T(8,128)(2,1)}, u32[]{:S(2)}, u32[]{:S(2)}) collective-permute-start(bf16[128,4608]{1,0:T(8,128)(2,1)S(1)} %collective-permute-done.29.refs_3_.refs_23_), channel_id=1, source_target_pairs={{0,4},{4,0},{8,12},{12,8},{16,20},{20,16},{24,28},{28,24},{1,5},{5... | collective-permute-start | bytes 3538952 | tf_op jit(solution)/shard_map/ppermute | solution.py:632
  718.6 63.1 %collective-permute-start.39 = (bf16[128,4608]{1,0:T(8,128)(2,1)}, bf16[128,4608]{1,0:T(8,128)(2,1)}, u32[]{:S(2)}, u32[]{:S(2)}) collective-permute-start(bf16[128,4608]{1,0:T(8,128)(2,1)} %slice.418), channel_id=1, source_target_pairs={{0,8},{4,12},{8,0},{12,4},{16,24},{20,28},{24,16},{28,20},{1,9},{5... | collective-permute-start | bytes 3538952 | tf_op jit(solution)/shard_map/ppermute | solution.py:632
  718.6 63.2 %collective-permute-start.40 = (bf16[128,4608]{1,0:T(8,128)(2,1)}, bf16[128,4608]{1,0:T(8,128)(2,1)}, u32[]{:S(2)}, u32[]{:S(2)}) collective-permute-start(bf16[128,4608]{1,0:T(8,128)(2,1)} %slice.419), channel_id=1, source_target_pairs={{0,16},{4,20},{8,24},{12,28},{16,0},{20,4},{24,8},{28,12},{1,17},{... | collective-permute-start | bytes 3538952 | tf_op jit(solution)/shard_map/ppermute | solution.py:632
  727.0 61.2 %collective-permute-start.32 = (bf16[256,4608]{1,0:T(8,128)(2,1)}, bf16[256,4608]{1,0:T(8,128)(2,1)}, u32[]{:S(2)}, u32[]{:S(2)}) collective-permute-start(bf16[256,4608]{1,0:T(8,128)(2,1)} %collective-permute-done.27.refs_1_.refs_21_), channel_id=1, source_target_pairs={{0,4},{4,0},{8,12},{12,8},{16,20},{20,16},{24,28},{28,24},{1,5},{5... | collective-permute-start | bytes 7077896 | tf_op jit(solution)/shard_map/ppermute | solution.py:632
  788.5 134.7 %collective-permute-start.48 = (bf16[544,2048]{1,0:T(8,128)(2,1)S(1)}, bf16[544,2048]{1,0:T(8,128)(2,1)}, u32[]{:S(2)}, u32[]{:S(2)}) collective-permute-start(bf16[544,2048]{1,0:T(8,128)(2,1)S(1)} %copy-done.17), channel_id=1, source_target_pairs={{0,1},{1,0},{2,3},{3,2},{4,5},{5,4},{6,7},{7,6},{8,9},{9,8},{10,11... | collective-permute-start | bytes 6684680 | tf_op jit(solution)/shard_map/ppermute | solution.py:632
  788.6 98.3 %collective-permute-start.46 = (bf16[544,2048]{1,0:T(8,128)(2,1)}, bf16[544,2048]{1,0:T(8,128)(2,1)}, u32[]{:S(2)}, u32[]{:S(2)}) collective-permute-start(bf16[544,2048]{1,0:T(8,128)(2,1)} %multiply_convert_fusion.refs_40_), channel_id=1, source_target_pairs={{0,1},{1,0},{2,3},{3,2},{4,5},{5,4},{6,7},{7,6},{8,9},{9,8},{10,11... | collective-permute-start | bytes 6684680 | tf_op jit(solution)/shard_map/ppermute | solution.py:632
  922.9 99.0 %collective-permute-start.47 = (bf16[544,2048]{1,0:T(8,128)(2,1)}, bf16[544,2048]{1,0:T(8,128)(2,1)S(1)}, u32[]{:S(2)}, u32[]{:S(2)}) collective-permute-start(bf16[544,2048]{1,0:T(8,128)(2,1)} %shard_map.284), channel_id=1, source_target_pairs={{0,1},{1,0},{2,3},{3,2},{4,5},{5,4},{6,7},{7,6},{8,9},{9,8},{10,11... | collective-permute-start | bytes 6684680 | tf_op jit(solution)/shard_map/ppermute | solution.py:632
  963.5 57.0 %collective-permute-start.49 = (bf16[544,2048]{1,0:T(8,128)(2,1)}, bf16[544,2048]{1,0:T(8,128)(2,1)S(1)}, u32[]{:S(2)}, u32[]{:S(2)}) collective-permute-start(bf16[544,2048]{1,0:T(8,128)(2,1)} %shard_map.290), channel_id=1, source_target_pairs={{0,1},{1,0},{2,3},{3,2},{4,5},{5,4},{6,7},{7,6},{8,9},{9,8},{10,11... | collective-permute-start | bytes 6684680 | tf_op jit(solution)/shard_map/ppermute | solution.py:632
  980.1 427.8 %collective-permute-start.84 = (bf16[1024,3072]{1,0:T(8,128)(2,1)}, bf16[1024,3072]{1,0:T(8,128)(2,1)}, u32[]{:S(2)}, u32[]{:S(2)}) collective-permute-start(bf16[1024,3072]{1,0:T(8,128)(2,1)} %convolution_convert_fusion.1), channel_id=1, source_target_pairs={{0,4},{4,0},{8,12},{12,8},{16,20},{20,16},{24,28},{28,24},{1,5},{5... | collective-permute-start | bytes 18874376 | tf_op jit(solution)/shard_map/ppermute | solution.py:632
  995.8 433.9 %collective-permute-start.78 = (bf16[1024,3072]{1,0:T(8,128)(2,1)}, bf16[1024,3072]{1,0:T(8,128)(2,1)}, u32[]{:S(2)}, u32[]{:S(2)}) collective-permute-start(bf16[1024,3072]{1,0:T(8,128)(2,1)} %convolution_convert_fusion.2), channel_id=1, source_target_pairs={{0,4},{4,0},{8,12},{12,8},{16,20},{20,16},{24,28},{28,24},{1,5},{5... | collective-permute-start | bytes 18874376 | tf_op jit(solution)/shard_map/ppermute | solution.py:632
  1201.8 76.5 %collective-permute-start.54 = (bf16[544,1024]{1,0:T(8,128)(2,1)}, bf16[544,1024]{1,0:T(8,128)(2,1)}, u32[]{:S(2)}, u32[]{:S(2)}) collective-permute-start(bf16[544,1024]{1,0:T(8,128)(2,1)} %pad_maximum_fusion.15), channel_id=1, source_target_pairs={{0,2},{1,3},{2,0},{3,1},{4,6},{5,7},{6,4},{7,5},{8,10},{9,11},{10,... | collective-permute-start | bytes 3342344 | tf_op jit(solution)/shard_map/ppermute | solution.py:632
  1204.9 76.7 %collective-permute-start.55 = (bf16[544,1024]{1,0:T(8,128)(2,1)}, bf16[544,1024]{1,0:T(8,128)(2,1)}, u32[]{:S(2)}, u32[]{:S(2)}) collective-permute-start(bf16[544,1024]{1,0:T(8,128)(2,1)} %pad_maximum_fusion.16), channel_id=1, source_target_pairs={{0,3},{1,2},{2,1},{3,0},{4,7},{5,6},{6,5},{7,4},{8,11},{9,10},{10,... | collective-permute-start | bytes 3342344 | tf_op jit(solution)/shard_map/ppermute | solution.py:632
  1247.5 201.1 %collective-permute-start.72 = (bf16[1024,3072]{1,0:T(8,128)(2,1)}, bf16[1024,3072]{1,0:T(8,128)(2,1)}, u32[]{:S(2)}, u32[]{:S(2)}) collective-permute-start(bf16[1024,3072]{1,0:T(8,128)(2,1)} %convolution_convert_fusion.3), channel_id=1, source_target_pairs={{0,4},{4,0},{8,12},{12,8},{16,20},{20,16},{24,28},{28,24},{1,5},{5... | collective-permute-start | bytes 18874376 | tf_op jit(solution)/shard_map/ppermute | solution.py:632
  1278.3 184.8 %collective-permute-start.64 = (bf16[1024,2048]{1,0:T(8,128)(2,1)}, bf16[1024,2048]{1,0:T(8,128)(2,1)}, u32[]{:S(2)}, u32[]{:S(2)}) collective-permute-start(bf16[1024,2048]{1,0:T(8,128)(2,1)} %convolution_convert_fusion.4), channel_id=1, source_target_pairs={{0,4},{4,0},{8,12},{12,8},{16,20},{20,16},{24,28},{28,24},{1,5},{5... | collective-permute-start | bytes 12582920 | tf_op jit(solution)/shard_map/ppermute | solution.py:632
  1334.3 212.6 %collective-permute-start.56 = (bf16[1024,4096]{1,0:T(8,128)(2,1)}, bf16[1024,4096]{1,0:T(8,128)(2,1)}, u32[]{:S(2)}, u32[]{:S(2)}) collective-permute-start(bf16[1024,4096]{1,0:T(8,128)(2,1)} %convolution_convert_fusion), channel_id=1, source_target_pairs={{0,4},{4,0},{8,12},{12,8},{16,20},{20,16},{24,28},{28,24},{1,5},{5... | collective-permute-start | bytes 25165832 | tf_op jit(solution)/shard_map/ppermute | solution.py:632
  1518.4 57.1 %collective-permute-start.88 = (bf16[256,3072]{1,0:T(8,128)(2,1)}, bf16[256,3072]{1,0:T(8,128)(2,1)}, u32[]{:S(2)}, u32[]{:S(2)}) collective-permute-start(bf16[256,3072]{1,0:T(8,128)(2,1)} %pad_maximum_fusion.12), channel_id=1, source_target_pairs={{0,16},{4,20},{8,24},{12,28},{16,0},{20,4},{24,8},{28,12},{1,17},{... | collective-permute-start | bytes 4718600 | tf_op jit(solution)/shard_map/ppermute | solution.py:632
  1519.2 57.5 %collective-permute-start.86 = (bf16[256,3072]{1,0:T(8,128)(2,1)}, bf16[256,3072]{1,0:T(8,128)(2,1)}, u32[]{:S(2)}, u32[]{:S(2)}) collective-permute-start(bf16[256,3072]{1,0:T(8,128)(2,1)} %pad_maximum_fusion.11), channel_id=1, source_target_pairs={{0,8},{4,12},{8,0},{12,4},{16,24},{20,28},{24,16},{28,20},{1,9},{5... | collective-permute-start | bytes 4718600 | tf_op jit(solution)/shard_map/ppermute | solution.py:632
  1559.5 81.5 %collective-permute-start.82 = (bf16[256,3072]{1,0:T(8,128)(2,1)}, bf16[256,3072]{1,0:T(8,128)(2,1)}, u32[]{:S(2)}, u32[]{:S(2)}) collective-permute-start(bf16[256,3072]{1,0:T(8,128)(2,1)} %pad_maximum_fusion.10), channel_id=1, source_target_pairs={{0,16},{4,20},{8,24},{12,28},{16,0},{20,4},{24,8},{28,12},{1,17},{... | collective-permute-start | bytes 4718600 | tf_op jit(solution)/shard_map/ppermute | solution.py:632
  1562.1 69.6 %collective-permute-start.57 = (bf16[128,4096]{1,0:T(8,128)(2,1)}, bf16[128,4096]{1,0:T(8,128)(2,1)}, u32[]{:S(2)}, u32[]{:S(2)}) collective-permute-start(bf16[128,4096]{1,0:T(8,128)(2,1)} %get-tuple-element.156), channel_id=1, source_target_pairs={{0,16},{4,20},{8,24},{12,28},{16,0},{20,4},{24,8},{28,12},{1,17},{... | collective-permute-start | bytes 3145736 | tf_op jit(solution)/shard_map/ppermute | solution.py:632
  1575.5 66.0 %collective-permute-start.80 = (bf16[256,3072]{1,0:T(8,128)(2,1)}, bf16[256,3072]{1,0:T(8,128)(2,1)S(1)}, u32[]{:S(2)}, u32[]{:S(2)}) collective-permute-start(bf16[256,3072]{1,0:T(8,128)(2,1)} %pad_maximum_fusion.9), channel_id=1, source_target_pairs={{0,8},{4,12},{8,0},{12,4},{16,24},{20,28},{24,16},{28,20},{1,9},{5... | collective-permute-start | bytes 4718600 | tf_op jit(solution)/shard_map/ppermute | solution.py:632
  1576.7 88.6 %collective-permute-start.76 = (bf16[256,3072]{1,0:T(8,128)(2,1)}, bf16[256,3072]{1,0:T(8,128)(2,1)S(1)}, u32[]{:S(2)}, u32[]{:S(2)}) collective-permute-start(bf16[256,3072]{1,0:T(8,128)(2,1)} %pad_maximum_fusion.8), channel_id=1, source_target_pairs={{0,16},{4,20},{8,24},{12,28},{16,0},{20,4},{24,8},{28,12},{1,17},{... | collective-permute-start | bytes 4718600 | tf_op jit(solution)/shard_map/ppermute | solution.py:632
  1597.1 71.1 %collective-permute-start.74 = (bf16[256,3072]{1,0:T(8,128)(2,1)S(1)}, bf16[256,3072]{1,0:T(8,128)(2,1)S(1)}, u32[]{:S(2)}, u32[]{:S(2)}) collective-permute-start(bf16[256,3072]{1,0:T(8,128)(2,1)S(1)} %copy-done.40), channel_id=1, source_target_pairs={{0,8},{4,12},{8,0},{12,4},{16,24},{20,28},{24,16},{28,20},{1,9},{5... | collective-permute-start | bytes 4718600 | tf_op jit(solution)/shard_map/ppermute | solution.py:632
  1641.1 75.7 %collective-permute-start.60 = (bf16[256,4096]{1,0:T(8,128)(2,1)}, bf16[256,4096]{1,0:T(8,128)(2,1)}, u32[]{:S(2)}, u32[]{:S(2)}) collective-permute-start(bf16[256,4096]{1,0:T(8,128)(2,1)} %pad_maximum_fusion.6), channel_id=1, source_target_pairs={{0,16},{4,20},{8,24},{12,28},{16,0},{20,4},{24,8},{28,12},{1,17},{... | collective-permute-start | bytes 6291464 | tf_op jit(solution)/shard_map/ppermute | solution.py:632
  1641.5 75.2 %collective-permute-start.58 = (bf16[256,4096]{1,0:T(8,128)(2,1)}, bf16[256,4096]{1,0:T(8,128)(2,1)}, u32[]{:S(2)}, u32[]{:S(2)}) collective-permute-start(bf16[256,4096]{1,0:T(8,128)(2,1)} %pad_maximum_fusion.5), channel_id=1, source_target_pairs={{0,8},{4,12},{8,0},{12,4},{16,24},{20,28},{24,16},{28,20},{1,9},{5... | collective-permute-start | bytes 6291464 | tf_op jit(solution)/shard_map/ppermute | solution.py:632
  1672.6 61.5 %collective-permute-start.77 = (bf16[256,1536]{1,0:T(8,128)(2,1)S(1)}, bf16[256,1536]{1,0:T(8,128)(2,1)}, u32[]{:S(2)}, u32[]{:S(2)}) collective-permute-start(bf16[256,1536]{1,0:T(8,128)(2,1)S(1)} %slice.578), channel_id=1, source_target_pairs={{0,2},{1,3},{2,0},{3,1},{4,6},{5,7},{6,4},{7,5},{8,10},{9,11},{10,... | collective-permute-start | bytes 2359304 | tf_op jit(solution)/shard_map/ppermute | solution.py:632
  (122 other events, 4364.5 us)

commit v2 on v1

v2 whole, which is shorter than its diff:
```python
import functools
import math

import jax
import jax.numpy as jnp
from jax import lax
from jax.experimental import pallas as pl
from jax.experimental.pallas import tpu as pltpu
from jax.sharding import PartitionSpec as P

HEAD_DIM = 128
TRUNK = 1152
BRANCH = 128
FORKS2 = 8
TREE_TOK = 2176
GROUP = 2

norm_eps = 1e-06
rope_base = 1000000.0
score_scale = HEAD_DIM ** (-0.5)
key_scale = score_scale * math.log2(math.e)
LN2 = math.log(2.0)
VMEM = 52 * 1024 * 1024
COST = 0.01

f32 = jnp.float32
bf16 = jnp.bfloat16


def dot_nn(a, b):
    return lax.dot_general(a, b, (((1,), (0,)), ((), ())), preferred_element_type=f32)


def dot_nt(a, b):
    return lax.dot_general(a, b, (((1,), (1,)), ((), ())), preferred_element_type=f32)


def contract_rows(a, b):
    return lax.dot_general(a, b, (((0,), (0,)), ((), ())), preferred_element_type=f32)


def params():
    return pltpu.CompilerParams(vmem_limit_bytes=VMEM)


def cost(flops, nbytes):
    return pl.CostEstimate(flops=int(flops * COST), bytes_accessed=int(nbytes * COST), transcendentals=0)


def nbytes(arrays):
    return sum(a.size * a.dtype.itemsize for a in arrays)


class Tiles:
    def __init__(self, arrays, parts, base, width):
        self.list = list(arrays)
        self.quarters = sum(a.shape[0] for a in self.list)
        self.depth = self.list[0].shape[1]
        self.parts, self.base, self.width = parts, base, width
        self.steps = self.quarters * parts

    def arrays(self):
        return self.list

    def scratch(self):
        return [pltpu.VMEM((2, self.depth, self.width), bf16), pltpu.SemaphoreType.DMA((2,))]

    def fetch(self, refs, buf, sems, step):
        slot = lax.rem(step, 2)
        quarter = lax.div(step, self.parts)
        part = step - quarter * self.parts
        col = pl.multiple_of((self.base + part) * self.width, 128)

        def begin(ref, at):
            pltpu.make_async_copy(
                ref.at[at, :, pl.ds(col, self.width)], buf.at[slot], sems.at[slot]
            ).start()

        split = self.list[0].shape[0]
        if len(refs) == 1:
            begin(refs[0], quarter)
        else:

            @pl.when(quarter < split)
            def _():
                begin(refs[0], quarter)

            @pl.when(quarter >= split)
            def _():
                begin(refs[1], quarter - split)

    def wait(self, refs, buf, sems, step):
        slot = lax.rem(step, 2)
        pltpu.make_async_copy(
            refs[0].at[0, :, pl.ds(0, self.width)], buf.at[slot], sems.at[slot]
        ).wait()
        return slot


def tiled_call(body, sets, seats, ins, in_specs, out_shape, out_specs, scratch, flops):
    steps = sets[0].steps
    counts = [len(s.arrays()) for s in sets]
    n_in, n_out = len(ins), len(out_shape)

    def kernel(seat_ref, *refs):
        at = 0
        piece_refs = []
        for c in counts:
            piece_refs.append(refs[at : at + c])
            at += c
        in_refs = refs[at : at + n_in]
        at += n_in
        out_refs = refs[at : at + n_out]
        at += n_out
        bufs = [(refs[at + 2 * i], refs[at + 2 * i + 1]) for i in range(len(sets))]
        own = refs[at + 2 * len(sets) :]
        step = pl.program_id(0)

        @pl.when(step == 0)
        def _():
            for s, p, (buf, sems) in zip(sets, piece_refs, bufs):
                s.fetch(p, buf, sems, step)

        @pl.when(step + 1 < steps)
        def _():
            for s, p, (buf, sems) in zip(sets, piece_refs, bufs):
                s.fetch(p, buf, sems, step + 1)

        tiles = []
        for s, p, (buf, sems) in zip(sets, piece_refs, bufs):
            slot = s.wait(p, buf, sems, step)
            tiles.append(buf.at[slot])
        body(step, tiles, in_refs, out_refs, own)

    weights = [a for s in sets for a in s.arrays()]
    return pl.pallas_call(
        kernel,
        grid_spec=pltpu.PrefetchScalarGridSpec(
            num_scalar_prefetch=1,
            grid=(steps,),
            in_specs=[pl.BlockSpec(memory_space=pl.ANY)] * len(weights) + in_specs,
            out_specs=out_specs,
            scratch_shapes=[x for s in sets for x in s.scratch()] + scratch,
        ),
        out_shape=out_shape,
        compiler_params=params(),
        cost_estimate=cost(flops, nbytes(weights) + nbytes(ins) + nbytes(out_shape)),
    )(seats, *weights, *ins)


def whole(array):
    return pl.BlockSpec(array.shape, lambda t, s: (0,) * len(array.shape))


def seated(rows, width, parts):
    return pl.BlockSpec(
        (None, rows, width),
        lambda t, s: (s[lax.div(t, parts)], 0, lax.rem(t, parts)),
    )


def head_slices(width):
    return [slice(h * HEAD_DIM, (h + 1) * HEAD_DIM) for h in range(width // HEAD_DIM)]


def project_qkv(normed, tiles, seats, cosine, sine, q_gain, k_gain):
    rows, tw = normed.shape[0], tiles.width

    def body(step, weights, ins, outs, own):
        a, cos_ref, sin_ref, qg, kg = ins
        hat, raw = outs
        acc = dot_nn(a[...], weights[0][...])
        part = lax.rem(step, 2)

        def turned(x, gain):
            inverse = lax.rsqrt(jnp.mean(x * x, axis=-1, keepdims=True) + norm_eps)
            u = x * inverse * gain
            return u * cos_ref[...] + pltpu.roll(u, HEAD_DIM // 2, 1) * sin_ref[...]

        @pl.when(part == 0)
        def _():
            for cut in head_slices(tw):
                hat[:, cut] = turned(acc[:, cut], qg[...]).astype(bf16)
            raw[...] = acc.astype(bf16)

        @pl.when(part == 1)
        def _():
            for cut in head_slices(tw // 2):
                hat[:, cut] = (turned(acc[:, cut], kg[...]) * key_scale).astype(bf16)
            hat[:, tw // 2 :] = acc[:, tw // 2 :].astype(bf16)
            raw[...] = acc.astype(bf16)

    ins = [normed, cosine, sine, q_gain, k_gain]
    shape = jax.ShapeDtypeStruct((tiles.quarters, rows, 2 * tw), bf16)
    return tiled_call(
        body,
        [tiles],
        seats,
        ins,
        [whole(x) for x in ins],
        [shape, shape],
        [seated(rows, tw, 2)] * 2,
        [],
        4 * rows * normed.shape[1] * tw * tiles.quarters,
    )


def project_rows(a, tiles, seats):
    rows, tw = a.shape[0], tiles.width

    def body(step, weights, ins, outs, own):
        outs[0][...] = dot_nn(ins[0][...], weights[0][...]).astype(bf16)

    return tiled_call(
        body,
        [tiles],
        seats,
        [a],
        [whole(a)],
        [jax.ShapeDtypeStruct((tiles.quarters, rows, tiles.parts * tw), bf16)],
        [seated(rows, tw, tiles.parts)],
        [],
        2 * rows * a.shape[1] * tw * tiles.steps,
    )[0]


def project_columns(lefts, sets, seats, depth, out_dtype):
    rows, tw, steps = lefts[0].shape[1], sets[0].width, sets[0].steps

    def body(step, weights, ins, outs, own):
        acc = own[0]
        total = dot_nt(ins[0][...], weights[0][...])
        for left, weight in zip(ins[1:], weights[1:]):
            total = total + dot_nt(left[...], weight[...])

        @pl.when(step == 0)
        def _():
            acc[...] = total

        @pl.when(step > 0)
        def _():
            acc[...] += total

        @pl.when(step == steps - 1)
        def _():
            outs[0][...] = acc[...].astype(out_dtype)

    return tiled_call(
        body,
        sets,
        seats,
        list(lefts),
        [seated(rows, tw, s.parts) for s in sets],
        [jax.ShapeDtypeStruct((rows, depth), out_dtype)],
        [pl.BlockSpec((rows, depth), lambda t, s: (0, 0))],
        [pltpu.VMEM((rows, depth), f32)],
        2 * rows * depth * tw * steps * len(sets),
    )[0]


def feed_forward(normed, gate_tiles, up_tiles, seats):
    rows, tw = normed.shape[0], gate_tiles.width

    def body(step, weights, ins, outs, own):
        a = ins[0][...]
        gate = dot_nn(a, weights[0][...])
        up = dot_nn(a, weights[1][...])
        outs[0][...] = (gate * jax.nn.sigmoid(gate) * up).astype(bf16)
        outs[1][...] = gate.astype(bf16)
        outs[2][...] = up.astype(bf16)

    shape = jax.ShapeDtypeStruct((gate_tiles.quarters, rows, gate_tiles.parts * tw), bf16)
    return tiled_call(
        body,
        [gate_tiles, up_tiles],
        seats,
        [normed],
        [whole(normed)],
        [shape] * 3,
        [seated(rows, tw, gate_tiles.parts)] * 3,
        [],
        4 * rows * normed.shape[1] * tw * gate_tiles.steps,
    )


def feed_back(cotangent, gate, up, down_tiles, seats):
    rows, tw = cotangent.shape[0], down_tiles.width

    def body(step, weights, ins, outs, own):
        grad = dot_nn(ins[0][...], weights[0][...])
        g = ins[1][...].astype(f32)
        u = ins[2][...].astype(f32)
        s = jax.nn.sigmoid(g)
        outs[0][...] = (grad * u * s * (1.0 + g * (1.0 - s))).astype(bf16)
        outs[1][...] = (grad * (g * s)).astype(bf16)

    shape = jax.ShapeDtypeStruct(gate.shape, bf16)
    tile = seated(rows, tw, down_tiles.parts)
    return tiled_call(
        body,
        [down_tiles],
        seats,
        [cotangent, gate, up],
        [whole(cotangent), tile, tile],
        [shape] * 2,
        [tile] * 2,
        [],
        2 * rows * cotangent.shape[1] * tw * down_tiles.steps,
    )


def qkv_back(grad_hat, raw, cosine, sine, q_gain, k_gain):
    quarters, rows, width = grad_hat.shape
    tw = width // 2

    def kernel(g_ref, r_ref, cos_ref, sin_ref, qg, kg, out, qsum, ksum):
        @pl.when(pl.program_id(0) == 0)
        def _():
            qsum[...] = jnp.zeros_like(qsum)
            ksum[...] = jnp.zeros_like(ksum)

        def back(cut, gain, total):
            w = g_ref[:, cut].astype(f32)
            w = w * cos_ref[...] + pltpu.roll(w * sin_ref[...], HEAD_DIM // 2, 1)
            x = r_ref[:, cut].astype(f32)
            inverse = lax.rsqrt(jnp.mean(x * x, axis=-1, keepdims=True) + norm_eps)
            u = x * inverse
            wu = w * u
            scaled = w * gain
            out[:, cut] = (
                inverse * (scaled - u * jnp.mean(wu * gain, axis=-1, keepdims=True))
            ).astype(bf16)
            return total + jnp.sum(wu, axis=0, keepdims=True)

        total = jnp.zeros((1, HEAD_DIM), f32)
        cuts = head_slices(width)
        n_query, n_key = tw // HEAD_DIM, tw // HEAD_DIM // 2
        for cut in cuts[:n_query]:
            total = back(cut, qg[...], total)
        qsum[...] += total
        total = jnp.zeros((1, HEAD_DIM), f32)
        for cut in cuts[n_query : n_query + n_key]:
            total = back(cut, kg[...], total)
        ksum[...] += total
        out[:, tw + tw // 2 :] = g_ref[:, tw + tw // 2 :]

    ins = [grad_hat, raw, cosine, sine, q_gain, k_gain]
    gain_shape = jax.ShapeDtypeStruct((1, HEAD_DIM), f32)
    out_shape = [jax.ShapeDtypeStruct(grad_hat.shape, bf16), gain_shape, gain_shape]
    tile = pl.BlockSpec((None, rows, width), lambda e: (e, 0, 0))
    fixed = lambda x: pl.BlockSpec(x.shape, lambda e: (0, 0))
    return pl.pallas_call(
        kernel,
        grid=(quarters,),
        in_specs=[tile, tile] + [fixed(x) for x in ins[2:]],
        out_specs=[tile, fixed(gain_shape), fixed(gain_shape)],
        out_shape=out_shape,
        compiler_params=params(),
        cost_estimate=cost(40 * quarters * rows * width, nbytes(ins) + nbytes(out_shape)),
    )(*ins)


def attention_specs(kv):
    q = pl.BlockSpec((TREE_TOK, GROUP * HEAD_DIM), lambda n, s: (0, n))
    k = pl.BlockSpec((TREE_TOK, HEAD_DIM), lambda n, s: (0, GROUP * kv + n))
    v = pl.BlockSpec((TREE_TOK, HEAD_DIM), lambda n, s: (0, (GROUP + 1) * kv + n))
    return q, k, v


def stacked(ref, start):
    rows = pl.ds(start, BRANCH)
    return jnp.concatenate(
        [ref[rows, h * HEAD_DIM : (h + 1) * HEAD_DIM] for h in range(GROUP)], axis=0
    )


def causal():
    key = lax.broadcasted_iota(jnp.int32, (BRANCH, GROUP * BRANCH), 0)
    query = lax.rem(lax.broadcasted_iota(jnp.int32, (BRANCH, GROUP * BRANCH), 1), BRANCH)
    return key <= query


TRUNK_BLOCKS = TRUNK // BRANCH
BLOCKS = TREE_TOK // BRANCH


def attention_forward(qkv, parents, kv):
    def kernel(parent_ref, q_ref, k_ref, v_ref, out_ref, log_ref, vt):
        vt[...] = v_ref[...].T
        mask = causal()

        def part(q, start, size, rule):
            score = dot_nt(k_ref[pl.ds(start, size), :], q)
            weight = jnp.exp2(score)
            if rule is not None:
                weight = rule(weight)
            out = dot_nn(vt[:, pl.ds(start, size)], weight.astype(bf16))
            return out, jnp.sum(weight, axis=0, keepdims=True)

        def finish(block, start, pieces):
            out = sum(p[0] for p in pieces)
            total = sum(p[1] for p in pieces)
            out = (out / total).T.astype(bf16)
            for h in range(GROUP):
                out_ref[pl.ds(start, BRANCH), h * HEAD_DIM : (h + 1) * HEAD_DIM] = out[
                    h * BRANCH : (h + 1) * BRANCH
                ]
            log_ref[0, pl.ds(block, 1), :] = jnp.log2(total)

        diagonal = lambda w: jnp.where(mask, w, 0.0)
        for block in range(TRUNK_BLOCKS):
            q = stacked(q_ref, block * BRANCH)
            pieces = [part(q, block * BRANCH, BRANCH, diagonal)]
            if block > 0:
                pieces.append(part(q, 0, block * BRANCH, None))
            finish(block, block * BRANCH, pieces)

        def branch(i, carry):
            block = TRUNK_BLOCKS + i
            start = pl.multiple_of(block * BRANCH, BRANCH)
            q = stacked(q_ref, start)
            parent = parent_ref[i]
            has = (parent != block).astype(f32)
            pieces = [
                part(q, start, BRANCH, diagonal),
                part(q, pl.multiple_of(parent * BRANCH, BRANCH), BRANCH, lambda w: w * has),
                part(q, 0, TRUNK, None),
            ]
            finish(block, start, pieces)
            return carry

        lax.fori_loop(0, FORKS2, branch, 0)

    q, k, v = attention_specs(kv)
    out_shape = [
        jax.ShapeDtypeStruct((TREE_TOK, GROUP * kv * HEAD_DIM), bf16),
        jax.ShapeDtypeStruct((kv, BLOCKS, GROUP * BRANCH), f32),
    ]
    return pl.pallas_call(
        kernel,
        grid_spec=pltpu.PrefetchScalarGridSpec(
            num_scalar_prefetch=1,
            grid=(kv,),
            in_specs=[q, k, v],
            out_specs=[
                q,
                pl.BlockSpec((1, BLOCKS, GROUP * BRANCH), lambda n, s: (n, 0, 0)),
            ],
            scratch_shapes=[pltpu.VMEM((HEAD_DIM, TREE_TOK), bf16)],
        ),
        out_shape=out_shape,
        compiler_params=params(),
        cost_estimate=cost(kv * 2.2e6 * 2 * GROUP * 256 * 2, nbytes([qkv]) + nbytes(out_shape)),
    )(parents, qkv, qkv, qkv)


def attention_backward(qkv, attended, grads, logs, parents, kv):
    width = qkv.shape[1]

    def kernel(
        parent_ref, q_ref, k_ref, v_ref, o_ref, do_ref, log_ref, out_ref, kt, dk, dv, dq_ref
    ):
        kt[...] = k_ref[...].T
        dk[...] = jnp.zeros_like(dk)
        dv[...] = jnp.zeros_like(dv)
        mask = causal()

        def part(q, do, log, delta, start, size, rule):
            rows = pl.ds(start, size)
            prob = jnp.exp2(dot_nt(k_ref[rows, :], q) - log)
            if rule is not None:
                prob = rule(prob)
            grad = dot_nt(v_ref[rows, :], do)
            score_grad = (prob * (grad - delta)).astype(bf16)
            dk[rows, :] += dot_nn(score_grad, q)
            dv[rows, :] += dot_nn(prob.astype(bf16), do)
            return dot_nn(kt[:, rows], score_grad)

        def one(block, start, ranges):
            q = stacked(q_ref, start)
            do = stacked(do_ref, start)
            o = stacked(o_ref, start)
            delta = jnp.sum((do.astype(f32) * o.astype(f32)).T, axis=0, keepdims=True)
            log = log_ref[0, pl.ds(block, 1), :]
            total = sum(part(q, do, log, delta, *r) for r in ranges)
            out = (total * LN2).T.astype(bf16)
            for h in range(GROUP):
                dq_ref[pl.ds(start, BRANCH), h * HEAD_DIM : (h + 1) * HEAD_DIM] = out[
                    h * BRANCH : (h + 1) * BRANCH
                ]

        diagonal = lambda p: jnp.where(mask, p, 0.0)
        for block in range(TRUNK_BLOCKS):
            ranges = [(block * BRANCH, BRANCH, diagonal)]
            if block > 0:
                ranges.append((0, block * BRANCH, None))
            one(block, block * BRANCH, ranges)

        def branch(i, carry):
            block = TRUNK_BLOCKS + i
            start = pl.multiple_of(block * BRANCH, BRANCH)
            parent = parent_ref[i]
            has = (parent != block).astype(f32)
            one(
                block,
                start,
                [
                    (start, BRANCH, diagonal),
                    (pl.multiple_of(parent * BRANCH, BRANCH), BRANCH, lambda p: p * has),
                    (0, TRUNK, None),
                ],
            )
            return carry

        lax.fori_loop(0, FORKS2, branch, 0)
        for head in range(kv):

            @pl.when(pl.program_id(0) == head)
            def _(head=head):
                wide = GROUP * HEAD_DIM
                out_ref[:, head * wide : (head + 1) * wide] = dq_ref[...]
                at = kv * wide + head * HEAD_DIM
                out_ref[:, at : at + HEAD_DIM] = (dk[...] * score_scale).astype(bf16)
                at += kv * HEAD_DIM
                out_ref[:, at : at + HEAD_DIM] = dv[...].astype(bf16)

    q, k, v = attention_specs(kv)
    out_shape = jax.ShapeDtypeStruct((TREE_TOK, width), bf16)
    return pl.pallas_call(
        kernel,
        grid_spec=pltpu.PrefetchScalarGridSpec(
            num_scalar_prefetch=1,
            grid=(kv,),
            in_specs=[
                q,
                k,
                v,
                q,
                q,
                pl.BlockSpec((1, BLOCKS, GROUP * BRANCH), lambda n, s: (n, 0, 0)),
            ],
            out_specs=pl.BlockSpec((TREE_TOK, width), lambda n, s: (0, 0)),
            scratch_shapes=[
                pltpu.VMEM((HEAD_DIM, TREE_TOK), bf16),
                pltpu.VMEM((TREE_TOK, HEAD_DIM), f32),
                pltpu.VMEM((TREE_TOK, HEAD_DIM), f32),
                pltpu.VMEM((TREE_TOK, GROUP * HEAD_DIM), bf16),
            ],
        ),
        out_shape=out_shape,
        compiler_params=params(),
        cost_estimate=cost(
            kv * 2.2e6 * 2 * GROUP * 640 * 2, nbytes([qkv, attended, grads, qkv])
        ),
    )(parents, qkv, qkv, qkv, attended, grads, logs)


def weight_gradient(lefts, rights, half, cut=None):
    pairs = len(lefts)
    rows, depth = lefts[0].shape
    quarters, _, width = rights[0].shape
    size = depth // 2
    if cut is None:
        tw = width // 2 if width > 1024 else width
        parts, first = width // tw, 0
    else:
        width = tw = width // 2
        parts, first = 1, cut

    def kernel(*refs):
        left_refs, right_refs = refs[:pairs], refs[pairs : 2 * pairs]
        out_ref, left_s, right_s = refs[2 * pairs :]

        @pl.when(pl.program_id(0) == 0)
        def _():
            for i, ref in enumerate(left_refs):
                left_s[i * rows : (i + 1) * rows] = ref[...]

        for i, ref in enumerate(right_refs):
            right_s[i * rows : (i + 1) * rows] = ref[...]
        out_ref[...] = contract_rows(left_s[...], right_s[...]).astype(bf16)

    out_shape = jax.ShapeDtypeStruct((size, quarters * width), bf16)
    arrays = list(lefts) + list(rights)
    return pl.pallas_call(
        kernel,
        grid=(quarters * parts,),
        in_specs=[pl.BlockSpec((rows, size), lambda t: (0, half))] * pairs
        + [pl.BlockSpec((None, rows, tw), lambda t: (t // parts, 0, first + t % parts))] * pairs,
        out_specs=pl.BlockSpec((size, tw), lambda t: (0, t)),
        out_shape=out_shape,
        scratch_shapes=[
            pltpu.VMEM((pairs * rows, size), bf16),
            pltpu.VMEM((pairs * rows, tw), bf16),
        ],
        compiler_params=params(),
        cost_estimate=cost(
            2 * pairs * rows * size * quarters * width, nbytes(arrays) + nbytes([out_shape])
        ),
    )(*arrays)


def flipped(index, mask):
    bit = 1
    while bit <= mask:
        if mask & bit:
            index = index + bit * (1 - 2 * lax.rem(lax.div(index, bit), 2))
        bit *= 2
    return index


def transfer_call(
    program, m, n, ins, outs, scratch, count, locals_, number, vmem_ins=(), aliases=None
):
    n_in, n_out, n_scratch = len(ins), len(outs), len(scratch)

    class Mover:
        def __init__(self, send, recv, own):
            self.send, self.recv, self.own = send, recv, own
            self.made, self.local = [], []

        def start(self, source, target, axis, mask):
            k = len(self.made)
            place = flipped(lax.axis_index(axis), mask)
            copy = pltpu.make_async_remote_copy(
                src_ref=source,
                dst_ref=target,
                send_sem=self.send.at[k],
                recv_sem=self.recv.at[k],
                device_id={axis: place},
                device_id_type=pl.DeviceIdType.MESH,
            )
            copy.start()
            self.made.append(copy)
            return copy

        def keep(self, source, target):
            copy = pltpu.make_async_copy(source, target, self.own.at[len(self.local)])
            copy.start()
            self.local.append(copy)
            return copy

    def kernel(*refs):
        in_refs, out_refs = refs[:n_in], refs[n_in : n_in + n_out]
        rest = refs[n_in + n_out :]
        mover = Mover(*rest[n_scratch:])
        barrier = pltpu.get_barrier_semaphore()
        partners = [("wide", k) for k in range(1, m)] if m != 8 else [
            ("wide", k) for k in (1, 2, 4)
        ]
        partners += [("tp", e) for e in range(1, n)]
        for axis, mask in partners:
            pl.semaphore_signal(
                barrier,
                inc=1,
                device_id={axis: flipped(lax.axis_index(axis), mask)},
                device_id_type=pl.DeviceIdType.MESH,
            )
        pl.semaphore_wait(barrier, len(partners))
        program(mover, in_refs, out_refs, rest[:n_scratch])
        for copy in mover.made:
            copy.wait_send()

    return pl.pallas_call(
        kernel,
        in_specs=[
            pl.BlockSpec(memory_space=pltpu.VMEM if i in vmem_ins else pl.ANY) for i in range(n_in)
        ],
        out_specs=[pl.BlockSpec(memory_space=pl.ANY)] * n_out,
        out_shape=outs,
        scratch_shapes=list(scratch)
        + [
            pltpu.SemaphoreType.DMA((count,)),
            pltpu.SemaphoreType.DMA((count,)),
            pltpu.SemaphoreType.DMA((locals_,)),
        ],
        input_output_aliases=aliases or {},
        compiler_params=pltpu.CompilerParams(
            collective_id=number, has_side_effects=True, vmem_limit_bytes=VMEM
        ),
        cost_estimate=cost(0, 1e6),
    )(*ins)


class Spread:
    def __init__(self, mover, m, source, target, block):
        self.mover, self.m, self.source, self.block = mover, m, source, block
        self.at = lambda start, size: target(pl.ds(start, size))

    def first(self):
        go, block, source = self.mover.start, self.block, self.source
        if self.m != 8:
            self.all = [
                go(source, self.at(k * block, block), "wide", k) for k in range(1, self.m)
            ]
            return
        self.x = go(source, self.at(block, block), "wide", 2)
        self.y = go(source, self.at(2 * block, block), "wide", 4)
        self.cores = [go(source, self.at(4 * block, block), "wide", 1)]

    def second(self):
        if self.m != 8:
            return
        go, block = self.mover.start, self.block
        half = block // 2
        self.x.wait_recv()
        low = self.at(block + half, half)
        self.low = go(low, self.at(3 * block + half, half), "wide", 4)
        self.cores.append(go(self.at(block, block), self.at(5 * block, block), "wide", 1))
        self.y.wait_recv()
        top = self.at(2 * block, half)
        self.top = go(top, self.at(3 * block, half), "wide", 2)
        self.cores.append(go(self.at(2 * block, block), self.at(6 * block, block), "wide", 1))

    def third(self):
        if self.m != 8:
            return
        go, block = self.mover.start, self.block
        self.low.wait_recv()
        self.top.wait_recv()
        self.cores.append(go(self.at(3 * block, block), self.at(7 * block, block), "wide", 1))

    def last(self):
        for copy in self.all if self.m != 8 else self.cores:
            copy.wait_recv()


def struct(*shape):
    return jax.ShapeDtypeStruct(shape, bf16)


def gather_front(m, n, qkv_block, in_block, down_block):
    block, qw = qkv_block.shape
    fw, dw = in_block.shape[1], down_block.shape[1]
    depth = block * m
    pairs = n // 2

    def program(mover, ins, outs, _):
        qkv, inner, down = ins
        weights, in_own, in_rest, down_rest = outs
        rows = pl.ds(0, block)
        waves = [mover.start(qkv, weights.at[e, rows], "tp", e) for e in range(1, n)]
        kept = [mover.keep(qkv, weights.at[0, rows]), mover.keep(inner, in_own.at[0, rows])]
        spreads = [
            Spread(
                mover,
                m,
                qkv if q == 0 else weights.at[q, rows],
                lambda r, q=q: weights.at[q, r],
                block,
            )
            for q in range(n)
        ]
        spreads[0].first()
        spreads[0].second()
        spreads[0].third()
        for q in range(1, n):
            waves[q - 1].wait_recv()
            spreads[q].first()
        late = []
        for e in range(1, pairs):
            late.append(mover.start(inner, in_rest.at[e - 1, rows], "tp", 2 * e))
            late.append(mover.start(down, down_rest.at[e - 1, rows], "tp", 2 * e))
        for q in range(1, n):
            spreads[q].second()
        own = Spread(mover, m, inner, lambda r: in_own.at[0, r], block)
        own.first()
        for q in range(1, n):
            spreads[q].third()
        own.second()
        own.third()
        for spread in spreads:
            spread.last()
        own.last()
        for copy in late:
            copy.wait_recv()
        for copy in kept:
            copy.wait()

    per = 8 if m == 8 else m - 1
    return transfer_call(
        program,
        m,
        n,
        [qkv_block, in_block, down_block],
        [
            struct(n, depth, qw),
            struct(1, depth, fw),
            struct(pairs - 1, depth, fw),
            struct(pairs - 1, depth, dw),
        ],
        [],
        (n - 1) + per * (n + 1) + 2 * (pairs - 1),
        2,
        1,
        vmem_ins=(0, 1, 2),
    )


def swap_heads(mover, n, mine, source, target):
    seat = lax.axis_index("tp")
    load = mover.keep(source.at[seat], mine)
    sends = [
        mover.start(source.at[flipped(seat, e)], target.at[seat], "tp", e) for e in range(1, n)
    ]
    load.wait()
    return sends, mover.keep(mine, target.at[seat])


def gather_middle(m, n, hats, in_rest, out_block, down_block):
    quarters, rows, width = hats.shape
    pairs, depth, fw = in_rest.shape
    block, ow = out_block.shape
    dw = down_block.shape[1]

    def program(mover, ins, outs, scratch):
        hat, _, out, down = ins
        heads, rest, weights, down_own = outs
        first = pl.ds(0, block)
        kept = [mover.keep(out, weights.at[0, first]), mover.keep(down, down_own.at[0, first])]
        waves = [mover.start(out, weights.at[e, first], "tp", e) for e in range(1, n)]
        spreads = [
            Spread(mover, m, rest.at[p, first], lambda r, p=p: rest.at[p, r], block)
            for p in range(pairs)
        ]
        for spread in spreads:
            spread.first()
        for copy in waves:
            copy.wait_recv()
        sends, own_row = swap_heads(mover, n, scratch[0], hat, heads)
        kept[0].wait()
        for spread in spreads:
            spread.second()
        quarter = Spread(mover, m, weights.at[:, first], lambda r: weights.at[:, r], block)
        quarter.first()
        for spread in spreads:
            spread.third()
        quarter.second()
        own = Spread(mover, m, down, lambda r: down_own.at[0, r], block)
        own.first()
        quarter.third()
        own.second()
        own.third()
        for spread in spreads + [own, quarter]:
            spread.last()
        for copy in sends:
            copy.wait_recv()
        kept[1].wait()
        own_row.wait()

    per = 8 if m == 8 else m - 1
    return transfer_call(
        program,
        m,
        n,
        [hats, in_rest, out_block, down_block],
        [
            struct(n, rows, width),
            struct(pairs, depth, fw),
            struct(n, depth, ow),
            struct(1, depth, dw),
        ],
        [pltpu.VMEM((rows, width), bf16)],
        2 * (n - 1) + per * (pairs + 2),
        4,
        2,
        vmem_ins=(2, 3),
        aliases={1: 1},
    )


def gather_late(m, n, heads, down_rest):
    quarters, rows, width = heads.shape
    pairs, depth, dw = down_rest.shape
    block = depth // m

    def program(mover, ins, outs, scratch):
        source, _ = ins
        target, rest = outs
        first = pl.ds(0, block)
        sends, own_row = swap_heads(mover, n, scratch[0], source, target)
        spreads = [
            Spread(mover, m, rest.at[p, first], lambda r, p=p: rest.at[p, r], block)
            for p in range(pairs)
        ]
        for stage in ("first", "second", "third", "last"):
            for spread in spreads:
                getattr(spread, stage)()
        for copy in sends:
            copy.wait_recv()
        own_row.wait()

    per = 8 if m == 8 else m - 1
    return transfer_call(
        program,
        m,
        n,
        [heads, down_rest],
        [struct(n, rows, width), struct(pairs, depth, dw)],
        [pltpu.VMEM((rows, width), bf16)],
        (n - 1) + per * pairs,
        2,
        3,
        aliases={1: 1},
    )


def shuffle_columns(a, order):
    rows, count = a.shape[0], order.shape[0]
    width = a.shape[1] // count

    def kernel(order_ref, in_ref, out_ref):
        out_ref[...] = in_ref[...]

    return pl.pallas_call(
        kernel,
        grid_spec=pltpu.PrefetchScalarGridSpec(
            num_scalar_prefetch=1,
            grid=(count,),
            in_specs=[pl.BlockSpec((rows, width), lambda k, s: (0, s[k]))],
            out_specs=pl.BlockSpec((rows, width), lambda k, s: (0, k)),
        ),
        out_shape=jax.ShapeDtypeStruct(a.shape, a.dtype),
        cost_estimate=cost(0, 2 * nbytes([a])),
    )(order, a)


def inverse_rms(values):
    return lax.rsqrt(jnp.mean(values * values, axis=-1, keepdims=True) + norm_eps)


def norm_back(grads, unit_values, inverse, gain):
    scaled = grads * gain
    return inverse * (scaled - unit_values * jnp.mean(scaled * unit_values, axis=-1, keepdims=True))


def after(values, *conditions):
    return lax.optimization_barrier((values, conditions))[0]


class Job:
    def __init__(self, stages):
        self.stages = stages
        self.result = None
        self.started, self.pending = next(stages)

    def advance(self, came):
        try:
            self.started, self.pending = self.stages.send(came)
        except StopIteration as stop:
            self.result = stop.value
            self.pending = None

    def finish(self):
        while self.result is None:
            self.advance(self.pending)
        return self.result


def tick(values, *jobs):
    jobs = [j for j in jobs if j.result is None]
    values, came = lax.optimization_barrier((values, [j.pending for j in jobs]))
    for j, c in zip(jobs, came):
        j.advance(c)
    return values


def local(
    m,
    n,
    tokens,
    out_grad,
    seg_ids,
    parent_table,
    path_pos,
    attn_gain,
    w_query,
    w_key,
    w_value,
    w_out,
    q_gain,
    k_gain,
    ffn_gain,
    w_gate,
    w_up,
    w_down,
):
    rows, depth = tokens.shape
    block = depth // m
    order = [0, 2, 4, 6, 1, 3, 5, 7] if m == 8 else list(range(m))
    where = lax.axis_index("wide").astype(jnp.int32)
    seat = lax.axis_index("tp").astype(jnp.int32)
    relative = jnp.asarray(order, jnp.int32) ^ where
    inverse_order = [order.index(k) for k in range(m)]
    absolute = jnp.take(jnp.asarray(inverse_order, jnp.int32), jnp.arange(m, dtype=jnp.int32) ^ where)
    seats = jnp.arange(n, dtype=jnp.int32) ^ seat
    plain = jnp.arange(n, dtype=jnp.int32)

    def over(axis, a, mask):
        size = m if axis == "wide" else n
        return lax.ppermute(a, axis, [(i, i ^ mask) for i in range(size)])

    def scatter(mine, other):
        if m != 8:
            both = jnp.concatenate([mine, other])
            got = yield both, [over("wide", both[k * block : (k + 1) * block], k) for k in range(1, m)]
            return sum((g.astype(f32) for g in got), both[:block].astype(f32))
        half = block // 2
        (came,) = yield (mine, other), [over("wide", other, 1)]

        def total(start, size):
            cut = slice(start, start + size)
            return mine[cut].astype(f32) + came[cut].astype(f32)

        sources = [
            total(3 * block, half).astype(bf16),
            total(3 * block + half, half).astype(bf16),
        ]
        top, low = yield sources, [over("wide", sources[0], 2), over("wide", sources[1], 4)]
        for_x = jnp.concatenate(
            [
                total(block, half).astype(bf16),
                (total(block + half, half) + low.astype(f32)).astype(bf16),
            ]
        )
        for_y = jnp.concatenate(
            [
                (total(2 * block, half) + top.astype(f32)).astype(bf16),
                total(2 * block + half, half).astype(bf16),
            ]
        )
        from_x, from_y = yield [for_x, for_y], [over("wide", for_x, 2), over("wide", for_y, 4)]
        return total(0, block) + from_x.astype(f32) + from_y.astype(f32)

    def wide_products(left, rights, cut=None):
        other = weight_gradient(left, rights, 1, cut)
        return weight_gradient(after(left, other), rights, 0, cut), other

    cotangent = shuffle_columns(out_grad, relative)

    def ffn_share(left, rights):
        total = yield from scatter(*wide_products(left, rights))
        parts = [total[:, e * fcols : (e + 1) * fcols].astype(bf16) for e in range(1, n // 2)]
        sent = yield parts, [over("tp", p, 2 * (e + 1)) for e, p in enumerate(parts)]
        return sum((x.astype(f32) for x in sent), total[:, :fcols])

    def swap(a):
        return lax.all_to_all(a, "tp", split_axis=0, concat_axis=0, tiled=True)

    def attn_share(left, right, cut=None):
        total = yield from scatter(*wide_products([left], [right], cut))
        parts = total.astype(bf16).reshape(block, n, -1).transpose(1, 0, 2)
        (came,) = yield parts, [swap(parts)]
        return jnp.sum(came.astype(f32), axis=0)

    def gather_small(a):
        stack = a[None]
        size = 1
        while size < m:
            stack = jnp.concatenate([stack, over("wide", stack, order[size])])
            size *= 2
        return stack

    qkv_block = jnp.concatenate([w_query, w_key, w_value], axis=1)
    out_block = w_out.T
    in_block = jnp.concatenate([w_gate, w_up], axis=1)
    down_block = w_down.T
    aw = w_query.shape[1]
    kv = w_key.shape[1] // HEAD_DIM
    fcols = w_gate.shape[1]
    fw = fcols // 3

    gains = gather_small(jnp.concatenate([attn_gain, ffn_gain, q_gain, k_gain])[None])[:, 0]
    gains = gains.astype(f32)
    small = q_gain.shape[0]
    gain_one = gains[:, :block].reshape(1, depth)
    gain_two = gains[:, block : 2 * block].reshape(1, depth)
    head_gains = jnp.take(gains[:, 2 * block :], absolute, axis=0)
    gain_q = head_gains[:, :small].reshape(1, HEAD_DIM)
    gain_k = head_gains[:, small:].reshape(1, HEAD_DIM)

    base = where * parent_table.shape[0]
    block_segs = seg_ids[TRUNK::BRANCH] - base
    hit = block_segs[:, None] == jnp.arange(parent_table.shape[0], dtype=jnp.int32)[None, :]
    block_parents = jnp.sum(jnp.where(hit, parent_table[None, :] - base, 0), axis=1)
    match = block_parents[:, None] == block_segs[None, :]
    number = TRUNK_BLOCKS + jnp.arange(FORKS2, dtype=jnp.int32)
    parents = jnp.where(
        jnp.any(match, axis=1), jnp.sum(jnp.where(match, number[None, :], 0), axis=1), number
    ).astype(jnp.int32)

    own_pos = lax.dynamic_slice_in_dim(path_pos, seat * rows, rows, 0).astype(f32)
    frequency = rope_base ** (-(jnp.arange(HEAD_DIM // 2, dtype=f32) * 2.0) / HEAD_DIM)
    angles = own_pos[:, None] * frequency[None, :]
    cosine, sine = jnp.cos(angles), jnp.sin(angles)
    cosine = jnp.concatenate([cosine, cosine], axis=-1)
    sine = jnp.concatenate([-sine, sine], axis=-1)

    stream = shuffle_columns(tokens, relative).astype(f32)
    inverse_one = inverse_rms(stream)
    unit_one = stream * inverse_one
    normed_one = (unit_one * gain_one).astype(bf16)

    qkv_all, in_own, in_rest, down_rest = gather_front(m, n, qkv_block, in_block, down_block)
    qkv_tiles = Tiles([qkv_all], 2, 0, aw)
    hats, raws = project_qkv(normed_one, qkv_tiles, seats, cosine, sine, gain_q, gain_k)
    qkv, in_rest, out_all, down_own = gather_middle(m, n, hats, in_rest, out_block, down_block)
    qkv = qkv.reshape(n * rows, -1)
    attended_heads, logs = attention_forward(qkv, parents, kv)
    attended, down_rest = gather_late(m, n, attended_heads.reshape(n, rows, -1), down_rest)
    out_tiles = Tiles([out_all], 1, 0, aw)
    after_attn = stream + project_columns([attended], [out_tiles], seats, depth, f32)

    inverse_two = inverse_rms(after_attn)
    unit_two = after_attn * inverse_two
    normed_two = (unit_two * gain_two).astype(bf16)
    normed_two_next = over("tp", normed_two, 1)

    gate_tiles = Tiles([in_own, in_rest], 3, 0, fw)
    up_tiles = Tiles([in_own, in_rest], 3, 3, fw)
    down_tiles = Tiles([down_own, down_rest], 3, 0, fw)

    hidden, gate, up = feed_forward(normed_two, gate_tiles, up_tiles, plain)
    down = project_columns([hidden], [down_tiles], plain, depth, f32)
    normed_two_next, cotangent_sent = after((normed_two_next, cotangent), (down, normed_two_next))
    cotangent_next = over("tp", cotangent_sent, 1)
    hidden_next, gate_next, up_next = feed_forward(normed_two_next, gate_tiles, up_tiles, plain)
    down_part = project_columns([hidden_next], [down_tiles], plain, depth, bf16)
    cotangent_next, hidden_late = after((cotangent_next, hidden), down_part)
    down_job = Job(ffn_share([cotangent, cotangent_next], [hidden_late, hidden_next]))
    cotangent_next = after(cotangent_next, down_job.started)
    gate_grad_next, up_grad_next = feed_back(
        cotangent_next, gate_next, up_next, down_tiles, plain
    )
    back_part = project_columns(
        [gate_grad_next, up_grad_next], [gate_tiles, up_tiles], plain, depth, bf16
    )
    back_next = over("tp", back_part, 1)
    own_grad = tick(after(cotangent, back_part), down_job)
    own_grad = after(own_grad, down_job.started)
    gate_grad, up_grad = feed_back(own_grad, gate, up, down_tiles, plain)
    gate_job = Job(ffn_share([normed_two, normed_two_next], [gate_grad, gate_grad_next]))
    gate_late, up_late = after((gate_grad, up_grad), gate_job.started)
    gate_late, up_late = tick((gate_late, up_late), down_job, gate_job)
    gate_late, up_late = after((gate_late, up_late), down_job.started, gate_job.started)
    back = project_columns([gate_late, up_late], [gate_tiles, up_tiles], plain, depth, f32)
    back, back_next = after((back, back_next), back)
    back = tick(back, down_job, gate_job)
    back = after(back, down_job.started, gate_job.started)
    normed_two_grad = back + back_next.astype(f32)

    ffn_gain_part = jnp.sum(normed_two_grad * unit_two, axis=0)
    stream_grad = cotangent.astype(f32) + norm_back(
        normed_two_grad, unit_two, inverse_two, gain_two
    )
    grad_low = stream_grad.astype(bf16)
    attended_grad = project_rows(grad_low, out_tiles, seats)
    grad_heads = swap(attended_grad).reshape(n * rows, -1)
    grad_heads = tick(grad_heads, gate_job)
    grad_heads = after(grad_heads, gate_job.started)
    down_next = over("tp", after(down_part, grad_heads), 1)
    back_hats = attention_backward(qkv, attended_heads, grad_heads, logs, parents, kv)
    back_hats_own = swap(back_hats.reshape(n, rows, -1))
    lefts, up_grads, grad_low, down_next, after_attn = after(
        (
            [normed_two, normed_two_next],
            [up_grad, up_grad_next],
            grad_low,
            down_next,
            after_attn,
        ),
        back_hats,
    )
    up_job = Job(ffn_share(lefts, up_grads))
    grad_low = tick(after(grad_low, up_job.started), up_job)
    grad_low = after(grad_low, up_job.started)
    out_job = Job(attn_share(grad_low, attended))
    down_next, after_attn = after((down_next, after_attn), out_job.started)
    mixed = (after_attn + down + down_next.astype(f32)).astype(bf16)
    mixed = shuffle_columns(mixed, absolute)
    mixed = tick(mixed, up_job, out_job)
    back_hats_own = after(back_hats_own, mixed, up_job.started, out_job.started)
    raw_grads, q_sum, k_sum = qkv_back(back_hats_own, raws, cosine, sine, gain_q, gain_k)
    q_job = Job(attn_share(normed_one, raw_grads, 0))
    raw_late = after(raw_grads, q_job.started)
    k_job = Job(attn_share(normed_one, raw_late, 1))
    raw_late = tick(after(raw_late, k_job.started), up_job, out_job, q_job)
    raw_late = after(raw_late, q_job.started, out_job.started)
    normed_one_grad = project_columns([raw_late], [qkv_tiles], seats, depth, f32)
    normed_one_grad = tick(normed_one_grad, out_job, q_job, k_job)
    normed_one_grad = after(normed_one_grad, q_job.started, k_job.started)
    attn_gain_part = jnp.sum(normed_one_grad * unit_one, axis=0)
    tokens_grad = (
        stream_grad + norm_back(normed_one_grad, unit_one, inverse_one, gain_one)
    ).astype(bf16)
    tokens_grad = shuffle_columns(tokens_grad, absolute)

    parts = jnp.concatenate(
        [
            attn_gain_part.reshape(m, block),
            ffn_gain_part.reshape(m, block),
            jnp.take(q_sum.reshape(m, small), relative, axis=0),
            jnp.take(k_sum.reshape(m, small), relative, axis=0),
        ],
        axis=1,
    )
    size = m
    while size > 1:
        size //= 2
        parts = parts[:size] + over("wide", parts[size:], order[size])
    step = 1
    while step < n:
        parts = parts + over("tp", parts, step)
        step *= 2
    sums = parts[0]
    gate_share, up_share = gate_job.finish(), up_job.finish()
    down_share, out_share = down_job.finish().T, out_job.finish().T
    q_share, k_share = q_job.finish(), k_job.finish()
    return (
        mixed,
        tokens_grad,
        sums[:block],
        q_share,
        k_share[:, : aw // 2],
        k_share[:, aw // 2 :],
        out_share,
        sums[2 * block : 2 * block + small],
        sums[2 * block + small :],
        sums[block : 2 * block],
        gate_share,
        up_share,
        down_share,
    )


def solution(mesh):
    both = P(("wide", "tp"), None)
    w, wt, tw = P("wide"), P("wide", "tp"), P("tp", "wide")
    return jax.shard_map(
        functools.partial(local, mesh.shape["wide"], mesh.shape["tp"]),
        mesh=mesh,
        in_specs=(both, both, w, w, w, w, wt, wt, wt, tw, w, w, w, wt, wt, tw),
        out_specs=(both, both, w, wt, wt, wt, tw, w, w, w, wt, wt, tw),
        check_vma=False,
    )
```

time: 1780 us -> 1280 us (0.72)
  waiting for transfers between devices: 733 us -> 259 us
  Pallas kernels: 531 us -> 789 us
  matrix products: 121 us -> 0 us
  blocking collectives: 85.5 us -> 0 us
  local copies, waits for them, and re-layouts: 75.4 us -> 25.2 us
  starting transfers between devices: 124 us -> 75.3 us
    ppermute x90 -> x45, waiting for transfers between devices: 733 us -> 189 us  [over(): return lax.ppermute(a, axis, [(i, i ^ mask) for i in range(size)])]
    pallas_call x21 -> x28, Pallas kernels: 449 us -> 706 us  [the longest x3 353 us: transfer_call(): pl.pallas_call(kernel, in_specs=[pl.BlockSpec(memory_space=pltpu.VMEM if...]
    dot_general x10 -> x0, matrix products: 121 us -> none  [contract_rows(): lax.dot_general(a, b, (((0,), (0,)), ((), ())), preferred_element_type=f32)]
    ppermute x90 -> x45, starting transfers between devices: 124 us -> 53.8 us  [over(): return lax.ppermute(a, axis, [(i, i ^ mask) for i in range(size)])]
    all_to_all x0 -> x5, waiting for transfers between devices: none -> 70.2 us  [swap(): return lax.all_to_all(a, 'tp', split_axis=0, concat_axis=0, tiled=True)]
    psum x1 -> x0, blocking collectives: 60.3 us -> none  [local(): lax.psum(parts, ('wide', 'tp'))]
    convert_element_type x0 -> x17, other arithmetic: none -> 49.4 us  [the longest x5 17.9 us: scatter(): (total(2 * block, half) + top.astype(f32)).astype(bf16)]
    another operation x9 -> x0, other arithmetic: 32.7 us -> none
  transfers between devices with their start and end apart: 90 -> 50, of which waited for: 31 -> 23; matrix products, arithmetic and copies ran while one was open for 16% -> 8% of each run, Pallas kernels for 30% -> 36%
where the time goes in v2:
time: 1280 us; the launch traced here: 1270 us
  Pallas kernels  789 us (62%)
  waiting for transfers between devices  259 us (20%)
  other arithmetic  116 us (9%)
  starting transfers between devices  75.3 us (6%)
  local copies, waits for them, and re-layouts  25.2 us (2%)
    pallas_call x3, Pallas kernels, transfer_call(): pl.pallas_call(kernel, in_specs=[pl.BlockSpec(memory_space=pltpu.VMEM if...  353 us
    pallas_call x12, Pallas kernels, tiled_call(): pl.pallas_call(kernel, grid_spec=pltpu.PrefetchScalarGridSpec(num_scalar_...  223 us
    ppermute x45, waiting for transfers between devices, over(): return lax.ppermute(a, axis, [(i, i ^ mask) for i in range(size)])  189 us
    pallas_call x12, Pallas kernels, weight_gradient(): pl.pallas_call(kernel, grid=(quarters * parts,), in_specs=[pl.BlockSpec((...  120 us
    all_to_all x5, waiting for transfers between devices, swap(): return lax.all_to_all(a, 'tp', split_axis=0, concat_axis=0, tiled=True)  70.2 us
    ppermute x45, starting transfers between devices, over(): return lax.ppermute(a, axis, [(i, i ^ mask) for i in range(size)])  53.8 us
    pallas_call x1, Pallas kernels, attention_backward(): pl.pallas_call(kernel, grid_spec=pltpu.PrefetchScalarGridSpec(num_scalar_...  37.1 us
  transfers between devices with their start and end apart: 50, of which 23 were waited for; matrix products, arithmetic and copies ran while one was open for 8% of the time, Pallas kernels for 36%

profile of v2, /device:TPU:0, one launch (start us, length us, event | category | flops | bytes accessed | tf_op | source)
XLA Modules:
  0.0 1266.2 jit_solution(6511703053481272863)
XLA Ops:
  7.4 6.4 shard_map.273
  25.4 155.9 %shard_map.274 = (bf16[4,2048,1024]{2,1,0:T(8,128)(2,1)}, bf16[1,2048,3072]{2,1,0:T(8,128)(2,1)}, bf16[1,2048,3072]{2,1,0:T(8,128)(2,1)}, bf16[1,2048,1536]{2,1,0:T(8,128)(2,1)}) custom-call(bf16[256,1024]{1,0:T(8,128)(2,1)S(1)} %pad_maximum_fusion.13.refs_0_, bf16[256,3072]{1,0:T(8,128)(2,1)} %pad_maximum_fusion.refs_1_, bf16[256,1536]{1,0:T(8,128)(2,1)S(1)} %bitcast.55), custom_call_target="tpu_custom_call" | custom-call | bytes 10000 | tf_op jit(solution)/shard_map/pallas_call | solution.py:664
  185.7 21.4 %shard_map.275 = (bf16[4,544,1024]{2,1,0:T(8,128)(2,1)}, bf16[4,544,1024]{2,1,0:T(8,128)(2,1)}) custom-call(s32[4]{0:T(128)S(1)} %iota_xor_fusion.seat_ref, bf16[4,2048,1024]{2,1,0:T(8,128)(2,1)} %get-tuple-element.115.refs_0_, bf16[544,2048]{1,0:T(8,128)(2,1)} %fusion.4.refs_1_.refs_0_, f32[544,128]{1,0:T(8,128)S(1)} %get-tuple-element.331.refs_2_.cos_ref, ...), custom_call_target="tpu_custom_call" | custom-call | flops 91268056 | bytes 284764 | tf_op jit(solution)/shard_map/pallas_call | solution.py:136
  207.1 152.6 %shard_map.276 = (bf16[4,544,1024]{2,1,0:T(8,128)(2,1)}, bf16[1,2048,3072]{2,1,0:T(8,128)(2,1)}, bf16[4,2048,512]{2,1,0:T(8,128)(2,1)}, bf16[1,2048,1536]{2,1,0:T(8,128)(2,1)}) custom-call(bf16[4,544,1024]{2,1,0:T(8,128)(2,1)} %get-tuple-element.116.refs_0_, bf16[1,2048,3072]{2,1,0:T(8,128)(2,1)} %get-tuple-element.117.refs_1_, ...), custom_call_target="tpu_custom_call", output_to_operand_aliasing={{1}: (1, {})} | custom-call | bytes 10000 | tf_op jit(solution)/shard_map/pallas_call | solution.py:664
  359.7 20.6 %shard_map.277 = (bf16[2176,512]{1,0:T(8,128)(2,1)}, f32[2,17,256]{2,1,0:T(8,128)S(1)}) custom-call(s32[8]{0:T(128)S(1)} %fusion.18.parent_ref, bf16[2176,1024]{1,0:T(8,128)(2,1)} %bitcast.58, bf16[2176,1024]{1,0:T(8,128)(2,1)} %bitcast.59, bf16[2176,1024]{1,0:T(8,128)(2,1)} %bitcast.60), custom_call_target="tpu_custom_call" | custom-call | flops 90112000 | bytes 67194 | tf_op jit(solution)/shard_map/pallas_call | solution.py:439
  380.3 44.2 %shard_map.278 = (bf16[4,544,512]{2,1,0:T(8,128)(2,1)}, bf16[1,2048,1536]{2,1,0:T(8,128)(2,1)}) custom-call(bf16[4,544,512]{2,1,0:T(8,128)(2,1)} %bitcast.77, bf16[1,2048,1536]{2,1,0:T(8,128)(2,1)} %get-tuple-element.121.refs_1_), custom_call_target="tpu_custom_call", output_to_operand_aliasing={{1}: (1, {})} | custom-call | bytes 10000 | tf_op jit(solution)/shard_map/pallas_call | solution.py:664
  424.5 13.3 %shard_map.279 = f32[544,2048]{1,0:T(8,128)} custom-call(s32[4]{0:T(128)S(1)} %iota_xor_fusion.seat_ref, bf16[4,2048,512]{2,1,0:T(8,128)(2,1)} %get-tuple-element.118.refs_0_, bf16[4,544,512]{2,1,0:T(8,128)(2,1)} %get-tuple-element.122.refs_1_), custom_call_target="tpu_custom_call" | custom-call | flops 45634028 | bytes 150732 | tf_op jit(solution)/shard_map/pallas_call | solution.py:136
  442.8 11.7 collective-permute-start.3
  454.5 6.4 shard_map.280.refs_0_.refs_2_
  461.0 21.3 %shard_map.281 = (bf16[2,544,1536]{2,1,0:T(8,128)(2,1)}, bf16[2,544,1536]{2,1,0:T(8,128)(2,1)}, bf16[2,544,1536]{2,1,0:T(8,128)(2,1)}) custom-call(s32[4]{0:T(128)S(1)} %iota.49.seat_ref, bf16[1,2048,3072]{2,1,0:T(8,128)(2,1)} %get-tuple-element.125.refs_0_.refs_2_, bf16[1,2048,3072]{2,1,0:T(8,128)(2,1)} %get-tuple-element.126.refs_1_.refs_3_, ...), custom_call_target="tpu_custom_call" | custom-call | flops 136902080 | bytes 625868 | tf_op jit(solution)/shard_map/pallas_call | solution.py:136
  482.3 16.4 %shard_map.282 = f32[544,2048]{1,0:T(8,128)} custom-call(s32[4]{0:T(128)S(1)} %iota.48.seat_ref, bf16[1,2048,1536]{2,1,0:T(8,128)(2,1)} %get-tuple-element.123.refs_0_, bf16[1,2048,1536]{2,1,0:T(8,128)(2,1)} %get-tuple-element.124.refs_1_, bf16[2,544,1536]{2,1,0:T(8,128)(2,1)} %get-tuple-element.132.refs_2_), custom_call_target="tpu_custom_call" | custom-call | flops 68451040 | bytes 203816 | tf_op jit(solution)/shard_map/pallas_call | solution.py:136
  504.3 21.3 %shard_map.283 = (bf16[2,544,1536]{2,1,0:T(8,128)(2,1)}, bf16[2,544,1536]{2,1,0:T(8,128)(2,1)}, bf16[2,544,1536]{2,1,0:T(8,128)(2,1)}) custom-call(s32[4]{0:T(128)S(1)} %iota.54.seat_ref, bf16[1,2048,3072]{2,1,0:T(8,128)(2,1)} %get-tuple-element.125.refs_0_.refs_2_, bf16[1,2048,3072]{2,1,0:T(8,128)(2,1)} %get-tuple-element.126.refs_1_.refs_3_, ...), custom_call_target="tpu_custom_call" | custom-call | flops 136902080 | bytes 625868 | tf_op jit(solution)/shard_map/pallas_call | solution.py:136
  525.7 15.6 %shard_map.284 = bf16[544,2048]{1,0:T(8,128)(2,1)} custom-call(s32[4]{0:T(128)S(1)} %iota.53.seat_ref, bf16[1,2048,1536]{2,1,0:T(8,128)(2,1)} %get-tuple-element.123.refs_0_, bf16[1,2048,1536]{2,1,0:T(8,128)(2,1)} %get-tuple-element.124.refs_1_, bf16[2,544,1536]{2,1,0:T(8,128)(2,1)} %get-tuple-element.130.refs_2_.refs_3_), custom_call_target="tpu_custom_call" | custom-call | flops 68451040 | bytes 181534 | tf_op jit(solution)/shard_map/pallas_call | solution.py:136
  541.3 10.4 collective-permute-done.4.refs_1_.refs_2_
  553.1 12.7 %shard_map.285 = bf16[1024,3072]{1,0:T(8,128)(2,1)} custom-call(bf16[544,2048]{1,0:T(8,128)(2,1)} %shard_map.280.refs_0_.refs_2_, bf16[544,2048]{1,0:T(8,128)(2,1)} %copy-done.7, bf16[2,544,1536]{2,1,0:T(8,128)(2,1)} %get-tuple-element.132.refs_2_, bf16[2,544,1536]{2,1,0:T(8,128)(2,1)} %get-tuple-element.130.refs_2_.refs_3_), custom_call_target="tpu_custom_call" | custom-call | flops 68451040 | bytes 174325 | tf_op jit(solution)/shard_map/pallas_call | solution.py:585
  565.8 12.7 %shard_map.286 = bf16[1024,3072]{1,0:T(8,128)(2,1)} custom-call(bf16[544,2048]{1,0:T(8,128)(2,1)} %shard_map.280.refs_0_.refs_2_, bf16[544,2048]{1,0:T(8,128)(2,1)} %copy-done.7, bf16[2,544,1536]{2,1,0:T(8,128)(2,1)} %get-tuple-element.132.refs_2_, bf16[2,544,1536]{2,1,0:T(8,128)(2,1)} %get-tuple-element.130.refs_2_.refs_3_), custom_call_target="tpu_custom_call" | custom-call | flops 68451040 | bytes 174325 | tf_op jit(solution)/shard_map/pallas_call | solution.py:585
  578.5 17.3 %shard_map.287 = (bf16[2,544,1536]{2,1,0:T(8,128)(2,1)}, bf16[2,544,1536]{2,1,0:T(8,128)(2,1)}) custom-call(s32[4]{0:T(128)S(1)} %iota.52.seat_ref, bf16[1,2048,1536]{2,1,0:T(8,128)(2,1)} %get-tuple-element.123.refs_0_, bf16[1,2048,1536]{2,1,0:T(8,128)(2,1)} %get-tuple-element.124.refs_1_, bf16[544,2048]{1,0:T(8,128)(2,1)} %copy-done.7, ...), custom_call_target="tpu_custom_call" | custom-call | flops 68451040 | bytes 281804 | tf_op jit(solution)/shard_map/pallas_call | solution.py:136
  595.9 24.1 %shard_map.288 = bf16[544,2048]{1,0:T(8,128)(2,1)} custom-call(s32[4]{0:T(128)S(1)} %iota.51.seat_ref, bf16[1,2048,3072]{2,1,0:T(8,128)(2,1)} %get-tuple-element.125.refs_0_.refs_2_, bf16[1,2048,3072]{2,1,0:T(8,128)(2,1)} %get-tuple-element.126.refs_1_.refs_3_, bf16[1,2048,3072]{2,1,0:T(8,128)(2,1)} %get-tuple-element.125.refs_0_.refs_2_, ...), custom_call_target="tpu_custom_call" | custom-call | flops 136902080 | bytes 592445 | tf_op jit(solution)/shard_map/pallas_call | solution.py:136
  623.0 16.8 %shard_map.289 = (bf16[2,544,1536]{2,1,0:T(8,128)(2,1)}, bf16[2,544,1536]{2,1,0:T(8,128)(2,1)}) custom-call(s32[4]{0:T(128)S(1)} %iota.50.seat_ref, bf16[1,2048,1536]{2,1,0:T(8,128)(2,1)} %get-tuple-element.123.refs_0_, bf16[1,2048,1536]{2,1,0:T(8,128)(2,1)} %get-tuple-element.124.refs_1_, bf16[544,2048]{1,0:T(8,128)(2,1)} %shard_map.280.refs_0_.refs_2_, ...), custom_call_target="tpu_custom_call" | custom-call | flops 68451040 | bytes 281804 | tf_op jit(solution)/shard_map/pallas_call | solution.py:136
  639.8 12.9 %shard_map.290 = bf16[1024,3072]{1,0:T(8,128)(2,1)} custom-call(bf16[544,2048]{1,0:T(8,128)(2,1)} %copy-done.3, bf16[544,2048]{1,0:T(8,128)(2,1)} %collective-permute-done.3.refs_4_.refs_1_, bf16[2,544,1536]{2,1,0:T(8,128)(2,1)} %get-tuple-element.157.refs_2_.refs_4_, bf16[2,544,1536]{2,1,0:T(8,128)(2,1)} %get-tuple-element.138.refs_4_.refs_3_), custom_call_target="tpu_custom_call" | custom-call | flops 68451040 | bytes 174325 | tf_op jit(solution)/shard_map/pallas_call | solution.py:585
  656.7 12.8 %shard_map.291 = bf16[1024,3072]{1,0:T(8,128)(2,1)} custom-call(bf16[544,2048]{1,0:T(8,128)(2,1)} %copy-done.3, bf16[544,2048]{1,0:T(8,128)(2,1)} %collective-permute-done.3.refs_4_.refs_1_, bf16[2,544,1536]{2,1,0:T(8,128)(2,1)} %get-tuple-element.157.refs_2_.refs_4_, bf16[2,544,1536]{2,1,0:T(8,128)(2,1)} %get-tuple-element.138.refs_4_.refs_3_), custom_call_target="tpu_custom_call" | custom-call | flops 68451040 | bytes 174325 | tf_op jit(solution)/shard_map/pallas_call | solution.py:585
  686.0 25.1 %shard_map.292 = f32[544,2048]{1,0:T(8,128)} custom-call(s32[4]{0:T(128)S(1)} %iota.55.seat_ref, bf16[1,2048,3072]{2,1,0:T(8,128)(2,1)} %get-tuple-element.125.refs_0_.refs_2_, bf16[1,2048,3072]{2,1,0:T(8,128)(2,1)} %get-tuple-element.126.refs_1_.refs_3_, bf16[1,2048,3072]{2,1,0:T(8,128)(2,1)} %get-tuple-element.125.refs_0_.refs_2_, ...), custom_call_target="tpu_custom_call" | custom-call | flops 136902080 | bytes 614727 | tf_op jit(solution)/shard_map/pallas_call | solution.py:136
  711.2 19.2 %collective-permute-done.12 = bf16[128,3072]{1,0:T(8,128)(2,1)} collective-permute-done((bf16[128,3072]{1,0:T(8,128)(2,1)}, bf16[128,3072]{1,0:T(8,128)(2,1)}, u32[]{:S(2)}, u32[]{:S(2)}) %collective-permute-start.12) | collective-permute-done | bytes 786464 | tf_op jit(solution)/shard_map/ppermute | solution.py:1001
  751.6 10.5 shard_map.293
  768.3 32.0 %collective-permute-done.14 = bf16[256,3072]{1,0:T(8,128)(2,1)S(1)} collective-permute-done((bf16[256,3072]{1,0:T(8,128)(2,1)}, bf16[256,3072]{1,0:T(8,128)(2,1)S(1)}, u32[]{:S(2)}, u32[]{:S(2)}) %collective-permute-start.14) | collective-permute-done | bytes 1572896 | tf_op jit(solution)/shard_map/ppermute | solution.py:1001
  801.5 13.7 %all-to-all-done = bf16[4,544,512]{2,1,0:T(8,128)(2,1)S(1)} async-done(((bf16[4,544,512]{2,1,0:T(8,128)(2,1)}), bf16[4,544,512]{2,1,0:T(8,128)(2,1)S(1)}, u32[]{:S(2)}, u32[]{:S(2)}) %all-to-all-start) | async-done | bytes 2228256 | tf_op jit(solution)/shard_map/all_to_all | solution.py:1048
  822.5 37.1 %shard_map.294 = bf16[2176,1024]{1,0:T(8,128)(2,1)} custom-call(s32[8]{0:T(128)S(1)} %fusion.18.parent_ref, bf16[2176,1024]{1,0:T(8,128)(2,1)} %bitcast.61, bf16[2176,1024]{1,0:T(8,128)(2,1)} %bitcast.62, bf16[2176,1024]{1,0:T(8,128)(2,1)} %bitcast.63, bf16[2176,512]{1,0:T(8,128)(2,1)} %get-tuple-element.120.o_ref, bf16[2176,512]{1,0:T(8,128)(2,1)} %bitcast.78, ...), custom_call_target="tpu_custom_call" | custom-call | flops 225280000 | bytes 133693 | tf_op jit(solution)/shard_map/pallas_call | solution.py:529
  859.6 12.3 collective-permute-done.16
  871.9 12.6 shard_map.295
  889.6 12.7 %shard_map.296 = bf16[1024,3072]{1,0:T(8,128)(2,1)} custom-call(bf16[544,2048]{1,0:T(8,128)(2,1)} %copy-done.3, bf16[544,2048]{1,0:T(8,128)(2,1)} %collective-permute-done.3.refs_4_.refs_1_, bf16[2,544,1536]{2,1,0:T(8,128)(2,1)} %get-tuple-element.178.refs_5_.refs_2_, bf16[2,544,1536]{2,1,0:T(8,128)(2,1)} %get-tuple-element.179.refs_5_.refs_3_), custom_call_target="tpu_custom_call" | custom-call | flops 68451040 | bytes 174325 | tf_op jit(solution)/shard_map/pallas_call | solution.py:585
  905.9 7.6 shard_map.297
  916.3 7.1 shard_map.298
  926.3 6.4 shard_map.299
  944.6 44.8 %all-to-all-done.1.g_ref = bf16[4,544,1024]{2,1,0:T(8,128)(2,1)} async-done(((bf16[4,544,1024]{2,1,0:T(8,128)(2,1)}), bf16[4,544,1024]{2,1,0:T(8,128)(2,1)}, u32[]{:S(2)}, u32[]{:S(2)}) %all-to-all-start.1) | async-done | bytes 4456480 | tf_op jit(solution)/shard_map/all_to_all | solution.py:1048
  989.4 9.9 shard_map.300
  999.3 7.2 shard_map.301
  1011.7 7.1 shard_map.302
  1018.7 7.3 shard_map.303
  1026.0 33.9 %collective-permute-done.44 = bf16[256,1536]{1,0:T(8,128)(2,1)S(1)} collective-permute-done((bf16[256,1536]{1,0:T(8,128)(2,1)S(1)}, bf16[256,1536]{1,0:T(8,128)(2,1)S(1)}, u32[]{:S(2)}, u32[]{:S(2)}) %collective-permute-start.44) | collective-permute-done | bytes 786464 | tf_op jit(solution)/shard_map/ppermute | solution.py:1001
  1060.0 16.7 %collective-permute-done.42 = bf16[256,1536]{1,0:T(8,128)(2,1)S(1)} collective-permute-done((bf16[256,1536]{1,0:T(8,128)(2,1)S(1)}, bf16[256,1536]{1,0:T(8,128)(2,1)S(1)}, u32[]{:S(2)}, u32[]{:S(2)}) %collective-permute-start.42) | collective-permute-done | bytes 786464 | tf_op jit(solution)/shard_map/ppermute | solution.py:1001
  1081.2 9.6 collective-permute-done.23
  1094.7 7.1 shard_map.304
  1120.8 20.0 %shard_map.305 = f32[544,2048]{1,0:T(8,128)} custom-call(s32[4]{0:T(128)S(1)} %iota_xor_fusion.seat_ref, bf16[4,2048,1024]{2,1,0:T(8,128)(2,1)} %get-tuple-element.115.refs_0_, bf16[4,544,1024]{2,1,0:T(8,128)(2,1)} %get-tuple-element.204.refs_1_), custom_call_target="tpu_custom_call" | custom-call | flops 91268056 | bytes 256901 | tf_op jit(solution)/shard_map/pallas_call | solution.py:136
  1166.9 19.2 %collective-permute-done.38 = bf16[128,2048]{1,0:T(8,128)(2,1)} collective-permute-done((bf16[128,2048]{1,0:T(8,128)(2,1)}, bf16[128,2048]{1,0:T(8,128)(2,1)}, u32[]{:S(2)}, u32[]{:S(2)}) %collective-permute-start.38) | collective-permute-done | bytes 524320 | tf_op jit(solution)/shard_map/ppermute | solution.py:1001
  1206.9 7.8 collective-permute-done.33
  1218.8 10.4 all-to-all-done.2
  1242.7 6.4 shard_map.306
  1249.1 9.8 collective-permute-done.35
  (308 shorter events, 223.4 us)
Async XLA Ops:
  1.4 19.7 %collective-permute-start = (bf16[1,1,544]{2,0,1:T(2,128)(2,1)S(1)}, bf16[1,1,544]{2,0,1:T(2,128)(2,1)S(1)}, u32[]{:S(2)}, u32[]{:S(2)}) collective-permute-start(bf16[1,1,544]{2,0,1:T(2,128)(2,1)S(1)} %broadcast_in_dim_broadcast_in_dim.3), channel_id=1, source_target_pairs={{0,8},{4,12},{8,0},{12,4},{16,24},{20,28},{24,16},{28,20},{1,9},{5... | collective-permute-start | bytes 3272 | tf_op jit(solution)/shard_map/ppermute | solution.py:1001
  24.8 156.4 %collective-permute-start.2 = (bf16[4,1,544]{2,0,1:T(4,128)(2,1)S(1)}, bf16[4,1,544]{2,0,1:T(4,128)(2,1)S(1)}, u32[]{:S(2)}, u32[]{:S(2)}) collective-permute-start(bf16[4,1,544]{2,0,1:T(4,128)(2,1)S(1)} %pad_maximum_fusion.17), channel_id=1, source_target_pairs={{0,4},{4,0},{8,12},{12,8},{16,20},{20,16},{24,28},{28,24},{1,5},{5... | collective-permute-start | bytes 13064 | tf_op jit(solution)/shard_map/ppermute | solution.py:1001
  442.8 59.8 %collective-permute-start.3 = (bf16[544,2048]{1,0:T(8,128)(2,1)S(1)}, bf16[544,2048]{1,0:T(8,128)(2,1)}, u32[]{:S(2)}, u32[]{:S(2)}) collective-permute-start(bf16[544,2048]{1,0:T(8,128)(2,1)S(1)} %multiply_convert_fusion.refs_4_.refs_0_), channel_id=1, source_target_pairs={{0,1},{1,0},{2,3},{3,2},{4,5},{5,4},{6,7},{7,6},{8,9},{9,8},{10,11... | collective-permute-start | bytes 6684680 | tf_op jit(solution)/shard_map/ppermute | solution.py:1001
  502.6 49.1 %collective-permute-start.4 = (bf16[544,2048]{1,0:T(8,128)(2,1)S(1)}, bf16[544,2048]{1,0:T(8,128)(2,1)S(1)}, u32[]{:S(2)}, u32[]{:S(2)}) collective-permute-start(bf16[544,2048]{1,0:T(8,128)(2,1)S(1)} %copy-done.4), channel_id=1, source_target_pairs={{0,1},{1,0},{2,3},{3,2},{4,5},{5,4},{6,7},{7,6},{8,9},{9,8},{10,11... | collective-permute-start | bytes 6684680 | tf_op jit(solution)/shard_map/ppermute | solution.py:1001
  565.8 54.2 %collective-permute-start.5 = (bf16[1024,3072]{1,0:T(8,128)(2,1)}, bf16[1024,3072]{1,0:T(8,128)(2,1)}, u32[]{:S(2)}, u32[]{:S(2)}) collective-permute-start(bf16[1024,3072]{1,0:T(8,128)(2,1)} %shard_map.285), channel_id=1, source_target_pairs={{0,4},{4,0},{8,12},{12,8},{16,20},{20,16},{24,28},{28,24},{1,5},{5... | collective-permute-start | bytes 18874376 | tf_op jit(solution)/shard_map/ppermute | solution.py:1001
  652.7 20.4 %collective-permute-start.8 = (bf16[1024,3072]{1,0:T(8,128)(2,1)}, bf16[1024,3072]{1,0:T(8,128)(2,1)}, u32[]{:S(2)}, u32[]{:S(2)}) collective-permute-start(bf16[1024,3072]{1,0:T(8,128)(2,1)} %shard_map.290), channel_id=1, source_target_pairs={{0,4},{4,0},{8,12},{12,8},{16,20},{20,16},{24,28},{28,24},{1,5},{5... | collective-permute-start | bytes 18874376 | tf_op jit(solution)/shard_map/ppermute | solution.py:1001
  653.2 19.8 %collective-permute-start.6 = (bf16[128,3072]{1,0:T(8,128)(2,1)}, bf16[128,3072]{1,0:T(8,128)(2,1)}, u32[]{:S(2)}, u32[]{:S(2)}) collective-permute-start(bf16[128,3072]{1,0:T(8,128)(2,1)} %get-tuple-element.297), channel_id=1, source_target_pairs={{0,8},{4,12},{8,0},{12,4},{16,24},{20,28},{24,16},{28,20},{1,9},{5... | collective-permute-start | bytes 2359304 | tf_op jit(solution)/shard_map/ppermute | solution.py:1001
  653.2 19.9 %collective-permute-start.7 = (bf16[128,3072]{1,0:T(8,128)(2,1)}, bf16[128,3072]{1,0:T(8,128)(2,1)}, u32[]{:S(2)}, u32[]{:S(2)}) collective-permute-start(bf16[128,3072]{1,0:T(8,128)(2,1)} %get-tuple-element.296), channel_id=1, source_target_pairs={{0,16},{4,20},{8,24},{12,28},{16,0},{20,4},{24,8},{28,12},{1,17},{... | collective-permute-start | bytes 2359304 | tf_op jit(solution)/shard_map/ppermute | solution.py:1001
  655.3 55.9 %collective-permute-start.9 = (bf16[544,2048]{1,0:T(8,128)(2,1)S(1)}, bf16[544,2048]{1,0:T(8,128)(2,1)S(1)}, u32[]{:S(2)}, u32[]{:S(2)}) collective-permute-start(bf16[544,2048]{1,0:T(8,128)(2,1)S(1)} %copy-done.13), channel_id=1, source_target_pairs={{0,1},{1,0},{2,3},{3,2},{4,5},{5,4},{6,7},{7,6},{8,9},{9,8},{10,11... | collective-permute-start | bytes 6684680 | tf_op jit(solution)/shard_map/ppermute | solution.py:1001
  677.7 55.0 %collective-permute-start.10 = (bf16[256,3072]{1,0:T(8,128)(2,1)}, bf16[256,3072]{1,0:T(8,128)(2,1)}, u32[]{:S(2)}, u32[]{:S(2)}) collective-permute-start(bf16[256,3072]{1,0:T(8,128)(2,1)} %pad_maximum_fusion.1), channel_id=1, source_target_pairs={{0,8},{4,12},{8,0},{12,4},{16,24},{20,28},{24,16},{28,20},{1,9},{5... | collective-permute-start | bytes 4718600 | tf_op jit(solution)/shard_map/ppermute | solution.py:1001
  680.6 52.1 %collective-permute-start.11 = (bf16[256,3072]{1,0:T(8,128)(2,1)}, bf16[256,3072]{1,0:T(8,128)(2,1)}, u32[]{:S(2)}, u32[]{:S(2)}) collective-permute-start(bf16[256,3072]{1,0:T(8,128)(2,1)} %pad_maximum_fusion.2), channel_id=1, source_target_pairs={{0,16},{4,20},{8,24},{12,28},{16,0},{20,4},{24,8},{28,12},{1,17},{... | collective-permute-start | bytes 4718600 | tf_op jit(solution)/shard_map/ppermute | solution.py:1001
  684.0 46.4 %collective-permute-start.12 = (bf16[128,3072]{1,0:T(8,128)(2,1)}, bf16[128,3072]{1,0:T(8,128)(2,1)}, u32[]{:S(2)}, u32[]{:S(2)}) collective-permute-start(bf16[128,3072]{1,0:T(8,128)(2,1)} %get-tuple-element.291), channel_id=1, source_target_pairs={{0,8},{4,12},{8,0},{12,4},{16,24},{20,28},{24,16},{28,20},{1,9},{5... | collective-permute-start | bytes 2359304 | tf_op jit(solution)/shard_map/ppermute | solution.py:1001
  685.8 46.9 %collective-permute-start.13 = (bf16[128,3072]{1,0:T(8,128)(2,1)}, bf16[128,3072]{1,0:T(8,128)(2,1)}, u32[]{:S(2)}, u32[]{:S(2)}) collective-permute-start(bf16[128,3072]{1,0:T(8,128)(2,1)} %get-tuple-element.290), channel_id=1, source_target_pairs={{0,16},{4,20},{8,24},{12,28},{16,0},{20,4},{24,8},{28,12},{1,17},{... | collective-permute-start | bytes 2359304 | tf_op jit(solution)/shard_map/ppermute | solution.py:1001
  762.1 53.1 %all-to-all-start = ((bf16[4,544,512]{2,1,0:T(8,128)(2,1)}), bf16[4,544,512]{2,1,0:T(8,128)(2,1)S(1)}, u32[]{:S(2)}, u32[]{:S(2)}) async-start(bf16[4,544,512]{2,1,0:T(8,128)(2,1)} %shard_map.293), calls=%async_computation | async-start | bytes 4456448 | tf_op jit(solution)/shard_map/all_to_all | solution.py:1048
  766.1 34.2 %collective-permute-start.14 = (bf16[256,3072]{1,0:T(8,128)(2,1)}, bf16[256,3072]{1,0:T(8,128)(2,1)S(1)}, u32[]{:S(2)}, u32[]{:S(2)}) collective-permute-start(bf16[256,3072]{1,0:T(8,128)(2,1)} %pad_maximum_fusion.3), channel_id=1, source_target_pairs={{0,8},{4,12},{8,0},{12,4},{16,24},{20,28},{24,16},{28,20},{1,9},{5... | collective-permute-start | bytes 4718600 | tf_op jit(solution)/shard_map/ppermute | solution.py:1001
  766.9 34.6 %collective-permute-start.15 = (bf16[256,3072]{1,0:T(8,128)(2,1)}, bf16[256,3072]{1,0:T(8,128)(2,1)}, u32[]{:S(2)}, u32[]{:S(2)}) collective-permute-start(bf16[256,3072]{1,0:T(8,128)(2,1)} %pad_maximum_fusion.4), channel_id=1, source_target_pairs={{0,16},{4,20},{8,24},{12,28},{16,0},{20,4},{24,8},{28,12},{1,17},{... | collective-permute-start | bytes 4718600 | tf_op jit(solution)/shard_map/ppermute | solution.py:1001
  822.5 49.4 %collective-permute-start.16 = (bf16[544,2048]{1,0:T(8,128)(2,1)S(1)}, bf16[544,2048]{1,0:T(8,128)(2,1)S(1)}, u32[]{:S(2)}, u32[]{:S(2)}) collective-permute-start(bf16[544,2048]{1,0:T(8,128)(2,1)S(1)} %copy-done.14), channel_id=1, source_target_pairs={{0,1},{1,0},{2,3},{3,2},{4,5},{5,4},{6,7},{7,6},{8,9},{9,8},{10,11... | collective-permute-start | bytes 6684680 | tf_op jit(solution)/shard_map/ppermute | solution.py:1001
  884.5 17.8 %collective-permute-start.17 = (bf16[1024,3072]{1,0:T(8,128)(2,1)}, bf16[1024,3072]{1,0:T(8,128)(2,1)}, u32[]{:S(2)}, u32[]{:S(2)}) collective-permute-start(bf16[1024,3072]{1,0:T(8,128)(2,1)} %shard_map.295), channel_id=1, source_target_pairs={{0,4},{4,0},{8,12},{12,8},{16,20},{20,16},{24,28},{28,24},{1,5},{5... | collective-permute-start | bytes 18874376 | tf_op jit(solution)/shard_map/ppermute | solution.py:1001
  884.5 104.9 %all-to-all-start.1 = ((bf16[4,544,1024]{2,1,0:T(8,128)(2,1)}), bf16[4,544,1024]{2,1,0:T(8,128)(2,1)}, u32[]{:S(2)}, u32[]{:S(2)}) async-start(bf16[4,544,1024]{2,1,0:T(8,128)(2,1)} %bitcast.76), calls=%async_computation.1 | async-start | bytes 8912896 | tf_op jit(solution)/shard_map/all_to_all | solution.py:1048
  913.6 21.1 %collective-permute-start.20 = (bf16[1024,2048]{1,0:T(8,128)(2,1)}, bf16[1024,2048]{1,0:T(8,128)(2,1)}, u32[]{:S(2)}, u32[]{:S(2)}) collective-permute-start(bf16[1024,2048]{1,0:T(8,128)(2,1)} %shard_map.297), channel_id=1, source_target_pairs={{0,4},{4,0},{8,12},{12,8},{16,20},{20,16},{24,28},{28,24},{1,5},{5... | collective-permute-start | bytes 12582920 | tf_op jit(solution)/shard_map/ppermute | solution.py:1001
  914.1 19.8 %collective-permute-start.18 = (bf16[128,3072]{1,0:T(8,128)(2,1)}, bf16[128,3072]{1,0:T(8,128)(2,1)}, u32[]{:S(2)}, u32[]{:S(2)}) collective-permute-start(bf16[128,3072]{1,0:T(8,128)(2,1)} %get-tuple-element.285), channel_id=1, source_target_pairs={{0,8},{4,12},{8,0},{12,4},{16,24},{20,28},{24,16},{28,20},{1,9},{5... | collective-permute-start | bytes 2359304 | tf_op jit(solution)/shard_map/ppermute | solution.py:1001
  915.1 19.6 %collective-permute-start.19 = (bf16[128,3072]{1,0:T(8,128)(2,1)}, bf16[128,3072]{1,0:T(8,128)(2,1)}, u32[]{:S(2)}, u32[]{:S(2)}) collective-permute-start(bf16[128,3072]{1,0:T(8,128)(2,1)} %get-tuple-element.284), channel_id=1, source_target_pairs={{0,16},{4,20},{8,24},{12,28},{16,0},{20,4},{24,8},{28,12},{1,17},{... | collective-permute-start | bytes 2359304 | tf_op jit(solution)/shard_map/ppermute | solution.py:1001
  1006.5 98.5 %collective-permute-start.25 = (bf16[1024,2048]{1,0:T(8,128)(2,1)}, bf16[1024,2048]{1,0:T(8,128)(2,1)}, u32[]{:S(2)}, u32[]{:S(2)}) collective-permute-start(bf16[1024,2048]{1,0:T(8,128)(2,1)} %shard_map.301), channel_id=1, source_target_pairs={{0,4},{4,0},{8,12},{12,8},{16,20},{20,16},{24,28},{28,24},{1,5},{5... | collective-permute-start | bytes 12582920 | tf_op jit(solution)/shard_map/ppermute | solution.py:1001
  1006.5 53.4 %collective-permute-start.44 = (bf16[256,1536]{1,0:T(8,128)(2,1)S(1)}, bf16[256,1536]{1,0:T(8,128)(2,1)S(1)}, u32[]{:S(2)}, u32[]{:S(2)}) collective-permute-start(bf16[256,1536]{1,0:T(8,128)(2,1)S(1)} %copy-done.18), channel_id=1, source_target_pairs={{0,2},{1,3},{2,0},{3,1},{4,6},{5,7},{6,4},{7,5},{8,10},{9,11},{10,... | collective-permute-start | bytes 2359304 | tf_op jit(solution)/shard_map/ppermute | solution.py:1001
  1006.6 70.1 %collective-permute-start.42 = (bf16[256,1536]{1,0:T(8,128)(2,1)S(1)}, bf16[256,1536]{1,0:T(8,128)(2,1)S(1)}, u32[]{:S(2)}, u32[]{:S(2)}) collective-permute-start(bf16[256,1536]{1,0:T(8,128)(2,1)S(1)} %copy-done.19), channel_id=1, source_target_pairs={{0,2},{1,3},{2,0},{3,1},{4,6},{5,7},{6,4},{7,5},{8,10},{9,11},{10,... | collective-permute-start | bytes 2359304 | tf_op jit(solution)/shard_map/ppermute | solution.py:1001
  1009.5 95.5 %collective-permute-start.21 = (bf16[256,3072]{1,0:T(8,128)(2,1)}, bf16[256,3072]{1,0:T(8,128)(2,1)}, u32[]{:S(2)}, u32[]{:S(2)}) collective-permute-start(bf16[256,3072]{1,0:T(8,128)(2,1)} %pad_maximum_fusion.5), channel_id=1, source_target_pairs={{0,8},{4,12},{8,0},{12,4},{16,24},{20,28},{24,16},{28,20},{1,9},{5... | collective-permute-start | bytes 4718600 | tf_op jit(solution)/shard_map/ppermute | solution.py:1001
  1010.5 94.5 %collective-permute-start.22 = (bf16[256,3072]{1,0:T(8,128)(2,1)}, bf16[256,3072]{1,0:T(8,128)(2,1)}, u32[]{:S(2)}, u32[]{:S(2)}) collective-permute-start(bf16[256,3072]{1,0:T(8,128)(2,1)} %pad_maximum_fusion.6), channel_id=1, source_target_pairs={{0,16},{4,20},{8,24},{12,28},{16,0},{20,4},{24,8},{28,12},{1,17},{... | collective-permute-start | bytes 4718600 | tf_op jit(solution)/shard_map/ppermute | solution.py:1001
  1059.9 80.9 %collective-permute-start.30 = (bf16[1024,2048]{1,0:T(8,128)(2,1)}, bf16[1024,2048]{1,0:T(8,128)(2,1)}, u32[]{:S(2)}, u32[]{:S(2)}) collective-permute-start(bf16[1024,2048]{1,0:T(8,128)(2,1)} %shard_map.303), channel_id=1, source_target_pairs={{0,4},{4,0},{8,12},{12,8},{16,20},{20,16},{24,28},{28,24},{1,5},{5... | collective-permute-start | bytes 12582920 | tf_op jit(solution)/shard_map/ppermute | solution.py:1001
  1076.7 14.1 %collective-permute-start.23 = (bf16[128,2048]{1,0:T(8,128)(2,1)}, bf16[128,2048]{1,0:T(8,128)(2,1)S(1)}, u32[]{:S(2)}, u32[]{:S(2)}) collective-permute-start(bf16[128,2048]{1,0:T(8,128)(2,1)} %get-tuple-element.315), channel_id=1, source_target_pairs={{0,8},{4,12},{8,0},{12,4},{16,24},{20,28},{24,16},{28,20},{1,9},{5... | collective-permute-start | bytes 1572872 | tf_op jit(solution)/shard_map/ppermute | solution.py:1001
  1090.8 14.2 %collective-permute-start.24 = (bf16[128,2048]{1,0:T(8,128)(2,1)S(1)}, bf16[128,2048]{1,0:T(8,128)(2,1)S(1)}, u32[]{:S(2)}, u32[]{:S(2)}) collective-permute-start(bf16[128,2048]{1,0:T(8,128)(2,1)S(1)} %get-tuple-element.314), channel_id=1, source_target_pairs={{0,16},{4,20},{8,24},{12,28},{16,0},{20,4},{24,8},{28,12},{1,17},{... | collective-permute-start | bytes 1572872 | tf_op jit(solution)/shard_map/ppermute | solution.py:1001
  1108.4 36.2 %collective-permute-start.26 = (bf16[256,2048]{1,0:T(8,128)(2,1)S(1)}, bf16[256,2048]{1,0:T(8,128)(2,1)S(1)}, u32[]{:S(2)}, u32[]{:S(2)}) collective-permute-start(bf16[256,2048]{1,0:T(8,128)(2,1)S(1)} %pad_maximum_fusion.7), channel_id=1, source_target_pairs={{0,8},{4,12},{8,0},{12,4},{16,24},{20,28},{24,16},{28,20},{1,9},{5... | collective-permute-start | bytes 3145736 | tf_op jit(solution)/shard_map/ppermute | solution.py:1001
  1109.6 35.0 %collective-permute-start.27 = (bf16[256,2048]{1,0:T(8,128)(2,1)S(1)}, bf16[256,2048]{1,0:T(8,128)(2,1)S(1)}, u32[]{:S(2)}, u32[]{:S(2)}) collective-permute-start(bf16[256,2048]{1,0:T(8,128)(2,1)S(1)} %pad_maximum_fusion.8), channel_id=1, source_target_pairs={{0,16},{4,20},{8,24},{12,28},{16,0},{20,4},{24,8},{28,12},{1,17},{... | collective-permute-start | bytes 3145736 | tf_op jit(solution)/shard_map/ppermute | solution.py:1001
  1112.1 31.5 %collective-permute-start.28 = (bf16[128,2048]{1,0:T(8,128)(2,1)S(1)}, bf16[128,2048]{1,0:T(8,128)(2,1)S(1)}, u32[]{:S(2)}, u32[]{:S(2)}) collective-permute-start(bf16[128,2048]{1,0:T(8,128)(2,1)S(1)} %get-tuple-element.313), channel_id=1, source_target_pairs={{0,8},{4,12},{8,0},{12,4},{16,24},{20,28},{24,16},{28,20},{1,9},{5... | collective-permute-start | bytes 1572872 | tf_op jit(solution)/shard_map/ppermute | solution.py:1001
  1113.2 31.4 %collective-permute-start.29 = (bf16[128,2048]{1,0:T(8,128)(2,1)S(1)}, bf16[128,2048]{1,0:T(8,128)(2,1)S(1)}, u32[]{:S(2)}, u32[]{:S(2)}) collective-permute-start(bf16[128,2048]{1,0:T(8,128)(2,1)S(1)} %get-tuple-element.312), channel_id=1, source_target_pairs={{0,16},{4,20},{8,24},{12,28},{16,0},{20,4},{24,8},{28,12},{1,17},{... | collective-permute-start | bytes 1572872 | tf_op jit(solution)/shard_map/ppermute | solution.py:1001
  1140.8 63.2 %collective-permute-start.43 = (bf16[256,1536]{1,0:T(8,128)(2,1)}, bf16[256,1536]{1,0:T(8,128)(2,1)}, u32[]{:S(2)}, u32[]{:S(2)}) collective-permute-start(bf16[256,1536]{1,0:T(8,128)(2,1)} %slice.621), channel_id=1, source_target_pairs={{0,2},{1,3},{2,0},{3,1},{4,6},{5,7},{6,4},{7,5},{8,10},{9,11},{10,... | collective-permute-start | bytes 2359304 | tf_op jit(solution)/shard_map/ppermute | solution.py:1001
  1151.7 41.1 %collective-permute-start.37 = (bf16[256,2048]{1,0:T(8,128)(2,1)}, bf16[256,2048]{1,0:T(8,128)(2,1)}, u32[]{:S(2)}, u32[]{:S(2)}) collective-permute-start(bf16[256,2048]{1,0:T(8,128)(2,1)} %pad_maximum_fusion.10), channel_id=1, source_target_pairs={{0,16},{4,20},{8,24},{12,28},{16,0},{20,4},{24,8},{28,12},{1,17},{... | collective-permute-start | bytes 3145736 | tf_op jit(solution)/shard_map/ppermute | solution.py:1001
  1152.6 13.3 %collective-permute-start.40 = (bf16[128,2048]{1,0:T(8,128)(2,1)}, bf16[128,2048]{1,0:T(8,128)(2,1)}, u32[]{:S(2)}, u32[]{:S(2)}) collective-permute-start(bf16[128,2048]{1,0:T(8,128)(2,1)} %get-tuple-element.303), channel_id=1, source_target_pairs={{0,8},{4,12},{8,0},{12,4},{16,24},{20,28},{24,16},{28,20},{1,9},{5... | collective-permute-start | bytes 1572872 | tf_op jit(solution)/shard_map/ppermute | solution.py:1001
  1153.6 32.5 %collective-permute-start.38 = (bf16[128,2048]{1,0:T(8,128)(2,1)}, bf16[128,2048]{1,0:T(8,128)(2,1)}, u32[]{:S(2)}, u32[]{:S(2)}) collective-permute-start(bf16[128,2048]{1,0:T(8,128)(2,1)} %get-tuple-element.302), channel_id=1, source_target_pairs={{0,16},{4,20},{8,24},{12,28},{16,0},{20,4},{24,8},{28,12},{1,17},{... | collective-permute-start | bytes 1572872 | tf_op jit(solution)/shard_map/ppermute | solution.py:1001
  1160.9 37.7 %all-to-all-start.4 = ((bf16[4,256,512]{2,1,0:T(8,128)(2,1)}), bf16[4,256,512]{2,1,0:T(8,128)(2,1)S(1)}, u32[]{:S(2)}, u32[]{:S(2)}) async-start(bf16[4,256,512]{2,1,0:T(8,128)(2,1)} %bitcast.82), calls=%async_computation.4 | async-start | bytes 2097152 | tf_op jit(solution)/shard_map/all_to_all | solution.py:1048
  1164.8 29.0 %collective-permute-start.36 = (bf16[256,2048]{1,0:T(8,128)(2,1)}, bf16[256,2048]{1,0:T(8,128)(2,1)S(1)}, u32[]{:S(2)}, u32[]{:S(2)}) collective-permute-start(bf16[256,2048]{1,0:T(8,128)(2,1)} %pad_maximum_fusion.9), channel_id=1, source_target_pairs={{0,8},{4,12},{8,0},{12,4},{16,24},{20,28},{24,16},{28,20},{1,9},{5... | collective-permute-start | bytes 3145736 | tf_op jit(solution)/shard_map/ppermute | solution.py:1001
  1165.9 37.0 %collective-permute-start.32 = (f32[2,544]{1,0:T(2,128)S(1)}, f32[2,544]{1,0:T(2,128)S(1)}, u32[]{:S(2)}, u32[]{:S(2)}) collective-permute-start(f32[2,544]{1,0:T(2,128)S(1)} %slice.501), channel_id=1, source_target_pairs={{0,16},{4,20},{8,24},{12,28},{16,0},{20,4},{24,8},{28,12},{1,17},{... | collective-permute-start | bytes 13064 | tf_op jit(solution)/shard_map/ppermute | solution.py:1001
  1190.8 24.1 %collective-permute-start.41 = (bf16[256,2048]{1,0:T(8,128)(2,1)}, bf16[256,2048]{1,0:T(8,128)(2,1)}, u32[]{:S(2)}, u32[]{:S(2)}) collective-permute-start(bf16[256,2048]{1,0:T(8,128)(2,1)} %pad_maximum_fusion.12), channel_id=1, source_target_pairs={{0,16},{4,20},{8,24},{12,28},{16,0},{20,4},{24,8},{28,12},{1,17},{... | collective-permute-start | bytes 3145736 | tf_op jit(solution)/shard_map/ppermute | solution.py:1001
  1192.8 22.0 %collective-permute-start.39 = (bf16[256,2048]{1,0:T(8,128)(2,1)}, bf16[256,2048]{1,0:T(8,128)(2,1)}, u32[]{:S(2)}, u32[]{:S(2)}) collective-permute-start(bf16[256,2048]{1,0:T(8,128)(2,1)} %pad_maximum_fusion.11), channel_id=1, source_target_pairs={{0,8},{4,12},{8,0},{12,4},{16,24},{20,28},{24,16},{28,20},{1,9},{5... | collective-permute-start | bytes 3145736 | tf_op jit(solution)/shard_map/ppermute | solution.py:1001
  1198.6 30.5 %all-to-all-start.2 = ((bf16[4,256,512]{2,1,0:T(8,128)(2,1)}), bf16[4,256,512]{2,1,0:T(8,128)(2,1)}, u32[]{:S(2)}, u32[]{:S(2)}) async-start(bf16[4,256,512]{2,1,0:T(8,128)(2,1)} %bitcast.83), calls=%async_computation.2 | async-start | bytes 2097152 | tf_op jit(solution)/shard_map/all_to_all | solution.py:1048
  1202.9 11.8 collective-permute-start.33
  1214.7 18.7 %collective-permute-start.34 = (f32[1,544]{1,0:T(1,128)S(1)}, f32[1,544]{1,0:T(1,128)S(1)}, u32[]{:S(2)}, u32[]{:S(2)}) collective-permute-start(f32[1,544]{1,0:T(1,128)S(1)} %slice_add_fusion.5), channel_id=1, source_target_pairs={{0,1},{1,0},{2,3},{3,2},{4,5},{5,4},{6,7},{7,6},{8,9},{9,8},{10,11... | collective-permute-start | bytes 6536 | tf_op jit(solution)/shard_map/ppermute | solution.py:1001
  1229.1 34.3 %all-to-all-start.3 = ((bf16[4,256,512]{2,1,0:T(8,128)(2,1)}), bf16[4,256,512]{2,1,0:T(8,128)(2,1)}, u32[]{:S(2)}, u32[]{:S(2)}) async-start(bf16[4,256,512]{2,1,0:T(8,128)(2,1)} %bitcast.84), calls=%async_computation.3 | async-start | bytes 2097152 | tf_op jit(solution)/shard_map/all_to_all | solution.py:1048
  1233.5 25.5 %collective-permute-start.35 = (f32[1,544]{1,0:T(1,128)S(1)}, f32[1,544]{1,0:T(1,128)S(1)}, u32[]{:S(2)}, u32[]{:S(2)}) collective-permute-start(f32[1,544]{1,0:T(1,128)S(1)} %add.372), channel_id=1, source_target_pairs={{0,2},{1,3},{2,0},{3,1},{4,6},{5,7},{6,4},{7,5},{8,10},{9,11},{10,... | collective-permute-start | bytes 6536 | tf_op jit(solution)/shard_map/ppermute | solution.py:1001
  (47 other events, 574.6 us)

commit v3 on v2

--- a/solution.py
+++ b/solution.py
@@ -22,6 +22,7 @@
 LN2 = math.log(2.0)
 VMEM = 52 * 1024 * 1024
 COST = 0.01
+GAIN_ROWS = 16
 
 f32 = jnp.float32
 bf16 = jnp.bfloat16
@@ -682,6 +683,177 @@
     )(*ins)
 
 
+def swap_own(source, target, mine, sems):
+    seat = lax.axis_index("tp")
+    return (
+        pltpu.make_async_copy(source.at[seat], mine, sems.at[0]),
+        pltpu.make_async_copy(mine, target.at[seat], sems.at[1]),
+    )
+
+
+def gradient_pair(lefts, rights, cut, number, ride=None):
+    pairs = len(lefts)
+    rows, depth = lefts[0].shape
+    quarters, _, width = rights[0].shape
+    size = depth // 2
+    block = size // 4
+    half = block // 2
+    if cut is None:
+        tw = width // 2 if width > 1024 else width
+        parts, first = width // tw, 0
+    else:
+        width = tw = width // 2
+        parts, first = 1, cut
+    steps = quarters * parts
+    n = ride.shape[0] if ride is not None else 1
+    rides = [] if ride is None else [ride]
+
+    def kernel(*refs):
+        left_refs, right_refs = refs[:pairs], refs[pairs : 2 * pairs]
+        at = 2 * pairs
+        ride_in = refs[at : at + len(rides)]
+        at += len(rides)
+        own_ref, x_ref, y_ref, top_ref, low_ref = refs[at : at + 5]
+        at += 5
+        ride_out = refs[at : at + len(rides)]
+        at += len(rides)
+        left_s, right_s, sent, came, send_sems, recv_sems = refs[at : at + 6]
+        extra = refs[at + 6 :]
+        step = pl.program_id(0)
+        other_core = {"wide": flipped(lax.axis_index("wide"), 1)}
+
+        def copy(k):
+            return pltpu.make_async_remote_copy(
+                src_ref=sent.at[k],
+                dst_ref=came.at[k],
+                send_sem=send_sems.at[k],
+                recv_sem=recv_sems.at[k],
+                device_id=other_core,
+                device_id_type=pl.DeviceIdType.MESH,
+            )
+
+        def ride_copies():
+            mine, ride_send, ride_recv, own_sems = extra
+            seat = lax.axis_index("tp")
+            return [
+                pltpu.make_async_remote_copy(
+                    src_ref=ride_in[0].at[flipped(seat, e)],
+                    dst_ref=ride_out[0].at[seat],
+                    send_sem=ride_send.at[e - 1],
+                    recv_sem=ride_recv.at[e - 1],
+                    device_id={"tp": flipped(seat, e)},
+                    device_id_type=pl.DeviceIdType.MESH,
+                )
+                for e in range(1, n)
+            ], swap_own(ride_in[0], ride_out[0], mine, own_sems)
+
+        @pl.when(step == 0)
+        def _():
+            barrier = pltpu.get_barrier_semaphore()
+            partners = [other_core] + [
+                {"tp": flipped(lax.axis_index("tp"), e)} for e in range(1, n)
+            ]
+            for partner in partners:
+                pl.semaphore_signal(
+                    barrier, inc=1, device_id=partner, device_id_type=pl.DeviceIdType.MESH
+                )
+            pl.semaphore_wait(barrier, len(partners))
+            if rides:
+                sends, (load, keep) = ride_copies()
+                for c in sends:
+                    c.start()
+                load.start()
+                load.wait()
+                keep.start()
+
+        @pl.when(lax.rem(step, steps) == 0)
+        def _():
+            for i, ref in enumerate(left_refs):
+                left_s[i * rows : (i + 1) * rows] = ref[...]
+
+        for i, ref in enumerate(right_refs):
+            right_s[i * rows : (i + 1) * rows] = ref[...]
+        product = contract_rows(left_s[...], right_s[...])
+
+        @pl.when(step < steps)
+        def _():
+            sent[step] = product.astype(bf16)
+            copy(step).start()
+
+        @pl.when(step >= steps)
+        def _():
+            k = step - steps
+            copy(k).wait_recv()
+            total = (product + came[k].astype(f32)).astype(bf16)
+            own_ref[...] = total[:block]
+            x_ref[...] = total[block : 2 * block]
+            y_ref[...] = total[2 * block : 3 * block]
+            top_ref[...] = total[3 * block : 3 * block + half]
+            low_ref[...] = total[3 * block + half :]
+
+        @pl.when(step == 2 * steps - 1)
+        def _():
+            for k in range(steps):
+                copy(k).wait_send()
+            if rides:
+                sends, (load, keep) = ride_copies()
+                for c in sends:
+                    c.wait_send()
+                    c.wait_recv()
+                keep.wait()
+
+    columns = quarters * width
+    heights = (block, block, block, half, half)
+    out_shape = [struct(h, columns) for h in heights]
+    arrays = list(lefts) + list(rights)
+    late = lambda t: (0, jnp.maximum(t - steps, 0))
+    ride_scratch = (
+        []
+        if ride is None
+        else [
+            pltpu.VMEM(ride.shape[1:], bf16),
+            pltpu.SemaphoreType.DMA((n - 1,)),
+            pltpu.SemaphoreType.DMA((n - 1,)),
+            pltpu.SemaphoreType.DMA((2,)),
+        ]
+    )
+
+    def right_map(t):
+        t = lax.rem(t, steps)
+        return (lax.div(t, parts), 0, first + lax.rem(t, parts))
+
+    result = pl.pallas_call(
+        kernel,
+        grid=(2 * steps,),
+        in_specs=[pl.BlockSpec((rows, size), lambda t: (0, 1 - lax.div(t, steps)))] * pairs
+        + [pl.BlockSpec((None, rows, tw), right_map)] * pairs
+        + [pl.BlockSpec(memory_space=pl.ANY)] * len(rides),
+        out_specs=[pl.BlockSpec((h, tw), late) for h in heights]
+        + [pl.BlockSpec(memory_space=pl.ANY)] * len(rides),
+        out_shape=out_shape + [struct(*r.shape) for r in rides],
+        scratch_shapes=[
+            pltpu.VMEM((pairs * rows, size), bf16),
+            pltpu.VMEM((pairs * rows, tw), bf16),
+            pltpu.VMEM((steps, size, tw), bf16),
+            pltpu.VMEM((steps, size, tw), bf16),
+            pltpu.SemaphoreType.DMA((steps,)),
+            pltpu.SemaphoreType.DMA((steps,)),
+        ]
+        + ride_scratch,
+        compiler_params=pltpu.CompilerParams(
+            collective_id=number, has_side_effects=True, vmem_limit_bytes=VMEM
+        ),
+        cost_estimate=cost(
+            4 * pairs * rows * size * columns, nbytes(arrays) + nbytes(out_shape)
+        ),
+    )(*arrays, *rides)
+    return (result[:5], result[5]) if rides else (result, None)
+
+
+def struct(*shape):
+    return jax.ShapeDtypeStruct(shape, bf16)
+
+
 class Spread:
     def __init__(self, mover, m, source, target, block):
         self.mover, self.m, self.source, self.block = mover, m, source, block
@@ -725,22 +897,24 @@
             copy.wait_recv()
 
 
-def struct(*shape):
-    return jax.ShapeDtypeStruct(shape, bf16)
-
-
-def gather_front(m, n, qkv_block, in_block, down_block):
+def gather_front(m, n, qkv_block, in_block, down_block, gain_block):
     block, qw = qkv_block.shape
     fw, dw = in_block.shape[1], down_block.shape[1]
     depth = block * m
     pairs = n // 2
 
     def program(mover, ins, outs, _):
-        qkv, inner, down = ins
-        weights, in_own, in_rest, down_rest = outs
+        qkv, inner, down, gain = ins
+        weights, in_own, in_rest, down_rest, gains = outs
         rows = pl.ds(0, block)
         waves = [mover.start(qkv, weights.at[e, rows], "tp", e) for e in range(1, n)]
-        kept = [mover.keep(qkv, weights.at[0, rows]), mover.keep(inner, in_own.at[0, rows])]
+        kept = [
+            mover.keep(qkv, weights.at[0, rows]),
+            mover.keep(inner, in_own.at[0, rows]),
+            mover.keep(gain, gains.at[pl.ds(0, GAIN_ROWS)]),
+        ]
+        spread_gains = Spread(mover, m, gain, lambda r: gains.at[r], GAIN_ROWS)
+        spread_gains.first()
         spreads = [
             Spread(
                 mover,
@@ -752,7 +926,9 @@
             for q in range(n)
         ]
         spreads[0].first()
+        spread_gains.second()
         spreads[0].second()
+        spread_gains.third()
         spreads[0].third()
         for q in range(1, n):
             waves[q - 1].wait_recv()
@@ -772,6 +948,7 @@
         for spread in spreads:
             spread.last()
         own.last()
+        spread_gains.last()
         for copy in late:
             copy.wait_recv()
         for copy in kept:
@@ -782,18 +959,19 @@
         program,
         m,
         n,
-        [qkv_block, in_block, down_block],
+        [qkv_block, in_block, down_block, gain_block],
         [
             struct(n, depth, qw),
             struct(1, depth, fw),
             struct(pairs - 1, depth, fw),
             struct(pairs - 1, depth, dw),
+            jax.ShapeDtypeStruct((m * GAIN_ROWS, gain_block.shape[1]), f32),
         ],
         [],
-        (n - 1) + per * (n + 1) + 2 * (pairs - 1),
-        2,
+        (n - 1) + per * (n + 2) + 2 * (pairs - 1),
+        3,
         1,
-        vmem_ins=(0, 1, 2),
+        vmem_ins=(0, 1, 2, 3),
     )
 
 
@@ -1000,46 +1178,29 @@
         size = m if axis == "wide" else n
         return lax.ppermute(a, axis, [(i, i ^ mask) for i in range(size)])
 
-    def scatter(mine, other):
+    def scatter(lefts, rights, cut, number, ride=None, rode=None):
         if m != 8:
+            if ride is not None:
+                rode.append(swap(ride))
+            other = weight_gradient(lefts, rights, 1, cut)
+            mine = weight_gradient(lefts, rights, 0, cut)
             both = jnp.concatenate([mine, other])
             got = yield both, [over("wide", both[k * block : (k + 1) * block], k) for k in range(1, m)]
             return sum((g.astype(f32) for g in got), both[:block].astype(f32))
+        (own, x, y, top_sent, low_sent), came = gradient_pair(lefts, rights, cut, number, ride)
+        if ride is not None:
+            rode.append(came)
         half = block // 2
-        (came,) = yield (mine, other), [over("wide", other, 1)]
-
-        def total(start, size):
-            cut = slice(start, start + size)
-            return mine[cut].astype(f32) + came[cut].astype(f32)
-
-        sources = [
-            total(3 * block, half).astype(bf16),
-            total(3 * block + half, half).astype(bf16),
-        ]
-        top, low = yield sources, [over("wide", sources[0], 2), over("wide", sources[1], 4)]
-        for_x = jnp.concatenate(
-            [
-                total(block, half).astype(bf16),
-                (total(block + half, half) + low.astype(f32)).astype(bf16),
-            ]
-        )
-        for_y = jnp.concatenate(
-            [
-                (total(2 * block, half) + top.astype(f32)).astype(bf16),
-                total(2 * block + half, half).astype(bf16),
-            ]
-        )
+        top, low = yield (top_sent, low_sent), [over("wide", top_sent, 2), over("wide", low_sent, 4)]
+        for_x = jnp.concatenate([x[:half], (x[half:].astype(f32) + low.astype(f32)).astype(bf16)])
+        for_y = jnp.concatenate([(y[:half].astype(f32) + top.astype(f32)).astype(bf16), y[half:]])
         from_x, from_y = yield [for_x, for_y], [over("wide", for_x, 2), over("wide", for_y, 4)]
-        return total(0, block) + from_x.astype(f32) + from_y.astype(f32)
-
-    def wide_products(left, rights, cut=None):
-        other = weight_gradient(left, rights, 1, cut)
-        return weight_gradient(after(left, other), rights, 0, cut), other
+        return own.astype(f32) + from_x.astype(f32) + from_y.astype(f32)
 
     cotangent = shuffle_columns(out_grad, relative)
 
-    def ffn_share(left, rights):
-        total = yield from scatter(*wide_products(left, rights))
+    def ffn_share(left, rights, number, ride=None, rode=None):
+        total = yield from scatter(left, rights, None, number, ride, rode)
         parts = [total[:, e * fcols : (e + 1) * fcols].astype(bf16) for e in range(1, n // 2)]
         sent = yield parts, [over("tp", p, 2 * (e + 1)) for e, p in enumerate(parts)]
         return sum((x.astype(f32) for x in sent), total[:, :fcols])
@@ -1047,19 +1208,11 @@
     def swap(a):
         return lax.all_to_all(a, "tp", split_axis=0, concat_axis=0, tiled=True)
 
-    def attn_share(left, right, cut=None):
-        total = yield from scatter(*wide_products([left], [right], cut))
+    def attn_share(left, right, cut, number):
+        total = yield from scatter([left], [right], cut, number)
         parts = total.astype(bf16).reshape(block, n, -1).transpose(1, 0, 2)
         (came,) = yield parts, [swap(parts)]
         return jnp.sum(came.astype(f32), axis=0)
-
-    def gather_small(a):
-        stack = a[None]
-        size = 1
-        while size < m:
-            stack = jnp.concatenate([stack, over("wide", stack, order[size])])
-            size *= 2
-        return stack
 
     qkv_block = jnp.concatenate([w_query, w_key, w_value], axis=1)
     out_block = w_out.T
@@ -1070,14 +1223,19 @@
     fcols = w_gate.shape[1]
     fw = fcols // 3
 
-    gains = gather_small(jnp.concatenate([attn_gain, ffn_gain, q_gain, k_gain])[None])[:, 0]
-    gains = gains.astype(f32)
+    gain_row = jnp.concatenate([attn_gain, ffn_gain, q_gain, k_gain]).astype(f32)[None]
+    gain_width = -(-gain_row.shape[1] // 128) * 128
+    gain_block = jnp.pad(gain_row, ((0, GAIN_ROWS - 1), (0, gain_width - gain_row.shape[1])))
+    qkv_all, in_own, in_rest, down_rest, gains = gather_front(
+        m, n, qkv_block, in_block, down_block, gain_block
+    )
+    gains = gains[::GAIN_ROWS]
     small = q_gain.shape[0]
     gain_one = gains[:, :block].reshape(1, depth)
     gain_two = gains[:, block : 2 * block].reshape(1, depth)
     head_gains = jnp.take(gains[:, 2 * block :], absolute, axis=0)
     gain_q = head_gains[:, :small].reshape(1, HEAD_DIM)
-    gain_k = head_gains[:, small:].reshape(1, HEAD_DIM)
+    gain_k = head_gains[:, small : 2 * small].reshape(1, HEAD_DIM)
 
     base = where * parent_table.shape[0]
     block_segs = seg_ids[TRUNK::BRANCH] - base
@@ -1101,7 +1259,6 @@
     unit_one = stream * inverse_one
     normed_one = (unit_one * gain_one).astype(bf16)
 
-    qkv_all, in_own, in_rest, down_rest = gather_front(m, n, qkv_block, in_block, down_block)
     qkv_tiles = Tiles([qkv_all], 2, 0, aw)
     hats, raws = project_qkv(normed_one, qkv_tiles, seats, cosine, sine, gain_q, gain_k)
     qkv, in_rest, out_all, down_own = gather_middle(m, n, hats, in_rest, out_block, down_block)
@@ -1127,26 +1284,25 @@
     hidden_next, gate_next, up_next = feed_forward(normed_two_next, gate_tiles, up_tiles, plain)
     down_part = project_columns([hidden_next], [down_tiles], plain, depth, bf16)
     cotangent_next, hidden_late = after((cotangent_next, hidden), down_part)
-    down_job = Job(ffn_share([cotangent, cotangent_next], [hidden_late, hidden_next]))
+    down_job = Job(ffn_share([cotangent, cotangent_next], [hidden_late, hidden_next], 4))
     cotangent_next = after(cotangent_next, down_job.started)
     gate_grad_next, up_grad_next = feed_back(
         cotangent_next, gate_next, up_next, down_tiles, plain
     )
-    back_part = project_columns(
-        [gate_grad_next, up_grad_next], [gate_tiles, up_tiles], plain, depth, bf16
-    )
+    gate_late, up_late = tick((gate_grad_next, up_grad_next), down_job)
+    gate_late, up_late = after((gate_late, up_late), down_job.started)
+    back_part = project_columns([gate_late, up_late], [gate_tiles, up_tiles], plain, depth, bf16)
     back_next = over("tp", back_part, 1)
-    own_grad = tick(after(cotangent, back_part), down_job)
-    own_grad = after(own_grad, down_job.started)
+    own_grad = after(cotangent, back_part)
     gate_grad, up_grad = feed_back(own_grad, gate, up, down_tiles, plain)
-    gate_job = Job(ffn_share([normed_two, normed_two_next], [gate_grad, gate_grad_next]))
+    gate_job = Job(ffn_share([normed_two, normed_two_next], [gate_grad, gate_grad_next], 5))
     gate_late, up_late = after((gate_grad, up_grad), gate_job.started)
-    gate_late, up_late = tick((gate_late, up_late), down_job, gate_job)
-    gate_late, up_late = after((gate_late, up_late), down_job.started, gate_job.started)
+    gate_late, up_late = tick((gate_late, up_late), down_job)
+    gate_late, up_late = after((gate_late, up_late), down_job.started)
     back = project_columns([gate_late, up_late], [gate_tiles, up_tiles], plain, depth, f32)
     back, back_next = after((back, back_next), back)
-    back = tick(back, down_job, gate_job)
-    back = after(back, down_job.started, gate_job.started)
+    back = tick(back, gate_job)
+    back = after(back, gate_job.started)
     normed_two_grad = back + back_next.astype(f32)
 
     ffn_gain_part = jnp.sum(normed_two_grad * unit_two, axis=0)
@@ -1154,41 +1310,37 @@
         normed_two_grad, unit_two, inverse_two, gain_two
     )
     grad_low = stream_grad.astype(bf16)
-    attended_grad = project_rows(grad_low, out_tiles, seats)
-    grad_heads = swap(attended_grad).reshape(n * rows, -1)
+    attended_grad = tick(project_rows(grad_low, out_tiles, seats), down_job)
+    lefts, up_grads = after(
+        ([normed_two, normed_two_next], [up_grad, up_grad_next]), attended_grad
+    )
+    rode = []
+    up_job = Job(ffn_share(lefts, up_grads, 6, attended_grad, rode))
+    grad_heads = after(rode[0].reshape(n * rows, -1), up_job.started)
     grad_heads = tick(grad_heads, gate_job)
     grad_heads = after(grad_heads, gate_job.started)
-    down_next = over("tp", after(down_part, grad_heads), 1)
     back_hats = attention_backward(qkv, attended_heads, grad_heads, logs, parents, kv)
+    back_hats = tick(back_hats, gate_job, up_job)
+    back_hats = after(back_hats, up_job.started)
     back_hats_own = swap(back_hats.reshape(n, rows, -1))
-    lefts, up_grads, grad_low, down_next, after_attn = after(
-        (
-            [normed_two, normed_two_next],
-            [up_grad, up_grad_next],
-            grad_low,
-            down_next,
-            after_attn,
-        ),
-        back_hats,
-    )
-    up_job = Job(ffn_share(lefts, up_grads))
-    grad_low = tick(after(grad_low, up_job.started), up_job)
-    grad_low = after(grad_low, up_job.started)
-    out_job = Job(attn_share(grad_low, attended))
-    down_next, after_attn = after((down_next, after_attn), out_job.started)
+    grad_low, down_sent, after_attn = after((grad_low, down_part, after_attn), back_hats)
+    out_job = Job(attn_share(grad_low, attended, None, 7))
+    fence = tick(after(grad_low, out_job.started), up_job)
+    back_hats_own = after(back_hats_own, fence, out_job.started)
+    raw_grads, q_sum, k_sum = qkv_back(back_hats_own, raws, cosine, sine, gain_q, gain_k)
+    raw_grads = tick(raw_grads, out_job)
+    down_next = over("tp", after(down_sent, raw_grads), 1)
+    q_job = Job(attn_share(normed_one, after(raw_grads, out_job.started), 0, 8))
+    raw_late = after(raw_grads, q_job.started)
+    k_job = Job(attn_share(normed_one, raw_late, 1, 9))
+    raw_late = tick(after(raw_late, k_job.started), q_job, out_job, up_job)
+    raw_late = after(raw_late, q_job.started, out_job.started, up_job.started)
+    normed_one_grad = project_columns([raw_late], [qkv_tiles], seats, depth, f32)
+    normed_one_grad, down_next = after((normed_one_grad, down_next), normed_one_grad)
+    normed_one_grad = tick(normed_one_grad, q_job, k_job, up_job, out_job)
+    normed_one_grad = after(normed_one_grad, q_job.started, k_job.started)
     mixed = (after_attn + down + down_next.astype(f32)).astype(bf16)
     mixed = shuffle_columns(mixed, absolute)
-    mixed = tick(mixed, up_job, out_job)
-    back_hats_own = after(back_hats_own, mixed, up_job.started, out_job.started)
-    raw_grads, q_sum, k_sum = qkv_back(back_hats_own, raws, cosine, sine, gain_q, gain_k)
-    q_job = Job(attn_share(normed_one, raw_grads, 0))
-    raw_late = after(raw_grads, q_job.started)
-    k_job = Job(attn_share(normed_one, raw_late, 1))
-    raw_late = tick(after(raw_late, k_job.started), up_job, out_job, q_job)
-    raw_late = after(raw_late, q_job.started, out_job.started)
-    normed_one_grad = project_columns([raw_late], [qkv_tiles], seats, depth, f32)
-    normed_one_grad = tick(normed_one_grad, out_job, q_job, k_job)
-    normed_one_grad = after(normed_one_grad, q_job.started, k_job.started)
     attn_gain_part = jnp.sum(normed_one_grad * unit_one, axis=0)
     tokens_grad = (
         stream_grad + norm_back(normed_one_grad, unit_one, inverse_one, gain_one)

time: 1280 us -> 1150 us (0.90)
  waiting for transfers between devices: 259 us -> 122 us
  other arithmetic: 116 us -> 88.7 us
    ppermute x45 -> x36, waiting for transfers between devices: 189 us -> 56.9 us  [over(): return lax.ppermute(a, axis, [(i, i ^ mask) for i in range(size)])]
    convert_element_type x13 -> x12, other arithmetic: 38.6 us -> 10.3 us  [the longest x6 5.5 us: scatter(): (x[half:].astype(f32) + low.astype(f32)).astype(bf16)]
    ppermute x45 -> x36, starting transfers between devices: 53.8 us -> 66.2 us  [over(): return lax.ppermute(a, axis, [(i, i ^ mask) for i in range(size)])]
    pallas_call x12 -> x6, Pallas kernels: 120 us -> 132 us  [gradient_pair(): pl.pallas_call(kernel, grid=(2 * steps,), in_specs=[pl.BlockSpec((rows, s...]
    all_to_all x5 -> x4, waiting for transfers between devices: 70.2 us -> 65 us  [swap(): return lax.all_to_all(a, 'tp', split_axis=0, concat_axis=0, tiled=True)]
  transfers between devices with their start and end apart: 50 -> 40, of which waited for: 23 -> 9; matrix products, arithmetic and copies ran while one was open for 8% -> 7% of each run, Pallas kernels for 36% -> 32%
where the time goes in v3:
time: 1150 us; the launch traced here: 1140 us
  Pallas kernels  801 us (70%)
  waiting for transfers between devices  122 us (11%)
  other arithmetic  88.7 us (8%)
  starting transfers between devices  84.6 us (7%)
  local copies, waits for them, and re-layouts  37.3 us (3%)
    pallas_call x3, Pallas kernels, transfer_call(): pl.pallas_call(kernel, in_specs=[pl.BlockSpec(memory_space=pltpu.VMEM if...  353 us
    pallas_call x12, Pallas kernels, tiled_call(): pl.pallas_call(kernel, grid_spec=pltpu.PrefetchScalarGridSpec(num_scalar_...  223 us
    pallas_call x6, Pallas kernels, gradient_pair(): pl.pallas_call(kernel, grid=(2 * steps,), in_specs=[pl.BlockSpec((rows, s...  132 us
    ppermute x36, starting transfers between devices, over(): return lax.ppermute(a, axis, [(i, i ^ mask) for i in range(size)])  66.2 us
    all_to_all x4, waiting for transfers between devices, swap(): return lax.all_to_all(a, 'tp', split_axis=0, concat_axis=0, tiled=True)  65 us
    ppermute x36, waiting for transfers between devices, over(): return lax.ppermute(a, axis, [(i, i ^ mask) for i in range(size)])  56.9 us
    pallas_call x1, Pallas kernels, attention_backward(): pl.pallas_call(kernel, grid_spec=pltpu.PrefetchScalarGridSpec(num_scalar_...  37.4 us
    pallas_call x4, Pallas kernels, shuffle_columns(): pl.pallas_call(kernel, grid_spec=pltpu.PrefetchScalarGridSpec(num_scalar_...  25.7 us
  transfers between devices with their start and end apart: 40, of which 9 were waited for; matrix products, arithmetic and copies ran while one was open for 7% of the time, Pallas kernels for 32%

profile of v3, /device:TPU:0, one launch (start us, length us, event | category | flops | bytes accessed | tf_op | source)
XLA Modules:
  0.0 1135.8 jit_solution(4052816659080683074)
XLA Ops:
  6.9 156.1 %shard_map.275 = (bf16[4,2048,1024]{2,1,0:T(8,128)(2,1)}, bf16[1,2048,3072]{2,1,0:T(8,128)(2,1)}, bf16[1,2048,3072]{2,1,0:T(8,128)(2,1)}, bf16[1,2048,1536]{2,1,0:T(8,128)(2,1)}, f32[128,640]{1,0:T(8,128)S(1)}) custom-call(bf16[256,1024]{1,0:T(8,128)(2,1)S(1)} %pad_maximum_fusion.13.refs_0_, bf16[256,3072]{1,0:T(8,128)(2,1)} %pad_maximum_fusion.refs_1_, ...), custom_call_target="tpu_custom_call" | custom-call | bytes 10000 | tf_op jit(solution)/shard_map/pallas_call | solution.py:665
  165.4 6.5 shard_map.274
  183.2 21.4 %shard_map.276 = (bf16[4,544,1024]{2,1,0:T(8,128)(2,1)}, bf16[4,544,1024]{2,1,0:T(8,128)(2,1)}) custom-call(s32[4]{0:T(128)S(1)} %iota_xor_fusion.seat_ref, bf16[4,2048,1024]{2,1,0:T(8,128)(2,1)} %get-tuple-element.144.refs_0_, bf16[544,2048]{1,0:T(8,128)(2,1)} %fusion.4.refs_1_.refs_0_, f32[544,128]{1,0:T(8,128)S(1)} %get-tuple-element.357.refs_2_.cos_ref, ...), custom_call_target="tpu_custom_call" | custom-call | flops 91268056 | bytes 284764 | tf_op jit(solution)/shard_map/pallas_call | solution.py:137
  204.6 152.8 %shard_map.277 = (bf16[4,544,1024]{2,1,0:T(8,128)(2,1)}, bf16[1,2048,3072]{2,1,0:T(8,128)(2,1)}, bf16[4,2048,512]{2,1,0:T(8,128)(2,1)}, bf16[1,2048,1536]{2,1,0:T(8,128)(2,1)}) custom-call(bf16[4,544,1024]{2,1,0:T(8,128)(2,1)} %get-tuple-element.146.refs_0_, bf16[1,2048,3072]{2,1,0:T(8,128)(2,1)} %get-tuple-element.147.refs_1_, ...), custom_call_target="tpu_custom_call", output_to_operand_aliasing={{1}: (1, {})} | custom-call | bytes 10000 | tf_op jit(solution)/shard_map/pallas_call | solution.py:665
  357.4 20.6 %shard_map.278 = (bf16[2176,512]{1,0:T(8,128)(2,1)}, f32[2,17,256]{2,1,0:T(8,128)S(1)}) custom-call(s32[8]{0:T(128)S(1)} %fusion.30.parent_ref, bf16[2176,1024]{1,0:T(8,128)(2,1)} %bitcast.55, bf16[2176,1024]{1,0:T(8,128)(2,1)} %bitcast.56, bf16[2176,1024]{1,0:T(8,128)(2,1)} %bitcast.57), custom_call_target="tpu_custom_call" | custom-call | flops 90112000 | bytes 67194 | tf_op jit(solution)/shard_map/pallas_call | solution.py:440
  378.0 44.2 %shard_map.279 = (bf16[4,544,512]{2,1,0:T(8,128)(2,1)}, bf16[1,2048,1536]{2,1,0:T(8,128)(2,1)}) custom-call(bf16[4,544,512]{2,1,0:T(8,128)(2,1)} %bitcast.64, bf16[1,2048,1536]{2,1,0:T(8,128)(2,1)} %get-tuple-element.151.refs_1_), custom_call_target="tpu_custom_call", output_to_operand_aliasing={{1}: (1, {})} | custom-call | bytes 10000 | tf_op jit(solution)/shard_map/pallas_call | solution.py:665
  422.2 13.1 %shard_map.280 = f32[544,2048]{1,0:T(8,128)} custom-call(s32[4]{0:T(128)S(1)} %iota_xor_fusion.seat_ref, bf16[4,2048,512]{2,1,0:T(8,128)(2,1)} %get-tuple-element.148.refs_0_, bf16[4,544,512]{2,1,0:T(8,128)(2,1)} %get-tuple-element.152.refs_1_), custom_call_target="tpu_custom_call" | custom-call | flops 45634028 | bytes 150732 | tf_op jit(solution)/shard_map/pallas_call | solution.py:137
  435.3 2.9 multiply_reduce_fusion.2
  440.3 10.7 collective-permute-start
  451.0 6.4 shard_map.273.refs_0_.refs_2_
  457.4 21.3 %shard_map.281 = (bf16[2,544,1536]{2,1,0:T(8,128)(2,1)}, bf16[2,544,1536]{2,1,0:T(8,128)(2,1)}, bf16[2,544,1536]{2,1,0:T(8,128)(2,1)}) custom-call(s32[4]{0:T(128)S(1)} %iota.53.seat_ref, bf16[1,2048,3072]{2,1,0:T(8,128)(2,1)} %get-tuple-element.153.refs_0_.refs_2_, bf16[1,2048,3072]{2,1,0:T(8,128)(2,1)} %get-tuple-element.154.refs_1_.refs_3_, ...), custom_call_target="tpu_custom_call" | custom-call | flops 136902080 | bytes 625868 | tf_op jit(solution)/shard_map/pallas_call | solution.py:137
  478.8 16.5 %shard_map.282 = f32[544,2048]{1,0:T(8,128)} custom-call(s32[4]{0:T(128)S(1)} %iota.52.seat_ref, bf16[1,2048,1536]{2,1,0:T(8,128)(2,1)} %get-tuple-element.155.refs_0_, bf16[1,2048,1536]{2,1,0:T(8,128)(2,1)} %get-tuple-element.156.refs_1_, bf16[2,544,1536]{2,1,0:T(8,128)(2,1)} %get-tuple-element.162.refs_2_), custom_call_target="tpu_custom_call" | custom-call | flops 68451040 | bytes 203816 | tf_op jit(solution)/shard_map/pallas_call | solution.py:137
  500.0 21.3 %shard_map.283 = (bf16[2,544,1536]{2,1,0:T(8,128)(2,1)}, bf16[2,544,1536]{2,1,0:T(8,128)(2,1)}, bf16[2,544,1536]{2,1,0:T(8,128)(2,1)}) custom-call(s32[4]{0:T(128)S(1)} %iota.55.seat_ref, bf16[1,2048,3072]{2,1,0:T(8,128)(2,1)} %get-tuple-element.153.refs_0_.refs_2_, bf16[1,2048,3072]{2,1,0:T(8,128)(2,1)} %get-tuple-element.154.refs_1_.refs_3_, ...), custom_call_target="tpu_custom_call" | custom-call | flops 136902080 | bytes 625868 | tf_op jit(solution)/shard_map/pallas_call | solution.py:137
  521.3 15.6 %shard_map.284 = bf16[544,2048]{1,0:T(8,128)(2,1)} custom-call(s32[4]{0:T(128)S(1)} %iota.54.seat_ref, bf16[1,2048,1536]{2,1,0:T(8,128)(2,1)} %get-tuple-element.155.refs_0_, bf16[1,2048,1536]{2,1,0:T(8,128)(2,1)} %get-tuple-element.156.refs_1_, bf16[2,544,1536]{2,1,0:T(8,128)(2,1)} %get-tuple-element.160.refs_2_.refs_3_), custom_call_target="tpu_custom_call" | custom-call | flops 68451040 | bytes 181534 | tf_op jit(solution)/shard_map/pallas_call | solution.py:137
  536.8 9.6 collective-permute-done.1.refs_1_.refs_2_
  547.8 24.4 %shard_map.285 = (bf16[256,3072]{1,0:T(8,128)(2,1)}, bf16[256,3072]{1,0:T(8,128)(2,1)}, bf16[256,3072]{1,0:T(8,128)(2,1)}, bf16[128,3072]{1,0:T(8,128)(2,1)S(1)}, bf16[128,3072]{1,0:T(8,128)(2,1)S(1)}) custom-call(bf16[544,2048]{1,0:T(8,128)(2,1)} %shard_map.273.refs_0_.refs_2_, bf16[544,2048]{1,0:T(8,128)(2,1)} %copy-done.18, ...), custom_call_target="tpu_custom_call" | custom-call | flops 136902080 | bytes 174325 | tf_op jit(solution)/shard_map/pallas_call | solution.py:825
  572.2 3.3 collective-permute-start.2
  578.1 17.0 %shard_map.286 = (bf16[2,544,1536]{2,1,0:T(8,128)(2,1)}, bf16[2,544,1536]{2,1,0:T(8,128)(2,1)}) custom-call(s32[4]{0:T(128)S(1)} %iota.51.seat_ref, bf16[1,2048,1536]{2,1,0:T(8,128)(2,1)} %get-tuple-element.155.refs_0_, bf16[1,2048,1536]{2,1,0:T(8,128)(2,1)} %get-tuple-element.156.refs_1_, bf16[544,2048]{1,0:T(8,128)(2,1)} %copy-done.18, ...), custom_call_target="tpu_custom_call" | custom-call | flops 68451040 | bytes 281804 | tf_op jit(solution)/shard_map/pallas_call | solution.py:137
  599.0 24.0 %shard_map.287 = bf16[544,2048]{1,0:T(8,128)(2,1)} custom-call(s32[4]{0:T(128)S(1)} %iota.50.seat_ref, bf16[1,2048,3072]{2,1,0:T(8,128)(2,1)} %get-tuple-element.153.refs_0_.refs_2_, bf16[1,2048,3072]{2,1,0:T(8,128)(2,1)} %get-tuple-element.154.refs_1_.refs_3_, bf16[1,2048,3072]{2,1,0:T(8,128)(2,1)} %get-tuple-element.153.refs_0_.refs_2_, ...), custom_call_target="tpu_custom_call" | custom-call | flops 136902080 | bytes 592445 | tf_op jit(solution)/shard_map/pallas_call | solution.py:137
  624.5 16.8 %shard_map.288 = (bf16[2,544,1536]{2,1,0:T(8,128)(2,1)}, bf16[2,544,1536]{2,1,0:T(8,128)(2,1)}) custom-call(s32[4]{0:T(128)S(1)} %iota.49.seat_ref, bf16[1,2048,1536]{2,1,0:T(8,128)(2,1)} %get-tuple-element.155.refs_0_, bf16[1,2048,1536]{2,1,0:T(8,128)(2,1)} %get-tuple-element.156.refs_1_, bf16[544,2048]{1,0:T(8,128)(2,1)} %shard_map.273.refs_0_.refs_2_, ...), custom_call_target="tpu_custom_call" | custom-call | flops 68451040 | bytes 281804 | tf_op jit(solution)/shard_map/pallas_call | solution.py:137
  641.3 24.5 %shard_map.289 = (bf16[256,3072]{1,0:T(8,128)(2,1)}, bf16[256,3072]{1,0:T(8,128)(2,1)}, bf16[256,3072]{1,0:T(8,128)(2,1)}, bf16[128,3072]{1,0:T(8,128)(2,1)S(1)}, bf16[128,3072]{1,0:T(8,128)(2,1)S(1)}) custom-call(bf16[544,2048]{1,0:T(8,128)(2,1)} %copy-done.11, bf16[544,2048]{1,0:T(8,128)(2,1)} %collective-permute-done.refs_4_.refs_1_, ...), custom_call_target="tpu_custom_call" | custom-call | flops 136902080 | bytes 174325 | tf_op jit(solution)/shard_map/pallas_call | solution.py:825
  678.8 25.0 %shard_map.290 = f32[544,2048]{1,0:T(8,128)} custom-call(s32[4]{0:T(128)S(1)} %iota.48.seat_ref, bf16[1,2048,3072]{2,1,0:T(8,128)(2,1)} %get-tuple-element.153.refs_0_.refs_2_, bf16[1,2048,3072]{2,1,0:T(8,128)(2,1)} %get-tuple-element.154.refs_1_.refs_3_, bf16[1,2048,3072]{2,1,0:T(8,128)(2,1)} %get-tuple-element.153.refs_0_.refs_2_, ...), custom_call_target="tpu_custom_call" | custom-call | flops 136902080 | bytes 614727 | tf_op jit(solution)/shard_map/pallas_call | solution.py:137
  713.4 4.1 fusion.31
  717.5 10.5 shard_map.291.refs_4_
  728.1 44.2 %shard_map.292 = (bf16[256,3072]{1,0:T(8,128)(2,1)}, bf16[256,3072]{1,0:T(8,128)(2,1)}, bf16[256,3072]{1,0:T(8,128)(2,1)}, bf16[128,3072]{1,0:T(8,128)(2,1)S(1)}...) custom-call(bf16[544,2048]{1,0:T(8,128)(2,1)} %copy-done.11, ...), custom_call_target="tpu_custom_call" | custom-call | flops 136902080 | bytes 174325 | tf_op jit(solution)/shard_map/pallas_call | solution.py:825
  777.1 11.7 %collective-permute-start.12 = (bf16[256,1536]{1,0:T(8,128)(2,1)S(1)}, bf16[256,1536]{1,0:T(8,128)(2,1)}, u32[]{:S(2)}, u32[]{:S(2)}) collective-permute-start(bf16[256,1536]{1,0:T(8,128)(2,1)S(1)} %slice.272), channel_id=1, source_target_pairs={{0,2},{1,3},{2,0},{3,1},{4,6},{5,7},{6,4},{7,5},{8,10},{9,11},{10,... | collective-permute-start | bytes 2359304 | tf_op jit(solution)/shard_map/ppermute | solution.py:1179
  789.0 37.4 %shard_map.293 = bf16[2176,1024]{1,0:T(8,128)(2,1)} custom-call(s32[8]{0:T(128)S(1)} %fusion.30.parent_ref, bf16[2176,1024]{1,0:T(8,128)(2,1)} %bitcast.58, bf16[2176,1024]{1,0:T(8,128)(2,1)} %bitcast.59, bf16[2176,1024]{1,0:T(8,128)(2,1)} %bitcast.60, bf16[2176,512]{1,0:T(8,128)(2,1)} %get-tuple-element.150.o_ref, bf16[2176,512]{1,0:T(8,128)(2,1)} %bitcast.70, ...), custom_call_target="tpu_custom_call" | custom-call | flops 225280000 | bytes 133693 | tf_op jit(solution)/shard_map/pallas_call | solution.py:530
  829.3 5.4 all-to-all-start
  836.9 12.8 %shard_map.294 = (bf16[256,2048]{1,0:T(8,128)(2,1)}, bf16[256,2048]{1,0:T(8,128)(2,1)}, bf16[256,2048]{1,0:T(8,128)(2,1)}, bf16[128,2048]{1,0:T(8,128)(2,1)S(1)}, bf16[128,2048]{1,0:T(8,128)(2,1)S(1)}) custom-call(bf16[544,2048]{1,0:T(8,128)(2,1)} %get-tuple-element.224.refs_1_.refs_0_, bf16[4,544,512]{2,1,0:T(8,128)(2,1)} %get-tuple-element.152.refs_1_), custom_call_target="tpu_custom_call" | custom-call | flops 45634028 | bytes 86507 | tf_op jit(solution)/shard_map/pallas_call | solution.py:825
  853.8 18.6 %collective-permute-done.22 = bf16[256,3072]{1,0:T(8,128)(2,1)} collective-permute-done((bf16[256,3072]{1,0:T(8,128)(2,1)}, bf16[256,3072]{1,0:T(8,128)(2,1)}, u32[]{:S(2)}, u32[]{:S(2)}) %collective-permute-start.22) | collective-permute-done | bytes 1572896 | tf_op jit(solution)/shard_map/ppermute | solution.py:1179
  872.7 59.7 %all-to-all-done.g_ref = bf16[4,544,1024]{2,1,0:T(8,128)(2,1)} async-done(((bf16[4,544,1024]{2,1,0:T(8,128)(2,1)}), bf16[4,544,1024]{2,1,0:T(8,128)(2,1)}, u32[]{:S(2)}, u32[]{:S(2)}) %all-to-all-start) | async-done | bytes 4456480 | tf_op jit(solution)/shard_map/all_to_all | solution.py:1209
  932.4 10.1 shard_map.295
  952.7 13.0 %shard_map.296 = (bf16[256,2048]{1,0:T(8,128)(2,1)}, bf16[256,2048]{1,0:T(8,128)(2,1)}, bf16[256,2048]{1,0:T(8,128)(2,1)}, bf16[128,2048]{1,0:T(8,128)(2,1)S(1)}, bf16[128,2048]{1,0:T(8,128)(2,1)S(1)}) custom-call(bf16[544,2048]{1,0:T(8,128)(2,1)} %fusion.4.refs_1_.refs_0_, bf16[4,544,1024]{2,1,0:T(8,128)(2,1)} %get-tuple-element.253.refs_1_), custom_call_target="tpu_custom_call" | custom-call | flops 45634028 | bytes 108789 | tf_op jit(solution)/shard_map/pallas_call | solution.py:825
  970.1 3.0 copy.54
  973.1 13.0 %shard_map.297 = (bf16[256,2048]{1,0:T(8,128)(2,1)}, bf16[256,2048]{1,0:T(8,128)(2,1)}, bf16[256,2048]{1,0:T(8,128)(2,1)}, bf16[128,2048]{1,0:T(8,128)(2,1)S(1)}, bf16[128,2048]{1,0:T(8,128)(2,1)S(1)}) custom-call(bf16[544,2048]{1,0:T(8,128)(2,1)} %fusion.4.refs_1_.refs_0_, bf16[4,544,1024]{2,1,0:T(8,128)(2,1)} %get-tuple-element.253.refs_1_), custom_call_target="tpu_custom_call" | custom-call | flops 45634028 | bytes 108789 | tf_op jit(solution)/shard_map/pallas_call | solution.py:825
  994.3 3.8 all-to-all-start.1
  1012.9 20.3 %shard_map.298 = f32[544,2048]{1,0:T(8,128)} custom-call(s32[4]{0:T(128)S(1)} %iota_xor_fusion.seat_ref, bf16[4,2048,1024]{2,1,0:T(8,128)(2,1)} %get-tuple-element.144.refs_0_, bf16[4,544,1024]{2,1,0:T(8,128)(2,1)} %get-tuple-element.253.refs_1_), custom_call_target="tpu_custom_call" | custom-call | flops 91268056 | bytes 256901 | tf_op jit(solution)/shard_map/pallas_call | solution.py:137
  1035.7 15.0 %collective-permute-done.24 = bf16[544,2048]{1,0:T(8,128)(2,1)} collective-permute-done((bf16[544,2048]{1,0:T(8,128)(2,1)}, bf16[544,2048]{1,0:T(8,128)(2,1)}, u32[]{:S(2)}, u32[]{:S(2)}) %collective-permute-start.24) | collective-permute-done | bytes 2228256 | tf_op jit(solution)/shard_map/ppermute | solution.py:1179
  1050.7 5.3 all-to-all-done.1
  1066.1 4.2 all-to-all-start.2
  1070.4 3.6 fusion.10
  1074.1 6.9 add_convert_fusion.in_ref
  1081.0 6.4 shard_map.299
  1096.0 5.0 all-to-all-start.3
  1103.2 6.3 fusion.9.in_ref
  1109.4 8.4 collective-permute-done.32
  1117.9 4.5 collective-permute-start.33
  1122.6 6.4 shard_map.300
  (305 shorter events, 140.2 us)
Async XLA Ops:
  6.7 157.0 %copy-start.51 = (s32[8]{0:T(128)S(1)}, s32[8]{0:T(128)}, u32[]{:S(2)}) copy-start(s32[8]{0:T(128)} %constant.82.clone) | copy-start | bytes 100
  6.7 157.5 %copy-start.4 = (s32[8]{0:T(128)S(1)}, s32[8]{0:T(128)}, u32[]{:S(2)}) copy-start(s32[8]{0:T(128)} %constant.83.clone) | copy-start | bytes 100
  183.2 21.4 %copy-start = (f32[544,128]{1,0:T(8,128)}, f32[544,128]{1,0:T(8,128)S(1)}, u32[]{:S(2)}) copy-start(f32[544,128]{1,0:T(8,128)S(1)} %get-tuple-element.357.refs_2_.cos_ref) | copy-start | bytes 835588
  440.3 57.9 %collective-permute-start = (bf16[544,2048]{1,0:T(8,128)(2,1)S(1)}, bf16[544,2048]{1,0:T(8,128)(2,1)}, u32[]{:S(2)}, u32[]{:S(2)}) collective-permute-start(bf16[544,2048]{1,0:T(8,128)(2,1)S(1)} %multiply_convert_fusion.refs_4_.refs_0_), channel_id=1, source_target_pairs={{0,1},{1,0},{2,3},{3,2},{4,5},{5,4},{6,7},{7,6},{8,9},{9,8},{10,11... | collective-permute-start | bytes 6684680 | tf_op jit(solution)/shard_map/ppermute | solution.py:1179
  498.2 48.2 %collective-permute-start.1 = (bf16[544,2048]{1,0:T(8,128)(2,1)S(1)}, bf16[544,2048]{1,0:T(8,128)(2,1)S(1)}, u32[]{:S(2)}, u32[]{:S(2)}) collective-permute-start(bf16[544,2048]{1,0:T(8,128)(2,1)S(1)} %copy-done.9), channel_id=1, source_target_pairs={{0,1},{1,0},{2,3},{3,2},{4,5},{5,4},{6,7},{7,6},{8,9},{9,8},{10,11... | collective-permute-start | bytes 6684680 | tf_op jit(solution)/shard_map/ppermute | solution.py:1179
  572.2 23.0 %collective-permute-start.2 = (bf16[128,3072]{1,0:T(8,128)(2,1)S(1)}, bf16[128,3072]{1,0:T(8,128)(2,1)S(1)}, u32[]{:S(2)}, u32[]{:S(2)}) collective-permute-start(bf16[128,3072]{1,0:T(8,128)(2,1)S(1)} %get-tuple-element.163), channel_id=1, source_target_pairs={{0,8},{4,12},{8,0},{12,4},{16,24},{20,28},{24,16},{28,20},{1,9},{5... | collective-permute-start | bytes 2359304 | tf_op jit(solution)/shard_map/ppermute | solution.py:1179
  575.5 19.7 %collective-permute-start.3 = (bf16[128,3072]{1,0:T(8,128)(2,1)S(1)}, bf16[128,3072]{1,0:T(8,128)(2,1)S(1)}, u32[]{:S(2)}, u32[]{:S(2)}) collective-permute-start(bf16[128,3072]{1,0:T(8,128)(2,1)S(1)} %get-tuple-element.164), channel_id=1, source_target_pairs={{0,16},{4,20},{8,24},{12,28},{16,0},{20,4},{24,8},{28,12},{1,17},{... | collective-permute-start | bytes 2359304 | tf_op jit(solution)/shard_map/ppermute | solution.py:1179
  596.8 74.3 %collective-permute-start.5 = (bf16[256,3072]{1,0:T(8,128)(2,1)S(1)}, bf16[256,3072]{1,0:T(8,128)(2,1)}, u32[]{:S(2)}, u32[]{:S(2)}) collective-permute-start(bf16[256,3072]{1,0:T(8,128)(2,1)S(1)} %pad_maximum_fusion.2), channel_id=1, source_target_pairs={{0,16},{4,20},{8,24},{12,28},{16,0},{20,4},{24,8},{28,12},{1,17},{... | collective-permute-start | bytes 4718600 | tf_op jit(solution)/shard_map/ppermute | solution.py:1179
  598.8 72.4 %collective-permute-start.4 = (bf16[256,3072]{1,0:T(8,128)(2,1)S(1)}, bf16[256,3072]{1,0:T(8,128)(2,1)S(1)}, u32[]{:S(2)}, u32[]{:S(2)}) collective-permute-start(bf16[256,3072]{1,0:T(8,128)(2,1)S(1)} %pad_maximum_fusion.1), channel_id=1, source_target_pairs={{0,8},{4,12},{8,0},{12,4},{16,24},{20,28},{24,16},{28,20},{1,9},{5... | collective-permute-start | bytes 4718600 | tf_op jit(solution)/shard_map/ppermute | solution.py:1179
  623.0 80.8 %collective-permute-start.6 = (bf16[544,2048]{1,0:T(8,128)(2,1)}, bf16[544,2048]{1,0:T(8,128)(2,1)S(1)}, u32[]{:S(2)}, u32[]{:S(2)}) collective-permute-start(bf16[544,2048]{1,0:T(8,128)(2,1)} %shard_map.287), channel_id=1, source_target_pairs={{0,1},{1,0},{2,3},{3,2},{4,5},{5,4},{6,7},{7,6},{8,9},{9,8},{10,11... | collective-permute-start | bytes 6684680 | tf_op jit(solution)/shard_map/ppermute | solution.py:1179
  665.8 38.0 %collective-permute-start.7 = (bf16[128,3072]{1,0:T(8,128)(2,1)S(1)}, bf16[128,3072]{1,0:T(8,128)(2,1)}, u32[]{:S(2)}, u32[]{:S(2)}) collective-permute-start(bf16[128,3072]{1,0:T(8,128)(2,1)S(1)} %get-tuple-element.183), channel_id=1, source_target_pairs={{0,8},{4,12},{8,0},{12,4},{16,24},{20,28},{24,16},{28,20},{1,9},{5... | collective-permute-start | bytes 2359304 | tf_op jit(solution)/shard_map/ppermute | solution.py:1179
  667.7 36.1 %collective-permute-start.8 = (bf16[128,3072]{1,0:T(8,128)(2,1)S(1)}, bf16[128,3072]{1,0:T(8,128)(2,1)}, u32[]{:S(2)}, u32[]{:S(2)}) collective-permute-start(bf16[128,3072]{1,0:T(8,128)(2,1)S(1)} %get-tuple-element.184), channel_id=1, source_target_pairs={{0,16},{4,20},{8,24},{12,28},{16,0},{20,4},{24,8},{28,12},{1,17},{... | collective-permute-start | bytes 2359304 | tf_op jit(solution)/shard_map/ppermute | solution.py:1179
  672.3 39.4 %slice-start = ((s8[4456448]{0:T(1024)(128)(4,1)}), s8[4194304]{0:T(1024)(128)(4,1)S(1)}, s32[]{:S(2)}) async-start(s8[4456448]{0:T(1024)(128)(4,1)} %bitcast.61), calls=%async_computation.4 | async-start | bytes 8388608
  676.9 51.2 %collective-permute-start.9 = (bf16[256,1536]{1,0:T(8,128)(2,1)}, bf16[256,1536]{1,0:T(8,128)(2,1)}, u32[]{:S(2)}, u32[]{:S(2)}) collective-permute-start(bf16[256,1536]{1,0:T(8,128)(2,1)} %slice.273), channel_id=1, source_target_pairs={{0,2},{1,3},{2,0},{3,1},{4,6},{5,7},{6,4},{7,5},{8,10},{9,11},{10,... | collective-permute-start | bytes 2359304 | tf_op jit(solution)/shard_map/ppermute | solution.py:1179
  678.8 32.9 %slice-start.1 = ((s8[4456448]{0:T(1024)(128)(4,1)}), s8[262144]{0:T(1024)(128)(4,1)S(1)}, s32[]{:S(2)}) async-start(s8[4456448]{0:T(1024)(128)(4,1)} %bitcast.61), calls=%async_computation.5 | async-start | bytes 524288
  708.3 65.9 %collective-permute-start.11 = (bf16[256,3072]{1,0:T(8,128)(2,1)}, bf16[256,3072]{1,0:T(8,128)(2,1)}, u32[]{:S(2)}, u32[]{:S(2)}) collective-permute-start(bf16[256,3072]{1,0:T(8,128)(2,1)} %pad_maximum_fusion.4), channel_id=1, source_target_pairs={{0,16},{4,20},{8,24},{12,28},{16,0},{20,4},{24,8},{28,12},{1,17},{... | collective-permute-start | bytes 4718600 | tf_op jit(solution)/shard_map/ppermute | solution.py:1179
  709.8 64.4 %collective-permute-start.10 = (bf16[256,3072]{1,0:T(8,128)(2,1)}, bf16[256,3072]{1,0:T(8,128)(2,1)}, u32[]{:S(2)}, u32[]{:S(2)}) collective-permute-start(bf16[256,3072]{1,0:T(8,128)(2,1)} %pad_maximum_fusion.3), channel_id=1, source_target_pairs={{0,8},{4,12},{8,0},{12,4},{16,24},{20,28},{24,16},{28,20},{1,9},{5... | collective-permute-start | bytes 4718600 | tf_op jit(solution)/shard_map/ppermute | solution.py:1179
  728.1 46.2 %copy-start.27 = (bf16[256,3072]{1,0:T(8,128)(2,1)S(1)}, bf16[256,3072]{1,0:T(8,128)(2,1)}, u32[]{:S(2)}) copy-start(bf16[256,3072]{1,0:T(8,128)(2,1)} %get-tuple-element.212) | copy-start | bytes 4718596
  772.3 54.1 %collective-permute-start.13 = (bf16[128,3072]{1,0:T(8,128)(2,1)S(1)}, bf16[128,3072]{1,0:T(8,128)(2,1)S(1)}, u32[]{:S(2)}, u32[]{:S(2)}) collective-permute-start(bf16[128,3072]{1,0:T(8,128)(2,1)S(1)} %get-tuple-element.208), channel_id=1, source_target_pairs={{0,8},{4,12},{8,0},{12,4},{16,24},{20,28},{24,16},{28,20},{1,9},{5... | collective-permute-start | bytes 2359304 | tf_op jit(solution)/shard_map/ppermute | solution.py:1179
  772.6 53.8 %collective-permute-start.14 = (bf16[128,3072]{1,0:T(8,128)(2,1)S(1)}, bf16[128,3072]{1,0:T(8,128)(2,1)S(1)}, u32[]{:S(2)}, u32[]{:S(2)}) collective-permute-start(bf16[128,3072]{1,0:T(8,128)(2,1)S(1)} %get-tuple-element.209), channel_id=1, source_target_pairs={{0,16},{4,20},{8,24},{12,28},{16,0},{20,4},{24,8},{28,12},{1,17},{... | collective-permute-start | bytes 2359304 | tf_op jit(solution)/shard_map/ppermute | solution.py:1179
  777.1 49.3 %collective-permute-start.12 = (bf16[256,1536]{1,0:T(8,128)(2,1)S(1)}, bf16[256,1536]{1,0:T(8,128)(2,1)}, u32[]{:S(2)}, u32[]{:S(2)}) collective-permute-start(bf16[256,1536]{1,0:T(8,128)(2,1)S(1)} %slice.272), channel_id=1, source_target_pairs={{0,2},{1,3},{2,0},{3,1},{4,6},{5,7},{6,4},{7,5},{8,10},{9,11},{10,... | collective-permute-start | bytes 2359304 | tf_op jit(solution)/shard_map/ppermute | solution.py:1179
  829.3 103.1 %all-to-all-start = ((bf16[4,544,1024]{2,1,0:T(8,128)(2,1)}), bf16[4,544,1024]{2,1,0:T(8,128)(2,1)}, u32[]{:S(2)}, u32[]{:S(2)}) async-start(bf16[4,544,1024]{2,1,0:T(8,128)(2,1)} %bitcast.63), calls=%async_computation | async-start | bytes 8912896 | tf_op jit(solution)/shard_map/all_to_all | solution.py:1209
  834.7 97.8 %copy-start.1 = (f32[544,128]{1,0:T(8,128)S(1)}, f32[544,128]{1,0:T(8,128)}, u32[]{:S(2)}) copy-start(f32[544,128]{1,0:T(8,128)} %copy-done) | copy-start | bytes 835588
  834.7 97.7 %copy-start.3 = (f32[544,128]{1,0:T(8,128)S(1)}, f32[544,128]{1,0:T(8,128)}, u32[]{:S(2)}) copy-start(f32[544,128]{1,0:T(8,128)} %copy-done.2) | copy-start | bytes 835588
  834.7 37.7 %collective-permute-start.22 = (bf16[256,3072]{1,0:T(8,128)(2,1)}, bf16[256,3072]{1,0:T(8,128)(2,1)}, u32[]{:S(2)}, u32[]{:S(2)}) collective-permute-start(bf16[256,3072]{1,0:T(8,128)(2,1)} %pad_maximum_fusion.6), channel_id=1, source_target_pairs={{0,16},{4,20},{8,24},{12,28},{16,0},{20,4},{24,8},{28,12},{1,17},{... | collective-permute-start | bytes 4718600 | tf_op jit(solution)/shard_map/ppermute | solution.py:1179
  835.1 37.6 %collective-permute-start.21 = (bf16[256,3072]{1,0:T(8,128)(2,1)}, bf16[256,3072]{1,0:T(8,128)(2,1)}, u32[]{:S(2)}, u32[]{:S(2)}) collective-permute-start(bf16[256,3072]{1,0:T(8,128)(2,1)} %pad_maximum_fusion.5), channel_id=1, source_target_pairs={{0,8},{4,12},{8,0},{12,4},{16,24},{20,28},{24,16},{28,20},{1,9},{5... | collective-permute-start | bytes 4718600 | tf_op jit(solution)/shard_map/ppermute | solution.py:1179
  849.7 92.8 %collective-permute-start.15 = (bf16[128,2048]{1,0:T(8,128)(2,1)S(1)}, bf16[128,2048]{1,0:T(8,128)(2,1)S(1)}, u32[]{:S(2)}, u32[]{:S(2)}) collective-permute-start(bf16[128,2048]{1,0:T(8,128)(2,1)S(1)} %get-tuple-element.225), channel_id=1, source_target_pairs={{0,8},{4,12},{8,0},{12,4},{16,24},{20,28},{24,16},{28,20},{1,9},{5... | collective-permute-start | bytes 1572872 | tf_op jit(solution)/shard_map/ppermute | solution.py:1179
  849.9 92.6 %collective-permute-start.16 = (bf16[128,2048]{1,0:T(8,128)(2,1)S(1)}, bf16[128,2048]{1,0:T(8,128)(2,1)}, u32[]{:S(2)}, u32[]{:S(2)}) collective-permute-start(bf16[128,2048]{1,0:T(8,128)(2,1)S(1)} %get-tuple-element.226), channel_id=1, source_target_pairs={{0,16},{4,20},{8,24},{12,28},{16,0},{20,4},{24,8},{28,12},{1,17},{... | collective-permute-start | bytes 1572872 | tf_op jit(solution)/shard_map/ppermute | solution.py:1179
  945.0 44.9 %collective-permute-start.20 = (bf16[256,2048]{1,0:T(8,128)(2,1)}, bf16[256,2048]{1,0:T(8,128)(2,1)}, u32[]{:S(2)}, u32[]{:S(2)}) collective-permute-start(bf16[256,2048]{1,0:T(8,128)(2,1)} %pad_maximum_fusion.8), channel_id=1, source_target_pairs={{0,16},{4,20},{8,24},{12,28},{16,0},{20,4},{24,8},{28,12},{1,17},{... | collective-permute-start | bytes 3145736 | tf_op jit(solution)/shard_map/ppermute | solution.py:1179
  945.6 44.3 %collective-permute-start.19 = (bf16[256,2048]{1,0:T(8,128)(2,1)S(1)}, bf16[256,2048]{1,0:T(8,128)(2,1)}, u32[]{:S(2)}, u32[]{:S(2)}) collective-permute-start(bf16[256,2048]{1,0:T(8,128)(2,1)S(1)} %pad_maximum_fusion.7), channel_id=1, source_target_pairs={{0,8},{4,12},{8,0},{12,4},{16,24},{20,28},{24,16},{28,20},{1,9},{5... | collective-permute-start | bytes 3145736 | tf_op jit(solution)/shard_map/ppermute | solution.py:1179
  952.6 35.2 %collective-permute-start.23 = (bf16[256,1536]{1,0:T(8,128)(2,1)}, bf16[256,1536]{1,0:T(8,128)(2,1)}, u32[]{:S(2)}, u32[]{:S(2)}) collective-permute-start(bf16[256,1536]{1,0:T(8,128)(2,1)} %slice.271), channel_id=1, source_target_pairs={{0,2},{1,3},{2,0},{3,1},{4,6},{5,7},{6,4},{7,5},{8,10},{9,11},{10,... | collective-permute-start | bytes 2359304 | tf_op jit(solution)/shard_map/ppermute | solution.py:1179
  965.7 24.2 %collective-permute-start.17 = (bf16[128,2048]{1,0:T(8,128)(2,1)S(1)}, bf16[128,2048]{1,0:T(8,128)(2,1)}, u32[]{:S(2)}, u32[]{:S(2)}) collective-permute-start(bf16[128,2048]{1,0:T(8,128)(2,1)S(1)} %get-tuple-element.236), channel_id=1, source_target_pairs={{0,8},{4,12},{8,0},{12,4},{16,24},{20,28},{24,16},{28,20},{1,9},{5... | collective-permute-start | bytes 1572872 | tf_op jit(solution)/shard_map/ppermute | solution.py:1179
  966.1 23.8 %collective-permute-start.18 = (bf16[128,2048]{1,0:T(8,128)(2,1)S(1)}, bf16[128,2048]{1,0:T(8,128)(2,1)}, u32[]{:S(2)}, u32[]{:S(2)}) collective-permute-start(bf16[128,2048]{1,0:T(8,128)(2,1)S(1)} %get-tuple-element.237), channel_id=1, source_target_pairs={{0,16},{4,20},{8,24},{12,28},{16,0},{20,4},{24,8},{28,12},{1,17},{... | collective-permute-start | bytes 1572872 | tf_op jit(solution)/shard_map/ppermute | solution.py:1179
  987.8 62.9 %collective-permute-start.24 = (bf16[544,2048]{1,0:T(8,128)(2,1)}, bf16[544,2048]{1,0:T(8,128)(2,1)}, u32[]{:S(2)}, u32[]{:S(2)}) collective-permute-start(bf16[544,2048]{1,0:T(8,128)(2,1)} %shard_map.284), channel_id=1, source_target_pairs={{0,1},{1,0},{2,3},{3,2},{4,5},{5,4},{6,7},{7,6},{8,9},{9,8},{10,11... | collective-permute-start | bytes 6684680 | tf_op jit(solution)/shard_map/ppermute | solution.py:1179
  994.3 61.8 %all-to-all-start.1 = ((bf16[4,256,512]{2,1,0:T(8,128)(2,1)}), bf16[4,256,512]{2,1,0:T(8,128)(2,1)S(1)}, u32[]{:S(2)}, u32[]{:S(2)}) async-start(bf16[4,256,512]{2,1,0:T(8,128)(2,1)} %bitcast.51), calls=%async_computation.1 | async-start | bytes 2097152 | tf_op jit(solution)/shard_map/all_to_all | solution.py:1209
  1000.5 50.2 %collective-permute-start.26 = (bf16[256,2048]{1,0:T(8,128)(2,1)}, bf16[256,2048]{1,0:T(8,128)(2,1)}, u32[]{:S(2)}, u32[]{:S(2)}) collective-permute-start(bf16[256,2048]{1,0:T(8,128)(2,1)} %pad_maximum_fusion.10), channel_id=1, source_target_pairs={{0,16},{4,20},{8,24},{12,28},{16,0},{20,4},{24,8},{28,12},{1,17},{... | collective-permute-start | bytes 3145736 | tf_op jit(solution)/shard_map/ppermute | solution.py:1179
  1004.2 46.5 %collective-permute-start.25 = (bf16[256,2048]{1,0:T(8,128)(2,1)}, bf16[256,2048]{1,0:T(8,128)(2,1)}, u32[]{:S(2)}, u32[]{:S(2)}) collective-permute-start(bf16[256,2048]{1,0:T(8,128)(2,1)} %pad_maximum_fusion.9), channel_id=1, source_target_pairs={{0,8},{4,12},{8,0},{12,4},{16,24},{20,28},{24,16},{28,20},{1,9},{5... | collective-permute-start | bytes 3145736 | tf_op jit(solution)/shard_map/ppermute | solution.py:1179
  1007.7 43.0 %collective-permute-start.27 = (bf16[128,2048]{1,0:T(8,128)(2,1)S(1)}, bf16[128,2048]{1,0:T(8,128)(2,1)}, u32[]{:S(2)}, u32[]{:S(2)}) collective-permute-start(bf16[128,2048]{1,0:T(8,128)(2,1)S(1)} %get-tuple-element.239), channel_id=1, source_target_pairs={{0,8},{4,12},{8,0},{12,4},{16,24},{20,28},{24,16},{28,20},{1,9},{5... | collective-permute-start | bytes 1572872 | tf_op jit(solution)/shard_map/ppermute | solution.py:1179
  1008.7 42.0 %collective-permute-start.28 = (bf16[128,2048]{1,0:T(8,128)(2,1)S(1)}, bf16[128,2048]{1,0:T(8,128)(2,1)}, u32[]{:S(2)}, u32[]{:S(2)}) collective-permute-start(bf16[128,2048]{1,0:T(8,128)(2,1)S(1)} %get-tuple-element.240), channel_id=1, source_target_pairs={{0,16},{4,20},{8,24},{12,28},{16,0},{20,4},{24,8},{28,12},{1,17},{... | collective-permute-start | bytes 1572872 | tf_op jit(solution)/shard_map/ppermute | solution.py:1179
  1058.4 34.1 %collective-permute-start.35 = (bf16[256,2048]{1,0:T(8,128)(2,1)}, bf16[256,2048]{1,0:T(8,128)(2,1)}, u32[]{:S(2)}, u32[]{:S(2)}) collective-permute-start(bf16[256,2048]{1,0:T(8,128)(2,1)} %pad_maximum_fusion.12), channel_id=1, source_target_pairs={{0,16},{4,20},{8,24},{12,28},{16,0},{20,4},{24,8},{28,12},{1,17},{... | collective-permute-start | bytes 3145736 | tf_op jit(solution)/shard_map/ppermute | solution.py:1179
  1062.4 30.1 %collective-permute-start.34 = (bf16[256,2048]{1,0:T(8,128)(2,1)}, bf16[256,2048]{1,0:T(8,128)(2,1)}, u32[]{:S(2)}, u32[]{:S(2)}) collective-permute-start(bf16[256,2048]{1,0:T(8,128)(2,1)} %pad_maximum_fusion.11), channel_id=1, source_target_pairs={{0,8},{4,12},{8,0},{12,4},{16,24},{20,28},{24,16},{28,20},{1,9},{5... | collective-permute-start | bytes 3145736 | tf_op jit(solution)/shard_map/ppermute | solution.py:1179
  1066.1 29.9 %all-to-all-start.2 = ((bf16[4,256,512]{2,1,0:T(8,128)(2,1)}), bf16[4,256,512]{2,1,0:T(8,128)(2,1)}, u32[]{:S(2)}, u32[]{:S(2)}) async-start(bf16[4,256,512]{2,1,0:T(8,128)(2,1)} %bitcast.65), calls=%async_computation.2 | async-start | bytes 2097152 | tf_op jit(solution)/shard_map/all_to_all | solution.py:1209
  1074.1 13.3 %collective-permute-start.29 = (f32[4,544]{1,0:T(4,128)S(1)}, f32[4,544]{1,0:T(4,128)S(1)}, u32[]{:S(2)}, u32[]{:S(2)}) collective-permute-start(f32[4,544]{1,0:T(4,128)S(1)} %slice.230), channel_id=1, source_target_pairs={{0,4},{4,0},{8,12},{12,8},{16,20},{20,16},{24,28},{28,24},{1,5},{5... | collective-permute-start | bytes 26120 | tf_op jit(solution)/shard_map/ppermute | solution.py:1179
  1087.4 3.7 collective-permute-start.30
  1091.1 10.0 collective-permute-start.31
  1096.0 37.3 %all-to-all-start.3 = ((bf16[4,256,512]{2,1,0:T(8,128)(2,1)}), bf16[4,256,512]{2,1,0:T(8,128)(2,1)}, u32[]{:S(2)}, u32[]{:S(2)}) async-start(bf16[4,256,512]{2,1,0:T(8,128)(2,1)} %bitcast.66), calls=%async_computation.3 | async-start | bytes 2097152 | tf_op jit(solution)/shard_map/all_to_all | solution.py:1209
  1101.1 16.8 %collective-permute-start.32 = (f32[1,544]{1,0:T(1,128)S(1)}, f32[1,544]{1,0:T(1,128)S(1)}, u32[]{:S(2)}, u32[]{:S(2)}) collective-permute-start(f32[1,544]{1,0:T(1,128)S(1)} %slice_add_fusion.5), channel_id=1, source_target_pairs={{0,1},{1,0},{2,3},{3,2},{4,5},{5,4},{6,7},{7,6},{8,9},{9,8},{10,11... | collective-permute-start | bytes 6536 | tf_op jit(solution)/shard_map/ppermute | solution.py:1179
  1117.9 12.1 %collective-permute-start.33 = (f32[1,544]{1,0:T(1,128)S(1)}, f32[1,544]{1,0:T(1,128)S(1)}, u32[]{:S(2)}, u32[]{:S(2)}) collective-permute-start(f32[1,544]{1,0:T(1,128)S(1)} %add.222), channel_id=1, source_target_pairs={{0,2},{1,3},{2,0},{3,1},{4,6},{5,7},{6,4},{7,5},{8,10},{9,11},{10,... | collective-permute-start | bytes 6536 | tf_op jit(solution)/shard_map/ppermute | solution.py:1179
  (46 other events, 344.5 us)

commit v4 on v3

--- a/solution.py
+++ b/solution.py
@@ -162,48 +162,6 @@
 
 def head_slices(width):
     return [slice(h * HEAD_DIM, (h + 1) * HEAD_DIM) for h in range(width // HEAD_DIM)]
-
-
-def project_qkv(normed, tiles, seats, cosine, sine, q_gain, k_gain):
-    rows, tw = normed.shape[0], tiles.width
-
-    def body(step, weights, ins, outs, own):
-        a, cos_ref, sin_ref, qg, kg = ins
-        hat, raw = outs
-        acc = dot_nn(a[...], weights[0][...])
-        part = lax.rem(step, 2)
-
-        def turned(x, gain):
-            inverse = lax.rsqrt(jnp.mean(x * x, axis=-1, keepdims=True) + norm_eps)
-            u = x * inverse * gain
-            return u * cos_ref[...] + pltpu.roll(u, HEAD_DIM // 2, 1) * sin_ref[...]
-
-        @pl.when(part == 0)
-        def _():
-            for cut in head_slices(tw):
-                hat[:, cut] = turned(acc[:, cut], qg[...]).astype(bf16)
-            raw[...] = acc.astype(bf16)
-
-        @pl.when(part == 1)
-        def _():
-            for cut in head_slices(tw // 2):
-                hat[:, cut] = (turned(acc[:, cut], kg[...]) * key_scale).astype(bf16)
-            hat[:, tw // 2 :] = acc[:, tw // 2 :].astype(bf16)
-            raw[...] = acc.astype(bf16)
-
-    ins = [normed, cosine, sine, q_gain, k_gain]
-    shape = jax.ShapeDtypeStruct((tiles.quarters, rows, 2 * tw), bf16)
-    return tiled_call(
-        body,
-        [tiles],
-        seats,
-        ins,
-        [whole(x) for x in ins],
-        [shape, shape],
-        [seated(rows, tw, 2)] * 2,
-        [],
-        4 * rows * normed.shape[1] * tw * tiles.quarters,
-    )
 
 
 def project_rows(a, tiles, seats):
@@ -796,11 +754,11 @@
             for k in range(steps):
                 copy(k).wait_send()
             if rides:
-                sends, (load, keep) = ride_copies()
+                sends, own_row = ride_copies()
                 for c in sends:
                     c.wait_send()
                     c.wait_recv()
-                keep.wait()
+                own_row[1].wait()
 
     columns = quarters * width
     heights = (block, block, block, half, half)
@@ -850,6 +808,21 @@
     return (result[:5], result[5]) if rides else (result, None)
 
 
+def waves_start(mover, n, source, target):
+    if n != 4:
+        return [mover.start(source, target(e), "tp", e) for e in range(1, n)]
+    far = mover.start(source, target(2), "tp", 2)
+    near = mover.start(source, target(1), "tp", 1)
+    return [near, far]
+
+
+def waves_forward(mover, n, waves, target):
+    if n != 4:
+        return waves
+    waves[1].wait_recv()
+    return waves + [mover.start(target(2), target(3), "tp", 1)]
+
+
 def struct(*shape):
     return jax.ShapeDtypeStruct(shape, bf16)
 
@@ -897,61 +870,179 @@
             copy.wait_recv()
 
 
-def gather_front(m, n, qkv_block, in_block, down_block, gain_block):
+def exclusive_or(a, b, count):
+    total, bit = 0, 1
+    while bit < count:
+        total = total + bit * lax.rem(lax.div(a, bit) + lax.div(b, bit), 2)
+        bit *= 2
+    return total
+
+
+def gather_front(
+    m, n, order, qkv_block, in_block, down_block, gain_block, tokens, out_grad, cosine, sine
+):
     block, qw = qkv_block.shape
     fw, dw = in_block.shape[1], down_block.shape[1]
     depth = block * m
     pairs = n // 2
-
-    def program(mover, ins, outs, _):
-        qkv, inner, down, gain = ins
-        weights, in_own, in_rest, down_rest, gains = outs
+    rows_in = tokens.shape[0]
+    tw = qw // 2
+    gain_width = gain_block.shape[1]
+    chunks = 2 if rows_in % 32 == 0 else 1
+    chunk = rows_in // chunks
+
+    def program(mover, ins, outs, scratch):
+        qkv, inner, down, gain, x_ref, dy_ref, cos_ref, sin_ref = ins
+        (
+            weights, in_own, in_rest, down_rest, gains,
+            x_out, dy_out, normed_out, hats, raws,
+        ) = outs
+        gain_s, normed_s, tile_s, hat_s, raw_s, tile_sems, hat_sems, raw_sems = scratch
+        where, seat = lax.axis_index("wide"), lax.axis_index("tp")
         rows = pl.ds(0, block)
-        waves = [mover.start(qkv, weights.at[e, rows], "tp", e) for e in range(1, n)]
+        place = lambda e: weights.at[e, rows]
+        waves = waves_start(mover, n, qkv, place)
+        spread_gains = Spread(mover, m, gain, lambda r: gains.at[r], GAIN_ROWS)
+        spread_gains.first()
+        spreads = [
+            Spread(mover, m, qkv if q == 0 else place(q), lambda r, q=q: weights.at[q, r], block)
+            for q in range(n)
+        ]
+        spreads[0].first()
         kept = [
             mover.keep(qkv, weights.at[0, rows]),
             mover.keep(inner, in_own.at[0, rows]),
-            mover.keep(gain, gains.at[pl.ds(0, GAIN_ROWS)]),
         ]
-        spread_gains = Spread(mover, m, gain, lambda r: gains.at[r], GAIN_ROWS)
-        spread_gains.first()
-        spreads = [
-            Spread(
-                mover,
-                m,
-                qkv if q == 0 else weights.at[q, rows],
-                lambda r, q=q: weights.at[q, r],
-                block,
-            )
-            for q in range(n)
-        ]
-        spreads[0].first()
+        kept_gain = mover.keep(gain, gains.at[pl.ds(0, GAIN_ROWS)])
         spread_gains.second()
         spreads[0].second()
         spread_gains.third()
         spreads[0].third()
-        for q in range(1, n):
-            waves[q - 1].wait_recv()
-            spreads[q].first()
+        columns = [
+            pl.ds(pl.multiple_of(flipped(where, k) * block, 128), block) for k in order
+        ]
+        for k in range(m):
+            cut = pl.ds(k * block, block)
+            kept.append(mover.keep(x_ref.at[:, columns[k]], x_out.at[:, cut]))
+            kept.append(mover.keep(dy_ref.at[:, columns[k]], dy_out.at[:, cut]))
+        if n == 4:
+            waves = waves_forward(mover, n, waves, place)
+            spreads[2].first()
+            waves[0].wait_recv()
+            spreads[1].first()
+            waves[2].wait_recv()
+            spreads[3].first()
+        else:
+            for q in range(1, n):
+                waves[q - 1].wait_recv()
+                spreads[q].first()
         late = []
         for e in range(1, pairs):
             late.append(mover.start(inner, in_rest.at[e - 1, rows], "tp", 2 * e))
             late.append(mover.start(down, down_rest.at[e - 1, rows], "tp", 2 * e))
-        for q in range(1, n):
+
+        spread_gains.last()
+        kept_gain.wait()
+        load = mover.keep(gains, gain_s)
+        load.wait()
+
+        def normalise(i, carry):
+            part = pl.ds(pl.multiple_of(i * chunk, 16), chunk)
+            x = x_ref[part, :].astype(f32)
+            inverse = lax.rsqrt(jnp.mean(x * x, axis=-1, keepdims=True) + norm_eps)
+            for k in range(m):
+                piece = x_ref[part, columns[k]].astype(f32) * inverse
+                scale = gain_s[k * GAIN_ROWS : k * GAIN_ROWS + 1, :block]
+                normed_s[part, k * block : (k + 1) * block] = (piece * scale).astype(bf16)
+            return carry
+
+        lax.fori_loop(0, chunks, normalise, 0)
+        kept.append(mover.keep(normed_s, normed_out))
+        heads_at = 2 * block
+
+        def head_gain(at):
+            total = gain_s[0:1, at : at + HEAD_DIM]
+            for k in range(1, m):
+                total = total + gain_s[k * GAIN_ROWS : k * GAIN_ROWS + 1, at : at + HEAD_DIM]
+            return total
+
+        gain_q, gain_k = head_gain(heads_at), head_gain(heads_at + HEAD_DIM)
+
+        turn = (2, 1, 3) if n == 4 else range(1, n)
+        for q in turn:
             spreads[q].second()
         own = Spread(mover, m, inner, lambda r: in_own.at[0, r], block)
         own.first()
-        for q in range(1, n):
+        for q in turn:
             spreads[q].third()
-        own.second()
-        own.third()
         for spread in spreads:
             spread.last()
+        kept[0].wait()
+
+        def fetch(q, part):
+            return pltpu.make_async_copy(
+                weights.at[q, :, pl.ds(part * tw, tw)], tile_s.at[part], tile_sems.at[part]
+            )
+
+        def leave(q, part):
+            home = exclusive_or(seat, q, n)
+            cut = pl.ds(part * tw, tw)
+            return (
+                pltpu.make_async_copy(
+                    hat_s.at[part], hats.at[home, :, cut], hat_sems.at[part]
+                ),
+                pltpu.make_async_copy(
+                    raw_s.at[part], raws.at[home, :, cut], raw_sems.at[part]
+                ),
+            )
+
+        def turned(x, gain):
+            inverse = lax.rsqrt(jnp.mean(x * x, axis=-1, keepdims=True) + norm_eps)
+            u = x * inverse * gain
+            return u * cos_ref[...] + pltpu.roll(u, HEAD_DIM // 2, 1) * sin_ref[...]
+
+        def quarter(q, carry):
+            for part in range(2):
+                if part == 0:
+                    fetch(q, 1).start()
+                else:
+
+                    @pl.when(q + 1 < n)
+                    def _():
+                        fetch(q + 1, 0).start()
+
+                fetch(q, part).wait()
+
+                @pl.when(q > 0)
+                def _(part=part):
+                    for c in leave(q, part):
+                        c.wait()
+
+                acc = dot_nn(normed_s[...], tile_s[part])
+                raw_s[part] = acc.astype(bf16)
+                if part == 0:
+                    for cut in head_slices(tw):
+                        hat_s[0, :, cut] = turned(acc[:, cut], gain_q).astype(bf16)
+                else:
+                    for cut in head_slices(tw // 2):
+                        hat_s[1, :, cut] = (turned(acc[:, cut], gain_k) * key_scale).astype(bf16)
+                    hat_s[1, :, tw // 2 :] = acc[:, tw // 2 :].astype(bf16)
+                for c in leave(q, part):
+                    c.start()
+            return carry
+
+        fetch(0, 0).start()
+        lax.fori_loop(0, n // 2, quarter, 0)
+        own.second()
+        lax.fori_loop(n // 2, n, quarter, 0)
+        own.third()
+        for part in range(2):
+            for c in leave(n - 1, part):
+                c.wait()
         own.last()
-        spread_gains.last()
         for copy in late:
             copy.wait_recv()
-        for copy in kept:
+        for copy in kept[1:]:
             copy.wait()
 
     per = 8 if m == 8 else m - 1
@@ -959,19 +1050,33 @@
         program,
         m,
         n,
-        [qkv_block, in_block, down_block, gain_block],
+        [qkv_block, in_block, down_block, gain_block, tokens, out_grad, cosine, sine],
         [
             struct(n, depth, qw),
             struct(1, depth, fw),
             struct(pairs - 1, depth, fw),
             struct(pairs - 1, depth, dw),
-            jax.ShapeDtypeStruct((m * GAIN_ROWS, gain_block.shape[1]), f32),
+            jax.ShapeDtypeStruct((m * GAIN_ROWS, gain_width), f32),
+            struct(rows_in, depth),
+            struct(rows_in, depth),
+            struct(rows_in, depth),
+            struct(n, rows_in, qw),
+            struct(n, rows_in, qw),
         ],
-        [],
+        [
+            pltpu.VMEM((m * GAIN_ROWS, gain_width), f32),
+            pltpu.VMEM((rows_in, depth), bf16),
+            pltpu.VMEM((2, depth, tw), bf16),
+            pltpu.VMEM((2, rows_in, tw), bf16),
+            pltpu.VMEM((2, rows_in, tw), bf16),
+            pltpu.SemaphoreType.DMA((2,)),
+            pltpu.SemaphoreType.DMA((2,)),
+            pltpu.SemaphoreType.DMA((2,)),
+        ],
         (n - 1) + per * (n + 2) + 2 * (pairs - 1),
-        3,
+        5 + 2 * m,
         1,
-        vmem_ins=(0, 1, 2, 3),
+        vmem_ins=tuple(range(8)),
     )
 
 
@@ -996,14 +1101,16 @@
         heads, rest, weights, down_own = outs
         first = pl.ds(0, block)
         kept = [mover.keep(out, weights.at[0, first]), mover.keep(down, down_own.at[0, first])]
-        waves = [mover.start(out, weights.at[e, first], "tp", e) for e in range(1, n)]
+        place = lambda e: weights.at[e, first]
+        waves = waves_start(mover, n, out, place)
         spreads = [
             Spread(mover, m, rest.at[p, first], lambda r, p=p: rest.at[p, r], block)
             for p in range(pairs)
         ]
         for spread in spreads:
             spread.first()
-        for copy in waves:
+        waves = waves_forward(mover, n, waves, place)
+        for copy in waves if n != 4 else (waves[0], waves[2]):
             copy.wait_recv()
         sends, own_row = swap_heads(mover, n, scratch[0], hat, heads)
         kept[0].wait()
@@ -1197,8 +1304,6 @@
         from_x, from_y = yield [for_x, for_y], [over("wide", for_x, 2), over("wide", for_y, 4)]
         return own.astype(f32) + from_x.astype(f32) + from_y.astype(f32)
 
-    cotangent = shuffle_columns(out_grad, relative)
-
     def ffn_share(left, rights, number, ride=None, rode=None):
         total = yield from scatter(left, rights, None, number, ride, rode)
         parts = [total[:, e * fcols : (e + 1) * fcols].astype(bf16) for e in range(1, n // 2)]
@@ -1223,20 +1328,14 @@
     fcols = w_gate.shape[1]
     fw = fcols // 3
 
-    gain_row = jnp.concatenate([attn_gain, ffn_gain, q_gain, k_gain]).astype(f32)[None]
-    gain_width = -(-gain_row.shape[1] // 128) * 128
-    gain_block = jnp.pad(gain_row, ((0, GAIN_ROWS - 1), (0, gain_width - gain_row.shape[1])))
-    qkv_all, in_own, in_rest, down_rest, gains = gather_front(
-        m, n, qkv_block, in_block, down_block, gain_block
-    )
-    gains = gains[::GAIN_ROWS]
     small = q_gain.shape[0]
-    gain_one = gains[:, :block].reshape(1, depth)
-    gain_two = gains[:, block : 2 * block].reshape(1, depth)
-    head_gains = jnp.take(gains[:, 2 * block :], absolute, axis=0)
-    gain_q = head_gains[:, :small].reshape(1, HEAD_DIM)
-    gain_k = head_gains[:, small : 2 * small].reshape(1, HEAD_DIM)
-
+    head_row = lambda g: lax.dynamic_update_slice(
+        jnp.zeros((HEAD_DIM,), f32), g.astype(f32), (where * small,)
+    )
+    gain_row = jnp.concatenate(
+        [attn_gain.astype(f32), ffn_gain.astype(f32), head_row(q_gain), head_row(k_gain)]
+    )[None]
+    gain_block = jnp.pad(gain_row, ((0, GAIN_ROWS - 1), (0, 0)))
     base = where * parent_table.shape[0]
     block_segs = seg_ids[TRUNK::BRANCH] - base
     hit = block_segs[:, None] == jnp.arange(parent_table.shape[0], dtype=jnp.int32)[None, :]
@@ -1254,18 +1353,23 @@
     cosine = jnp.concatenate([cosine, cosine], axis=-1)
     sine = jnp.concatenate([-sine, sine], axis=-1)
 
-    stream = shuffle_columns(tokens, relative).astype(f32)
-    inverse_one = inverse_rms(stream)
-    unit_one = stream * inverse_one
-    normed_one = (unit_one * gain_one).astype(bf16)
-
+    (
+        qkv_all, in_own, in_rest, down_rest, gains, stream_low, cotangent, normed_one, hats, raws,
+    ) = gather_front(
+        m, n, order, qkv_block, in_block, down_block, gain_block, tokens, out_grad, cosine, sine
+    )
+    gains = gains[::GAIN_ROWS]
+    gain_one = gains[:, :block].reshape(1, depth)
+    gain_two = gains[:, block : 2 * block].reshape(1, depth)
+    gain_q = jnp.sum(gains[:, 2 * block : 2 * block + HEAD_DIM], axis=0, keepdims=True)
+    gain_k = jnp.sum(gains[:, 2 * block + HEAD_DIM :], axis=0, keepdims=True)
     qkv_tiles = Tiles([qkv_all], 2, 0, aw)
-    hats, raws = project_qkv(normed_one, qkv_tiles, seats, cosine, sine, gain_q, gain_k)
     qkv, in_rest, out_all, down_own = gather_middle(m, n, hats, in_rest, out_block, down_block)
     qkv = qkv.reshape(n * rows, -1)
     attended_heads, logs = attention_forward(qkv, parents, kv)
     attended, down_rest = gather_late(m, n, attended_heads.reshape(n, rows, -1), down_rest)
     out_tiles = Tiles([out_all], 1, 0, aw)
+    stream = stream_low.astype(f32)
     after_attn = stream + project_columns([attended], [out_tiles], seats, depth, f32)
 
     inverse_two = inverse_rms(after_attn)
@@ -1283,18 +1387,21 @@
     cotangent_next = over("tp", cotangent_sent, 1)
     hidden_next, gate_next, up_next = feed_forward(normed_two_next, gate_tiles, up_tiles, plain)
     down_part = project_columns([hidden_next], [down_tiles], plain, depth, bf16)
-    cotangent_next, hidden_late = after((cotangent_next, hidden), down_part)
+    own_grad = after(cotangent, down_part)
+    gate_grad, up_grad = feed_back(own_grad, gate, up, down_tiles, plain)
+    cotangent_next, hidden_late = after((cotangent_next, hidden), gate_grad)
     down_job = Job(ffn_share([cotangent, cotangent_next], [hidden_late, hidden_next], 4))
-    cotangent_next = after(cotangent_next, down_job.started)
+    cotangent_next, down_sent = after((cotangent_next, down_part), down_job.started)
+    down_next = over("tp", down_sent, 1)
     gate_grad_next, up_grad_next = feed_back(
         cotangent_next, gate_next, up_next, down_tiles, plain
     )
     gate_late, up_late = tick((gate_grad_next, up_grad_next), down_job)
     gate_late, up_late = after((gate_late, up_late), down_job.started)
     back_part = project_columns([gate_late, up_late], [gate_tiles, up_tiles], plain, depth, bf16)
+    back_part, down_next = after((back_part, down_next), back_part)
     back_next = over("tp", back_part, 1)
-    own_grad = after(cotangent, back_part)
-    gate_grad, up_grad = feed_back(own_grad, gate, up, down_tiles, plain)
+    gate_grad, up_grad = after((gate_grad, up_grad), back_part)
     gate_job = Job(ffn_share([normed_two, normed_two_next], [gate_grad, gate_grad_next], 5))
     gate_late, up_late = after((gate_grad, up_grad), gate_job.started)
     gate_late, up_late = tick((gate_late, up_late), down_job)
@@ -1323,24 +1430,25 @@
     back_hats = tick(back_hats, gate_job, up_job)
     back_hats = after(back_hats, up_job.started)
     back_hats_own = swap(back_hats.reshape(n, rows, -1))
-    grad_low, down_sent, after_attn = after((grad_low, down_part, after_attn), back_hats)
+    grad_low, down_next, after_attn = after((grad_low, down_next, after_attn), back_hats)
     out_job = Job(attn_share(grad_low, attended, None, 7))
     fence = tick(after(grad_low, out_job.started), up_job)
     back_hats_own = after(back_hats_own, fence, out_job.started)
     raw_grads, q_sum, k_sum = qkv_back(back_hats_own, raws, cosine, sine, gain_q, gain_k)
     raw_grads = tick(raw_grads, out_job)
-    down_next = over("tp", after(down_sent, raw_grads), 1)
     q_job = Job(attn_share(normed_one, after(raw_grads, out_job.started), 0, 8))
     raw_late = after(raw_grads, q_job.started)
     k_job = Job(attn_share(normed_one, raw_late, 1, 9))
     raw_late = tick(after(raw_late, k_job.started), q_job, out_job, up_job)
-    raw_late = after(raw_late, q_job.started, out_job.started, up_job.started)
+    raw_late = after(raw_late, q_job.started)
     normed_one_grad = project_columns([raw_late], [qkv_tiles], seats, depth, f32)
-    normed_one_grad, down_next = after((normed_one_grad, down_next), normed_one_grad)
     normed_one_grad = tick(normed_one_grad, q_job, k_job, up_job, out_job)
     normed_one_grad = after(normed_one_grad, q_job.started, k_job.started)
     mixed = (after_attn + down + down_next.astype(f32)).astype(bf16)
     mixed = shuffle_columns(mixed, absolute)
+    stream = after(stream_low, normed_one_grad).astype(f32)
+    inverse_one = inverse_rms(stream)
+    unit_one = stream * inverse_one
     attn_gain_part = jnp.sum(normed_one_grad * unit_one, axis=0)
     tokens_grad = (
         stream_grad + norm_back(normed_one_grad, unit_one, inverse_one, gain_one)

time: 1150 us -> 1050 us (0.913)
  Pallas kernels: 801 us -> 722 us
    pallas_call x3, Pallas kernels: 353 us -> 308 us  [transfer_call(): pl.pallas_call(kernel, in_specs=[pl.BlockSpec(memory_space=pltpu.VMEM if...]
    pallas_call x12 -> x11, Pallas kernels: 223 us -> 201 us  [tiled_call(): pl.pallas_call(kernel, grid_spec=pltpu.PrefetchScalarGridSpec(num_scalar_...]
    pallas_call x4 -> x2, Pallas kernels: 25.7 us -> 12.8 us  [shuffle_columns(): pl.pallas_call(kernel, grid_spec=pltpu.PrefetchScalarGridSpec(num_scalar_...]
  transfers between devices with their start and end apart: 40 -> 40, of which waited for: 9 -> 9; matrix products, arithmetic and copies ran while one was open for 7% -> 8% of each run, Pallas kernels for 32% -> 34%
where the time goes in v4:
time: 1050 us; the launch traced here: 1040 us
  Pallas kernels  722 us (69%)
  waiting for transfers between devices  112 us (11%)
  other arithmetic  89.4 us (9%)
  starting transfers between devices  80.1 us (8%)
  local copies, waits for them, and re-layouts  33.7 us (3%)
    pallas_call x3, Pallas kernels, transfer_call(): pl.pallas_call(kernel, in_specs=[pl.BlockSpec(memory_space=pltpu.VMEM if...  308 us
    pallas_call x11, Pallas kernels, tiled_call(): pl.pallas_call(kernel, grid_spec=pltpu.PrefetchScalarGridSpec(num_scalar_...  201 us
    pallas_call x6, Pallas kernels, gradient_pair(): pl.pallas_call(kernel, grid=(2 * steps,), in_specs=[pl.BlockSpec((rows, s...  133 us
    all_to_all x4, waiting for transfers between devices, swap(): return lax.all_to_all(a, 'tp', split_axis=0, concat_axis=0, tiled=True)  64.9 us
    ppermute x36, starting transfers between devices, over(): return lax.ppermute(a, axis, [(i, i ^ mask) for i in range(size)])  61.2 us
    ppermute x36, waiting for transfers between devices, over(): return lax.ppermute(a, axis, [(i, i ^ mask) for i in range(size)])  47.3 us
    pallas_call x1, Pallas kernels, attention_backward(): pl.pallas_call(kernel, grid_spec=pltpu.PrefetchScalarGridSpec(num_scalar_...  37.3 us
  transfers between devices with their start and end apart: 40, of which 9 were waited for; matrix products, arithmetic and copies ran while one was open for 8% of the time, Pallas kernels for 34%

profile of v4, /device:TPU:0, one launch (start us, length us, event | category | flops | bytes accessed | tf_op | source)
XLA Modules:
  0.0 1040.0 jit_solution(8867452400710153167)
XLA Ops:
  12.6 148.0 %shard_map.273 = (bf16[4,2048,1024]{2,1,0:T(8,128)(2,1)}, bf16[1,2048,3072]{2,1,0:T(8,128)(2,1)}, bf16[1,2048,3072]{2,1,0:T(8,128)(2,1)}, bf16[1,2048,1536]{2,1,...) custom-call(bf16[256,1024]{1,0:T(8,128)(2,1)S(1)} %pad_maximum_fusio, ...), custom_call_target="tpu_custom_call" | custom-call | bytes 10000 | tf_op jit(solution)/shard_map/pallas_call | solution.py:623
  160.6 119.0 %shard_map.274 = (bf16[4,544,1024]{2,1,0:T(8,128)(2,1)}, bf16[1,2048,3072]{2,1,0:T(8,128)(2,1)}, bf16[4,2048,512]{2,1,0:T(8,128)(2,1)}, bf16[1,2048,1536]{2,1,0:T(8,128)(2,1)}) custom-call(bf16[4,544,1024]{2,1,0:T(8,128)(2,1)} %get-tuple-element.152.refs_0_, bf16[1,2048,3072]{2,1,0:T(8,128)(2,1)} %get-tuple-element.153.refs_1_, ...), custom_call_target="tpu_custom_call", output_to_operand_aliasing={{1}: (1, {})} | custom-call | bytes 10000 | tf_op jit(solution)/shard_map/pallas_call | solution.py:623
  279.6 20.6 %shard_map.275 = (bf16[2176,512]{1,0:T(8,128)(2,1)}, f32[2,17,256]{2,1,0:T(8,128)S(1)}) custom-call(s32[8]{0:T(128)S(1)} %fusion.14.parent_ref, bf16[2176,1024]{1,0:T(8,128)(2,1)} %bitcast.51, bf16[2176,1024]{1,0:T(8,128)(2,1)} %bitcast.52, bf16[2176,1024]{1,0:T(8,128)(2,1)} %bitcast.53), custom_call_target="tpu_custom_call" | custom-call | flops 90112000 | bytes 67194 | tf_op jit(solution)/shard_map/pallas_call | solution.py:398
  300.2 41.3 %shard_map.276 = (bf16[4,544,512]{2,1,0:T(8,128)(2,1)}, bf16[1,2048,1536]{2,1,0:T(8,128)(2,1)}) custom-call(bf16[4,544,512]{2,1,0:T(8,128)(2,1)} %bitcast.60, bf16[1,2048,1536]{2,1,0:T(8,128)(2,1)} %get-tuple-element.157.refs_1_), custom_call_target="tpu_custom_call", output_to_operand_aliasing={{1}: (1, {})} | custom-call | bytes 10000 | tf_op jit(solution)/shard_map/pallas_call | solution.py:623
  341.5 13.0 %shard_map.277 = f32[544,2048]{1,0:T(8,128)} custom-call(s32[4]{0:T(128)S(1)} %iota_xor_fusion.seat_ref, bf16[4,2048,512]{2,1,0:T(8,128)(2,1)} %get-tuple-element.154.refs_0_, bf16[4,544,512]{2,1,0:T(8,128)(2,1)} %get-tuple-element.158.refs_1_), custom_call_target="tpu_custom_call" | custom-call | flops 45634028 | bytes 150732 | tf_op jit(solution)/shard_map/pallas_call | solution.py:137
  354.5 5.1 multiply_reduce_fusion.2
  359.7 2.7 multiply_convert_fusion.refs_4_.refs_0_
  362.4 11.6 %collective-permute-start = (bf16[544,2048]{1,0:T(8,128)(2,1)S(1)}, bf16[544,2048]{1,0:T(8,128)(2,1)S(1)}, u32[]{:S(2)}, u32[]{:S(2)}) collective-permute-start(bf16[544,2048]{1,0:T(8,128)(2,1)S(1)} %multiply_convert_fusion.refs_4_.refs_0_), channel_id=1, source_target_pairs={{0,1},{1,0},{2,3},{3,2},{4,5},{5,4},{6,7},{7,6},{8,9},{9,8},{10,11... | collective-permute-start | bytes 6684680 | tf_op jit(solution)/shard_map/ppermute | solution.py:1286
  374.0 21.3 %shard_map.278 = (bf16[2,544,1536]{2,1,0:T(8,128)(2,1)}, bf16[2,544,1536]{2,1,0:T(8,128)(2,1)}, bf16[2,544,1536]{2,1,0:T(8,128)(2,1)}) custom-call(s32[4]{0:T(128)S(1)} %iota.52.seat_ref, bf16[1,2048,3072]{2,1,0:T(8,128)(2,1)} %get-tuple-element.159.refs_0_.refs_2_, bf16[1,2048,3072]{2,1,0:T(8,128)(2,1)} %get-tuple-element.160.refs_1_.refs_3_, ...), custom_call_target="tpu_custom_call" | custom-call | flops 136902080 | bytes 625868 | tf_op jit(solution)/shard_map/pallas_call | solution.py:137
  395.4 16.5 %shard_map.279 = f32[544,2048]{1,0:T(8,128)} custom-call(s32[4]{0:T(128)S(1)} %iota.51.seat_ref, bf16[1,2048,1536]{2,1,0:T(8,128)(2,1)} %get-tuple-element.161.refs_0_, bf16[1,2048,1536]{2,1,0:T(8,128)(2,1)} %get-tuple-element.162.refs_1_, bf16[2,544,1536]{2,1,0:T(8,128)(2,1)} %get-tuple-element.174.refs_2_), custom_call_target="tpu_custom_call" | custom-call | flops 68451040 | bytes 203816 | tf_op jit(solution)/shard_map/pallas_call | solution.py:137
  411.9 10.4 %collective-permute-done.refs_4_.refs_1_ = bf16[544,2048]{1,0:T(8,128)(2,1)S(1)} collective-permute-done((bf16[544,2048]{1,0:T(8,128)(2,1)S(1)}, bf16[544,2048]{1,0:T(8,128)(2,1)S(1)}, u32[]{:S(2)}, u32[]{:S(2)}) %collective-permute-start) | collective-permute-done | bytes 2228256 | tf_op jit(solution)/shard_map/ppermute | solution.py:1286
  424.0 21.3 %shard_map.280 = (bf16[2,544,1536]{2,1,0:T(8,128)(2,1)}, bf16[2,544,1536]{2,1,0:T(8,128)(2,1)}, bf16[2,544,1536]{2,1,0:T(8,128)(2,1)}) custom-call(s32[4]{0:T(128)S(1)} %iota.50.seat_ref, bf16[1,2048,3072]{2,1,0:T(8,128)(2,1)} %get-tuple-element.159.refs_0_.refs_2_, bf16[1,2048,3072]{2,1,0:T(8,128)(2,1)} %get-tuple-element.160.refs_1_.refs_3_, ...), custom_call_target="tpu_custom_call" | custom-call | flops 136902080 | bytes 625868 | tf_op jit(solution)/shard_map/pallas_call | solution.py:137
  445.3 15.6 %shard_map.281 = bf16[544,2048]{1,0:T(8,128)(2,1)} custom-call(s32[4]{0:T(128)S(1)} %iota.49.seat_ref, bf16[1,2048,1536]{2,1,0:T(8,128)(2,1)} %get-tuple-element.161.refs_0_, bf16[1,2048,1536]{2,1,0:T(8,128)(2,1)} %get-tuple-element.162.refs_1_, bf16[2,544,1536]{2,1,0:T(8,128)(2,1)} %get-tuple-element.166.refs_2_.refs_3_), custom_call_target="tpu_custom_call" | custom-call | flops 68451040 | bytes 181534 | tf_op jit(solution)/shard_map/pallas_call | solution.py:137
  460.9 16.8 %shard_map.282 = (bf16[2,544,1536]{2,1,0:T(8,128)(2,1)}, bf16[2,544,1536]{2,1,0:T(8,128)(2,1)}) custom-call(s32[4]{0:T(128)S(1)} %iota.48.seat_ref, bf16[1,2048,1536]{2,1,0:T(8,128)(2,1)} %get-tuple-element.161.refs_0_, bf16[1,2048,1536]{2,1,0:T(8,128)(2,1)} %get-tuple-element.162.refs_1_, bf16[544,2048]{1,0:T(8,128)(2,1)} %get-tuple-element.172.refs_2_.refs_0_, ...), custom_call_target="tpu_custom_call" | custom-call | flops 68451040 | bytes 281804 | tf_op jit(solution)/shard_map/pallas_call | solution.py:137
  479.1 24.8 %shard_map.283 = (bf16[256,3072]{1,0:T(8,128)(2,1)}, bf16[256,3072]{1,0:T(8,128)(2,1)}, bf16[256,3072]{1,0:T(8,128)(2,1)}, bf16[128,3072]{1,0:T(8,128)(2,1)S(1)}, bf16[128,3072]{1,0:T(8,128)(2,1)S(1)}) custom-call(bf16[544,2048]{1,0:T(8,128)(2,1)} %get-tuple-element.172.refs_2_.refs_0_, bf16[544,2048]{1,0:T(8,128)(2,1)} %copy-done.18, ...), custom_call_target="tpu_custom_call" | custom-call | flops 136902080 | bytes 174325 | tf_op jit(solution)/shard_map/pallas_call | solution.py:783
  510.5 16.8 %shard_map.284 = (bf16[2,544,1536]{2,1,0:T(8,128)(2,1)}, bf16[2,544,1536]{2,1,0:T(8,128)(2,1)}) custom-call(s32[4]{0:T(128)S(1)} %iota.54.seat_ref, bf16[1,2048,1536]{2,1,0:T(8,128)(2,1)} %get-tuple-element.161.refs_0_, bf16[1,2048,1536]{2,1,0:T(8,128)(2,1)} %get-tuple-element.162.refs_1_, bf16[544,2048]{1,0:T(8,128)(2,1)} %copy-done.18, ...), custom_call_target="tpu_custom_call" | custom-call | flops 68451040 | bytes 281804 | tf_op jit(solution)/shard_map/pallas_call | solution.py:137
  531.5 23.9 %shard_map.285 = bf16[544,2048]{1,0:T(8,128)(2,1)} custom-call(s32[4]{0:T(128)S(1)} %iota.53.seat_ref, bf16[1,2048,3072]{2,1,0:T(8,128)(2,1)} %get-tuple-element.159.refs_0_.refs_2_, bf16[1,2048,3072]{2,1,0:T(8,128)(2,1)} %get-tuple-element.160.refs_1_.refs_3_, bf16[1,2048,3072]{2,1,0:T(8,128)(2,1)} %get-tuple-element.159.refs_0_.refs_2_, ...), custom_call_target="tpu_custom_call" | custom-call | flops 136902080 | bytes 592445 | tf_op jit(solution)/shard_map/pallas_call | solution.py:137
  555.5 4.0 collective-permute-done.4
  560.8 24.4 %shard_map.286 = (bf16[256,3072]{1,0:T(8,128)(2,1)}, bf16[256,3072]{1,0:T(8,128)(2,1)}, bf16[256,3072]{1,0:T(8,128)(2,1)}, bf16[128,3072]{1,0:T(8,128)(2,1)S(1)}, bf16[128,3072]{1,0:T(8,128)(2,1)S(1)}) custom-call(bf16[544,2048]{1,0:T(8,128)(2,1)} %copy-done.9, bf16[544,2048]{1,0:T(8,128)(2,1)} %copy-done.12, ...), custom_call_target="tpu_custom_call" | custom-call | flops 136902080 | bytes 174325 | tf_op jit(solution)/shard_map/pallas_call | solution.py:783
  596.6 25.0 %shard_map.287 = f32[544,2048]{1,0:T(8,128)} custom-call(s32[4]{0:T(128)S(1)} %iota.47.seat_ref, bf16[1,2048,3072]{2,1,0:T(8,128)(2,1)} %get-tuple-element.159.refs_0_.refs_2_, bf16[1,2048,3072]{2,1,0:T(8,128)(2,1)} %get-tuple-element.160.refs_1_.refs_3_, bf16[1,2048,3072]{2,1,0:T(8,128)(2,1)} %get-tuple-element.159.refs_0_.refs_2_, ...), custom_call_target="tpu_custom_call" | custom-call | flops 136902080 | bytes 614727 | tf_op jit(solution)/shard_map/pallas_call | solution.py:137
  630.7 4.2 fusion.15
  635.0 10.5 %shard_map.288.refs_4_ = bf16[4,544,512]{2,1,0:T(8,128)(2,1)} custom-call(s32[4]{0:T(128)S(1)} %iota_xor_fusion.seat_ref, bf16[4,2048,512]{2,1,0:T(8,128)(2,1)} %get-tuple-element.154.refs_0_, bf16[544,2048]{1,0:T(8,128)(2,1)} %get-tuple-element.238.refs_1_.refs_0_), custom_call_target="tpu_custom_call" | custom-call | flops 45634028 | bytes 128450 | tf_op jit(solution)/shard_map/pallas_call | solution.py:137
  645.5 44.8 %shard_map.289 = (bf16[256,3072]{1,0:T(8,128)(2,1)}, bf16[256,3072]{1,0:T(8,128)(2,1)}, bf16[256,3072]{1,0:T(8,128)(2,1)}, bf16[128,3072]{1,0:T(8,128)(2,1)S(1)}...) custom-call(bf16[544,2048]{1,0:T(8,128)(2,1)} %copy-done.9, bf16[544,2048]{1,0:T(8,128)(2,1)} %copy-done.12, ...), custom_call_target="tpu_custom_call" | custom-call | flops 136902080 | bytes 174325 | tf_op jit(solution)/shard_map/pallas_call | solution.py:783
  692.0 2.8 convert_add_fusion.3
  694.9 11.7 %collective-permute-start.13 = (bf16[256,1536]{1,0:T(8,128)(2,1)S(1)}, bf16[256,1536]{1,0:T(8,128)(2,1)}, u32[]{:S(2)}, u32[]{:S(2)}) collective-permute-start(bf16[256,1536]{1,0:T(8,128)(2,1)S(1)} %slice.269), channel_id=1, source_target_pairs={{0,2},{1,3},{2,0},{3,1},{4,6},{5,7},{6,4},{7,5},{8,10},{9,11},{10,... | collective-permute-start | bytes 2359304 | tf_op jit(solution)/shard_map/ppermute | solution.py:1286
  706.7 37.3 %shard_map.290 = bf16[2176,1024]{1,0:T(8,128)(2,1)} custom-call(s32[8]{0:T(128)S(1)} %fusion.14.parent_ref, bf16[2176,1024]{1,0:T(8,128)(2,1)} %bitcast.54, bf16[2176,1024]{1,0:T(8,128)(2,1)} %bitcast.55, bf16[2176,1024]{1,0:T(8,128)(2,1)} %bitcast.56, bf16[2176,512]{1,0:T(8,128)(2,1)} %get-tuple-element.156.o_ref, bf16[2176,512]{1,0:T(8,128)(2,1)} %bitcast.66, ...), custom_call_target="tpu_custom_call" | custom-call | flops 225280000 | bytes 133693 | tf_op jit(solution)/shard_map/pallas_call | solution.py:488
  746.9 5.3 all-to-all-start
  754.7 12.8 %shard_map.292 = (bf16[256,2048]{1,0:T(8,128)(2,1)}, bf16[256,2048]{1,0:T(8,128)(2,1)}, bf16[256,2048]{1,0:T(8,128)(2,1)}, bf16[128,2048]{1,0:T(8,128)(2,1)S(1)}, bf16[128,2048]{1,0:T(8,128)(2,1)S(1)}) custom-call(bf16[544,2048]{1,0:T(8,128)(2,1)} %get-tuple-element.238.refs_1_.refs_0_, bf16[4,544,512]{2,1,0:T(8,128)(2,1)} %get-tuple-element.158.refs_1_), custom_call_target="tpu_custom_call" | custom-call | flops 45634028 | bytes 86507 | tf_op jit(solution)/shard_map/pallas_call | solution.py:783
  772.1 17.8 %collective-permute-done.23 = bf16[256,3072]{1,0:T(8,128)(2,1)} collective-permute-done((bf16[256,3072]{1,0:T(8,128)(2,1)}, bf16[256,3072]{1,0:T(8,128)(2,1)}, u32[]{:S(2)}, u32[]{:S(2)}) %collective-permute-start.23) | collective-permute-done | bytes 1572896 | tf_op jit(solution)/shard_map/ppermute | solution.py:1286
  791.0 58.3 %all-to-all-done.g_ref = bf16[4,544,1024]{2,1,0:T(8,128)(2,1)} async-done(((bf16[4,544,1024]{2,1,0:T(8,128)(2,1)}), bf16[4,544,1024]{2,1,0:T(8,128)(2,1)}, u32[]{:S(2)}, u32[]{:S(2)}) %all-to-all-start) | async-done | bytes 4456480 | tf_op jit(solution)/shard_map/all_to_all | solution.py:1314
  849.2 10.1 shard_map.293
  868.5 12.9 %shard_map.294 = (bf16[256,2048]{1,0:T(8,128)(2,1)}, bf16[256,2048]{1,0:T(8,128)(2,1)}, bf16[256,2048]{1,0:T(8,128)(2,1)}, bf16[128,2048]{1,0:T(8,128)(2,1)S(1)}, bf16[128,2048]{1,0:T(8,128)(2,1)S(1)}) custom-call(bf16[544,2048]{1,0:T(8,128)(2,1)} %get-tuple-element.245.refs_0_, bf16[4,544,1024]{2,1,0:T(8,128)(2,1)} %get-tuple-element.265.refs_1_), custom_call_target="tpu_custom_call" | custom-call | flops 45634028 | bytes 108789 | tf_op jit(solution)/shard_map/pallas_call | solution.py:783
  885.9 3.0 copy.54
  889.0 13.0 %shard_map.295 = (bf16[256,2048]{1,0:T(8,128)(2,1)}, bf16[256,2048]{1,0:T(8,128)(2,1)}, bf16[256,2048]{1,0:T(8,128)(2,1)}, bf16[128,2048]{1,0:T(8,128)(2,1)S(1)}, bf16[128,2048]{1,0:T(8,128)(2,1)S(1)}) custom-call(bf16[544,2048]{1,0:T(8,128)(2,1)} %get-tuple-element.245.refs_0_, bf16[4,544,1024]{2,1,0:T(8,128)(2,1)} %get-tuple-element.265.refs_1_), custom_call_target="tpu_custom_call" | custom-call | flops 45634028 | bytes 108789 | tf_op jit(solution)/shard_map/pallas_call | solution.py:783
  907.0 4.2 all-to-all-start.1
  919.1 6.4 add_convert_fusion.in_ref
  929.2 6.4 shard_map.291
  940.9 20.0 %shard_map.296 = f32[544,2048]{1,0:T(8,128)} custom-call(s32[4]{0:T(128)S(1)} %iota_xor_fusion.seat_ref, bf16[4,2048,1024]{2,1,0:T(8,128)(2,1)} %get-tuple-element.237.refs_0_, bf16[4,544,1024]{2,1,0:T(8,128)(2,1)} %get-tuple-element.265.refs_1_), custom_call_target="tpu_custom_call" | custom-call | flops 91268056 | bytes 256901 | tf_op jit(solution)/shard_map/pallas_call | solution.py:137
  971.8 5.1 all-to-all-start.2
  977.4 3.6 fusion.8
  981.1 3.0 slice_add_fusion.1
  984.5 3.6 collective-permute-done.30
  994.5 6.7 all-to-all-done.2
  1001.1 4.2 all-to-all-start.3
  1007.5 6.3 fusion.7.in_ref
  1013.8 8.3 collective-permute-done.32
  1022.1 4.5 collective-permute-start.33
  1026.8 6.4 shard_map.297
  (290 shorter events, 122.7 us)
Async XLA Ops:
  12.5 148.1 %copy-start.1 = (f32[544,128]{1,0:T(8,128)}, f32[544,128]{1,0:T(8,128)S(1)}, u32[]{:S(2)}) copy-start(f32[544,128]{1,0:T(8,128)S(1)} %get-tuple-element.363.refs_6_.cos_ref) | copy-start | bytes 835588
  12.5 148.1 %copy-start.3 = (f32[544,128]{1,0:T(8,128)}, f32[544,128]{1,0:T(8,128)S(1)}, u32[]{:S(2)}) copy-start(f32[544,128]{1,0:T(8,128)S(1)} %get-tuple-element.364.refs_7_.sin_ref) | copy-start | bytes 835588
  12.6 148.0 %copy-start = (bf16[1536,256]{0,1:T(8,128)(2,1)S(1)}, bf16[1536,256]{0,1:T(8,128)(2,1)}, u32[]{:S(2)}) copy-start(bf16[1536,256]{0,1:T(8,128)(2,1)} %copy.47) | copy-start | bytes 2359300
  362.4 59.9 %collective-permute-start = (bf16[544,2048]{1,0:T(8,128)(2,1)S(1)}, bf16[544,2048]{1,0:T(8,128)(2,1)S(1)}, u32[]{:S(2)}, u32[]{:S(2)}) collective-permute-start(bf16[544,2048]{1,0:T(8,128)(2,1)S(1)} %multiply_convert_fusion.refs_4_.refs_0_), channel_id=1, source_target_pairs={{0,1},{1,0},{2,3},{3,2},{4,5},{5,4},{6,7},{7,6},{8,9},{9,8},{10,11... | collective-permute-start | bytes 6684680 | tf_op jit(solution)/shard_map/ppermute | solution.py:1286
  422.3 55.5 %collective-permute-start.1 = (bf16[544,2048]{1,0:T(8,128)(2,1)S(1)}, bf16[544,2048]{1,0:T(8,128)(2,1)S(1)}, u32[]{:S(2)}, u32[]{:S(2)}) collective-permute-start(bf16[544,2048]{1,0:T(8,128)(2,1)S(1)} %copy-done.10), channel_id=1, source_target_pairs={{0,1},{1,0},{2,3},{3,2},{4,5},{5,4},{6,7},{7,6},{8,9},{9,8},{10,11... | collective-permute-start | bytes 6684680 | tf_op jit(solution)/shard_map/ppermute | solution.py:1286
  503.9 23.4 %collective-permute-start.2 = (bf16[128,3072]{1,0:T(8,128)(2,1)S(1)}, bf16[128,3072]{1,0:T(8,128)(2,1)S(1)}, u32[]{:S(2)}, u32[]{:S(2)}) collective-permute-start(bf16[128,3072]{1,0:T(8,128)(2,1)S(1)} %get-tuple-element.175), channel_id=1, source_target_pairs={{0,8},{4,12},{8,0},{12,4},{16,24},{20,28},{24,16},{28,20},{1,9},{5... | collective-permute-start | bytes 2359304 | tf_op jit(solution)/shard_map/ppermute | solution.py:1286
  505.0 22.3 %collective-permute-start.3 = (bf16[128,3072]{1,0:T(8,128)(2,1)S(1)}, bf16[128,3072]{1,0:T(8,128)(2,1)S(1)}, u32[]{:S(2)}, u32[]{:S(2)}) collective-permute-start(bf16[128,3072]{1,0:T(8,128)(2,1)S(1)} %get-tuple-element.176), channel_id=1, source_target_pairs={{0,16},{4,20},{8,24},{12,28},{16,0},{20,4},{24,8},{28,12},{1,17},{... | collective-permute-start | bytes 2359304 | tf_op jit(solution)/shard_map/ppermute | solution.py:1286
  509.1 50.3 %collective-permute-start.4 = (bf16[544,2048]{1,0:T(8,128)(2,1)S(1)}, bf16[544,2048]{1,0:T(8,128)(2,1)S(1)}, u32[]{:S(2)}, u32[]{:S(2)}) collective-permute-start(bf16[544,2048]{1,0:T(8,128)(2,1)S(1)} %copy-done.22), channel_id=1, source_target_pairs={{0,1},{1,0},{2,3},{3,2},{4,5},{5,4},{6,7},{7,6},{8,9},{9,8},{10,11... | collective-permute-start | bytes 6684680 | tf_op jit(solution)/shard_map/ppermute | solution.py:1286
  528.8 61.1 %collective-permute-start.6 = (bf16[256,3072]{1,0:T(8,128)(2,1)}, bf16[256,3072]{1,0:T(8,128)(2,1)}, u32[]{:S(2)}, u32[]{:S(2)}) collective-permute-start(bf16[256,3072]{1,0:T(8,128)(2,1)} %pad_maximum_fusion.2), channel_id=1, source_target_pairs={{0,16},{4,20},{8,24},{12,28},{16,0},{20,4},{24,8},{28,12},{1,17},{... | collective-permute-start | bytes 4718600 | tf_op jit(solution)/shard_map/ppermute | solution.py:1286
  530.6 59.3 %collective-permute-start.5 = (bf16[256,3072]{1,0:T(8,128)(2,1)}, bf16[256,3072]{1,0:T(8,128)(2,1)S(1)}, u32[]{:S(2)}, u32[]{:S(2)}) collective-permute-start(bf16[256,3072]{1,0:T(8,128)(2,1)} %pad_maximum_fusion.1), channel_id=1, source_target_pairs={{0,8},{4,12},{8,0},{12,4},{16,24},{20,28},{24,16},{28,20},{1,9},{5... | collective-permute-start | bytes 4718600 | tf_op jit(solution)/shard_map/ppermute | solution.py:1286
  559.4 62.2 %collective-permute-start.7 = (bf16[544,2048]{1,0:T(8,128)(2,1)}, bf16[544,2048]{1,0:T(8,128)(2,1)S(1)}, u32[]{:S(2)}, u32[]{:S(2)}) collective-permute-start(bf16[544,2048]{1,0:T(8,128)(2,1)} %shard_map.285), channel_id=1, source_target_pairs={{0,1},{1,0},{2,3},{3,2},{4,5},{5,4},{6,7},{7,6},{8,9},{9,8},{10,11... | collective-permute-start | bytes 6684680 | tf_op jit(solution)/shard_map/ppermute | solution.py:1286
  585.2 36.4 %collective-permute-start.8 = (bf16[128,3072]{1,0:T(8,128)(2,1)S(1)}, bf16[128,3072]{1,0:T(8,128)(2,1)}, u32[]{:S(2)}, u32[]{:S(2)}) collective-permute-start(bf16[128,3072]{1,0:T(8,128)(2,1)S(1)} %get-tuple-element.194), channel_id=1, source_target_pairs={{0,8},{4,12},{8,0},{12,4},{16,24},{20,28},{24,16},{28,20},{1,9},{5... | collective-permute-start | bytes 2359304 | tf_op jit(solution)/shard_map/ppermute | solution.py:1286
  585.6 36.0 %collective-permute-start.9 = (bf16[128,3072]{1,0:T(8,128)(2,1)S(1)}, bf16[128,3072]{1,0:T(8,128)(2,1)}, u32[]{:S(2)}, u32[]{:S(2)}) collective-permute-start(bf16[128,3072]{1,0:T(8,128)(2,1)S(1)} %get-tuple-element.195), channel_id=1, source_target_pairs={{0,16},{4,20},{8,24},{12,28},{16,0},{20,4},{24,8},{28,12},{1,17},{... | collective-permute-start | bytes 2359304 | tf_op jit(solution)/shard_map/ppermute | solution.py:1286
  591.0 38.1 %slice-start = ((s8[4456448]{0:T(1024)(128)(4,1)}), s8[4194304]{0:T(1024)(128)(4,1)S(1)}, s32[]{:S(2)}) async-start(s8[4456448]{0:T(1024)(128)(4,1)} %bitcast.57), calls=%async_computation.4 | async-start | bytes 8388608
  595.6 49.9 %collective-permute-start.10 = (bf16[256,1536]{1,0:T(8,128)(2,1)}, bf16[256,1536]{1,0:T(8,128)(2,1)}, u32[]{:S(2)}, u32[]{:S(2)}) collective-permute-start(bf16[256,1536]{1,0:T(8,128)(2,1)} %slice.270), channel_id=1, source_target_pairs={{0,2},{1,3},{2,0},{3,1},{4,6},{5,7},{6,4},{7,5},{8,10},{9,11},{10,... | collective-permute-start | bytes 2359304 | tf_op jit(solution)/shard_map/ppermute | solution.py:1286
  596.6 32.5 %slice-start.1 = ((s8[4456448]{0:T(1024)(128)(4,1)}), s8[262144]{0:T(1024)(128)(4,1)S(1)}, s32[]{:S(2)}) async-start(s8[4456448]{0:T(1024)(128)(4,1)} %bitcast.57), calls=%async_computation.5 | async-start | bytes 524288
  626.1 65.8 %collective-permute-start.12 = (bf16[256,3072]{1,0:T(8,128)(2,1)}, bf16[256,3072]{1,0:T(8,128)(2,1)}, u32[]{:S(2)}, u32[]{:S(2)}) collective-permute-start(bf16[256,3072]{1,0:T(8,128)(2,1)} %pad_maximum_fusion.4), channel_id=1, source_target_pairs={{0,16},{4,20},{8,24},{12,28},{16,0},{20,4},{24,8},{28,12},{1,17},{... | collective-permute-start | bytes 4718600 | tf_op jit(solution)/shard_map/ppermute | solution.py:1286
  628.4 63.6 %collective-permute-start.11 = (bf16[256,3072]{1,0:T(8,128)(2,1)}, bf16[256,3072]{1,0:T(8,128)(2,1)}, u32[]{:S(2)}, u32[]{:S(2)}) collective-permute-start(bf16[256,3072]{1,0:T(8,128)(2,1)} %pad_maximum_fusion.3), channel_id=1, source_target_pairs={{0,8},{4,12},{8,0},{12,4},{16,24},{20,28},{24,16},{28,20},{1,9},{5... | collective-permute-start | bytes 4718600 | tf_op jit(solution)/shard_map/ppermute | solution.py:1286
  645.5 46.5 %copy-start.31 = (bf16[256,3072]{1,0:T(8,128)(2,1)S(1)}, bf16[256,3072]{1,0:T(8,128)(2,1)}, u32[]{:S(2)}) copy-start(bf16[256,3072]{1,0:T(8,128)(2,1)} %get-tuple-element.224) | copy-start | bytes 4718596
  690.3 53.7 %collective-permute-start.14 = (bf16[128,3072]{1,0:T(8,128)(2,1)S(1)}, bf16[128,3072]{1,0:T(8,128)(2,1)S(1)}, u32[]{:S(2)}, u32[]{:S(2)}) collective-permute-start(bf16[128,3072]{1,0:T(8,128)(2,1)S(1)} %get-tuple-element.220), channel_id=1, source_target_pairs={{0,8},{4,12},{8,0},{12,4},{16,24},{20,28},{24,16},{28,20},{1,9},{5... | collective-permute-start | bytes 2359304 | tf_op jit(solution)/shard_map/ppermute | solution.py:1286
  690.9 53.1 %collective-permute-start.15 = (bf16[128,3072]{1,0:T(8,128)(2,1)S(1)}, bf16[128,3072]{1,0:T(8,128)(2,1)S(1)}, u32[]{:S(2)}, u32[]{:S(2)}) collective-permute-start(bf16[128,3072]{1,0:T(8,128)(2,1)S(1)} %get-tuple-element.221), channel_id=1, source_target_pairs={{0,16},{4,20},{8,24},{12,28},{16,0},{20,4},{24,8},{28,12},{1,17},{... | collective-permute-start | bytes 2359304 | tf_op jit(solution)/shard_map/ppermute | solution.py:1286
  694.9 49.1 %collective-permute-start.13 = (bf16[256,1536]{1,0:T(8,128)(2,1)S(1)}, bf16[256,1536]{1,0:T(8,128)(2,1)}, u32[]{:S(2)}, u32[]{:S(2)}) collective-permute-start(bf16[256,1536]{1,0:T(8,128)(2,1)S(1)} %slice.269), channel_id=1, source_target_pairs={{0,2},{1,3},{2,0},{3,1},{4,6},{5,7},{6,4},{7,5},{8,10},{9,11},{10,... | collective-permute-start | bytes 2359304 | tf_op jit(solution)/shard_map/ppermute | solution.py:1286
  746.9 102.3 %all-to-all-start = ((bf16[4,544,1024]{2,1,0:T(8,128)(2,1)}), bf16[4,544,1024]{2,1,0:T(8,128)(2,1)}, u32[]{:S(2)}, u32[]{:S(2)}) async-start(bf16[4,544,1024]{2,1,0:T(8,128)(2,1)} %bitcast.59), calls=%async_computation | async-start | bytes 8912896 | tf_op jit(solution)/shard_map/all_to_all | solution.py:1314
  752.2 37.7 %collective-permute-start.23 = (bf16[256,3072]{1,0:T(8,128)(2,1)}, bf16[256,3072]{1,0:T(8,128)(2,1)}, u32[]{:S(2)}, u32[]{:S(2)}) collective-permute-start(bf16[256,3072]{1,0:T(8,128)(2,1)} %pad_maximum_fusion.6), channel_id=1, source_target_pairs={{0,16},{4,20},{8,24},{12,28},{16,0},{20,4},{24,8},{28,12},{1,17},{... | collective-permute-start | bytes 4718600 | tf_op jit(solution)/shard_map/ppermute | solution.py:1286
  753.3 37.6 %collective-permute-start.22 = (bf16[256,3072]{1,0:T(8,128)(2,1)}, bf16[256,3072]{1,0:T(8,128)(2,1)}, u32[]{:S(2)}, u32[]{:S(2)}) collective-permute-start(bf16[256,3072]{1,0:T(8,128)(2,1)} %pad_maximum_fusion.5), channel_id=1, source_target_pairs={{0,8},{4,12},{8,0},{12,4},{16,24},{20,28},{24,16},{28,20},{1,9},{5... | collective-permute-start | bytes 4718600 | tf_op jit(solution)/shard_map/ppermute | solution.py:1286
  767.5 81.7 %copy-start.2 = (f32[544,128]{1,0:T(8,128)S(1)}, f32[544,128]{1,0:T(8,128)}, u32[]{:S(2)}) copy-start(f32[544,128]{1,0:T(8,128)} %copy-done.1) | copy-start | bytes 835588
  767.5 81.7 %copy-start.4 = (f32[544,128]{1,0:T(8,128)S(1)}, f32[544,128]{1,0:T(8,128)}, u32[]{:S(2)}) copy-start(f32[544,128]{1,0:T(8,128)} %copy-done.3) | copy-start | bytes 835588
  767.6 91.8 %collective-permute-start.16 = (bf16[128,2048]{1,0:T(8,128)(2,1)S(1)}, bf16[128,2048]{1,0:T(8,128)(2,1)S(1)}, u32[]{:S(2)}, u32[]{:S(2)}) collective-permute-start(bf16[128,2048]{1,0:T(8,128)(2,1)S(1)} %get-tuple-element.239), channel_id=1, source_target_pairs={{0,8},{4,12},{8,0},{12,4},{16,24},{20,28},{24,16},{28,20},{1,9},{5... | collective-permute-start | bytes 1572872 | tf_op jit(solution)/shard_map/ppermute | solution.py:1286
  768.2 91.1 %collective-permute-start.17 = (bf16[128,2048]{1,0:T(8,128)(2,1)S(1)}, bf16[128,2048]{1,0:T(8,128)(2,1)}, u32[]{:S(2)}, u32[]{:S(2)}) collective-permute-start(bf16[128,2048]{1,0:T(8,128)(2,1)S(1)} %get-tuple-element.240), channel_id=1, source_target_pairs={{0,16},{4,20},{8,24},{12,28},{16,0},{20,4},{24,8},{28,12},{1,17},{... | collective-permute-start | bytes 1572872 | tf_op jit(solution)/shard_map/ppermute | solution.py:1286
  861.8 41.9 %collective-permute-start.21 = (bf16[256,2048]{1,0:T(8,128)(2,1)}, bf16[256,2048]{1,0:T(8,128)(2,1)}, u32[]{:S(2)}, u32[]{:S(2)}) collective-permute-start(bf16[256,2048]{1,0:T(8,128)(2,1)} %pad_maximum_fusion.8), channel_id=1, source_target_pairs={{0,16},{4,20},{8,24},{12,28},{16,0},{20,4},{24,8},{28,12},{1,17},{... | collective-permute-start | bytes 3145736 | tf_op jit(solution)/shard_map/ppermute | solution.py:1286
  862.9 40.9 %collective-permute-start.20 = (bf16[256,2048]{1,0:T(8,128)(2,1)S(1)}, bf16[256,2048]{1,0:T(8,128)(2,1)}, u32[]{:S(2)}, u32[]{:S(2)}) collective-permute-start(bf16[256,2048]{1,0:T(8,128)(2,1)S(1)} %pad_maximum_fusion.7), channel_id=1, source_target_pairs={{0,8},{4,12},{8,0},{12,4},{16,24},{20,28},{24,16},{28,20},{1,9},{5... | collective-permute-start | bytes 3145736 | tf_op jit(solution)/shard_map/ppermute | solution.py:1286
  867.8 35.9 %collective-permute-start.24 = (bf16[256,1536]{1,0:T(8,128)(2,1)}, bf16[256,1536]{1,0:T(8,128)(2,1)}, u32[]{:S(2)}, u32[]{:S(2)}) collective-permute-start(bf16[256,1536]{1,0:T(8,128)(2,1)} %slice.268), channel_id=1, source_target_pairs={{0,2},{1,3},{2,0},{3,1},{4,6},{5,7},{6,4},{7,5},{8,10},{9,11},{10,... | collective-permute-start | bytes 2359304 | tf_op jit(solution)/shard_map/ppermute | solution.py:1286
  881.5 22.2 %collective-permute-start.18 = (bf16[128,2048]{1,0:T(8,128)(2,1)S(1)}, bf16[128,2048]{1,0:T(8,128)(2,1)}, u32[]{:S(2)}, u32[]{:S(2)}) collective-permute-start(bf16[128,2048]{1,0:T(8,128)(2,1)S(1)} %get-tuple-element.251), channel_id=1, source_target_pairs={{0,8},{4,12},{8,0},{12,4},{16,24},{20,28},{24,16},{28,20},{1,9},{5... | collective-permute-start | bytes 1572872 | tf_op jit(solution)/shard_map/ppermute | solution.py:1286
  882.3 21.4 %collective-permute-start.19 = (bf16[128,2048]{1,0:T(8,128)(2,1)S(1)}, bf16[128,2048]{1,0:T(8,128)(2,1)}, u32[]{:S(2)}, u32[]{:S(2)}) collective-permute-start(bf16[128,2048]{1,0:T(8,128)(2,1)S(1)} %get-tuple-element.252), channel_id=1, source_target_pairs={{0,16},{4,20},{8,24},{12,28},{16,0},{20,4},{24,8},{28,12},{1,17},{... | collective-permute-start | bytes 1572872 | tf_op jit(solution)/shard_map/ppermute | solution.py:1286
  907.0 54.0 %all-to-all-start.1 = ((bf16[4,256,512]{2,1,0:T(8,128)(2,1)}), bf16[4,256,512]{2,1,0:T(8,128)(2,1)S(1)}, u32[]{:S(2)}, u32[]{:S(2)}) async-start(bf16[4,256,512]{2,1,0:T(8,128)(2,1)} %bitcast.45), calls=%async_computation.1 | async-start | bytes 2097152 | tf_op jit(solution)/shard_map/all_to_all | solution.py:1314
  915.0 45.9 %collective-permute-start.26 = (bf16[256,2048]{1,0:T(8,128)(2,1)}, bf16[256,2048]{1,0:T(8,128)(2,1)}, u32[]{:S(2)}, u32[]{:S(2)}) collective-permute-start(bf16[256,2048]{1,0:T(8,128)(2,1)} %pad_maximum_fusion.10), channel_id=1, source_target_pairs={{0,16},{4,20},{8,24},{12,28},{16,0},{20,4},{24,8},{28,12},{1,17},{... | collective-permute-start | bytes 3145736 | tf_op jit(solution)/shard_map/ppermute | solution.py:1286
  917.5 43.5 %collective-permute-start.25 = (bf16[256,2048]{1,0:T(8,128)(2,1)}, bf16[256,2048]{1,0:T(8,128)(2,1)}, u32[]{:S(2)}, u32[]{:S(2)}) collective-permute-start(bf16[256,2048]{1,0:T(8,128)(2,1)} %pad_maximum_fusion.9), channel_id=1, source_target_pairs={{0,8},{4,12},{8,0},{12,4},{16,24},{20,28},{24,16},{28,20},{1,9},{5... | collective-permute-start | bytes 3145736 | tf_op jit(solution)/shard_map/ppermute | solution.py:1286
  925.5 35.4 %collective-permute-start.27 = (bf16[128,2048]{1,0:T(8,128)(2,1)S(1)}, bf16[128,2048]{1,0:T(8,128)(2,1)}, u32[]{:S(2)}, u32[]{:S(2)}) collective-permute-start(bf16[128,2048]{1,0:T(8,128)(2,1)S(1)} %get-tuple-element.254), channel_id=1, source_target_pairs={{0,8},{4,12},{8,0},{12,4},{16,24},{20,28},{24,16},{28,20},{1,9},{5... | collective-permute-start | bytes 1572872 | tf_op jit(solution)/shard_map/ppermute | solution.py:1286
  926.0 35.0 %collective-permute-start.28 = (bf16[128,2048]{1,0:T(8,128)(2,1)S(1)}, bf16[128,2048]{1,0:T(8,128)(2,1)}, u32[]{:S(2)}, u32[]{:S(2)}) collective-permute-start(bf16[128,2048]{1,0:T(8,128)(2,1)S(1)} %get-tuple-element.255), channel_id=1, source_target_pairs={{0,16},{4,20},{8,24},{12,28},{16,0},{20,4},{24,8},{28,12},{1,17},{... | collective-permute-start | bytes 1572872 | tf_op jit(solution)/shard_map/ppermute | solution.py:1286
  963.5 25.8 %collective-permute-start.35 = (bf16[256,2048]{1,0:T(8,128)(2,1)}, bf16[256,2048]{1,0:T(8,128)(2,1)}, u32[]{:S(2)}, u32[]{:S(2)}) collective-permute-start(bf16[256,2048]{1,0:T(8,128)(2,1)} %pad_maximum_fusion.12), channel_id=1, source_target_pairs={{0,16},{4,20},{8,24},{12,28},{16,0},{20,4},{24,8},{28,12},{1,17},{... | collective-permute-start | bytes 3145736 | tf_op jit(solution)/shard_map/ppermute | solution.py:1286
  967.2 24.2 %collective-permute-start.34 = (bf16[256,2048]{1,0:T(8,128)(2,1)}, bf16[256,2048]{1,0:T(8,128)(2,1)}, u32[]{:S(2)}, u32[]{:S(2)}) collective-permute-start(bf16[256,2048]{1,0:T(8,128)(2,1)} %pad_maximum_fusion.11), channel_id=1, source_target_pairs={{0,8},{4,12},{8,0},{12,4},{16,24},{20,28},{24,16},{28,20},{1,9},{5... | collective-permute-start | bytes 3145736 | tf_op jit(solution)/shard_map/ppermute | solution.py:1286
  971.8 29.3 %all-to-all-start.2 = ((bf16[4,256,512]{2,1,0:T(8,128)(2,1)}), bf16[4,256,512]{2,1,0:T(8,128)(2,1)}, u32[]{:S(2)}, u32[]{:S(2)}) async-start(bf16[4,256,512]{2,1,0:T(8,128)(2,1)} %bitcast.61), calls=%async_computation.2 | async-start | bytes 2097152 | tf_op jit(solution)/shard_map/all_to_all | solution.py:1314
  981.1 3.0 collective-permute-start.29
  984.1 3.9 collective-permute-start.30
  988.1 17.3 %collective-permute-start.31 = (f32[1,544]{1,0:T(1,128)S(1)}, f32[1,544]{1,0:T(1,128)S(1)}, u32[]{:S(2)}, u32[]{:S(2)}) collective-permute-start(f32[1,544]{1,0:T(1,128)S(1)} %slice.229), channel_id=1, source_target_pairs={{0,8},{4,12},{8,0},{12,4},{16,24},{20,28},{24,16},{28,20},{1,9},{5... | collective-permute-start | bytes 6536 | tf_op jit(solution)/shard_map/ppermute | solution.py:1286
  1001.1 36.4 %all-to-all-start.3 = ((bf16[4,256,512]{2,1,0:T(8,128)(2,1)}), bf16[4,256,512]{2,1,0:T(8,128)(2,1)}, u32[]{:S(2)}, u32[]{:S(2)}) async-start(bf16[4,256,512]{2,1,0:T(8,128)(2,1)} %bitcast.62), calls=%async_computation.3 | async-start | bytes 2097152 | tf_op jit(solution)/shard_map/all_to_all | solution.py:1314
  1005.4 16.6 %collective-permute-start.32 = (f32[1,544]{1,0:T(1,128)S(1)}, f32[1,544]{1,0:T(1,128)S(1)}, u32[]{:S(2)}, u32[]{:S(2)}) collective-permute-start(f32[1,544]{1,0:T(1,128)S(1)} %slice_add_fusion.5), channel_id=1, source_target_pairs={{0,1},{1,0},{2,3},{3,2},{4,5},{5,4},{6,7},{7,6},{8,9},{9,8},{10,11... | collective-permute-start | bytes 6536 | tf_op jit(solution)/shard_map/ppermute | solution.py:1286
  1022.1 12.1 %collective-permute-start.33 = (f32[1,544]{1,0:T(1,128)S(1)}, f32[1,544]{1,0:T(1,128)S(1)}, u32[]{:S(2)}, u32[]{:S(2)}) collective-permute-start(f32[1,544]{1,0:T(1,128)S(1)} %add.204), channel_id=1, source_target_pairs={{0,2},{1,3},{2,0},{3,1},{4,6},{5,7},{6,4},{7,5},{8,10},{9,11},{10,... | collective-permute-start | bytes 6536 | tf_op jit(solution)/shard_map/ppermute | solution.py:1286
  (41 other events, 331.6 us)

commit v5 on v4

--- a/solution.py
+++ b/solution.py
@@ -215,6 +215,42 @@
         [pltpu.VMEM((rows, depth), f32)],
         2 * rows * depth * tw * steps * len(sets),
     )[0]
+
+
+def project_residual(left, tiles, seats, stream, gain):
+    rows, depth = stream.shape
+    tw, steps = tiles.width, tiles.steps
+
+    def body(step, weights, ins, outs, own):
+        acc = own[0]
+        total = dot_nt(ins[0][...], weights[0][...])
+
+        @pl.when(step == 0)
+        def _():
+            acc[...] = ins[1][...].astype(f32) + total
+
+        @pl.when(step > 0)
+        def _():
+            acc[...] += total
+
+        @pl.when(step == steps - 1)
+        def _():
+            value = acc[...]
+            outs[0][...] = value
+            inverse = lax.rsqrt(jnp.mean(value * value, axis=-1, keepdims=True) + norm_eps)
+            outs[1][...] = (value * inverse * ins[2][...]).astype(bf16)
+
+    return tiled_call(
+        body,
+        [tiles],
+        seats,
+        [left, stream, gain],
+        [seated(rows, tw, tiles.parts), whole(stream), whole(gain)],
+        [jax.ShapeDtypeStruct((rows, depth), f32), struct(rows, depth)],
+        [pl.BlockSpec((rows, depth), lambda t, s: (0, 0))] * 2,
+        [pltpu.VMEM((rows, depth), f32)],
+        2 * rows * depth * tw * steps,
+    )
 
 
 def feed_forward(normed, gate_tiles, up_tiles, seats):
@@ -1369,12 +1405,8 @@
     attended_heads, logs = attention_forward(qkv, parents, kv)
     attended, down_rest = gather_late(m, n, attended_heads.reshape(n, rows, -1), down_rest)
     out_tiles = Tiles([out_all], 1, 0, aw)
-    stream = stream_low.astype(f32)
-    after_attn = stream + project_columns([attended], [out_tiles], seats, depth, f32)
-
-    inverse_two = inverse_rms(after_attn)
-    unit_two = after_attn * inverse_two
-    normed_two = (unit_two * gain_two).astype(bf16)
+    after_attn, normed_two = project_residual(attended, out_tiles, seats, stream_low, gain_two)
+
     normed_two_next = over("tp", normed_two, 1)
 
     gate_tiles = Tiles([in_own, in_rest], 3, 0, fw)
@@ -1411,6 +1443,8 @@
     back = tick(back, gate_job)
     back = after(back, gate_job.started)
     normed_two_grad = back + back_next.astype(f32)
+    inverse_two = inverse_rms(after(after_attn, normed_two_next))
+    unit_two = after_attn * inverse_two
 
     ffn_gain_part = jnp.sum(normed_two_grad * unit_two, axis=0)
     stream_grad = cotangent.astype(f32) + norm_back(
@@ -1433,7 +1467,12 @@
     grad_low, down_next, after_attn = after((grad_low, down_next, after_attn), back_hats)
     out_job = Job(attn_share(grad_low, attended, None, 7))
     fence = tick(after(grad_low, out_job.started), up_job)
-    back_hats_own = after(back_hats_own, fence, out_job.started)
+    mixed = (after_attn + down + down_next.astype(f32)).astype(bf16)
+    mixed = shuffle_columns(mixed, absolute)
+    inverse_one = inverse_rms(after(stream_low, back_hats).astype(f32))
+    back_hats_own, inverse_one, mixed = after(
+        (back_hats_own, inverse_one, mixed), fence, out_job.started
+    )
     raw_grads, q_sum, k_sum = qkv_back(back_hats_own, raws, cosine, sine, gain_q, gain_k)
     raw_grads = tick(raw_grads, out_job)
     q_job = Job(attn_share(normed_one, after(raw_grads, out_job.started), 0, 8))
@@ -1444,11 +1483,7 @@
     normed_one_grad = project_columns([raw_late], [qkv_tiles], seats, depth, f32)
     normed_one_grad = tick(normed_one_grad, q_job, k_job, up_job, out_job)
     normed_one_grad = after(normed_one_grad, q_job.started, k_job.started)
-    mixed = (after_attn + down + down_next.astype(f32)).astype(bf16)
-    mixed = shuffle_columns(mixed, absolute)
-    stream = after(stream_low, normed_one_grad).astype(f32)
-    inverse_one = inverse_rms(stream)
-    unit_one = stream * inverse_one
+    unit_one = stream_low.astype(f32) * inverse_one
     attn_gain_part = jnp.sum(normed_one_grad * unit_one, axis=0)
     tokens_grad = (
         stream_grad + norm_back(normed_one_grad, unit_one, inverse_one, gain_one)

time: 1050 us -> 1020 us (0.971)
  other arithmetic: 89.4 us -> 75.9 us
  transfers between devices with their start and end apart: 40 -> 40, of which waited for: 9 -> 12; matrix products, arithmetic and copies ran while one was open for 8% -> 7% of each run, Pallas kernels for 34% -> 35%
where the time goes in v5:
time: 1020 us
  Pallas kernels  725 us (71%)
  waiting for transfers between devices  106 us (10%)
  starting transfers between devices  78.9 us (8%)
  other arithmetic  75.9 us (7%)
  local copies, waits for them, and re-layouts  28.7 us (3%)
    pallas_call x3, Pallas kernels, transfer_call(): pl.pallas_call(kernel, in_specs=[pl.BlockSpec(memory_space=pltpu.VMEM if...  308 us
    pallas_call x11, Pallas kernels, tiled_call(): pl.pallas_call(kernel, grid_spec=pltpu.PrefetchScalarGridSpec(num_scalar_...  203 us
    pallas_call x6, Pallas kernels, gradient_pair(): pl.pallas_call(kernel, grid=(2 * steps,), in_specs=[pl.BlockSpec((rows, s...  133 us
    all_to_all x4, waiting for transfers between devices, swap(): return lax.all_to_all(a, 'tp', split_axis=0, concat_axis=0, tiled=True)  62.1 us
    ppermute x36, starting transfers between devices, over(): return lax.ppermute(a, axis, [(i, i ^ mask) for i in range(size)])  60.1 us
    ppermute x36, waiting for transfers between devices, over(): return lax.ppermute(a, axis, [(i, i ^ mask) for i in range(size)])  44.1 us
    pallas_call x1, Pallas kernels, attention_backward(): pl.pallas_call(kernel, grid_spec=pltpu.PrefetchScalarGridSpec(num_scalar_...  37.3 us
    pallas_call x1, Pallas kernels, attention_forward(): pl.pallas_call(kernel, grid_spec=pltpu.PrefetchScalarGridSpec(num_scalar_...  20.6 us
  transfers between devices with their start and end apart: 40, of which 12 were waited for; matrix products, arithmetic and copies ran while one was open for 7% of the time, Pallas kernels for 35%

profile of v5, /device:TPU:0, one launch (start us, length us, event | category | flops | bytes accessed | tf_op | source)
XLA Modules:
  0.0 1017.3 jit_solution(1057171252524528790)
XLA Ops:
  12.6 148.0 %shard_map.273 = (bf16[4,2048,1024]{2,1,0:T(8,128)(2,1)}, bf16[1,2048,3072]{2,1,0:T(8,128)(2,1)}, bf16[1,2048,3072]{2,1,0:T(8,128)(2,1)}, bf16[1,2048,1536]{2,1,...) custom-call(bf16[256,1024]{1,0:T(8,128)(2,1)S(1)} %pad_maximum_fusio, ...), custom_call_target="tpu_custom_call" | custom-call | bytes 10000 | tf_op jit(solution)/shard_map/pallas_call | solution.py:659
  161.3 119.0 %shard_map.274 = (bf16[4,544,1024]{2,1,0:T(8,128)(2,1)}, bf16[1,2048,3072]{2,1,0:T(8,128)(2,1)}, bf16[4,2048,512]{2,1,0:T(8,128)(2,1)}, bf16[1,2048,1536]{2,1,0:T(8,128)(2,1)}) custom-call(bf16[4,544,1024]{2,1,0:T(8,128)(2,1)} %get-tuple-element.155.refs_0_, bf16[1,2048,3072]{2,1,0:T(8,128)(2,1)} %get-tuple-element.156.refs_1_, ...), custom_call_target="tpu_custom_call", output_to_operand_aliasing={{1}: (1, {})} | custom-call | bytes 10000 | tf_op jit(solution)/shard_map/pallas_call | solution.py:659
  280.3 20.6 %shard_map.275 = (bf16[2176,512]{1,0:T(8,128)(2,1)}, f32[2,17,256]{2,1,0:T(8,128)S(1)}) custom-call(s32[8]{0:T(128)S(1)} %fusion.4.parent_ref, bf16[2176,1024]{1,0:T(8,128)(2,1)} %bitcast.56, bf16[2176,1024]{1,0:T(8,128)(2,1)} %bitcast.57, bf16[2176,1024]{1,0:T(8,128)(2,1)} %bitcast.58), custom_call_target="tpu_custom_call" | custom-call | flops 90112000 | bytes 67194 | tf_op jit(solution)/shard_map/pallas_call | solution.py:434
  300.9 41.3 %shard_map.276 = (bf16[4,544,512]{2,1,0:T(8,128)(2,1)}, bf16[1,2048,1536]{2,1,0:T(8,128)(2,1)}) custom-call(bf16[4,544,512]{2,1,0:T(8,128)(2,1)} %bitcast.65, bf16[1,2048,1536]{2,1,0:T(8,128)(2,1)} %get-tuple-element.160.refs_1_), custom_call_target="tpu_custom_call", output_to_operand_aliasing={{1}: (1, {})} | custom-call | bytes 10000 | tf_op jit(solution)/shard_map/pallas_call | solution.py:659
  342.2 15.1 %shard_map.277 = (f32[544,2048]{1,0:T(8,128)}, bf16[544,2048]{1,0:T(8,128)(2,1)}) custom-call(s32[4]{0:T(128)S(1)} %iota_xor_fusion.seat_ref, bf16[4,2048,512]{2,1,0:T(8,128)(2,1)} %get-tuple-element.159.refs_0_, bf16[4,544,512]{2,1,0:T(8,128)(2,1)} %get-tuple-element.161.refs_1_, bf16[544,2048]{1,0:T(8,128)(2,1)} %get-tuple-element.242.refs_2_, ...), custom_call_target="tpu_custom_call" | custom-call | flops 45634028 | bytes 195379 | tf_op jit(solution)/shard_map/pallas_call | solution.py:137
  357.3 11.6 %collective-permute-start = (bf16[544,2048]{1,0:T(8,128)(2,1)}, bf16[544,2048]{1,0:T(8,128)(2,1)S(1)}, u32[]{:S(2)}, u32[]{:S(2)}) collective-permute-start(bf16[544,2048]{1,0:T(8,128)(2,1)} %get-tuple-element.222.refs_4_.refs_0_), channel_id=1, source_target_pairs={{0,1},{1,0},{2,3},{3,2},{4,5},{5,4},{6,7},{7,6},{8,9},{9,8},{10,11... | collective-permute-start | bytes 6684680 | tf_op jit(solution)/shard_map/ppermute | solution.py:1322
  368.9 21.3 %shard_map.278 = (bf16[2,544,1536]{2,1,0:T(8,128)(2,1)}, bf16[2,544,1536]{2,1,0:T(8,128)(2,1)}, bf16[2,544,1536]{2,1,0:T(8,128)(2,1)}) custom-call(s32[4]{0:T(128)S(1)} %iota.46.seat_ref, bf16[1,2048,3072]{2,1,0:T(8,128)(2,1)} %get-tuple-element.168.refs_0_.refs_2_, bf16[1,2048,3072]{2,1,0:T(8,128)(2,1)} %get-tuple-element.169.refs_1_.refs_3_, ...), custom_call_target="tpu_custom_call" | custom-call | flops 136902080 | bytes 625868 | tf_op jit(solution)/shard_map/pallas_call | solution.py:137
  390.2 16.5 %shard_map.279 = f32[544,2048]{1,0:T(8,128)} custom-call(s32[4]{0:T(128)S(1)} %iota.45.seat_ref, bf16[1,2048,1536]{2,1,0:T(8,128)(2,1)} %get-tuple-element.166.refs_0_, bf16[1,2048,1536]{2,1,0:T(8,128)(2,1)} %get-tuple-element.167.refs_1_, bf16[2,544,1536]{2,1,0:T(8,128)(2,1)} %get-tuple-element.180.refs_2_), custom_call_target="tpu_custom_call" | custom-call | flops 68451040 | bytes 203816 | tf_op jit(solution)/shard_map/pallas_call | solution.py:137
  406.7 10.6 %collective-permute-done.refs_4_.refs_1_ = bf16[544,2048]{1,0:T(8,128)(2,1)S(1)} collective-permute-done((bf16[544,2048]{1,0:T(8,128)(2,1)}, bf16[544,2048]{1,0:T(8,128)(2,1)S(1)}, u32[]{:S(2)}, u32[]{:S(2)}) %collective-permute-start) | collective-permute-done | bytes 2228256 | tf_op jit(solution)/shard_map/ppermute | solution.py:1322
  419.1 21.3 %shard_map.280 = (bf16[2,544,1536]{2,1,0:T(8,128)(2,1)}, bf16[2,544,1536]{2,1,0:T(8,128)(2,1)}, bf16[2,544,1536]{2,1,0:T(8,128)(2,1)}) custom-call(s32[4]{0:T(128)S(1)} %iota.49.seat_ref, bf16[1,2048,3072]{2,1,0:T(8,128)(2,1)} %get-tuple-element.168.refs_0_.refs_2_, bf16[1,2048,3072]{2,1,0:T(8,128)(2,1)} %get-tuple-element.169.refs_1_.refs_3_, ...), custom_call_target="tpu_custom_call" | custom-call | flops 136902080 | bytes 625868 | tf_op jit(solution)/shard_map/pallas_call | solution.py:137
  440.4 15.6 %shard_map.281 = bf16[544,2048]{1,0:T(8,128)(2,1)} custom-call(s32[4]{0:T(128)S(1)} %iota.48.seat_ref, bf16[1,2048,1536]{2,1,0:T(8,128)(2,1)} %get-tuple-element.166.refs_0_, bf16[1,2048,1536]{2,1,0:T(8,128)(2,1)} %get-tuple-element.167.refs_1_, bf16[2,544,1536]{2,1,0:T(8,128)(2,1)} %get-tuple-element.172.refs_2_.refs_3_), custom_call_target="tpu_custom_call" | custom-call | flops 68451040 | bytes 181534 | tf_op jit(solution)/shard_map/pallas_call | solution.py:137
  456.1 16.8 %shard_map.282 = (bf16[2,544,1536]{2,1,0:T(8,128)(2,1)}, bf16[2,544,1536]{2,1,0:T(8,128)(2,1)}) custom-call(s32[4]{0:T(128)S(1)} %iota.47.seat_ref, bf16[1,2048,1536]{2,1,0:T(8,128)(2,1)} %get-tuple-element.166.refs_0_, bf16[1,2048,1536]{2,1,0:T(8,128)(2,1)} %get-tuple-element.167.refs_1_, bf16[544,2048]{1,0:T(8,128)(2,1)} %get-tuple-element.178.refs_2_.refs_0_, ...), custom_call_target="tpu_custom_call" | custom-call | flops 68451040 | bytes 281804 | tf_op jit(solution)/shard_map/pallas_call | solution.py:137
  474.2 25.0 %shard_map.283 = (bf16[256,3072]{1,0:T(8,128)(2,1)}, bf16[256,3072]{1,0:T(8,128)(2,1)}, bf16[256,3072]{1,0:T(8,128)(2,1)}, bf16[128,3072]{1,0:T(8,128)(2,1)S(1)}, bf16[128,3072]{1,0:T(8,128)(2,1)S(1)}) custom-call(bf16[544,2048]{1,0:T(8,128)(2,1)} %get-tuple-element.178.refs_2_.refs_0_, bf16[544,2048]{1,0:T(8,128)(2,1)} %copy-done.16, ...), custom_call_target="tpu_custom_call" | custom-call | flops 136902080 | bytes 174325 | tf_op jit(solution)/shard_map/pallas_call | solution.py:819
  506.0 16.8 %shard_map.284 = (bf16[2,544,1536]{2,1,0:T(8,128)(2,1)}, bf16[2,544,1536]{2,1,0:T(8,128)(2,1)}) custom-call(s32[4]{0:T(128)S(1)} %iota.51.seat_ref, bf16[1,2048,1536]{2,1,0:T(8,128)(2,1)} %get-tuple-element.166.refs_0_, bf16[1,2048,1536]{2,1,0:T(8,128)(2,1)} %get-tuple-element.167.refs_1_, bf16[544,2048]{1,0:T(8,128)(2,1)} %copy-done.16, ...), custom_call_target="tpu_custom_call" | custom-call | flops 68451040 | bytes 281804 | tf_op jit(solution)/shard_map/pallas_call | solution.py:137
  526.0 24.3 %shard_map.285 = bf16[544,2048]{1,0:T(8,128)(2,1)} custom-call(s32[4]{0:T(128)S(1)} %iota.50.seat_ref, bf16[1,2048,3072]{2,1,0:T(8,128)(2,1)} %get-tuple-element.168.refs_0_.refs_2_, bf16[1,2048,3072]{2,1,0:T(8,128)(2,1)} %get-tuple-element.169.refs_1_.refs_3_, bf16[1,2048,3072]{2,1,0:T(8,128)(2,1)} %get-tuple-element.168.refs_0_.refs_2_, ...), custom_call_target="tpu_custom_call" | custom-call | flops 136902080 | bytes 592445 | tf_op jit(solution)/shard_map/pallas_call | solution.py:137
  550.3 4.7 collective-permute-done.4
  556.8 24.6 %shard_map.286 = (bf16[256,3072]{1,0:T(8,128)(2,1)}, bf16[256,3072]{1,0:T(8,128)(2,1)}, bf16[256,3072]{1,0:T(8,128)(2,1)}, bf16[128,3072]{1,0:T(8,128)(2,1)S(1)}, bf16[128,3072]{1,0:T(8,128)(2,1)S(1)}) custom-call(bf16[544,2048]{1,0:T(8,128)(2,1)} %get-tuple-element.222.refs_4_.refs_0_, bf16[544,2048]{1,0:T(8,128)(2,1)} %copy-done.11, ...), custom_call_target="tpu_custom_call" | custom-call | flops 136902080 | bytes 174325 | tf_op jit(solution)/shard_map/pallas_call | solution.py:819
  585.2 2.5 convert_add_fusion.3
  590.2 24.9 %shard_map.287 = f32[544,2048]{1,0:T(8,128)} custom-call(s32[4]{0:T(128)S(1)} %iota.52.seat_ref, bf16[1,2048,3072]{2,1,0:T(8,128)(2,1)} %get-tuple-element.168.refs_0_.refs_2_, bf16[1,2048,3072]{2,1,0:T(8,128)(2,1)} %get-tuple-element.169.refs_1_.refs_3_, bf16[1,2048,3072]{2,1,0:T(8,128)(2,1)} %get-tuple-element.168.refs_0_.refs_2_, ...), custom_call_target="tpu_custom_call" | custom-call | flops 136902080 | bytes 614727 | tf_op jit(solution)/shard_map/pallas_call | solution.py:137
  623.6 4.2 fusion.5
  627.8 10.5 %shard_map.288.refs_4_ = bf16[4,544,512]{2,1,0:T(8,128)(2,1)} custom-call(s32[4]{0:T(128)S(1)} %iota_xor_fusion.seat_ref, bf16[4,2048,512]{2,1,0:T(8,128)(2,1)} %get-tuple-element.159.refs_0_, bf16[544,2048]{1,0:T(8,128)(2,1)} %get-tuple-element.246.refs_1_.refs_0_), custom_call_target="tpu_custom_call" | custom-call | flops 45634028 | bytes 128450 | tf_op jit(solution)/shard_map/pallas_call | solution.py:137
  638.3 44.8 %shard_map.289 = (bf16[256,3072]{1,0:T(8,128)(2,1)}, bf16[256,3072]{1,0:T(8,128)(2,1)}, bf16[256,3072]{1,0:T(8,128)(2,1)}, bf16[128,3072]{1,0:T(8,128)(2,1)S(1)}...) custom-call(bf16[544,2048]{1,0:T(8,128)(2,1)} %get-tuple-element.222.refs_4_.refs_0_, ...), custom_call_target="tpu_custom_call" | custom-call | flops 136902080 | bytes 174325 | tf_op jit(solution)/shard_map/pallas_call | solution.py:819
  687.4 11.0 %collective-permute-start.13 = (bf16[256,1536]{1,0:T(8,128)(2,1)S(1)}, bf16[256,1536]{1,0:T(8,128)(2,1)S(1)}, u32[]{:S(2)}, u32[]{:S(2)}) collective-permute-start(bf16[256,1536]{1,0:T(8,128)(2,1)S(1)} %slice.270), channel_id=1, source_target_pairs={{0,2},{1,3},{2,0},{3,1},{4,6},{5,7},{6,4},{7,5},{8,10},{9,11},{10,... | collective-permute-start | bytes 2359304 | tf_op jit(solution)/shard_map/ppermute | solution.py:1322
  698.6 37.3 %shard_map.290 = bf16[2176,1024]{1,0:T(8,128)(2,1)} custom-call(s32[8]{0:T(128)S(1)} %fusion.4.parent_ref, bf16[2176,1024]{1,0:T(8,128)(2,1)} %bitcast.59, bf16[2176,1024]{1,0:T(8,128)(2,1)} %bitcast.60, bf16[2176,1024]{1,0:T(8,128)(2,1)} %bitcast.61, bf16[2176,512]{1,0:T(8,128)(2,1)} %get-tuple-element.158.o_ref, bf16[2176,512]{1,0:T(8,128)(2,1)} %bitcast.71, ...), custom_call_target="tpu_custom_call" | custom-call | flops 225280000 | bytes 133693 | tf_op jit(solution)/shard_map/pallas_call | solution.py:524
  739.3 5.5 all-to-all-start
  749.3 12.8 %shard_map.292 = (bf16[256,2048]{1,0:T(8,128)(2,1)}, bf16[256,2048]{1,0:T(8,128)(2,1)}, bf16[256,2048]{1,0:T(8,128)(2,1)}, bf16[128,2048]{1,0:T(8,128)(2,1)S(1)}, bf16[128,2048]{1,0:T(8,128)(2,1)S(1)}) custom-call(bf16[544,2048]{1,0:T(8,128)(2,1)} %get-tuple-element.246.refs_1_.refs_0_, bf16[4,544,512]{2,1,0:T(8,128)(2,1)} %get-tuple-element.161.refs_1_), custom_call_target="tpu_custom_call" | custom-call | flops 45634028 | bytes 86507 | tf_op jit(solution)/shard_map/pallas_call | solution.py:819
  766.4 6.9 add_convert_fusion.1.in_ref
  773.3 6.5 shard_map.291
  779.8 3.3 collective-permute-done.23
  783.9 57.2 %all-to-all-done.g_ref = bf16[4,544,1024]{2,1,0:T(8,128)(2,1)} async-done(((bf16[4,544,1024]{2,1,0:T(8,128)(2,1)}), bf16[4,544,1024]{2,1,0:T(8,128)(2,1)}, u32[]{:S(2)}, u32[]{:S(2)}) %all-to-all-start) | async-done | bytes 4456480 | tf_op jit(solution)/shard_map/all_to_all | solution.py:1350
  841.1 10.1 shard_map.293
  859.1 12.9 %shard_map.294 = (bf16[256,2048]{1,0:T(8,128)(2,1)}, bf16[256,2048]{1,0:T(8,128)(2,1)}, bf16[256,2048]{1,0:T(8,128)(2,1)}, bf16[128,2048]{1,0:T(8,128)(2,1)S(1)}, bf16[128,2048]{1,0:T(8,128)(2,1)S(1)}) custom-call(bf16[544,2048]{1,0:T(8,128)(2,1)} %get-tuple-element.256.refs_0_, bf16[4,544,1024]{2,1,0:T(8,128)(2,1)} %get-tuple-element.276.refs_1_), custom_call_target="tpu_custom_call" | custom-call | flops 45634028 | bytes 108789 | tf_op jit(solution)/shard_map/pallas_call | solution.py:819
  874.1 13.0 %shard_map.295 = (bf16[256,2048]{1,0:T(8,128)(2,1)}, bf16[256,2048]{1,0:T(8,128)(2,1)}, bf16[256,2048]{1,0:T(8,128)(2,1)}, bf16[128,2048]{1,0:T(8,128)(2,1)S(1)}, bf16[128,2048]{1,0:T(8,128)(2,1)S(1)}) custom-call(bf16[544,2048]{1,0:T(8,128)(2,1)} %get-tuple-element.256.refs_0_, bf16[4,544,1024]{2,1,0:T(8,128)(2,1)} %get-tuple-element.276.refs_1_), custom_call_target="tpu_custom_call" | custom-call | flops 45634028 | bytes 108789 | tf_op jit(solution)/shard_map/pallas_call | solution.py:819
  887.2 5.3 collective-permute-done.24
  894.2 4.4 all-to-all-start.1
  910.3 2.9 slice_add_fusion.2
  916.6 19.9 %shard_map.296 = f32[544,2048]{1,0:T(8,128)} custom-call(s32[4]{0:T(128)S(1)} %iota_xor_fusion.seat_ref, bf16[4,2048,1024]{2,1,0:T(8,128)(2,1)} %get-tuple-element.251.refs_0_, bf16[4,544,1024]{2,1,0:T(8,128)(2,1)} %get-tuple-element.276.refs_1_), custom_call_target="tpu_custom_call" | custom-call | flops 91268056 | bytes 256901 | tf_op jit(solution)/shard_map/pallas_call | solution.py:137
  936.6 3.4 collective-permute-done.27
  949.8 4.8 all-to-all-start.2
  954.5 3.6 multiply_reduce_fusion.1
  958.2 3.0 slice_add_fusion.1
  962.6 4.1 collective-permute-done.30
  973.4 5.0 all-to-all-done.2
  978.4 4.2 all-to-all-start.3
  984.7 6.3 add_convert_fusion.in_ref
  991.0 8.3 collective-permute-done.32
  999.3 4.5 collective-permute-start.33
  1005.3 6.4 shard_map.297
  (290 shorter events, 112.5 us)
Async XLA Ops:
  12.5 148.1 %copy-start.1 = (f32[544,128]{1,0:T(8,128)}, f32[544,128]{1,0:T(8,128)S(1)}, u32[]{:S(2)}) copy-start(f32[544,128]{1,0:T(8,128)S(1)} %get-tuple-element.374.refs_6_.cos_ref) | copy-start | bytes 835588
  12.5 148.1 %copy-start.3 = (f32[544,128]{1,0:T(8,128)}, f32[544,128]{1,0:T(8,128)S(1)}, u32[]{:S(2)}) copy-start(f32[544,128]{1,0:T(8,128)S(1)} %get-tuple-element.375.refs_7_.sin_ref) | copy-start | bytes 835588
  12.6 148.7 %copy-start = (bf16[1536,256]{0,1:T(8,128)(2,1)S(1)}, bf16[1536,256]{0,1:T(8,128)(2,1)}, u32[]{:S(2)}) copy-start(bf16[1536,256]{0,1:T(8,128)(2,1)} %copy.47) | copy-start | bytes 2359300
  160.7 119.6 %copy-start.43 = (f32[8,768]{1,0:T(8,128)}, f32[8,768]{1,0:T(8,128)S(1)}, u32[]{:S(2)}) copy-start(f32[8,768]{1,0:T(8,128)S(1)} %slice.160) | copy-start | bytes 73732
  357.3 60.1 %collective-permute-start = (bf16[544,2048]{1,0:T(8,128)(2,1)}, bf16[544,2048]{1,0:T(8,128)(2,1)S(1)}, u32[]{:S(2)}, u32[]{:S(2)}) collective-permute-start(bf16[544,2048]{1,0:T(8,128)(2,1)} %get-tuple-element.222.refs_4_.refs_0_), channel_id=1, source_target_pairs={{0,1},{1,0},{2,3},{3,2},{4,5},{5,4},{6,7},{7,6},{8,9},{9,8},{10,11... | collective-permute-start | bytes 6684680 | tf_op jit(solution)/shard_map/ppermute | solution.py:1322
  417.3 55.5 %collective-permute-start.1 = (bf16[544,2048]{1,0:T(8,128)(2,1)S(1)}, bf16[544,2048]{1,0:T(8,128)(2,1)S(1)}, u32[]{:S(2)}, u32[]{:S(2)}) collective-permute-start(bf16[544,2048]{1,0:T(8,128)(2,1)S(1)} %copy-done.9), channel_id=1, source_target_pairs={{0,1},{1,0},{2,3},{3,2},{4,5},{5,4},{6,7},{7,6},{8,9},{9,8},{10,11... | collective-permute-start | bytes 6684680 | tf_op jit(solution)/shard_map/ppermute | solution.py:1322
  499.3 23.5 %collective-permute-start.2 = (bf16[128,3072]{1,0:T(8,128)(2,1)S(1)}, bf16[128,3072]{1,0:T(8,128)(2,1)S(1)}, u32[]{:S(2)}, u32[]{:S(2)}) collective-permute-start(bf16[128,3072]{1,0:T(8,128)(2,1)S(1)} %get-tuple-element.181), channel_id=1, source_target_pairs={{0,8},{4,12},{8,0},{12,4},{16,24},{20,28},{24,16},{28,20},{1,9},{5... | collective-permute-start | bytes 2359304 | tf_op jit(solution)/shard_map/ppermute | solution.py:1322
  500.4 22.4 %collective-permute-start.3 = (bf16[128,3072]{1,0:T(8,128)(2,1)S(1)}, bf16[128,3072]{1,0:T(8,128)(2,1)S(1)}, u32[]{:S(2)}, u32[]{:S(2)}) collective-permute-start(bf16[128,3072]{1,0:T(8,128)(2,1)S(1)} %get-tuple-element.182), channel_id=1, source_target_pairs={{0,16},{4,20},{8,24},{12,28},{16,0},{20,4},{24,8},{28,12},{1,17},{... | collective-permute-start | bytes 2359304 | tf_op jit(solution)/shard_map/ppermute | solution.py:1322
  504.5 50.5 %collective-permute-start.4 = (bf16[544,2048]{1,0:T(8,128)(2,1)S(1)}, bf16[544,2048]{1,0:T(8,128)(2,1)}, u32[]{:S(2)}, u32[]{:S(2)}) collective-permute-start(bf16[544,2048]{1,0:T(8,128)(2,1)S(1)} %copy-done.17), channel_id=1, source_target_pairs={{0,1},{1,0},{2,3},{3,2},{4,5},{5,4},{6,7},{7,6},{8,9},{9,8},{10,11... | collective-permute-start | bytes 6684680 | tf_op jit(solution)/shard_map/ppermute | solution.py:1322
  523.2 61.9 %collective-permute-start.6 = (bf16[256,3072]{1,0:T(8,128)(2,1)S(1)}, bf16[256,3072]{1,0:T(8,128)(2,1)}, u32[]{:S(2)}, u32[]{:S(2)}) collective-permute-start(bf16[256,3072]{1,0:T(8,128)(2,1)S(1)} %pad_maximum_fusion.2), channel_id=1, source_target_pairs={{0,16},{4,20},{8,24},{12,28},{16,0},{20,4},{24,8},{28,12},{1,17},{... | collective-permute-start | bytes 4718600 | tf_op jit(solution)/shard_map/ppermute | solution.py:1322
  525.7 59.4 %collective-permute-start.5 = (bf16[256,3072]{1,0:T(8,128)(2,1)}, bf16[256,3072]{1,0:T(8,128)(2,1)}, u32[]{:S(2)}, u32[]{:S(2)}) collective-permute-start(bf16[256,3072]{1,0:T(8,128)(2,1)} %pad_maximum_fusion.1), channel_id=1, source_target_pairs={{0,8},{4,12},{8,0},{12,4},{16,24},{20,28},{24,16},{28,20},{1,9},{5... | collective-permute-start | bytes 4718600 | tf_op jit(solution)/shard_map/ppermute | solution.py:1322
  526.0 30.4 %slice-start = ((s8[4456448]{0:T(1024)(128)(4,1)}), s8[4194304]{0:T(1024)(128)(4,1)S(1)}, s32[]{:S(2)}) async-start(s8[4456448]{0:T(1024)(128)(4,1)} %bitcast.62), calls=%async_computation.4 | async-start | bytes 8388608
  555.0 61.4 %collective-permute-start.7 = (bf16[544,2048]{1,0:T(8,128)(2,1)}, bf16[544,2048]{1,0:T(8,128)(2,1)S(1)}, u32[]{:S(2)}, u32[]{:S(2)}) collective-permute-start(bf16[544,2048]{1,0:T(8,128)(2,1)} %shard_map.285), channel_id=1, source_target_pairs={{0,1},{1,0},{2,3},{3,2},{4,5},{5,4},{6,7},{7,6},{8,9},{9,8},{10,11... | collective-permute-start | bytes 6684680 | tf_op jit(solution)/shard_map/ppermute | solution.py:1322
  581.4 35.0 %collective-permute-start.8 = (bf16[128,3072]{1,0:T(8,128)(2,1)S(1)}, bf16[128,3072]{1,0:T(8,128)(2,1)}, u32[]{:S(2)}, u32[]{:S(2)}) collective-permute-start(bf16[128,3072]{1,0:T(8,128)(2,1)S(1)} %get-tuple-element.202), channel_id=1, source_target_pairs={{0,8},{4,12},{8,0},{12,4},{16,24},{20,28},{24,16},{28,20},{1,9},{5... | collective-permute-start | bytes 2359304 | tf_op jit(solution)/shard_map/ppermute | solution.py:1322
  581.8 34.6 %collective-permute-start.9 = (bf16[128,3072]{1,0:T(8,128)(2,1)S(1)}, bf16[128,3072]{1,0:T(8,128)(2,1)}, u32[]{:S(2)}, u32[]{:S(2)}) collective-permute-start(bf16[128,3072]{1,0:T(8,128)(2,1)S(1)} %get-tuple-element.203), channel_id=1, source_target_pairs={{0,16},{4,20},{8,24},{12,28},{16,0},{20,4},{24,8},{28,12},{1,17},{... | collective-permute-start | bytes 2359304 | tf_op jit(solution)/shard_map/ppermute | solution.py:1322
  589.3 49.1 %collective-permute-start.10 = (bf16[256,1536]{1,0:T(8,128)(2,1)S(1)}, bf16[256,1536]{1,0:T(8,128)(2,1)}, u32[]{:S(2)}, u32[]{:S(2)}) collective-permute-start(bf16[256,1536]{1,0:T(8,128)(2,1)S(1)} %slice.271), channel_id=1, source_target_pairs={{0,2},{1,3},{2,0},{3,1},{4,6},{5,7},{6,4},{7,5},{8,10},{9,11},{10,... | collective-permute-start | bytes 2359304 | tf_op jit(solution)/shard_map/ppermute | solution.py:1322
  619.3 65.9 %collective-permute-start.12 = (bf16[256,3072]{1,0:T(8,128)(2,1)S(1)}, bf16[256,3072]{1,0:T(8,128)(2,1)}, u32[]{:S(2)}, u32[]{:S(2)}) collective-permute-start(bf16[256,3072]{1,0:T(8,128)(2,1)S(1)} %pad_maximum_fusion.4), channel_id=1, source_target_pairs={{0,16},{4,20},{8,24},{12,28},{16,0},{20,4},{24,8},{28,12},{1,17},{... | collective-permute-start | bytes 4718600 | tf_op jit(solution)/shard_map/ppermute | solution.py:1322
  621.4 63.8 %collective-permute-start.11 = (bf16[256,3072]{1,0:T(8,128)(2,1)}, bf16[256,3072]{1,0:T(8,128)(2,1)S(1)}, u32[]{:S(2)}, u32[]{:S(2)}) collective-permute-start(bf16[256,3072]{1,0:T(8,128)(2,1)} %pad_maximum_fusion.3), channel_id=1, source_target_pairs={{0,8},{4,12},{8,0},{12,4},{16,24},{20,28},{24,16},{28,20},{1,9},{5... | collective-permute-start | bytes 4718600 | tf_op jit(solution)/shard_map/ppermute | solution.py:1322
  638.3 46.8 %copy-start.25 = (bf16[256,3072]{1,0:T(8,128)(2,1)S(1)}, bf16[256,3072]{1,0:T(8,128)(2,1)}, u32[]{:S(2)}) copy-start(bf16[256,3072]{1,0:T(8,128)(2,1)} %get-tuple-element.231) | copy-start | bytes 4718596
  683.1 52.7 %collective-permute-start.14 = (bf16[128,3072]{1,0:T(8,128)(2,1)S(1)}, bf16[128,3072]{1,0:T(8,128)(2,1)S(1)}, u32[]{:S(2)}, u32[]{:S(2)}) collective-permute-start(bf16[128,3072]{1,0:T(8,128)(2,1)S(1)} %get-tuple-element.227), channel_id=1, source_target_pairs={{0,8},{4,12},{8,0},{12,4},{16,24},{20,28},{24,16},{28,20},{1,9},{5... | collective-permute-start | bytes 2359304 | tf_op jit(solution)/shard_map/ppermute | solution.py:1322
  683.9 52.0 %collective-permute-start.15 = (bf16[128,3072]{1,0:T(8,128)(2,1)S(1)}, bf16[128,3072]{1,0:T(8,128)(2,1)S(1)}, u32[]{:S(2)}, u32[]{:S(2)}) collective-permute-start(bf16[128,3072]{1,0:T(8,128)(2,1)S(1)} %get-tuple-element.228), channel_id=1, source_target_pairs={{0,16},{4,20},{8,24},{12,28},{16,0},{20,4},{24,8},{28,12},{1,17},{... | collective-permute-start | bytes 2359304 | tf_op jit(solution)/shard_map/ppermute | solution.py:1322
  687.4 48.5 %collective-permute-start.13 = (bf16[256,1536]{1,0:T(8,128)(2,1)S(1)}, bf16[256,1536]{1,0:T(8,128)(2,1)S(1)}, u32[]{:S(2)}, u32[]{:S(2)}) collective-permute-start(bf16[256,1536]{1,0:T(8,128)(2,1)S(1)} %slice.270), channel_id=1, source_target_pairs={{0,2},{1,3},{2,0},{3,1},{4,6},{5,7},{6,4},{7,5},{8,10},{9,11},{10,... | collective-permute-start | bytes 2359304 | tf_op jit(solution)/shard_map/ppermute | solution.py:1322
  739.3 101.8 %all-to-all-start = ((bf16[4,544,1024]{2,1,0:T(8,128)(2,1)}), bf16[4,544,1024]{2,1,0:T(8,128)(2,1)}, u32[]{:S(2)}, u32[]{:S(2)}) async-start(bf16[4,544,1024]{2,1,0:T(8,128)(2,1)} %bitcast.64), calls=%async_computation | async-start | bytes 8912896 | tf_op jit(solution)/shard_map/all_to_all | solution.py:1350
  745.4 37.7 %collective-permute-start.23 = (bf16[256,3072]{1,0:T(8,128)(2,1)}, bf16[256,3072]{1,0:T(8,128)(2,1)}, u32[]{:S(2)}, u32[]{:S(2)}) collective-permute-start(bf16[256,3072]{1,0:T(8,128)(2,1)} %pad_maximum_fusion.6), channel_id=1, source_target_pairs={{0,16},{4,20},{8,24},{12,28},{16,0},{20,4},{24,8},{28,12},{1,17},{... | collective-permute-start | bytes 4718600 | tf_op jit(solution)/shard_map/ppermute | solution.py:1322
  746.2 37.6 %collective-permute-start.22 = (bf16[256,3072]{1,0:T(8,128)(2,1)}, bf16[256,3072]{1,0:T(8,128)(2,1)}, u32[]{:S(2)}, u32[]{:S(2)}) collective-permute-start(bf16[256,3072]{1,0:T(8,128)(2,1)} %pad_maximum_fusion.5), channel_id=1, source_target_pairs={{0,8},{4,12},{8,0},{12,4},{16,24},{20,28},{24,16},{28,20},{1,9},{5... | collective-permute-start | bytes 4718600 | tf_op jit(solution)/shard_map/ppermute | solution.py:1322
  762.2 89.0 %collective-permute-start.16 = (bf16[128,2048]{1,0:T(8,128)(2,1)S(1)}, bf16[128,2048]{1,0:T(8,128)(2,1)S(1)}, u32[]{:S(2)}, u32[]{:S(2)}) collective-permute-start(bf16[128,2048]{1,0:T(8,128)(2,1)S(1)} %get-tuple-element.247), channel_id=1, source_target_pairs={{0,8},{4,12},{8,0},{12,4},{16,24},{20,28},{24,16},{28,20},{1,9},{5... | collective-permute-start | bytes 1572872 | tf_op jit(solution)/shard_map/ppermute | solution.py:1322
  762.9 88.3 %collective-permute-start.17 = (bf16[128,2048]{1,0:T(8,128)(2,1)S(1)}, bf16[128,2048]{1,0:T(8,128)(2,1)}, u32[]{:S(2)}, u32[]{:S(2)}) collective-permute-start(bf16[128,2048]{1,0:T(8,128)(2,1)S(1)} %get-tuple-element.248), channel_id=1, source_target_pairs={{0,16},{4,20},{8,24},{12,28},{16,0},{20,4},{24,8},{28,12},{1,17},{... | collective-permute-start | bytes 1572872 | tf_op jit(solution)/shard_map/ppermute | solution.py:1322
  773.3 67.7 %copy-start.2 = (f32[544,128]{1,0:T(8,128)S(1)}, f32[544,128]{1,0:T(8,128)}, u32[]{:S(2)}) copy-start(f32[544,128]{1,0:T(8,128)} %copy-done.1) | copy-start | bytes 835588
  773.3 67.7 %copy-start.4 = (f32[544,128]{1,0:T(8,128)S(1)}, f32[544,128]{1,0:T(8,128)}, u32[]{:S(2)}) copy-start(f32[544,128]{1,0:T(8,128)} %copy-done.3) | copy-start | bytes 835588
  852.7 39.8 %collective-permute-start.21 = (bf16[256,2048]{1,0:T(8,128)(2,1)S(1)}, bf16[256,2048]{1,0:T(8,128)(2,1)S(1)}, u32[]{:S(2)}, u32[]{:S(2)}) collective-permute-start(bf16[256,2048]{1,0:T(8,128)(2,1)S(1)} %pad_maximum_fusion.8), channel_id=1, source_target_pairs={{0,16},{4,20},{8,24},{12,28},{16,0},{20,4},{24,8},{28,12},{1,17},{... | collective-permute-start | bytes 3145736 | tf_op jit(solution)/shard_map/ppermute | solution.py:1322
  853.5 39.0 %collective-permute-start.20 = (bf16[256,2048]{1,0:T(8,128)(2,1)S(1)}, bf16[256,2048]{1,0:T(8,128)(2,1)S(1)}, u32[]{:S(2)}, u32[]{:S(2)}) collective-permute-start(bf16[256,2048]{1,0:T(8,128)(2,1)S(1)} %pad_maximum_fusion.7), channel_id=1, source_target_pairs={{0,8},{4,12},{8,0},{12,4},{16,24},{20,28},{24,16},{28,20},{1,9},{5... | collective-permute-start | bytes 3145736 | tf_op jit(solution)/shard_map/ppermute | solution.py:1322
  857.6 34.9 %collective-permute-start.24 = (bf16[256,1536]{1,0:T(8,128)(2,1)S(1)}, bf16[256,1536]{1,0:T(8,128)(2,1)S(1)}, u32[]{:S(2)}, u32[]{:S(2)}) collective-permute-start(bf16[256,1536]{1,0:T(8,128)(2,1)S(1)} %slice.269), channel_id=1, source_target_pairs={{0,2},{1,3},{2,0},{3,1},{4,6},{5,7},{6,4},{7,5},{8,10},{9,11},{10,... | collective-permute-start | bytes 2359304 | tf_op jit(solution)/shard_map/ppermute | solution.py:1322
  872.0 20.5 %collective-permute-start.18 = (bf16[128,2048]{1,0:T(8,128)(2,1)S(1)}, bf16[128,2048]{1,0:T(8,128)(2,1)}, u32[]{:S(2)}, u32[]{:S(2)}) collective-permute-start(bf16[128,2048]{1,0:T(8,128)(2,1)S(1)} %get-tuple-element.262), channel_id=1, source_target_pairs={{0,8},{4,12},{8,0},{12,4},{16,24},{20,28},{24,16},{28,20},{1,9},{5... | collective-permute-start | bytes 1572872 | tf_op jit(solution)/shard_map/ppermute | solution.py:1322
  872.7 19.8 %collective-permute-start.19 = (bf16[128,2048]{1,0:T(8,128)(2,1)S(1)}, bf16[128,2048]{1,0:T(8,128)(2,1)}, u32[]{:S(2)}, u32[]{:S(2)}) collective-permute-start(bf16[128,2048]{1,0:T(8,128)(2,1)S(1)} %get-tuple-element.263), channel_id=1, source_target_pairs={{0,16},{4,20},{8,24},{12,28},{16,0},{20,4},{24,8},{28,12},{1,17},{... | collective-permute-start | bytes 1572872 | tf_op jit(solution)/shard_map/ppermute | solution.py:1322
  894.2 45.7 %all-to-all-start.1 = ((bf16[4,256,512]{2,1,0:T(8,128)(2,1)}), bf16[4,256,512]{2,1,0:T(8,128)(2,1)}, u32[]{:S(2)}, u32[]{:S(2)}) async-start(bf16[4,256,512]{2,1,0:T(8,128)(2,1)} %bitcast.49), calls=%async_computation.1 | async-start | bytes 2097152 | tf_op jit(solution)/shard_map/all_to_all | solution.py:1350
  902.2 37.7 %collective-permute-start.26 = (bf16[256,2048]{1,0:T(8,128)(2,1)}, bf16[256,2048]{1,0:T(8,128)(2,1)}, u32[]{:S(2)}, u32[]{:S(2)}) collective-permute-start(bf16[256,2048]{1,0:T(8,128)(2,1)} %pad_maximum_fusion.10), channel_id=1, source_target_pairs={{0,16},{4,20},{8,24},{12,28},{16,0},{20,4},{24,8},{28,12},{1,17},{... | collective-permute-start | bytes 3145736 | tf_op jit(solution)/shard_map/ppermute | solution.py:1322
  903.6 36.4 %collective-permute-start.25 = (bf16[256,2048]{1,0:T(8,128)(2,1)}, bf16[256,2048]{1,0:T(8,128)(2,1)}, u32[]{:S(2)}, u32[]{:S(2)}) collective-permute-start(bf16[256,2048]{1,0:T(8,128)(2,1)} %pad_maximum_fusion.9), channel_id=1, source_target_pairs={{0,8},{4,12},{8,0},{12,4},{16,24},{20,28},{24,16},{28,20},{1,9},{5... | collective-permute-start | bytes 3145736 | tf_op jit(solution)/shard_map/ppermute | solution.py:1322
  907.8 32.1 %collective-permute-start.27 = (bf16[128,2048]{1,0:T(8,128)(2,1)S(1)}, bf16[128,2048]{1,0:T(8,128)(2,1)}, u32[]{:S(2)}, u32[]{:S(2)}) collective-permute-start(bf16[128,2048]{1,0:T(8,128)(2,1)S(1)} %get-tuple-element.265), channel_id=1, source_target_pairs={{0,8},{4,12},{8,0},{12,4},{16,24},{20,28},{24,16},{28,20},{1,9},{5... | collective-permute-start | bytes 1572872 | tf_op jit(solution)/shard_map/ppermute | solution.py:1322
  908.6 31.3 %collective-permute-start.28 = (bf16[128,2048]{1,0:T(8,128)(2,1)S(1)}, bf16[128,2048]{1,0:T(8,128)(2,1)}, u32[]{:S(2)}, u32[]{:S(2)}) collective-permute-start(bf16[128,2048]{1,0:T(8,128)(2,1)S(1)} %get-tuple-element.266), channel_id=1, source_target_pairs={{0,16},{4,20},{8,24},{12,28},{16,0},{20,4},{24,8},{28,12},{1,17},{... | collective-permute-start | bytes 1572872 | tf_op jit(solution)/shard_map/ppermute | solution.py:1322
  942.4 25.7 %collective-permute-start.35 = (bf16[256,2048]{1,0:T(8,128)(2,1)}, bf16[256,2048]{1,0:T(8,128)(2,1)}, u32[]{:S(2)}, u32[]{:S(2)}) collective-permute-start(bf16[256,2048]{1,0:T(8,128)(2,1)} %pad_maximum_fusion.12), channel_id=1, source_target_pairs={{0,16},{4,20},{8,24},{12,28},{16,0},{20,4},{24,8},{28,12},{1,17},{... | collective-permute-start | bytes 3145736 | tf_op jit(solution)/shard_map/ppermute | solution.py:1322
  946.4 24.0 %collective-permute-start.34 = (bf16[256,2048]{1,0:T(8,128)(2,1)}, bf16[256,2048]{1,0:T(8,128)(2,1)}, u32[]{:S(2)}, u32[]{:S(2)}) collective-permute-start(bf16[256,2048]{1,0:T(8,128)(2,1)} %pad_maximum_fusion.11), channel_id=1, source_target_pairs={{0,8},{4,12},{8,0},{12,4},{16,24},{20,28},{24,16},{28,20},{1,9},{5... | collective-permute-start | bytes 3145736 | tf_op jit(solution)/shard_map/ppermute | solution.py:1322
  949.8 28.6 %all-to-all-start.2 = ((bf16[4,256,512]{2,1,0:T(8,128)(2,1)}), bf16[4,256,512]{2,1,0:T(8,128)(2,1)S(1)}, u32[]{:S(2)}, u32[]{:S(2)}) async-start(bf16[4,256,512]{2,1,0:T(8,128)(2,1)} %bitcast.66), calls=%async_computation.2 | async-start | bytes 2097152 | tf_op jit(solution)/shard_map/all_to_all | solution.py:1350
  958.2 3.0 collective-permute-start.29
  961.3 5.4 collective-permute-start.30
  966.7 15.9 %collective-permute-start.31 = (f32[1,544]{1,0:T(1,128)S(1)}, f32[1,544]{1,0:T(1,128)S(1)}, u32[]{:S(2)}, u32[]{:S(2)}) collective-permute-start(f32[1,544]{1,0:T(1,128)S(1)} %slice.229), channel_id=1, source_target_pairs={{0,8},{4,12},{8,0},{12,4},{16,24},{20,28},{24,16},{28,20},{1,9},{5... | collective-permute-start | bytes 6536 | tf_op jit(solution)/shard_map/ppermute | solution.py:1322
  978.4 36.4 %all-to-all-start.3 = ((bf16[4,256,512]{2,1,0:T(8,128)(2,1)}), bf16[4,256,512]{2,1,0:T(8,128)(2,1)}, u32[]{:S(2)}, u32[]{:S(2)}) async-start(bf16[4,256,512]{2,1,0:T(8,128)(2,1)} %bitcast.67), calls=%async_computation.3 | async-start | bytes 2097152 | tf_op jit(solution)/shard_map/all_to_all | solution.py:1350
  982.7 16.6 %collective-permute-start.32 = (f32[1,544]{1,0:T(1,128)S(1)}, f32[1,544]{1,0:T(1,128)S(1)}, u32[]{:S(2)}, u32[]{:S(2)}) collective-permute-start(f32[1,544]{1,0:T(1,128)S(1)} %slice_add_fusion.5), channel_id=1, source_target_pairs={{0,1},{1,0},{2,3},{3,2},{4,5},{5,4},{6,7},{7,6},{8,9},{9,8},{10,11... | collective-permute-start | bytes 6536 | tf_op jit(solution)/shard_map/ppermute | solution.py:1322
  999.3 13.4 %collective-permute-start.33 = (f32[1,544]{1,0:T(1,128)S(1)}, f32[1,544]{1,0:T(1,128)S(1)}, u32[]{:S(2)}, u32[]{:S(2)}) collective-permute-start(f32[1,544]{1,0:T(1,128)S(1)} %add.204), channel_id=1, source_target_pairs={{0,2},{1,3},{2,0},{3,1},{4,6},{5,7},{6,4},{7,5},{8,10},{9,11},{10,... | collective-permute-start | bytes 6536 | tf_op jit(solution)/shard_map/ppermute | solution.py:1322
  (40 other events, 324.6 us)

commit v6 on v5

--- a/solution.py
+++ b/solution.py
@@ -1503,6 +1503,7 @@
     while size > 1:
         size //= 2
         parts = parts[:size] + over("wide", parts[size:], order[size])
+    parts = after(parts, tokens_grad)
     step = 1
     while step < n:
         parts = parts + over("tp", parts, step)

time: 1020 us -> 1020 us (level)
  no operation moved by 1% of the time
where the time goes in v6:
time: 1020 us; the launch traced here: 1010 us
  Pallas kernels  725 us (71%)
  waiting for transfers between devices  102 us (10%)
  starting transfers between devices  78.1 us (8%)
  other arithmetic  75.6 us (7%)
  local copies, waits for them, and re-layouts  28.7 us (3%)
    pallas_call x3, Pallas kernels, transfer_call(): pl.pallas_call(kernel, in_specs=[pl.BlockSpec(memory_space=pltpu.VMEM if...  308 us
    pallas_call x11, Pallas kernels, tiled_call(): pl.pallas_call(kernel, grid_spec=pltpu.PrefetchScalarGridSpec(num_scalar_...  203 us
    pallas_call x6, Pallas kernels, gradient_pair(): pl.pallas_call(kernel, grid=(2 * steps,), in_specs=[pl.BlockSpec((rows, s...  133 us
    ppermute x36, starting transfers between devices, over(): return lax.ppermute(a, axis, [(i, i ^ mask) for i in range(size)])  59.2 us
    all_to_all x4, waiting for transfers between devices, swap(): return lax.all_to_all(a, 'tp', split_axis=0, concat_axis=0, tiled=True)  57.7 us
    ppermute x36, waiting for transfers between devices, over(): return lax.ppermute(a, axis, [(i, i ^ mask) for i in range(size)])  44.5 us
    pallas_call x1, Pallas kernels, attention_backward(): pl.pallas_call(kernel, grid_spec=pltpu.PrefetchScalarGridSpec(num_scalar_...  37.3 us
    pallas_call x1, Pallas kernels, attention_forward(): pl.pallas_call(kernel, grid_spec=pltpu.PrefetchScalarGridSpec(num_scalar_...  20.6 us
  transfers between devices with their start and end apart: 40, of which 12 were waited for; matrix products, arithmetic and copies ran while one was open for 7% of the time, Pallas kernels for 35%

profile of v6, /device:TPU:0, one launch (start us, length us, event | category | flops | bytes accessed | tf_op | source)
XLA Modules:
  0.0 1011.9 jit_solution(2966128783626723806)
XLA Ops:
  3.6 2.3 copy.47
  12.6 148.0 %shard_map.273 = (bf16[4,2048,1024]{2,1,0:T(8,128)(2,1)}, bf16[1,2048,3072]{2,1,0:T(8,128)(2,1)}, bf16[1,2048,3072]{2,1,0:T(8,128)(2,1)}, bf16[1,2048,1536]{2,1,...) custom-call(bf16[256,1024]{1,0:T(8,128)(2,1)S(1)} %pad_maximum_fusio, ...), custom_call_target="tpu_custom_call" | custom-call | bytes 10000 | tf_op jit(solution)/shard_map/pallas_call | solution.py:659
  161.3 119.0 %shard_map.274 = (bf16[4,544,1024]{2,1,0:T(8,128)(2,1)}, bf16[1,2048,3072]{2,1,0:T(8,128)(2,1)}, bf16[4,2048,512]{2,1,0:T(8,128)(2,1)}, bf16[1,2048,1536]{2,1,0:T(8,128)(2,1)}) custom-call(bf16[4,544,1024]{2,1,0:T(8,128)(2,1)} %get-tuple-element.156.refs_0_, bf16[1,2048,3072]{2,1,0:T(8,128)(2,1)} %get-tuple-element.157.refs_1_, ...), custom_call_target="tpu_custom_call", output_to_operand_aliasing={{1}: (1, {})} | custom-call | bytes 10000 | tf_op jit(solution)/shard_map/pallas_call | solution.py:659
  280.3 20.6 %shard_map.275 = (bf16[2176,512]{1,0:T(8,128)(2,1)}, f32[2,17,256]{2,1,0:T(8,128)S(1)}) custom-call(s32[8]{0:T(128)S(1)} %fusion.4.parent_ref, bf16[2176,1024]{1,0:T(8,128)(2,1)} %bitcast.56, bf16[2176,1024]{1,0:T(8,128)(2,1)} %bitcast.57, bf16[2176,1024]{1,0:T(8,128)(2,1)} %bitcast.58), custom_call_target="tpu_custom_call" | custom-call | flops 90112000 | bytes 67194 | tf_op jit(solution)/shard_map/pallas_call | solution.py:434
  300.9 41.3 %shard_map.276 = (bf16[4,544,512]{2,1,0:T(8,128)(2,1)}, bf16[1,2048,1536]{2,1,0:T(8,128)(2,1)}) custom-call(bf16[4,544,512]{2,1,0:T(8,128)(2,1)} %bitcast.65, bf16[1,2048,1536]{2,1,0:T(8,128)(2,1)} %get-tuple-element.161.refs_1_), custom_call_target="tpu_custom_call", output_to_operand_aliasing={{1}: (1, {})} | custom-call | bytes 10000 | tf_op jit(solution)/shard_map/pallas_call | solution.py:659
  342.2 15.1 %shard_map.277 = (f32[544,2048]{1,0:T(8,128)}, bf16[544,2048]{1,0:T(8,128)(2,1)}) custom-call(s32[4]{0:T(128)S(1)} %iota_xor_fusion.seat_ref, bf16[4,2048,512]{2,1,0:T(8,128)(2,1)} %get-tuple-element.160.refs_0_, bf16[4,544,512]{2,1,0:T(8,128)(2,1)} %get-tuple-element.162.refs_1_, bf16[544,2048]{1,0:T(8,128)(2,1)} %get-tuple-element.243.refs_2_, ...), custom_call_target="tpu_custom_call" | custom-call | flops 45634028 | bytes 195379 | tf_op jit(solution)/shard_map/pallas_call | solution.py:137
  357.3 11.6 %collective-permute-start = (bf16[544,2048]{1,0:T(8,128)(2,1)}, bf16[544,2048]{1,0:T(8,128)(2,1)S(1)}, u32[]{:S(2)}, u32[]{:S(2)}) collective-permute-start(bf16[544,2048]{1,0:T(8,128)(2,1)} %get-tuple-element.223.refs_4_.refs_0_), channel_id=1, source_target_pairs={{0,1},{1,0},{2,3},{3,2},{4,5},{5,4},{6,7},{7,6},{8,9},{9,8},{10,11... | collective-permute-start | bytes 6684680 | tf_op jit(solution)/shard_map/ppermute | solution.py:1322
  368.9 21.4 %shard_map.278 = (bf16[2,544,1536]{2,1,0:T(8,128)(2,1)}, bf16[2,544,1536]{2,1,0:T(8,128)(2,1)}, bf16[2,544,1536]{2,1,0:T(8,128)(2,1)}) custom-call(s32[4]{0:T(128)S(1)} %iota.46.seat_ref, bf16[1,2048,3072]{2,1,0:T(8,128)(2,1)} %get-tuple-element.169.refs_0_.refs_2_, bf16[1,2048,3072]{2,1,0:T(8,128)(2,1)} %get-tuple-element.170.refs_1_.refs_3_, ...), custom_call_target="tpu_custom_call" | custom-call | flops 136902080 | bytes 625868 | tf_op jit(solution)/shard_map/pallas_call | solution.py:137
  390.3 16.5 %shard_map.279 = f32[544,2048]{1,0:T(8,128)} custom-call(s32[4]{0:T(128)S(1)} %iota.45.seat_ref, bf16[1,2048,1536]{2,1,0:T(8,128)(2,1)} %get-tuple-element.167.refs_0_, bf16[1,2048,1536]{2,1,0:T(8,128)(2,1)} %get-tuple-element.168.refs_1_, bf16[2,544,1536]{2,1,0:T(8,128)(2,1)} %get-tuple-element.181.refs_2_), custom_call_target="tpu_custom_call" | custom-call | flops 68451040 | bytes 203816 | tf_op jit(solution)/shard_map/pallas_call | solution.py:137
  406.8 10.6 %collective-permute-done.refs_4_.refs_1_ = bf16[544,2048]{1,0:T(8,128)(2,1)S(1)} collective-permute-done((bf16[544,2048]{1,0:T(8,128)(2,1)}, bf16[544,2048]{1,0:T(8,128)(2,1)S(1)}, u32[]{:S(2)}, u32[]{:S(2)}) %collective-permute-start) | collective-permute-done | bytes 2228256 | tf_op jit(solution)/shard_map/ppermute | solution.py:1322
  419.1 21.3 %shard_map.280 = (bf16[2,544,1536]{2,1,0:T(8,128)(2,1)}, bf16[2,544,1536]{2,1,0:T(8,128)(2,1)}, bf16[2,544,1536]{2,1,0:T(8,128)(2,1)}) custom-call(s32[4]{0:T(128)S(1)} %iota.49.seat_ref, bf16[1,2048,3072]{2,1,0:T(8,128)(2,1)} %get-tuple-element.169.refs_0_.refs_2_, bf16[1,2048,3072]{2,1,0:T(8,128)(2,1)} %get-tuple-element.170.refs_1_.refs_3_, ...), custom_call_target="tpu_custom_call" | custom-call | flops 136902080 | bytes 625868 | tf_op jit(solution)/shard_map/pallas_call | solution.py:137
  440.4 15.6 %shard_map.281 = bf16[544,2048]{1,0:T(8,128)(2,1)} custom-call(s32[4]{0:T(128)S(1)} %iota.48.seat_ref, bf16[1,2048,1536]{2,1,0:T(8,128)(2,1)} %get-tuple-element.167.refs_0_, bf16[1,2048,1536]{2,1,0:T(8,128)(2,1)} %get-tuple-element.168.refs_1_, bf16[2,544,1536]{2,1,0:T(8,128)(2,1)} %get-tuple-element.173.refs_2_.refs_3_), custom_call_target="tpu_custom_call" | custom-call | flops 68451040 | bytes 181534 | tf_op jit(solution)/shard_map/pallas_call | solution.py:137
  456.0 16.8 %shard_map.282 = (bf16[2,544,1536]{2,1,0:T(8,128)(2,1)}, bf16[2,544,1536]{2,1,0:T(8,128)(2,1)}) custom-call(s32[4]{0:T(128)S(1)} %iota.47.seat_ref, bf16[1,2048,1536]{2,1,0:T(8,128)(2,1)} %get-tuple-element.167.refs_0_, bf16[1,2048,1536]{2,1,0:T(8,128)(2,1)} %get-tuple-element.168.refs_1_, bf16[544,2048]{1,0:T(8,128)(2,1)} %get-tuple-element.179.refs_2_.refs_0_, ...), custom_call_target="tpu_custom_call" | custom-call | flops 68451040 | bytes 281804 | tf_op jit(solution)/shard_map/pallas_call | solution.py:137
  474.2 24.8 %shard_map.283 = (bf16[256,3072]{1,0:T(8,128)(2,1)}, bf16[256,3072]{1,0:T(8,128)(2,1)}, bf16[256,3072]{1,0:T(8,128)(2,1)}, bf16[128,3072]{1,0:T(8,128)(2,1)S(1)}, bf16[128,3072]{1,0:T(8,128)(2,1)S(1)}) custom-call(bf16[544,2048]{1,0:T(8,128)(2,1)} %get-tuple-element.179.refs_2_.refs_0_, bf16[544,2048]{1,0:T(8,128)(2,1)} %copy-done.17, ...), custom_call_target="tpu_custom_call" | custom-call | flops 136902080 | bytes 174325 | tf_op jit(solution)/shard_map/pallas_call | solution.py:819
  505.7 16.8 %shard_map.284 = (bf16[2,544,1536]{2,1,0:T(8,128)(2,1)}, bf16[2,544,1536]{2,1,0:T(8,128)(2,1)}) custom-call(s32[4]{0:T(128)S(1)} %iota.51.seat_ref, bf16[1,2048,1536]{2,1,0:T(8,128)(2,1)} %get-tuple-element.167.refs_0_, bf16[1,2048,1536]{2,1,0:T(8,128)(2,1)} %get-tuple-element.168.refs_1_, bf16[544,2048]{1,0:T(8,128)(2,1)} %copy-done.17, ...), custom_call_target="tpu_custom_call" | custom-call | flops 68451040 | bytes 281804 | tf_op jit(solution)/shard_map/pallas_call | solution.py:137
  525.7 24.3 %shard_map.285 = bf16[544,2048]{1,0:T(8,128)(2,1)} custom-call(s32[4]{0:T(128)S(1)} %iota.50.seat_ref, bf16[1,2048,3072]{2,1,0:T(8,128)(2,1)} %get-tuple-element.169.refs_0_.refs_2_, bf16[1,2048,3072]{2,1,0:T(8,128)(2,1)} %get-tuple-element.170.refs_1_.refs_3_, bf16[1,2048,3072]{2,1,0:T(8,128)(2,1)} %get-tuple-element.169.refs_0_.refs_2_, ...), custom_call_target="tpu_custom_call" | custom-call | flops 136902080 | bytes 592445 | tf_op jit(solution)/shard_map/pallas_call | solution.py:137
  550.0 4.7 collective-permute-done.4
  556.5 24.4 %shard_map.286 = (bf16[256,3072]{1,0:T(8,128)(2,1)}, bf16[256,3072]{1,0:T(8,128)(2,1)}, bf16[256,3072]{1,0:T(8,128)(2,1)}, bf16[128,3072]{1,0:T(8,128)(2,1)S(1)}, bf16[128,3072]{1,0:T(8,128)(2,1)S(1)}) custom-call(bf16[544,2048]{1,0:T(8,128)(2,1)} %get-tuple-element.223.refs_4_.refs_0_, bf16[544,2048]{1,0:T(8,128)(2,1)} %copy-done.11, ...), custom_call_target="tpu_custom_call" | custom-call | flops 136902080 | bytes 174325 | tf_op jit(solution)/shard_map/pallas_call | solution.py:819
  584.7 2.5 convert_add_fusion.3
  589.7 24.9 %shard_map.287 = f32[544,2048]{1,0:T(8,128)} custom-call(s32[4]{0:T(128)S(1)} %iota.52.seat_ref, bf16[1,2048,3072]{2,1,0:T(8,128)(2,1)} %get-tuple-element.169.refs_0_.refs_2_, bf16[1,2048,3072]{2,1,0:T(8,128)(2,1)} %get-tuple-element.170.refs_1_.refs_3_, bf16[1,2048,3072]{2,1,0:T(8,128)(2,1)} %get-tuple-element.169.refs_0_.refs_2_, ...), custom_call_target="tpu_custom_call" | custom-call | flops 136902080 | bytes 614727 | tf_op jit(solution)/shard_map/pallas_call | solution.py:137
  623.6 4.2 fusion.5
  627.7 10.5 %shard_map.288.refs_4_ = bf16[4,544,512]{2,1,0:T(8,128)(2,1)} custom-call(s32[4]{0:T(128)S(1)} %iota_xor_fusion.seat_ref, bf16[4,2048,512]{2,1,0:T(8,128)(2,1)} %get-tuple-element.160.refs_0_, bf16[544,2048]{1,0:T(8,128)(2,1)} %get-tuple-element.247.refs_1_.refs_0_), custom_call_target="tpu_custom_call" | custom-call | flops 45634028 | bytes 128450 | tf_op jit(solution)/shard_map/pallas_call | solution.py:137
  638.3 44.9 %shard_map.289 = (bf16[256,3072]{1,0:T(8,128)(2,1)}, bf16[256,3072]{1,0:T(8,128)(2,1)}, bf16[256,3072]{1,0:T(8,128)(2,1)}, bf16[128,3072]{1,0:T(8,128)(2,1)S(1)}...) custom-call(bf16[544,2048]{1,0:T(8,128)(2,1)} %get-tuple-element.223.refs_4_.refs_0_, ...), custom_call_target="tpu_custom_call" | custom-call | flops 136902080 | bytes 174325 | tf_op jit(solution)/shard_map/pallas_call | solution.py:819
  687.4 10.6 %collective-permute-start.13 = (bf16[256,1536]{1,0:T(8,128)(2,1)S(1)}, bf16[256,1536]{1,0:T(8,128)(2,1)S(1)}, u32[]{:S(2)}, u32[]{:S(2)}) collective-permute-start(bf16[256,1536]{1,0:T(8,128)(2,1)S(1)} %slice.270), channel_id=1, source_target_pairs={{0,2},{1,3},{2,0},{3,1},{4,6},{5,7},{6,4},{7,5},{8,10},{9,11},{10,... | collective-permute-start | bytes 2359304 | tf_op jit(solution)/shard_map/ppermute | solution.py:1322
  698.2 37.3 %shard_map.290 = bf16[2176,1024]{1,0:T(8,128)(2,1)} custom-call(s32[8]{0:T(128)S(1)} %fusion.4.parent_ref, bf16[2176,1024]{1,0:T(8,128)(2,1)} %bitcast.59, bf16[2176,1024]{1,0:T(8,128)(2,1)} %bitcast.60, bf16[2176,1024]{1,0:T(8,128)(2,1)} %bitcast.61, bf16[2176,512]{1,0:T(8,128)(2,1)} %get-tuple-element.159.o_ref, bf16[2176,512]{1,0:T(8,128)(2,1)} %bitcast.70, ...), custom_call_target="tpu_custom_call" | custom-call | flops 225280000 | bytes 133693 | tf_op jit(solution)/shard_map/pallas_call | solution.py:524
  738.9 5.5 all-to-all-start
  749.0 12.8 %shard_map.292 = (bf16[256,2048]{1,0:T(8,128)(2,1)}, bf16[256,2048]{1,0:T(8,128)(2,1)}, bf16[256,2048]{1,0:T(8,128)(2,1)}, bf16[128,2048]{1,0:T(8,128)(2,1)S(1)}, bf16[128,2048]{1,0:T(8,128)(2,1)S(1)}) custom-call(bf16[544,2048]{1,0:T(8,128)(2,1)} %get-tuple-element.247.refs_1_.refs_0_, bf16[4,544,512]{2,1,0:T(8,128)(2,1)} %get-tuple-element.162.refs_1_), custom_call_target="tpu_custom_call" | custom-call | flops 45634028 | bytes 86507 | tf_op jit(solution)/shard_map/pallas_call | solution.py:819
  766.0 6.9 add_convert_fusion.1.in_ref
  772.9 6.5 shard_map.291
  779.4 3.3 collective-permute-done.23
  783.5 56.8 %all-to-all-done.g_ref = bf16[4,544,1024]{2,1,0:T(8,128)(2,1)} async-done(((bf16[4,544,1024]{2,1,0:T(8,128)(2,1)}), bf16[4,544,1024]{2,1,0:T(8,128)(2,1)}, u32[]{:S(2)}, u32[]{:S(2)}) %all-to-all-start) | async-done | bytes 4456480 | tf_op jit(solution)/shard_map/all_to_all | solution.py:1350
  840.3 10.1 shard_map.293
  854.1 2.5 convert_add_fusion.1
  858.2 12.8 %shard_map.294 = (bf16[256,2048]{1,0:T(8,128)(2,1)}, bf16[256,2048]{1,0:T(8,128)(2,1)}, bf16[256,2048]{1,0:T(8,128)(2,1)}, bf16[128,2048]{1,0:T(8,128)(2,1)S(1)}, bf16[128,2048]{1,0:T(8,128)(2,1)S(1)}) custom-call(bf16[544,2048]{1,0:T(8,128)(2,1)} %get-tuple-element.257.refs_0_, bf16[4,544,1024]{2,1,0:T(8,128)(2,1)} %get-tuple-element.277.refs_1_), custom_call_target="tpu_custom_call" | custom-call | flops 45634028 | bytes 108789 | tf_op jit(solution)/shard_map/pallas_call | solution.py:819
  873.2 13.0 %shard_map.295 = (bf16[256,2048]{1,0:T(8,128)(2,1)}, bf16[256,2048]{1,0:T(8,128)(2,1)}, bf16[256,2048]{1,0:T(8,128)(2,1)}, bf16[128,2048]{1,0:T(8,128)(2,1)S(1)}, bf16[128,2048]{1,0:T(8,128)(2,1)S(1)}) custom-call(bf16[544,2048]{1,0:T(8,128)(2,1)} %get-tuple-element.257.refs_0_, bf16[4,544,1024]{2,1,0:T(8,128)(2,1)} %get-tuple-element.277.refs_1_), custom_call_target="tpu_custom_call" | custom-call | flops 45634028 | bytes 108789 | tf_op jit(solution)/shard_map/pallas_call | solution.py:819
  886.3 4.8 collective-permute-done.24
  892.7 4.4 all-to-all-start.1
  908.9 2.9 slice_add_fusion.2
  915.1 19.9 %shard_map.296 = f32[544,2048]{1,0:T(8,128)} custom-call(s32[4]{0:T(128)S(1)} %iota_xor_fusion.seat_ref, bf16[4,2048,1024]{2,1,0:T(8,128)(2,1)} %get-tuple-element.252.refs_0_, bf16[4,544,1024]{2,1,0:T(8,128)(2,1)} %get-tuple-element.277.refs_1_), custom_call_target="tpu_custom_call" | custom-call | flops 91268056 | bytes 256901 | tf_op jit(solution)/shard_map/pallas_call | solution.py:137
  935.1 3.4 collective-permute-done.27
  947.3 4.8 all-to-all-start.2
  952.1 3.6 multiply_reduce_fusion.1
  958.3 6.3 add_convert_fusion.in_ref
  964.6 6.5 shard_map.297
  976.1 4.3 all-to-all-start.3
  982.5 2.5 slice_add_fusion.1
  985.0 12.4 %collective-permute-done.32 = f32[1,544]{1,0:T(1,128)S(1)} collective-permute-done((f32[1,544]{1,0:T(1,128)S(1)}, f32[1,544]{1,0:T(1,128)S(1)}, u32[]{:S(2)}, u32[]{:S(2)}) %collective-permute-start.32) | collective-permute-done | bytes 2208 | tf_op jit(solution)/shard_map/ppermute | solution.py:1322
  997.3 4.5 collective-permute-start.33
  (292 shorter events, 109.5 us)
Async XLA Ops:
  12.5 148.1 %copy-start.1 = (f32[544,128]{1,0:T(8,128)}, f32[544,128]{1,0:T(8,128)S(1)}, u32[]{:S(2)}) copy-start(f32[544,128]{1,0:T(8,128)S(1)} %get-tuple-element.376.refs_6_.cos_ref) | copy-start | bytes 835588
  12.5 148.1 %copy-start.3 = (f32[544,128]{1,0:T(8,128)}, f32[544,128]{1,0:T(8,128)S(1)}, u32[]{:S(2)}) copy-start(f32[544,128]{1,0:T(8,128)S(1)} %get-tuple-element.377.refs_7_.sin_ref) | copy-start | bytes 835588
  12.6 148.7 %copy-start = (bf16[1536,256]{0,1:T(8,128)(2,1)S(1)}, bf16[1536,256]{0,1:T(8,128)(2,1)}, u32[]{:S(2)}) copy-start(bf16[1536,256]{0,1:T(8,128)(2,1)} %copy.47) | copy-start | bytes 2359300
  160.7 119.6 %copy-start.44 = (f32[8,768]{1,0:T(8,128)}, f32[8,768]{1,0:T(8,128)S(1)}, u32[]{:S(2)}) copy-start(f32[8,768]{1,0:T(8,128)S(1)} %slice.160) | copy-start | bytes 73732
  357.3 60.1 %collective-permute-start = (bf16[544,2048]{1,0:T(8,128)(2,1)}, bf16[544,2048]{1,0:T(8,128)(2,1)S(1)}, u32[]{:S(2)}, u32[]{:S(2)}) collective-permute-start(bf16[544,2048]{1,0:T(8,128)(2,1)} %get-tuple-element.223.refs_4_.refs_0_), channel_id=1, source_target_pairs={{0,1},{1,0},{2,3},{3,2},{4,5},{5,4},{6,7},{7,6},{8,9},{9,8},{10,11... | collective-permute-start | bytes 6684680 | tf_op jit(solution)/shard_map/ppermute | solution.py:1322
  417.3 55.5 %collective-permute-start.1 = (bf16[544,2048]{1,0:T(8,128)(2,1)S(1)}, bf16[544,2048]{1,0:T(8,128)(2,1)S(1)}, u32[]{:S(2)}, u32[]{:S(2)}) collective-permute-start(bf16[544,2048]{1,0:T(8,128)(2,1)S(1)} %copy-done.9), channel_id=1, source_target_pairs={{0,1},{1,0},{2,3},{3,2},{4,5},{5,4},{6,7},{7,6},{8,9},{9,8},{10,11... | collective-permute-start | bytes 6684680 | tf_op jit(solution)/shard_map/ppermute | solution.py:1322
  499.0 23.5 %collective-permute-start.2 = (bf16[128,3072]{1,0:T(8,128)(2,1)S(1)}, bf16[128,3072]{1,0:T(8,128)(2,1)S(1)}, u32[]{:S(2)}, u32[]{:S(2)}) collective-permute-start(bf16[128,3072]{1,0:T(8,128)(2,1)S(1)} %get-tuple-element.182), channel_id=1, source_target_pairs={{0,8},{4,12},{8,0},{12,4},{16,24},{20,28},{24,16},{28,20},{1,9},{5... | collective-permute-start | bytes 2359304 | tf_op jit(solution)/shard_map/ppermute | solution.py:1322
  500.1 22.4 %collective-permute-start.3 = (bf16[128,3072]{1,0:T(8,128)(2,1)S(1)}, bf16[128,3072]{1,0:T(8,128)(2,1)S(1)}, u32[]{:S(2)}, u32[]{:S(2)}) collective-permute-start(bf16[128,3072]{1,0:T(8,128)(2,1)S(1)} %get-tuple-element.183), channel_id=1, source_target_pairs={{0,16},{4,20},{8,24},{12,28},{16,0},{20,4},{24,8},{28,12},{1,17},{... | collective-permute-start | bytes 2359304 | tf_op jit(solution)/shard_map/ppermute | solution.py:1322
  504.3 50.5 %collective-permute-start.4 = (bf16[544,2048]{1,0:T(8,128)(2,1)S(1)}, bf16[544,2048]{1,0:T(8,128)(2,1)}, u32[]{:S(2)}, u32[]{:S(2)}) collective-permute-start(bf16[544,2048]{1,0:T(8,128)(2,1)S(1)} %copy-done.18), channel_id=1, source_target_pairs={{0,1},{1,0},{2,3},{3,2},{4,5},{5,4},{6,7},{7,6},{8,9},{9,8},{10,11... | collective-permute-start | bytes 6684680 | tf_op jit(solution)/shard_map/ppermute | solution.py:1322
  522.9 61.8 %collective-permute-start.6 = (bf16[256,3072]{1,0:T(8,128)(2,1)S(1)}, bf16[256,3072]{1,0:T(8,128)(2,1)}, u32[]{:S(2)}, u32[]{:S(2)}) collective-permute-start(bf16[256,3072]{1,0:T(8,128)(2,1)S(1)} %pad_maximum_fusion.2), channel_id=1, source_target_pairs={{0,16},{4,20},{8,24},{12,28},{16,0},{20,4},{24,8},{28,12},{1,17},{... | collective-permute-start | bytes 4718600 | tf_op jit(solution)/shard_map/ppermute | solution.py:1322
  525.4 59.3 %collective-permute-start.5 = (bf16[256,3072]{1,0:T(8,128)(2,1)}, bf16[256,3072]{1,0:T(8,128)(2,1)}, u32[]{:S(2)}, u32[]{:S(2)}) collective-permute-start(bf16[256,3072]{1,0:T(8,128)(2,1)} %pad_maximum_fusion.1), channel_id=1, source_target_pairs={{0,8},{4,12},{8,0},{12,4},{16,24},{20,28},{24,16},{28,20},{1,9},{5... | collective-permute-start | bytes 4718600 | tf_op jit(solution)/shard_map/ppermute | solution.py:1322
  525.7 30.4 %slice-start = ((s8[4456448]{0:T(1024)(128)(4,1)}), s8[4194304]{0:T(1024)(128)(4,1)S(1)}, s32[]{:S(2)}) async-start(s8[4456448]{0:T(1024)(128)(4,1)} %bitcast.62), calls=%async_computation.4 | async-start | bytes 8388608
  554.7 61.6 %collective-permute-start.7 = (bf16[544,2048]{1,0:T(8,128)(2,1)}, bf16[544,2048]{1,0:T(8,128)(2,1)S(1)}, u32[]{:S(2)}, u32[]{:S(2)}) collective-permute-start(bf16[544,2048]{1,0:T(8,128)(2,1)} %shard_map.285), channel_id=1, source_target_pairs={{0,1},{1,0},{2,3},{3,2},{4,5},{5,4},{6,7},{7,6},{8,9},{9,8},{10,11... | collective-permute-start | bytes 6684680 | tf_op jit(solution)/shard_map/ppermute | solution.py:1322
  580.9 35.4 %collective-permute-start.8 = (bf16[128,3072]{1,0:T(8,128)(2,1)S(1)}, bf16[128,3072]{1,0:T(8,128)(2,1)}, u32[]{:S(2)}, u32[]{:S(2)}) collective-permute-start(bf16[128,3072]{1,0:T(8,128)(2,1)S(1)} %get-tuple-element.203), channel_id=1, source_target_pairs={{0,8},{4,12},{8,0},{12,4},{16,24},{20,28},{24,16},{28,20},{1,9},{5... | collective-permute-start | bytes 2359304 | tf_op jit(solution)/shard_map/ppermute | solution.py:1322
  581.4 35.0 %collective-permute-start.9 = (bf16[128,3072]{1,0:T(8,128)(2,1)S(1)}, bf16[128,3072]{1,0:T(8,128)(2,1)}, u32[]{:S(2)}, u32[]{:S(2)}) collective-permute-start(bf16[128,3072]{1,0:T(8,128)(2,1)S(1)} %get-tuple-element.204), channel_id=1, source_target_pairs={{0,16},{4,20},{8,24},{12,28},{16,0},{20,4},{24,8},{28,12},{1,17},{... | collective-permute-start | bytes 2359304 | tf_op jit(solution)/shard_map/ppermute | solution.py:1322
  588.8 49.5 %collective-permute-start.10 = (bf16[256,1536]{1,0:T(8,128)(2,1)S(1)}, bf16[256,1536]{1,0:T(8,128)(2,1)}, u32[]{:S(2)}, u32[]{:S(2)}) collective-permute-start(bf16[256,1536]{1,0:T(8,128)(2,1)S(1)} %slice.271), channel_id=1, source_target_pairs={{0,2},{1,3},{2,0},{3,1},{4,6},{5,7},{6,4},{7,5},{8,10},{9,11},{10,... | collective-permute-start | bytes 2359304 | tf_op jit(solution)/shard_map/ppermute | solution.py:1322
  619.2 66.0 %collective-permute-start.12 = (bf16[256,3072]{1,0:T(8,128)(2,1)S(1)}, bf16[256,3072]{1,0:T(8,128)(2,1)}, u32[]{:S(2)}, u32[]{:S(2)}) collective-permute-start(bf16[256,3072]{1,0:T(8,128)(2,1)S(1)} %pad_maximum_fusion.4), channel_id=1, source_target_pairs={{0,16},{4,20},{8,24},{12,28},{16,0},{20,4},{24,8},{28,12},{1,17},{... | collective-permute-start | bytes 4718600 | tf_op jit(solution)/shard_map/ppermute | solution.py:1322
  621.3 63.9 %collective-permute-start.11 = (bf16[256,3072]{1,0:T(8,128)(2,1)}, bf16[256,3072]{1,0:T(8,128)(2,1)S(1)}, u32[]{:S(2)}, u32[]{:S(2)}) collective-permute-start(bf16[256,3072]{1,0:T(8,128)(2,1)} %pad_maximum_fusion.3), channel_id=1, source_target_pairs={{0,8},{4,12},{8,0},{12,4},{16,24},{20,28},{24,16},{28,20},{1,9},{5... | collective-permute-start | bytes 4718600 | tf_op jit(solution)/shard_map/ppermute | solution.py:1322
  638.3 46.9 %copy-start.26 = (bf16[256,3072]{1,0:T(8,128)(2,1)S(1)}, bf16[256,3072]{1,0:T(8,128)(2,1)}, u32[]{:S(2)}) copy-start(bf16[256,3072]{1,0:T(8,128)(2,1)} %get-tuple-element.232) | copy-start | bytes 4718596
  683.2 52.3 %collective-permute-start.14 = (bf16[128,3072]{1,0:T(8,128)(2,1)S(1)}, bf16[128,3072]{1,0:T(8,128)(2,1)S(1)}, u32[]{:S(2)}, u32[]{:S(2)}) collective-permute-start(bf16[128,3072]{1,0:T(8,128)(2,1)S(1)} %get-tuple-element.228), channel_id=1, source_target_pairs={{0,8},{4,12},{8,0},{12,4},{16,24},{20,28},{24,16},{28,20},{1,9},{5... | collective-permute-start | bytes 2359304 | tf_op jit(solution)/shard_map/ppermute | solution.py:1322
  683.9 51.6 %collective-permute-start.15 = (bf16[128,3072]{1,0:T(8,128)(2,1)S(1)}, bf16[128,3072]{1,0:T(8,128)(2,1)S(1)}, u32[]{:S(2)}, u32[]{:S(2)}) collective-permute-start(bf16[128,3072]{1,0:T(8,128)(2,1)S(1)} %get-tuple-element.229), channel_id=1, source_target_pairs={{0,16},{4,20},{8,24},{12,28},{16,0},{20,4},{24,8},{28,12},{1,17},{... | collective-permute-start | bytes 2359304 | tf_op jit(solution)/shard_map/ppermute | solution.py:1322
  687.4 48.1 %collective-permute-start.13 = (bf16[256,1536]{1,0:T(8,128)(2,1)S(1)}, bf16[256,1536]{1,0:T(8,128)(2,1)S(1)}, u32[]{:S(2)}, u32[]{:S(2)}) collective-permute-start(bf16[256,1536]{1,0:T(8,128)(2,1)S(1)} %slice.270), channel_id=1, source_target_pairs={{0,2},{1,3},{2,0},{3,1},{4,6},{5,7},{6,4},{7,5},{8,10},{9,11},{10,... | collective-permute-start | bytes 2359304 | tf_op jit(solution)/shard_map/ppermute | solution.py:1322
  738.9 101.4 %all-to-all-start = ((bf16[4,544,1024]{2,1,0:T(8,128)(2,1)}), bf16[4,544,1024]{2,1,0:T(8,128)(2,1)}, u32[]{:S(2)}, u32[]{:S(2)}) async-start(bf16[4,544,1024]{2,1,0:T(8,128)(2,1)} %bitcast.64), calls=%async_computation | async-start | bytes 8912896 | tf_op jit(solution)/shard_map/all_to_all | solution.py:1350
  745.0 37.7 %collective-permute-start.23 = (bf16[256,3072]{1,0:T(8,128)(2,1)}, bf16[256,3072]{1,0:T(8,128)(2,1)}, u32[]{:S(2)}, u32[]{:S(2)}) collective-permute-start(bf16[256,3072]{1,0:T(8,128)(2,1)} %pad_maximum_fusion.6), channel_id=1, source_target_pairs={{0,16},{4,20},{8,24},{12,28},{16,0},{20,4},{24,8},{28,12},{1,17},{... | collective-permute-start | bytes 4718600 | tf_op jit(solution)/shard_map/ppermute | solution.py:1322
  745.8 37.6 %collective-permute-start.22 = (bf16[256,3072]{1,0:T(8,128)(2,1)}, bf16[256,3072]{1,0:T(8,128)(2,1)}, u32[]{:S(2)}, u32[]{:S(2)}) collective-permute-start(bf16[256,3072]{1,0:T(8,128)(2,1)} %pad_maximum_fusion.5), channel_id=1, source_target_pairs={{0,8},{4,12},{8,0},{12,4},{16,24},{20,28},{24,16},{28,20},{1,9},{5... | collective-permute-start | bytes 4718600 | tf_op jit(solution)/shard_map/ppermute | solution.py:1322
  761.8 88.5 %collective-permute-start.16 = (bf16[128,2048]{1,0:T(8,128)(2,1)S(1)}, bf16[128,2048]{1,0:T(8,128)(2,1)S(1)}, u32[]{:S(2)}, u32[]{:S(2)}) collective-permute-start(bf16[128,2048]{1,0:T(8,128)(2,1)S(1)} %get-tuple-element.248), channel_id=1, source_target_pairs={{0,8},{4,12},{8,0},{12,4},{16,24},{20,28},{24,16},{28,20},{1,9},{5... | collective-permute-start | bytes 1572872 | tf_op jit(solution)/shard_map/ppermute | solution.py:1322
  762.5 87.8 %collective-permute-start.17 = (bf16[128,2048]{1,0:T(8,128)(2,1)S(1)}, bf16[128,2048]{1,0:T(8,128)(2,1)}, u32[]{:S(2)}, u32[]{:S(2)}) collective-permute-start(bf16[128,2048]{1,0:T(8,128)(2,1)S(1)} %get-tuple-element.249), channel_id=1, source_target_pairs={{0,16},{4,20},{8,24},{12,28},{16,0},{20,4},{24,8},{28,12},{1,17},{... | collective-permute-start | bytes 1572872 | tf_op jit(solution)/shard_map/ppermute | solution.py:1322
  772.9 67.4 %copy-start.2 = (f32[544,128]{1,0:T(8,128)S(1)}, f32[544,128]{1,0:T(8,128)}, u32[]{:S(2)}) copy-start(f32[544,128]{1,0:T(8,128)} %copy-done.1) | copy-start | bytes 835588
  772.9 67.4 %copy-start.4 = (f32[544,128]{1,0:T(8,128)S(1)}, f32[544,128]{1,0:T(8,128)}, u32[]{:S(2)}) copy-start(f32[544,128]{1,0:T(8,128)} %copy-done.3) | copy-start | bytes 835588
  851.8 39.2 %collective-permute-start.21 = (bf16[256,2048]{1,0:T(8,128)(2,1)S(1)}, bf16[256,2048]{1,0:T(8,128)(2,1)S(1)}, u32[]{:S(2)}, u32[]{:S(2)}) collective-permute-start(bf16[256,2048]{1,0:T(8,128)(2,1)S(1)} %pad_maximum_fusion.8), channel_id=1, source_target_pairs={{0,16},{4,20},{8,24},{12,28},{16,0},{20,4},{24,8},{28,12},{1,17},{... | collective-permute-start | bytes 3145736 | tf_op jit(solution)/shard_map/ppermute | solution.py:1322
  852.6 38.5 %collective-permute-start.20 = (bf16[256,2048]{1,0:T(8,128)(2,1)S(1)}, bf16[256,2048]{1,0:T(8,128)(2,1)S(1)}, u32[]{:S(2)}, u32[]{:S(2)}) collective-permute-start(bf16[256,2048]{1,0:T(8,128)(2,1)S(1)} %pad_maximum_fusion.7), channel_id=1, source_target_pairs={{0,8},{4,12},{8,0},{12,4},{16,24},{20,28},{24,16},{28,20},{1,9},{5... | collective-permute-start | bytes 3145736 | tf_op jit(solution)/shard_map/ppermute | solution.py:1322
  856.6 34.4 %collective-permute-start.24 = (bf16[256,1536]{1,0:T(8,128)(2,1)S(1)}, bf16[256,1536]{1,0:T(8,128)(2,1)S(1)}, u32[]{:S(2)}, u32[]{:S(2)}) collective-permute-start(bf16[256,1536]{1,0:T(8,128)(2,1)S(1)} %slice.269), channel_id=1, source_target_pairs={{0,2},{1,3},{2,0},{3,1},{4,6},{5,7},{6,4},{7,5},{8,10},{9,11},{10,... | collective-permute-start | bytes 2359304 | tf_op jit(solution)/shard_map/ppermute | solution.py:1322
  871.0 20.1 %collective-permute-start.18 = (bf16[128,2048]{1,0:T(8,128)(2,1)S(1)}, bf16[128,2048]{1,0:T(8,128)(2,1)}, u32[]{:S(2)}, u32[]{:S(2)}) collective-permute-start(bf16[128,2048]{1,0:T(8,128)(2,1)S(1)} %get-tuple-element.263), channel_id=1, source_target_pairs={{0,8},{4,12},{8,0},{12,4},{16,24},{20,28},{24,16},{28,20},{1,9},{5... | collective-permute-start | bytes 1572872 | tf_op jit(solution)/shard_map/ppermute | solution.py:1322
  871.7 19.4 %collective-permute-start.19 = (bf16[128,2048]{1,0:T(8,128)(2,1)S(1)}, bf16[128,2048]{1,0:T(8,128)(2,1)}, u32[]{:S(2)}, u32[]{:S(2)}) collective-permute-start(bf16[128,2048]{1,0:T(8,128)(2,1)S(1)} %get-tuple-element.264), channel_id=1, source_target_pairs={{0,16},{4,20},{8,24},{12,28},{16,0},{20,4},{24,8},{28,12},{1,17},{... | collective-permute-start | bytes 1572872 | tf_op jit(solution)/shard_map/ppermute | solution.py:1322
  892.7 45.7 %all-to-all-start.1 = ((bf16[4,256,512]{2,1,0:T(8,128)(2,1)}), bf16[4,256,512]{2,1,0:T(8,128)(2,1)}, u32[]{:S(2)}, u32[]{:S(2)}) async-start(bf16[4,256,512]{2,1,0:T(8,128)(2,1)} %bitcast.49), calls=%async_computation.1 | async-start | bytes 2097152 | tf_op jit(solution)/shard_map/all_to_all | solution.py:1350
  900.7 37.7 %collective-permute-start.26 = (bf16[256,2048]{1,0:T(8,128)(2,1)}, bf16[256,2048]{1,0:T(8,128)(2,1)}, u32[]{:S(2)}, u32[]{:S(2)}) collective-permute-start(bf16[256,2048]{1,0:T(8,128)(2,1)} %pad_maximum_fusion.10), channel_id=1, source_target_pairs={{0,16},{4,20},{8,24},{12,28},{16,0},{20,4},{24,8},{28,12},{1,17},{... | collective-permute-start | bytes 3145736 | tf_op jit(solution)/shard_map/ppermute | solution.py:1322
  902.1 36.4 %collective-permute-start.25 = (bf16[256,2048]{1,0:T(8,128)(2,1)}, bf16[256,2048]{1,0:T(8,128)(2,1)}, u32[]{:S(2)}, u32[]{:S(2)}) collective-permute-start(bf16[256,2048]{1,0:T(8,128)(2,1)} %pad_maximum_fusion.9), channel_id=1, source_target_pairs={{0,8},{4,12},{8,0},{12,4},{16,24},{20,28},{24,16},{28,20},{1,9},{5... | collective-permute-start | bytes 3145736 | tf_op jit(solution)/shard_map/ppermute | solution.py:1322
  906.4 32.1 %collective-permute-start.27 = (bf16[128,2048]{1,0:T(8,128)(2,1)S(1)}, bf16[128,2048]{1,0:T(8,128)(2,1)}, u32[]{:S(2)}, u32[]{:S(2)}) collective-permute-start(bf16[128,2048]{1,0:T(8,128)(2,1)S(1)} %get-tuple-element.266), channel_id=1, source_target_pairs={{0,8},{4,12},{8,0},{12,4},{16,24},{20,28},{24,16},{28,20},{1,9},{5... | collective-permute-start | bytes 1572872 | tf_op jit(solution)/shard_map/ppermute | solution.py:1322
  907.1 31.3 %collective-permute-start.28 = (bf16[128,2048]{1,0:T(8,128)(2,1)S(1)}, bf16[128,2048]{1,0:T(8,128)(2,1)}, u32[]{:S(2)}, u32[]{:S(2)}) collective-permute-start(bf16[128,2048]{1,0:T(8,128)(2,1)S(1)} %get-tuple-element.267), channel_id=1, source_target_pairs={{0,16},{4,20},{8,24},{12,28},{16,0},{20,4},{24,8},{28,12},{1,17},{... | collective-permute-start | bytes 1572872 | tf_op jit(solution)/shard_map/ppermute | solution.py:1322
  940.9 31.1 %collective-permute-start.35 = (bf16[256,2048]{1,0:T(8,128)(2,1)}, bf16[256,2048]{1,0:T(8,128)(2,1)}, u32[]{:S(2)}, u32[]{:S(2)}) collective-permute-start(bf16[256,2048]{1,0:T(8,128)(2,1)} %pad_maximum_fusion.12), channel_id=1, source_target_pairs={{0,16},{4,20},{8,24},{12,28},{16,0},{20,4},{24,8},{28,12},{1,17},{... | collective-permute-start | bytes 3145736 | tf_op jit(solution)/shard_map/ppermute | solution.py:1322
  943.8 28.1 %collective-permute-start.34 = (bf16[256,2048]{1,0:T(8,128)(2,1)S(1)}, bf16[256,2048]{1,0:T(8,128)(2,1)}, u32[]{:S(2)}, u32[]{:S(2)}) collective-permute-start(bf16[256,2048]{1,0:T(8,128)(2,1)S(1)} %pad_maximum_fusion.11), channel_id=1, source_target_pairs={{0,8},{4,12},{8,0},{12,4},{16,24},{20,28},{24,16},{28,20},{1,9},{5... | collective-permute-start | bytes 3145736 | tf_op jit(solution)/shard_map/ppermute | solution.py:1322
  947.3 28.8 %all-to-all-start.2 = ((bf16[4,256,512]{2,1,0:T(8,128)(2,1)}), bf16[4,256,512]{2,1,0:T(8,128)(2,1)}, u32[]{:S(2)}, u32[]{:S(2)}) async-start(bf16[4,256,512]{2,1,0:T(8,128)(2,1)} %bitcast.47), calls=%async_computation.2 | async-start | bytes 2097152 | tf_op jit(solution)/shard_map/all_to_all | solution.py:1350
  955.7 1.2 collective-permute-start.29
  956.9 14.2 %collective-permute-start.30 = (f32[2,544]{1,0:T(2,128)S(1)}, f32[2,544]{1,0:T(2,128)S(1)}, u32[]{:S(2)}, u32[]{:S(2)}) collective-permute-start(f32[2,544]{1,0:T(2,128)S(1)} %slice.227), channel_id=1, source_target_pairs={{0,16},{4,20},{8,24},{12,28},{16,0},{20,4},{24,8},{28,12},{1,17},{... | collective-permute-start | bytes 13064 | tf_op jit(solution)/shard_map/ppermute | solution.py:1322
  971.1 9.2 collective-permute-start.31
  976.1 33.4 %all-to-all-start.3 = ((bf16[4,256,512]{2,1,0:T(8,128)(2,1)}), bf16[4,256,512]{2,1,0:T(8,128)(2,1)}, u32[]{:S(2)}, u32[]{:S(2)}) async-start(bf16[4,256,512]{2,1,0:T(8,128)(2,1)} %bitcast.66), calls=%async_computation.3 | async-start | bytes 2097152 | tf_op jit(solution)/shard_map/all_to_all | solution.py:1350
  980.4 16.9 %collective-permute-start.32 = (f32[1,544]{1,0:T(1,128)S(1)}, f32[1,544]{1,0:T(1,128)S(1)}, u32[]{:S(2)}, u32[]{:S(2)}) collective-permute-start(f32[1,544]{1,0:T(1,128)S(1)} %slice_add_fusion.5), channel_id=1, source_target_pairs={{0,1},{1,0},{2,3},{3,2},{4,5},{5,4},{6,7},{7,6},{8,9},{9,8},{10,11... | collective-permute-start | bytes 6536 | tf_op jit(solution)/shard_map/ppermute | solution.py:1322
  997.3 8.7 collective-permute-start.33
  (41 other events, 325.9 us)
